TPU v7x, 32 devices: a whole 2x2x4 slice. The times are simulated.
32 devices in a mesh: groups: 1, sec: 32 (over z, y, x, core).
Axes of the slice: x: 2, y: 2, z: 4, core: 2. Of those that a mesh axis runs over, the one named last changes fastest.
Arguments:
- wavefunction: bfloat16 [32, 192, 192], P(('groups', 'sec')), may hold values from -6 to 6
- left_environment: bfloat16 [192, 192, 768], P(('groups', 'sec'))
- right_environment: bfloat16 [192, 192, 768], P(('groups', 'sec'))
- sector_sizes: int32 [2, 2], P(None, 'groups'), may hold values from 64 to 768, as said below
- pairing: int32 [2], P('groups'), may hold values from 0 to 1, each once
- term_mask: int32 [2, 24], P('groups'), may hold values 0 or 1
- coupling: int32 [2, 24], P('groups'), may hold values from 0 to 1
Outputs:
- first_image: bfloat16 [32, 192, 192], P(('groups', 'sec'))
- second_image: bfloat16 [32, 192, 192], P(('groups', 'sec'))
Inputs may be any that keep to these rules, and one draw needn't show every extreme that they name: `sector_sizes`: each row reaches 768. `pairing`: A permutation of the sectors.
All inputs are finite; a program needn't handle non-finite values.
Results may differ from a plain program's by a relative error of at most 0.007.
Values may be sent and summed in bfloat16 or wider, within the bound.
No kernel may reach another device: no remote copies, remote signals or barrier semaphores. Data moves between devices by JAX's collectives and lax.ppermute only.
A program may use at most 128 MiB of HBM per device.

v0:
```python
import jax
import jax.numpy as jnp
from jax import lax
from jax.sharding import PartitionSpec as P

GRID_ROWS = 4
GRID_COLS = 4


EPSILON = 1e-06


def from_partner(block, axis, apart):
    count = lax.axis_size(axis)
    route = []
    for low in range(count):
        high = low | 1 << apart
        if high != low and high < count:
            route += [(low, high), (high, low)]
    return lax.ppermute(block, axis, route)


def doubling(block_part, levels, device_index, sender):
    for bit_number, axis_dim in levels:
        partner_part = sender(block_part, bit_number)
        high_side = device_index >> bit_number & 1 == 1
        block_part = jnp.where(
            high_side,
            jnp.concatenate([partner_part, block_part], axis_dim),
            jnp.concatenate([block_part, partner_part], axis_dim),
        )
    return block_part


def halving(partial_sum, levels, device_index, sender):
    for bit_number, axis_dim in levels:
        middle = partial_sum.shape[axis_dim] // 2
        low_half = lax.slice_in_dim(partial_sum, 0, middle, axis=axis_dim)
        high_half = lax.slice_in_dim(partial_sum, middle, 2 * middle, axis=axis_dim)
        high_side = device_index >> bit_number & 1 == 1
        kept_half = jnp.where(high_side, high_half, low_half)
        sent_half = jnp.where(high_side, low_half, high_half)
        partial_sum = kept_half + sender(sent_half, bit_number)
    return partial_sum


def on_device(
    wavefunction, left_environment, right_environment, sector_sizes, pairing, term_mask, coupling
):
    tile_rows = wavefunction.shape[1]
    tile_cols = wavefunction.shape[2]
    terms_here = left_environment.shape[0]
    sector_count = sector_sizes.shape[1]
    device_index = lax.axis_index("sec")
    sector = device_index // (GRID_ROWS * GRID_COLS)
    row_group = device_index // GRID_COLS % GRID_ROWS
    col_group = device_index % GRID_COLS
    positions = jnp.arange(sector_count, dtype=jnp.int32)
    is_sector = positions == sector
    left_size = jnp.sum(jnp.where(is_sector, sector_sizes[0], 0))
    partner = jnp.sum(jnp.where(is_sector, pairing, 0))
    right_size = jnp.sum(jnp.where(positions == partner, sector_sizes[1], 0))
    term_row = jnp.sum(jnp.where(is_sector[:, None], term_mask, 0), axis=0)
    weights = lax.dynamic_slice_in_dim(term_row, col_group * terms_here, terms_here).astype(
        jnp.float32
    )
    source_row = jnp.sum(jnp.where(is_sector[:, None], coupling, 0), axis=0)
    my_sources = lax.dynamic_slice_in_dim(source_row, col_group * terms_here, terms_here)
    row_ids = row_group * tile_rows + jnp.arange(tile_rows, dtype=jnp.int32)
    col_ids = col_group * tile_cols + jnp.arange(tile_cols, dtype=jnp.int32)
    live_mask = ((row_ids < left_size)[:, None] & (col_ids < right_size)[None, :]).astype(
        jnp.float32
    )
    capacity = tile_rows * GRID_ROWS

    def fetch(tile_data):
        gathered = lax.all_gather(tile_data[None], "sec", axis=0, tiled=True)
        tiled = gathered.reshape(sector_count, GRID_ROWS, GRID_COLS, tile_rows, tile_cols)
        return jnp.take(tiled, my_sources, axis=0)

    right_full = doubling(
        right_environment,
        ((2, 1), (3, 1)),
        device_index,
        lambda part_data, bit_number: from_partner(part_data, "sec", bit_number),
    )
    left_split = left_environment.reshape(terms_here, tile_rows, GRID_ROWS, tile_rows)

    def operate(tile_data):
        sources = fetch(tile_data)
        mixed_terms = jnp.einsum(
            "kria,kijab->krjb", left_split, sources, preferred_element_type=jnp.float32
        )
        mixed_terms = mixed_terms.reshape(terms_here, tile_rows, capacity)
        mixed_terms = (mixed_terms * weights[:, None, None]).astype(jnp.bfloat16)
        summed = jnp.einsum(
            "krs,kst->rt", mixed_terms, right_full, preferred_element_type=jnp.float32
        )
        return halving(
            summed,
            ((1, 1), (0, 1)),
            device_index,
            lambda part_data, bit_number: from_partner(part_data, "sec", bit_number),
        )

    start_tile = (wavefunction[0].astype(jnp.float32) * live_mask).astype(jnp.bfloat16)
    first_tile = (operate(start_tile) * live_mask).astype(jnp.bfloat16)
    start_value = start_tile.astype(jnp.float32)
    first_value = first_tile.astype(jnp.float32)
    inner_sum, square = lax.psum(
        (jnp.sum(start_value * first_value), jnp.sum(start_value * start_value)), "sec"
    )
    quotient = inner_sum / square
    residual = first_value - quotient * start_value
    residual_square = lax.psum(jnp.sum(residual * residual), "sec")
    second_input = (residual * lax.rsqrt(residual_square / square + EPSILON)).astype(jnp.bfloat16)
    second_tile = (operate(second_input) * live_mask).astype(jnp.bfloat16)
    return (first_tile[None], second_tile[None])


def solution(mesh):
    return jax.shard_map(
        on_device,
        mesh=mesh,
        in_specs=(
            P(("groups", "sec"), None, None),
            P(("groups", "sec"), None, None),
            P(("groups", "sec"), None, None),
            P(None, "groups"),
            P("groups"),
            P("groups", None),
            P("groups", None),
        ),
        out_specs=(P(("groups", "sec"), None, None), P(("groups", "sec"), None, None)),
        check_vma=False,
    )
```

profile of v0, /device:TPU:0, one launch (start us, length us, event | category | flops | bytes accessed | tf_op | source)
XLA Modules:
  0.0 362.4 jit_solution(6108078952009153565)
XLA Ops:
  8.5 2.1 fusion.26
  13.7 3.0 collective-permute-start
  16.8 41.0 %collective-permute-done = bf16[6,192,768]{2,1,0:T(8,128)(2,1)} collective-permute-done((bf16[6,192,768]{2,1,0:T(8,128)(2,1)}, bf16[6,192,768]{2,1,0:T(8,128)(2,1)}, u32[]{:S(2)}, u32[]{:S(2)}) %collective-permute-start) | collective-permute-done | bytes 1769504 | tf_op jit(solution)/shard_map/ppermute | solution.py:20
  57.8 3.9 %maximum_select_fusion.1 = bf16[6,384,768]{2,1,0:T(8,128)(2,1)S(1)} fusion(bf16[6,192,768]{2,1,0:T(8,128)(2,1)} %param.11, bf16[6,192,768]{2,1,0:T(8,128)(2,1)} %collective-permute-done, pred[]{:T(512)S(6)} %eq.40), kind=kLoop, calls=%fused_computation.11 | loop fusion | flops 15925248 | bytes 7077889 | tf_op jit(solution)/shard_map/jit(_where)/select_n | solution.py:27
  61.7 1.9 collective-permute-start.1
  63.5 5.8 %reshape.85 = bf16[6,192,4,192]{3,2,1,0:T(4,128)(2,1)} reshape(bf16[6,192,768]{2,1,0:T(8,128)(2,1)} %param.10) | data formatting | bytes 3538944 | tf_op jit(solution)/shard_map/reshape | solution.py:87
  70.2 6.9 %all-gather.4.cloned.1.call-done = bf16[32,192,192]{2,1,0:T(8,128)(2,1)} async-done(((bf16[1,192,192]{2,1,0:T(8,128)(2,1)}), bf16[32,192,192]{2,1,0:T(8,128)(2,1)}) %all-gather.4.cloned.1.call-update) | async-done | bytes 2359312 | tf_op jit(solution)/shard_map/all_gather | solution.py:77
  77.1 7.1 %gather_fusion = bf16[6,4,4,192,192]{4,3,2,1,0:T(8,128)(2,1)} fusion(bf16[2,4,4,192,192]{4,3,2,1,0:T(8,128)(2,1)} %bitcast.53, s32[1024]{0:T(1024)S(1)} %pad_clamp_fusion), kind=kCustom, calls=%fused_computation.clone | custom fusion | bytes 14155800 | tf_op jit(solution)/shard_map/jit(_take)/gather | solution.py:79
  84.2 10.1 %fusion.2 = f32[6,4,192,192,1]{3,2,1,4,0:T(8,128)} fusion(bf16[6,4,4,192,192]{4,3,2,1,0:T(8,128)(2,1)} %gather_fusion, pred[6]{0:T(512)(128)(4,1)S(1)} %get-tuple-element.12, bf16[6,192,4,192,1]{3,2,1,0,4:T(4,128)(2,1)} %bitcast.57), kind=kOutput, calls=%fused_computation.4 | convolution fusion | flops 1362493440 | bytes 12386310 | tf_op jit(solution)/shard_map/kria,kijab->krjb/dot_general | solution.py:91
  94.3 5.6 %copy.21 = f32[6,192,768]{2,1,0:T(8,128)} copy(f32[6,192,768]{1,2,0:T(8,128)} %bitcast.56) | data formatting | bytes 7077888 | tf_op jit(solution)/shard_map/reshape | solution.py:94
  99.9 45.9 %collective-permute-done.1 = bf16[6,384,768]{2,1,0:T(8,128)(2,1)} collective-permute-done((bf16[6,384,768]{2,1,0:T(8,128)(2,1)S(1)}, bf16[6,384,768]{2,1,0:T(8,128)(2,1)}, u32[]{:S(2)}, u32[]{:S(2)}) %collective-permute-start.1) | collective-permute-done | bytes 3538976 | tf_op jit(solution)/shard_map/ppermute | solution.py:20
  145.8 6.5 %fusion.17 = f32[192,768]{1,0:T(8,128)S(1)} fusion(f32[6,192,768]{2,1,0:T(8,128)} %copy.21, f32[6]{0:T(128)} %dynamic-slice_convert_fusion, bf16[6,384,768]{2,1,0:T(8,128)(2,1)S(1)} %maximum_select_fusion.1, bf16[6,384,768]{2,1,0:T(8,128)(2,1)} %collective-permute-done.1, pred[]{:T(512)S(6)} %eq.39), kind=kOutput, calls=%fused_computation.23 | convolution fusion | flops 1392574464 | bytes 11206681 | tf_op jit(solution)/shard_map/krs,kst->rt/dot_general | solution.py:96
  155.3 6.9 %collective-permute-done.2 = f32[192,384]{1,0:T(8,128)} collective-permute-done((f32[192,384]{1,0:T(8,128)}, f32[192,384]{1,0:T(8,128)}, u32[]{:S(2)}, u32[]{:S(2)}) %collective-permute-start.2) | collective-permute-done | bytes 294944 | tf_op jit(solution)/shard_map/ppermute | solution.py:20
  165.1 2.4 fusion.20
  167.4 40.8 %all-reduce = (f32[]{:T(128)}, f32[]{:T(128)}) all-reduce(f32[]{:T(128)} %get-tuple-element.4, f32[]{:T(128)} %get-tuple-element.3), channel_id=1, replica_groups=mesh['groups'=1,'sec'=32] {'sec'}, use_global_device_ids=true, to_apply=%region_6.8 | all-reduce | flops 2 | bytes 16 | tf_op jit(solution)/shard_map/psum | solution.py:110
  209.4 1.8 multiply_reduce_fusion
  211.2 39.5 %psum.23 = f32[]{:T(128)} all-reduce(f32[]{:T(128)} %multiply_reduce_fusion), channel_id=1, replica_groups=mesh['groups'=1,'sec'=32] {'sec'}, use_global_device_ids=true, to_apply=%region_10.12 | all-reduce | flops 1 | bytes 8 | tf_op jit(solution)/shard_map/psum | solution.py:115
  252.2 1.7 multiply_convert_fusion.8
  253.9 60.3 %all-gather.6.cloned.1.call-done = bf16[6144,192]{1,0:T(8,128)(2,1)} async-done(((bf16[192,192]{1,0:T(8,128)(2,1)}), bf16[6144,192]{1,0:T(8,128)(2,1)}) %all-gather.6.cloned.1.call-update) | async-done | bytes 2359312 | tf_op jit(solution)/shard_map/all_gather | solution.py:77
  314.2 7.1 %gather_fusion.1 = bf16[6,4,4,192,192]{4,3,2,1,0:T(8,128)(2,1)} fusion(bf16[2,4,4,192,192]{4,3,2,1,0:T(8,128)(2,1)} %bitcast.54, s32[1024]{0:T(1024)S(1)} %pad_clamp_fusion), kind=kCustom, calls=%fused_computation.1.clone | custom fusion | bytes 14155800 | tf_op jit(solution)/shard_map/jit(_take)/gather | solution.py:79
  321.3 10.1 %fusion = f32[6,4,192,192,1]{3,2,1,4,0:T(8,128)} fusion(bf16[6,4,4,192,192]{4,3,2,1,0:T(8,128)(2,1)} %gather_fusion.1, pred[6]{0:T(512)(128)(4,1)S(1)} %get-tuple-element.12, bf16[6,192,4,192,1]{3,2,1,0,4:T(4,128)(2,1)} %bitcast.58), kind=kOutput, calls=%fused_computation.2 | convolution fusion | flops 1362493440 | bytes 12386310 | tf_op jit(solution)/shard_map/kria,kijab->krjb/dot_general | solution.py:91
  331.4 5.6 %copy.24 = f32[6,192,768]{2,1,0:T(8,128)} copy(f32[6,192,768]{1,2,0:T(8,128)} %bitcast.55) | data formatting | bytes 7077888 | tf_op jit(solution)/shard_map/reshape | solution.py:94
  337.0 6.5 %fusion.16 = f32[192,768]{1,0:T(8,128)S(1)} fusion(f32[6,192,768]{2,1,0:T(8,128)} %copy.24, f32[6]{0:T(128)S(1)} %copy-done.3, bf16[6,384,768]{2,1,0:T(8,128)(2,1)S(1)} %maximum_select_fusion.1, bf16[6,384,768]{2,1,0:T(8,128)(2,1)} %collective-permute-done.1, pred[]{:T(512)S(6)} %eq.39), kind=kOutput, calls=%fused_computation.22 | convolution fusion | flops 1392574464 | bytes 11206681 | tf_op jit(solution)/shard_map/krs,kst->rt/dot_general | solution.py:96
  345.2 7.9 %collective-permute-done.4 = f32[192,384]{1,0:T(8,128)S(1)} collective-permute-done((f32[192,384]{1,0:T(8,128)S(1)}, f32[192,384]{1,0:T(8,128)S(1)}, u32[]{:S(2)}, u32[]{:S(2)}) %collective-permute-start.4) | collective-permute-done | bytes 294944 | tf_op jit(solution)/shard_map/ppermute | solution.py:20
  (33 shorter events, 15.1 us)
Async XLA Ops:
  7.2 69.9 %all-gather.4.cloned.1.call-start = ((), (), s32[]{:S(2)}) async-start(), calls=%async_computation | async-start | bytes 3244032 | tf_op jit(solution)/shard_map/all_gather | solution.py:77
  13.7 300.5 %all-gather.6.cloned.1.call-start = ((), (), s32[]{:S(2)}) async-start(), calls=%async_computation.1 | async-start | bytes 3244032 | tf_op jit(solution)/shard_map/all_gather | solution.py:77
  13.7 44.1 %collective-permute-start = (bf16[6,192,768]{2,1,0:T(8,128)(2,1)}, bf16[6,192,768]{2,1,0:T(8,128)(2,1)}, u32[]{:S(2)}, u32[]{:S(2)}) collective-permute-start(bf16[6,192,768]{2,1,0:T(8,128)(2,1)} %param.11), channel_id=1, source_target_pairs={{0,4},{4,0},{1,5},{5,1},{2,6},{6,2},{3,7},{7,3},{8,12},{12,8},{9,1... | collective-permute-start | bytes 5308424 | tf_op jit(solution)/shard_map/ppermute | solution.py:20
  16.8 52.6 %copy-start.1 = (s32[2,24]{1,0:T(2,128)S(1)}, s32[2,24]{1,0:T(2,128)}, u32[]{:S(2)}) copy-start(s32[2,24]{1,0:T(2,128)} %param.14) | copy-start | bytes 580
  16.8 52.6 %copy-start.2 = (s32[2,24]{1,0:T(2,128)S(1)}, s32[2,24]{1,0:T(2,128)}, u32[]{:S(2)}) copy-start(s32[2,24]{1,0:T(2,128)} %param.15) | copy-start | bytes 580
  61.7 84.1 %collective-permute-start.1 = (bf16[6,384,768]{2,1,0:T(8,128)(2,1)S(1)}, bf16[6,384,768]{2,1,0:T(8,128)(2,1)}, u32[]{:S(2)}, u32[]{:S(2)}) collective-permute-start(bf16[6,384,768]{2,1,0:T(8,128)(2,1)S(1)} %maximum_select_fusion.1), channel_id=1, source_target_pairs={{0,8},{8,0},{1,9},{9,1},{2,10},{10,2},{3,11},{11,3},{4,12},{12,4},... | collective-permute-start | bytes 10616840 | tf_op jit(solution)/shard_map/ppermute | solution.py:20
  152.3 0.8 copy-start
  153.8 8.4 %collective-permute-start.2 = (f32[192,384]{1,0:T(8,128)}, f32[192,384]{1,0:T(8,128)}, u32[]{:S(2)}, u32[]{:S(2)}) collective-permute-start(f32[192,384]{1,0:T(8,128)} %slice_select_fusion.1), channel_id=1, source_target_pairs={{0,2},{2,0},{1,3},{3,1},{4,6},{6,4},{5,7},{7,5},{8,10},{10,8},{9,1... | collective-permute-start | bytes 884744 | tf_op jit(solution)/shard_map/ppermute | solution.py:20
  163.6 1.5 collective-permute-start.3
  331.4 5.6 %copy-start.3 = (f32[6]{0:T(128)S(1)}, f32[6]{0:T(128)}, u32[]{:S(2)}) copy-start(f32[6]{0:T(128)} %dynamic-slice_convert_fusion) | copy-start | bytes 76
  343.6 9.5 %collective-permute-start.4 = (f32[192,384]{1,0:T(8,128)S(1)}, f32[192,384]{1,0:T(8,128)S(1)}, u32[]{:S(2)}, u32[]{:S(2)}) collective-permute-start(f32[192,384]{1,0:T(8,128)S(1)} %slice_select_fusion), channel_id=1, source_target_pairs={{0,2},{2,0},{1,3},{3,1},{4,6},{6,4},{5,7},{7,5},{8,10},{10,8},{9,1... | collective-permute-start | bytes 884744 | tf_op jit(solution)/shard_map/ppermute | solution.py:20
  353.2 1.5 collective-permute-start.5
Sparse Core Ops, SparseCore 0:
  13.8 63.2 all-gather.3
  254.0 60.1 all-gather.5
where the time goes:
time: 363 us; the launch traced here: 362 us
  waiting for transfers between devices  172 us (47%)
  blocking collectives  80.3 us (22%)
  matrix products  33.3 us (9%)
  local copies, waits for them, and re-layouts  32 us (9%)
  other arithmetic  19.9 us (5%)
  between operations  16.9 us (5%)
  starting transfers between devices  8.18 us (2%)
    ppermute x6, waiting for transfers between devices, from_partner(): return lax.ppermute(block, axis, route)  105 us
    all_gather x2, waiting for transfers between devices, fetch(): gathered = lax.all_gather(tile_data[None], 'sec', axis=0, tiled=True)  67.2 us
    psum x1, blocking collectives, on_device(): lax.psum((jnp.sum(start_value * first_value), jnp.sum(start_value * start...  40.8 us
    psum x1, blocking collectives, on_device(): residual_square = lax.psum(jnp.sum(residual * residual), 'sec')  39.5 us
    dot_general x2, matrix products, operate(): jnp.einsum('kria,kijab->krjb', left_split, sources, preferred_element_typ...  20.2 us
    gather x2, local copies, waits for them, and re-layouts, fetch(): return jnp.take(tiled, my_sources, axis=0)  14.1 us
    dot_general x2, matrix products, operate(): jnp.einsum('krs,kst->rt', mixed_terms, right_full, preferred_element_type...  13.1 us
    reshape x2, local copies, waits for them, and re-layouts, operate(): mixed_terms = mixed_terms.reshape(terms_here, tile_rows, capacity)  11.2 us
  transfers between devices with their start and end apart: 8, of which 8 were waited for; matrix products, arithmetic and copies ran while one was open for 9% of the time, Pallas kernels for 0%

commit v1 on v0

v1 whole, which is shorter than its diff:
```python
import jax
import jax.numpy as jnp
from jax import lax
from jax.experimental import pallas as pl
from jax.experimental.pallas import tpu as pltpu
from jax.sharding import PartitionSpec as P

GRID_ROWS = 4
GRID_COLS = 4
CORE, XBIT, YBIT, ZBIT = 1, 2, 4, 8
SECTOR_BIT = GRID_ROWS * GRID_COLS
EPSILON = 1e-06
SCALAR_ROWS = 16


def exchange(block, flip):
    count = lax.axis_size("sec")
    return lax.ppermute(block, "sec", [(i, i ^ flip) for i in range(count)])


def swap_xz(block):
    count = lax.axis_size("sec")
    route = []
    for i in range(count):
        x, z = i // XBIT % 2, i // ZBIT % 2
        route.append((i, i - x * XBIT - z * ZBIT + z * XBIT + x * ZBIT))
    return lax.ppermute(block, "sec", route)


def place():
    index = lax.axis_index("sec")
    return index % 2, index // XBIT % 2, index // YBIT % 2, index // ZBIT % 2, index // SECTOR_BIT


def smem():
    return pl.BlockSpec(memory_space=pltpu.SMEM)


def vmem():
    return pl.BlockSpec(memory_space=pltpu.VMEM)


def live_block(sizes, row_start, col_start, shape):
    rows = row_start + lax.broadcasted_iota(jnp.int32, shape, 0)
    cols = col_start + lax.broadcasted_iota(jnp.int32, shape, 1)
    return (rows < sizes[0]) & (cols < sizes[1])


def sizes_of(sizes_ref, pairing_ref, sector):
    return sizes_ref[0, sector], sizes_ref[1, pairing_ref[sector]]


def start_kernel(index_ref, sizes_ref, pairing_ref, wave_ref, out_ref):
    index = index_ref[0]
    sector = index // SECTOR_BIT
    rows, cols = out_ref.shape
    keep = live_block(
        sizes_of(sizes_ref, pairing_ref, sector),
        index // GRID_COLS % GRID_ROWS * rows,
        index % GRID_COLS * cols,
        (rows, cols),
    )
    out_ref[...] = jnp.where(keep, wave_ref[0].astype(jnp.float32), 0.0).astype(jnp.bfloat16)


def copies_in(index, refs, scratch, sems, count):
    left_own, left_peer, right_own, right_peer = refs
    lefts, rights = scratch
    tile = left_own.shape[1]
    y, z = index // YBIT % 2, index // ZBIT % 2
    found = []
    for k in range(count):
        found.append(
            [
                pltpu.make_async_copy(left_own.at[k], lefts.at[k, pl.ds(z * tile, tile)], sems.at[k, 0]),
                pltpu.make_async_copy(
                    left_peer.at[k], lefts.at[k, pl.ds((1 - z) * tile, tile)], sems.at[k, 1]
                ),
                pltpu.make_async_copy(
                    right_own.at[k], rights.at[pl.ds(k * 2 * tile + y * tile, tile)], sems.at[k, 2]
                ),
                pltpu.make_async_copy(
                    right_peer.at[k], rights.at[pl.ds(k * 2 * tile + (1 - y) * tile, tile)], sems.at[k, 3]
                ),
            ]
        )
    return found


def apply_terms(index, first_term, mask_ref, coupling_ref, vector, lefts, rights, mixed, copies):
    sector = index // SECTOR_BIT
    group = index % GRID_COLS
    count, height, _ = lefts.shape
    width = vector.shape[2]
    terms = mask_ref.shape[1] // GRID_COLS
    for k in range(count):
        term = group * terms + first_term + k
        for copy in copies[k]:
            copy.wait()
        source = coupling_ref[sector, term]
        product = jnp.dot(lefts[k], vector[source], preferred_element_type=jnp.float32)
        weight = mask_ref[sector, term].astype(jnp.float32)
        mixed[:, k * width : (k + 1) * width] = (product * weight).astype(jnp.bfloat16)
    return jnp.dot(mixed[...], rights[...], preferred_element_type=jnp.float32)


def first_kernel(
    first_term,
    last,
    index_ref,
    mask_ref,
    coupling_ref,
    pieces_ref,
    left_own,
    left_peer,
    right_own,
    right_peer,
    *rest,
):
    index = index_ref[0]
    rest = list(rest)
    before = rest.pop(0) if first_term else None
    if last:
        kept_ref, sent_ref = rest[:2]
        rest = rest[2:]
    else:
        total_ref = rest[0]
        rest = rest[1:]
    vector, lefts, rights, mixed, sems = rest
    count, height, _ = lefts.shape
    tile = height // 2
    copies = copies_in(index, (left_own, left_peer, right_own, right_peer), (lefts, rights), sems, count)
    for group in copies:
        for copy in group:
            copy.start()
    core, x, y = index % 2, index // XBIT % 2, index // YBIT % 2
    sector = index // SECTOR_BIT
    for xr in range(2):
        for yr in range(2):
            for sr in range(vector.shape[0]):
                row = (2 * (x ^ xr) + (y ^ yr)) * tile
                vector[sector ^ sr, pl.ds(pl.multiple_of(row, 64), tile), :] = pieces_ref[xr, yr, sr]
    total = apply_terms(index, first_term, mask_ref, coupling_ref, vector, lefts, rights, mixed, copies)
    if before is not None:
        total = total + before[...]
    if not last:
        total_ref[...] = total
    else:

        @pl.when(core == 0)
        def _():
            kept_ref[...] = total[:tile]
            sent_ref[...] = total[tile:].astype(jnp.bfloat16)

        @pl.when(core == 1)
        def _():
            kept_ref[...] = total[tile:]
            sent_ref[...] = total[:tile].astype(jnp.bfloat16)


def split_kernel(index_ref, kept_ref, got_ref, own_ref, to_x, to_z, to_xz):
    index = index_ref[0]
    x, z = index // XBIT % 2, index // ZBIT % 2
    rows, cols = own_ref.shape

    def part(row_half, col_half):
        at = (
            pl.ds(pl.multiple_of(row_half * rows, 32), rows),
            pl.ds(pl.multiple_of(col_half * cols, 128), cols),
        )
        return kept_ref[at] + got_ref[at].astype(jnp.float32)

    own_ref[...] = part(x, z)
    to_x[...] = part(1 - x, z).astype(jnp.bfloat16)
    to_z[...] = part(x, 1 - z).astype(jnp.bfloat16)
    to_xz[...] = part(1 - x, 1 - z).astype(jnp.bfloat16)


def join_kernel(index_ref, sizes_ref, pairing_ref, own_ref, from_x, from_z, from_xz, out_ref):
    index = index_ref[0]
    core, x, y, z = index % 2, index // XBIT % 2, index // YBIT % 2, index // ZBIT % 2
    rows, cols = out_ref.shape
    total = own_ref[...] + from_x[...].astype(jnp.float32)
    total += from_z[...].astype(jnp.float32) + from_xz[...].astype(jnp.float32)
    keep = live_block(
        sizes_of(sizes_ref, pairing_ref, index // SECTOR_BIT),
        (2 * core + y) * 2 * rows + x * rows,
        z * cols,
        (rows, cols),
    )
    out_ref[...] = jnp.where(keep, total, 0.0).astype(jnp.bfloat16)


def second_kernel(
    index_ref,
    mask_ref,
    coupling_ref,
    start_ref,
    pieces_own,
    pieces_peer,
    left_own,
    left_peer,
    right_own,
    right_peer,
    kept_ref,
    sent_ref,
    tile_ref,
    sums_ref,
    vector,
    lefts,
    rights,
    mixed,
    sems,
):
    index = index_ref[0]
    count, height, _ = lefts.shape
    tile = height // 2
    half = tile // 2
    copies = copies_in(index, (left_own, left_peer, right_own, right_peer), (lefts, rights), sems, count)
    for group in copies:
        for copy in group:
            copy.start()
    core, x, y = index % 2, index // XBIT % 2, index // YBIT % 2
    sector = index // SECTOR_BIT
    sectors = vector.shape[0]
    for pieces, z_row in ((pieces_own, core), (pieces_peer, 1 - core)):
        for xr in range(2):
            for yr in range(2):
                for sr in range(sectors):
                    row = (2 * z_row + (y ^ yr)) * tile + (x ^ xr) * half
                    vector[sector ^ sr, pl.ds(pl.multiple_of(row, 32), half), :] = pieces[2 * xr + yr, sr]
    square = jnp.zeros((8, vector.shape[2]), jnp.float32)
    inner, norm = square, square
    for xr in range(2):
        for yr in range(2):
            for sr in range(sectors):
                row = (2 * (x ^ xr) + (y ^ yr)) * tile
                image = vector[sector ^ sr, pl.ds(pl.multiple_of(row, 64), tile), :].astype(jnp.float32)
                start = start_ref[xr, yr, sr].astype(jnp.float32)
                image = image.reshape(tile // 8, 8, -1)
                start = start.reshape(tile // 8, 8, -1)
                square += jnp.sum(start * start, axis=0)
                inner += jnp.sum(start * image, axis=0)
                norm += jnp.sum(image * image, axis=0)
    for k, sums in enumerate((square, inner, norm)):
        sums_ref[8 * k : 8 * (k + 1), :] = jnp.broadcast_to(jnp.sum(sums), (8, sums_ref.shape[1]))
    total = apply_terms(index, 0, mask_ref, coupling_ref, vector, lefts, rights, mixed, copies)
    image_tile = vector[sector, pl.ds(pl.multiple_of((2 * x + y) * tile, 64), tile), :]

    def give(mine, other):
        for col_half in range(2):
            base = col_half * 2 * tile
            kept_ref[col_half] = total[:, base + mine * tile : base + (mine + 1) * tile]
            sent_ref[col_half] = total[:, base + other * tile : base + (other + 1) * tile].astype(
                jnp.bfloat16
            )
        tile_ref[...] = image_tile[:, mine * tile : (mine + 1) * tile]

    @pl.when(core == 0)
    def _():
        give(0, 1)

    @pl.when(core == 1)
    def _():
        give(1, 0)


def last_split_kernel(index_ref, kept_ref, got_ref, sums_ref, own_ref, to_x, to_z, to_xz):
    index = index_ref[0]
    x, z = index // XBIT % 2, index // ZBIT % 2
    rows, cols = own_ref.shape

    def part(row_half, col_half):
        at = (col_half, pl.ds(pl.multiple_of(row_half * rows, 64), rows))
        return kept_ref[at] + got_ref[at].astype(jnp.float32)

    own_ref[...] = part(z, x)
    to_x[...] = part(z, 1 - x).astype(jnp.bfloat16)
    to_z[:rows, :] = part(1 - z, x).astype(jnp.bfloat16)
    to_xz[...] = part(1 - z, 1 - x).astype(jnp.bfloat16)
    for k in range(3):
        value = jnp.broadcast_to(sums_ref[8 * k : 8 * k + 1, :cols], (SCALAR_ROWS, cols))
        for level in range(3):
            piece = value.astype(jnp.bfloat16)
            to_z[pl.ds(rows + (3 * k + level) * SCALAR_ROWS, SCALAR_ROWS), :] = piece
            value = value - piece.astype(jnp.float32)


def last_join_kernel(
    index_ref, sizes_ref, pairing_ref, own_ref, from_x, from_z, from_xz, sums_ref, image_ref, out_ref
):
    index = index_ref[0]
    _, rows, cols = out_ref.shape
    total = own_ref[...] + from_x[...].astype(jnp.float32)
    total += from_z[:rows, :].astype(jnp.float32) + from_xz[...].astype(jnp.float32)
    sums = []
    for k in range(3):
        value = sums_ref[8 * k : 8 * k + 1, :cols]
        for level in range(3):
            at = rows + (3 * k + level) * SCALAR_ROWS
            value = value + from_z[at : at + SCALAR_ROWS, :].astype(jnp.float32)[:1]
        sums.append(value)
    square, inner, norm = sums
    quotient = inner / square
    residual_square = norm - quotient * inner
    scale = lax.rsqrt(jnp.maximum(residual_square, 0.0) / square + EPSILON)
    keep = live_block(
        sizes_of(sizes_ref, pairing_ref, index // SECTOR_BIT),
        index // GRID_COLS % GRID_ROWS * rows,
        index % GRID_COLS * cols,
        (rows, cols),
    )
    second = (total - quotient * image_ref[...].astype(jnp.float32)) * scale
    out_ref[0] = jnp.where(keep, second, 0.0).astype(jnp.bfloat16)


def on_device(
    wavefunction, left_environment, right_environment, sector_sizes, pairing, term_mask, coupling
):
    tile = wavefunction.shape[1]
    terms = left_environment.shape[0]
    sectors = lax.axis_size("sec") // SECTOR_BIT
    capacity = tile * GRID_ROWS
    bf16, f32 = jnp.bfloat16, jnp.float32
    index = lax.axis_index("sec").astype(jnp.int32)[None]
    core = index[0] % 2
    limit = pltpu.CompilerParams(vmem_limit_bytes=40 * 2**20)
    anywhere = pl.BlockSpec(memory_space=pl.ANY)

    def shaped(*shape, dtype=bf16):
        return jax.ShapeDtypeStruct(shape, dtype)

    left_peer, right_peer = [], []
    chunks = ((0, terms // 2), (terms // 2, terms))
    for low, high in chunks:
        left_peer.append(exchange(left_environment[low:high], ZBIT))
        right_peer.append(exchange(right_environment[low:high], YBIT))

    start_tile = pl.pallas_call(
        start_kernel,
        out_shape=shaped(tile, tile),
        in_specs=[smem(), smem(), smem(), vmem()],
        out_specs=vmem(),
    )(index, sector_sizes, pairing, wavefunction)

    def sector_pieces(piece):
        gathered = piece[None]
        flip = SECTOR_BIT
        while flip < lax.axis_size("sec"):
            gathered = jnp.concatenate([gathered, exchange(gathered, flip)])
            flip *= 2
        return gathered

    pieces = sector_pieces(swap_xz(start_tile))
    pieces = jnp.stack([pieces, exchange(pieces, YBIT)])
    pieces = jnp.stack([pieces, exchange(pieces, XBIT)])
    peer = exchange(pieces, CORE)
    start_pieces = jnp.where(
        core == 0, jnp.concatenate([pieces, peer], -1), jnp.concatenate([peer, pieces], -1)
    )

    def scratch(count):
        return [
            pltpu.VMEM((sectors, capacity, 2 * tile), bf16),
            pltpu.VMEM((count, 2 * tile, capacity), bf16),
            pltpu.VMEM((count * 2 * tile, capacity), bf16),
            pltpu.VMEM((2 * tile, count * 2 * tile), bf16),
            pltpu.SemaphoreType.DMA((count, 4)),
        ]

    def work(count):
        macs = count * 2 * tile * capacity * 2 * tile * 2
        return pl.CostEstimate(
            flops=2 * macs, bytes_accessed=count * 4 * tile * capacity * 2, transcendentals=0
        )

    total = None
    for number, (low, high) in enumerate(chunks):
        last = high == terms
        count = high - low
        extra = [] if total is None else [total]
        total = pl.pallas_call(
            lambda *refs, low=low, last=last: first_kernel(low, last, *refs),
            out_shape=(
                [shaped(tile, capacity, dtype=f32), shaped(tile, capacity)]
                if last
                else shaped(2 * tile, capacity, dtype=f32)
            ),
            in_specs=[smem()] * 3 + [vmem()] + [anywhere] * 4 + [vmem()] * len(extra),
            out_specs=[vmem(), vmem()] if last else vmem(),
            scratch_shapes=scratch(count),
            compiler_params=limit,
            cost_estimate=work(count),
        )(
            index,
            term_mask,
            coupling,
            start_pieces,
            left_environment[low:high],
            left_peer[number],
            right_environment[low:high],
            right_peer[number],
            *extra,
        )
    kept, sent = total
    got = exchange(sent, CORE)
    unit = (tile // 2, 2 * tile)
    own, to_x, to_z, to_xz = pl.pallas_call(
        split_kernel,
        out_shape=[shaped(*unit, dtype=f32)] + [shaped(*unit)] * 3,
        in_specs=[smem(), vmem(), vmem()],
        out_specs=[vmem()] * 4,
    )(index, kept, got)
    image_unit = pl.pallas_call(
        join_kernel,
        out_shape=shaped(*unit),
        in_specs=[smem()] * 3 + [vmem()] * 4,
        out_specs=vmem(),
    )(
        index,
        sector_sizes,
        pairing,
        own,
        exchange(to_x, XBIT),
        exchange(to_z, ZBIT),
        exchange(to_xz, XBIT | ZBIT),
    )

    units = sector_pieces(image_unit)
    units = jnp.stack(
        [units, exchange(units, YBIT), exchange(units, XBIT), exchange(units, XBIT | YBIT)]
    )
    units_peer = exchange(units, CORE)
    kept, sent, image_tile, sums = pl.pallas_call(
        second_kernel,
        out_shape=[
            shaped(2, 2 * tile, tile, dtype=f32),
            shaped(2, 2 * tile, tile),
            shaped(tile, tile),
            shaped(24, 2 * 128, dtype=f32),
        ],
        in_specs=[smem()] * 3 + [vmem()] * 3 + [anywhere] * 4,
        out_specs=[vmem()] * 4,
        scratch_shapes=scratch(terms),
        compiler_params=limit,
        cost_estimate=work(terms),
    )(
        index,
        term_mask,
        coupling,
        start_pieces,
        units,
        units_peer,
        left_environment,
        jnp.concatenate(left_peer),
        right_environment,
        jnp.concatenate(right_peer),
    )
    got = exchange(sent, CORE)
    first_tile = swap_xz(image_tile)
    own, to_x, to_z, to_xz = pl.pallas_call(
        last_split_kernel,
        out_shape=[
            shaped(tile, tile, dtype=f32),
            shaped(tile, tile),
            shaped(tile + 9 * SCALAR_ROWS, tile),
            shaped(tile, tile),
        ],
        in_specs=[smem()] + [vmem()] * 3,
        out_specs=[vmem()] * 4,
    )(index, kept, got, sums)
    second = pl.pallas_call(
        last_join_kernel,
        out_shape=shaped(1, tile, tile),
        in_specs=[smem()] * 3 + [vmem()] * 6,
        out_specs=vmem(),
    )(
        index,
        sector_sizes,
        pairing,
        own,
        exchange(to_x, XBIT),
        exchange(to_z, ZBIT),
        exchange(to_xz, XBIT | ZBIT),
        sums,
        first_tile,
    )
    return first_tile[None], second


def solution(mesh):
    return jax.shard_map(
        on_device,
        mesh=mesh,
        in_specs=(
            P(("groups", "sec"), None, None),
            P(("groups", "sec"), None, None),
            P(("groups", "sec"), None, None),
            P(None, "groups"),
            P("groups"),
            P("groups", None),
            P("groups", None),
        ),
        out_specs=(P(("groups", "sec"), None, None), P(("groups", "sec"), None, None)),
        check_vma=False,
    )
```

time: 363 us -> 138 us (0.38)
  waiting for transfers between devices: 172 us -> 55.1 us
  blocking collectives: 80.3 us -> 0 us
  matrix products: 33.3 us -> 0 us
  starting transfers between devices: 8.18 us -> 37 us
  Pallas kernels: 0 us -> 26.7 us
  local copies, waits for them, and re-layouts: 32 us -> 10.9 us
  between operations: 16.9 us -> 0.84 us
  other arithmetic: 19.9 us -> 6.69 us
    psum x2 -> x0, blocking collectives: 80.3 us -> none  [the longest x1 40.8 us: on_device(): lax.psum((jnp.sum(start_value * first_value), jnp.sum(start_value * start...]
    all_gather x2 -> x0, waiting for transfers between devices: 67.2 us -> none  [fetch(): gathered = lax.all_gather(tile_data[None], 'sec', axis=0, tiled=True)]
    ppermute x6 -> x23, waiting for transfers between devices: 105 us -> 55.1 us  [the longest x21 55.1 us: exchange(): return lax.ppermute(block, 'sec', [(i, i ^ flip) for i in range(count)])]
    dot_general x4 -> x0, matrix products: 33.3 us -> none  [the longest x2 20.2 us: operate(): jnp.einsum('kria,kijab->krjb', left_split, sources, preferred_element_typ...]
    ppermute x6 -> x23, starting transfers between devices: 8.1 us -> 37 us  [the longest x21 34.8 us: exchange(): return lax.ppermute(block, 'sec', [(i, i ^ flip) for i in range(count)])]
    pallas_call x0 -> x8, Pallas kernels: none -> 26.7 us  [the longest x2 9.11 us: on_device(): pl.pallas_call(lambda *refs, low=low, last=last: first_kernel(low, last,...]
    reshape x3 -> x0, local copies, waits for them, and re-layouts: 17 us -> none  [the longest x2 11.2 us: operate(): mixed_terms = mixed_terms.reshape(terms_here, tile_rows, capacity)]
    gather x2 -> x0, local copies, waits for them, and re-layouts: 14.1 us -> none  [fetch(): return jnp.take(tiled, my_sources, axis=0)]
  transfers between devices with their start and end apart: 8 -> 23, of which waited for: 8 -> 17; matrix products, arithmetic and copies ran while one was open for 9% -> 6% of each run, Pallas kernels for 0% -> 3%
where the time goes in v1:
time: 138 us; the launch traced here: 137 us
  waiting for transfers between devices  55.1 us (40%)
  starting transfers between devices  37 us (27%)
  Pallas kernels  26.7 us (19%)
  local copies, waits for them, and re-layouts  10.9 us (8%)
  other arithmetic  6.69 us (5%)
    ppermute x21, waiting for transfers between devices, exchange(): return lax.ppermute(block, 'sec', [(i, i ^ flip) for i in range(count)])  55.1 us
    ppermute x21, starting transfers between devices, exchange(): return lax.ppermute(block, 'sec', [(i, i ^ flip) for i in range(count)])  34.8 us
    pallas_call x2, Pallas kernels, on_device(): pl.pallas_call(lambda *refs, low=low, last=last: first_kernel(low, last,...  9.11 us
    pallas_call x1, Pallas kernels, on_device(): pl.pallas_call(second_kernel, out_shape=[shaped(2, 2 * tile, tile, dtype=...  8.2 us
    unnamed x39, local copies, waits for them, and re-layouts  8.19 us
  transfers between devices with their start and end apart: 23, of which 17 were waited for; matrix products, arithmetic and copies ran while one was open for 6% of the time, Pallas kernels for 3%

profile of v1, /device:TPU:0, one launch (start us, length us, event | category | flops | bytes accessed | tf_op | source)
XLA Modules:
  0.0 137.2 jit_solution(9295233454994988596)
XLA Ops:
  0.6 1.7 %shard_map.86 = bf16[192,192]{1,0:T(8,128)(2,1)} custom-call(s32[1]{0:T(128)} %bitcast.index_ref.refs_0_, s32[2,2]{1,0:T(2,128)} %sizes_ref.5, s32[2]{0:T(128)} %pairing_ref.5, bf16[1,192,192]{2,1,0:T(8,128)(2,1)} %wave_ref.1), custom_call_target="tpu_custom_call" | custom-call | tf_op jit(solution)/shard_map/pallas_call | solution.py:339
  3.9 4.0 %collective-permute-start.1 = (bf16[1,192,192]{2,1,0:T(8,128)(2,1)S(1)}, bf16[1,192,192]{2,1,0:T(8,128)(2,1)S(1)}, u32[]{:S(2)}, u32[]{:S(2)}) collective-permute-start(bf16[1,192,192]{2,1,0:T(8,128)(2,1)S(1)} %bitcast.24), channel_id=1, source_target_pairs={{0,16},{1,17},{2,18},{3,19},{4,20},{5,21},{6,22},{7,23},{8,24},{9,... | collective-permute-start | bytes 221192 | tf_op jit(solution)/shard_map/ppermute | solution.py:18
  7.9 2.9 %collective-permute-done.1 = bf16[1,192,192]{2,1,0:T(8,128)(2,1)S(1)} collective-permute-done((bf16[1,192,192]{2,1,0:T(8,128)(2,1)S(1)}, bf16[1,192,192]{2,1,0:T(8,128)(2,1)S(1)}, u32[]{:S(2)}, u32[]{:S(2)}) %collective-permute-start.1) | collective-permute-done | bytes 73760 | tf_op jit(solution)/shard_map/ppermute | solution.py:18
  10.9 1.6 %collective-permute-start.2 = (bf16[2,192,192]{2,1,0:T(8,128)(2,1)S(1)}, bf16[2,192,192]{2,1,0:T(8,128)(2,1)S(1)}, u32[]{:S(2)}, u32[]{:S(2)}) collective-permute-start(bf16[2,192,192]{2,1,0:T(8,128)(2,1)S(1)} %get-tuple-element.37), channel_id=1, source_target_pairs={{0,4},{1,5},{2,6},{3,7},{4,0},{5,1},{6,2},{7,3},{8,12},{9,13},{10,... | collective-permute-start | bytes 442376 | tf_op jit(solution)/shard_map/ppermute | solution.py:18
  12.5 4.4 %collective-permute-done.2 = bf16[2,192,192]{2,1,0:T(8,128)(2,1)S(1)} collective-permute-done((bf16[2,192,192]{2,1,0:T(8,128)(2,1)S(1)}, bf16[2,192,192]{2,1,0:T(8,128)(2,1)S(1)}, u32[]{:S(2)}, u32[]{:S(2)}) %collective-permute-start.2) | collective-permute-done | bytes 147488 | tf_op jit(solution)/shard_map/ppermute | solution.py:18
  17.0 9.1 %collective-permute-start.3 = (bf16[2,2,192,192]{3,2,1,0:T(8,128)(2,1)S(1)}, bf16[2,2,192,192]{3,2,1,0:T(8,128)(2,1)S(1)}, u32[]{:S(2)}, u32[]{:S(2)}) collective-permute-start(bf16[2,2,192,192]{3,2,1,0:T(8,128)(2,1)S(1)} %get-tuple-element.35), channel_id=1, source_target_pairs={{0,2},{1,3},{2,0},{3,1},{4,6},{5,7},{6,4},{7,5},{8,10},{9,11},{10,... | collective-permute-start | bytes 884744 | tf_op jit(solution)/shard_map/ppermute | solution.py:18
  30.4 3.3 %collective-permute-done.3 = bf16[2,2,192,192]{3,2,1,0:T(8,128)(2,1)S(1)} collective-permute-done((bf16[2,2,192,192]{3,2,1,0:T(8,128)(2,1)S(1)}, bf16[2,2,192,192]{3,2,1,0:T(8,128)(2,1)S(1)}, u32[]{:S(2)}, u32[]{:S(2)}) %collective-permute-start.3) | collective-permute-done | bytes 294944 | tf_op jit(solution)/shard_map/ppermute | solution.py:18
  37.4 2.6 %maximum_select_fusion.refs_3_.start_ref = bf16[2,2,2,192,384]{4,3,2,1,0:T(8,128)(2,1)S(1)} fusion(bf16[2,2,2,192,192]{4,3,2,1,0:T(8,128)(2,1)} %collective-permute-done.4, bf16[1,2,2,192,192]{4,3,2,1,0:T(8,128)(2,1)} %bitcast.16, bf16[1,2,2,192,192]{4,3,2,1,0:T(8,128)(2,1)S(1)} %get-tuple-element.34, pred[]{:T(512)S(6)} %eq.5), kind=kLoop, calls=%fused_computation.2 | loop fusion | flops 7667712 | bytes 2359297 | tf_op jit(solution)/shard_map/jit(_where)/select_n | solution.py:358
  40.0 10.3 %collective-permute-done.7.refs_5_ = bf16[3,192,768]{2,1,0:T(8,128)(2,1)S(1)} collective-permute-done((bf16[3,192,768]{2,1,0:T(8,128)(2,1)}, bf16[3,192,768]{2,1,0:T(8,128)(2,1)S(1)}, u32[]{:S(2)}, u32[]{:S(2)}) %collective-permute-start.7) | collective-permute-done | bytes 884768 | tf_op jit(solution)/shard_map/ppermute | solution.py:18
  51.6 4.4 %shard_map.87.refs_8_ = f32[384,768]{1,0:T(8,128)S(1)} custom-call(s32[1]{0:T(128)} %bitcast.index_ref.refs_0_, s32[2,24]{1,0:T(2,128)S(1)} %copy-done.7, s32[2,24]{1,0:T(2,128)S(1)} %copy-done.8, bf16[2,2,2,192,384]{4,3,2,1,0:T(8,128)(2,1)S(1)} %maximum_select_fusion.refs_3_.start_ref, bf16[3,192,768]{2,1,0:T(8,128)(2,1)} %get-tuple-element.32.refs_4_, ...), custom_call_target="tpu_custom_call" | custom-call | flops 1358954496 | bytes 3538944 | tf_op jit(solution)/shard_map/pallas_call | solution.py:382
  56.1 10.2 %collective-permute-done.5.refs_5_ = bf16[3,192,768]{2,1,0:T(8,128)(2,1)} collective-permute-done((bf16[3,192,768]{2,1,0:T(8,128)(2,1)}, bf16[3,192,768]{2,1,0:T(8,128)(2,1)}, u32[]{:S(2)}, u32[]{:S(2)}) %collective-permute-start.5) | collective-permute-done | bytes 884768 | tf_op jit(solution)/shard_map/ppermute | solution.py:18
  67.6 4.7 %shard_map.88 = (f32[192,768]{1,0:T(8,128)S(1)}, bf16[192,768]{1,0:T(8,128)(2,1)S(1)}) custom-call(s32[1]{0:T(128)} %bitcast.index_ref.refs_0_, s32[2,24]{1,0:T(2,128)S(1)} %copy-done.7, s32[2,24]{1,0:T(2,128)S(1)} %copy-done.8, bf16[2,2,2,192,384]{4,3,2,1,0:T(8,128)(2,1)S(1)} %maximum_select_fusion.refs_3_.start_ref, ...), custom_call_target="tpu_custom_call" | custom-call | flops 1358954496 | bytes 3538944 | tf_op jit(solution)/shard_map/pallas_call | solution.py:382
  75.4 1.9 %shard_map.89 = (f32[96,384]{1,0:T(8,128)}, bf16[96,384]{1,0:T(8,128)(2,1)}, bf16[96,384]{1,0:T(8,128)(2,1)}, bf16[96,384]{1,0:T(8,128)(2,1)}) custom-call(s32[1]{0:T(128)} %bitcast.index_ref.refs_0_, f32[192,768]{1,0:T(8,128)} %copy-done.5, bf16[192,768]{1,0:T(8,128)(2,1)} %copy-done.12), custom_call_target="tpu_custom_call" | custom-call | tf_op jit(solution)/shard_map/pallas_call | solution.py:408
  83.1 1.9 %collective-permute-done.12.from_xz = bf16[96,384]{1,0:T(8,128)(2,1)S(1)} collective-permute-done((bf16[96,384]{1,0:T(8,128)(2,1)}, bf16[96,384]{1,0:T(8,128)(2,1)S(1)}, u32[]{:S(2)}, u32[]{:S(2)}) %collective-permute-start.12) | collective-permute-done | bytes 73760 | tf_op jit(solution)/shard_map/ppermute | solution.py:18
  85.6 1.7 %shard_map.90 = bf16[96,384]{1,0:T(8,128)(2,1)} custom-call(s32[1]{0:T(128)} %bitcast.index_ref.refs_0_, s32[2,2]{1,0:T(2,128)} %sizes_ref.5, s32[2]{0:T(128)} %pairing_ref.5, f32[96,384]{1,0:T(8,128)} %get-tuple-element.18.own_ref, bf16[96,384]{1,0:T(8,128)(2,1)} %copy-done.16, bf16[96,384]{1,0:T(8,128)(2,1)} %copy-done.17, bf16[96,384]{1,0:T(8,128)(2,1)} %copy-done.18), custom_call_target="tpu_custom_call" | custom-call | tf_op jit(solution)/shard_map/pallas_call | solution.py:414
  87.3 2.0 %collective-permute-start.13 = (bf16[1,96,384]{2,1,0:T(8,128)(2,1)}, bf16[1,96,384]{2,1,0:T(8,128)(2,1)S(1)}, u32[]{:S(2)}, u32[]{:S(2)}) collective-permute-start(bf16[1,96,384]{2,1,0:T(8,128)(2,1)} %bitcast.18), channel_id=1, source_target_pairs={{0,16},{1,17},{2,18},{3,19},{4,20},{5,21},{6,22},{7,23},{8,24},{9,... | collective-permute-start | bytes 221192 | tf_op jit(solution)/shard_map/ppermute | solution.py:18
  89.3 3.5 %collective-permute-done.13 = bf16[1,96,384]{2,1,0:T(8,128)(2,1)S(1)} collective-permute-done((bf16[1,96,384]{2,1,0:T(8,128)(2,1)}, bf16[1,96,384]{2,1,0:T(8,128)(2,1)S(1)}, u32[]{:S(2)}, u32[]{:S(2)}) %collective-permute-start.13) | collective-permute-done | bytes 73760 | tf_op jit(solution)/shard_map/ppermute | solution.py:18
  93.7 3.3 %collective-permute-start.16 = (bf16[2,96,384]{2,1,0:T(8,128)(2,1)S(1)}, bf16[2,96,384]{2,1,0:T(8,128)(2,1)S(1)}, u32[]{:S(2)}, u32[]{:S(2)}) collective-permute-start(bf16[2,96,384]{2,1,0:T(8,128)(2,1)S(1)} %get-tuple-element.39), channel_id=1, source_target_pairs={{0,6},{1,7},{2,4},{3,5},{4,2},{5,3},{6,0},{7,1},{8,14},{9,15},{10,... | collective-permute-start | bytes 442376 | tf_op jit(solution)/shard_map/ppermute | solution.py:18
  97.7 3.5 %collective-permute-done.16 = bf16[2,96,384]{2,1,0:T(8,128)(2,1)S(1)} collective-permute-done((bf16[2,96,384]{2,1,0:T(8,128)(2,1)S(1)}, bf16[2,96,384]{2,1,0:T(8,128)(2,1)S(1)}, u32[]{:S(2)}, u32[]{:S(2)}) %collective-permute-start.16) | collective-permute-done | bytes 147488 | tf_op jit(solution)/shard_map/ppermute | solution.py:18
  106.5 8.2 %shard_map.91 = (f32[2,384,192]{2,1,0:T(8,128)S(1)}, bf16[2,384,192]{2,1,0:T(8,128)(2,1)S(1)}, bf16[192,192]{1,0:T(8,128)(2,1)S(1)}, f32[24,256]{1,0:T(8,128)S(1)}) custom-call(s32[1]{0:T(128)} %bitcast.index_ref.refs_0_, s32[2,24]{1,0:T(2,128)S(1)} %copy-done.7, s32[2,24]{1,0:T(2,128)S(1)} %copy-done.8, ...), custom_call_target="tpu_custom_call" | custom-call | flops 2717908992 | bytes 7077888 | tf_op jit(solution)/shard_map/pallas_call | solution.py:434
  119.0 2.1 %shard_map.92 = (f32[192,192]{1,0:T(8,128)}, bf16[192,192]{1,0:T(8,128)(2,1)}, bf16[336,192]{1,0:T(8,128)(2,1)}, bf16[192,192]{1,0:T(8,128)(2,1)}) custom-call(s32[1]{0:T(128)} %bitcast.index_ref.refs_0_, f32[2,384,192]{2,1,0:T(8,128)} %copy-done.4, bf16[2,384,192]{2,1,0:T(8,128)(2,1)} %copy-done.11, f32[24,256]{1,0:T(8,128)} %copy-done.6), custom_call_target="tpu_custom_call" | custom-call | tf_op jit(solution)/shard_map/pallas_call | solution.py:461
  122.2 4.4 %collective-permute-start.20 = (bf16[192,192]{1,0:T(8,128)(2,1)}, bf16[192,192]{1,0:T(8,128)(2,1)S(1)}, u32[]{:S(2)}, u32[]{:S(2)}) collective-permute-start(bf16[192,192]{1,0:T(8,128)(2,1)} %get-tuple-element.27), channel_id=1, source_target_pairs={{0,2},{1,3},{2,0},{3,1},{4,6},{5,7},{6,4},{7,5},{8,10},{9,11},{10,... | collective-permute-start | bytes 221192 | tf_op jit(solution)/shard_map/ppermute | solution.py:18
  127.3 5.6 %collective-permute-done.20.from_x = bf16[192,192]{1,0:T(8,128)(2,1)S(1)} collective-permute-done((bf16[192,192]{1,0:T(8,128)(2,1)}, bf16[192,192]{1,0:T(8,128)(2,1)S(1)}, u32[]{:S(2)}, u32[]{:S(2)}) %collective-permute-start.20) | collective-permute-done | bytes 73760 | tf_op jit(solution)/shard_map/ppermute | solution.py:18
  133.7 1.9 %shard_map.93 = bf16[1,192,192]{2,1,0:T(8,128)(2,1)} custom-call(s32[1]{0:T(128)} %bitcast.index_ref.refs_0_, s32[2,2]{1,0:T(2,128)} %sizes_ref.5, s32[2]{0:T(128)} %pairing_ref.5, f32[192,192]{1,0:T(8,128)} %get-tuple-element.26.own_ref, bf16[192,192]{1,0:T(8,128)(2,1)} %copy-done.14, bf16[336,192]{1,0:T(8,128)(2,1)} %copy-done.13, ...), custom_call_target="tpu_custom_call" | custom-call | tf_op jit(solution)/shard_map/pallas_call | solution.py:472
  (79 shorter events, 36.9 us)
Async XLA Ops:
  0.6 25.5 %copy-start = (bf16[6,192,768]{2,1,0:T(8,128)(2,1)S(1)}, bf16[6,192,768]{2,1,0:T(8,128)(2,1)}, u32[]{:S(2)}) copy-start(bf16[6,192,768]{2,1,0:T(8,128)(2,1)} %left_own.1) | copy-start | bytes 5308420
  2.4 1.5 %collective-permute-start = (bf16[192,192]{1,0:T(8,128)(2,1)}, bf16[192,192]{1,0:T(8,128)(2,1)S(1)}, u32[]{:S(2)}, u32[]{:S(2)}) collective-permute-start(bf16[192,192]{1,0:T(8,128)(2,1)} %shard_map.86), channel_id=1, source_target_pairs={{0,0},{1,1},{2,8},{3,9},{4,4},{5,5},{6,12},{7,13},{8,2},{9,3},{10,... | collective-permute-start | bytes 221192 | tf_op jit(solution)/shard_map/ppermute | solution.py:27
  3.9 6.9 %collective-permute-start.1 = (bf16[1,192,192]{2,1,0:T(8,128)(2,1)S(1)}, bf16[1,192,192]{2,1,0:T(8,128)(2,1)S(1)}, u32[]{:S(2)}, u32[]{:S(2)}) collective-permute-start(bf16[1,192,192]{2,1,0:T(8,128)(2,1)S(1)} %bitcast.24), channel_id=1, source_target_pairs={{0,16},{1,17},{2,18},{3,19},{4,20},{5,21},{6,22},{7,23},{8,24},{9,... | collective-permute-start | bytes 221192 | tf_op jit(solution)/shard_map/ppermute | solution.py:18
  10.9 6.1 %collective-permute-start.2 = (bf16[2,192,192]{2,1,0:T(8,128)(2,1)S(1)}, bf16[2,192,192]{2,1,0:T(8,128)(2,1)S(1)}, u32[]{:S(2)}, u32[]{:S(2)}) collective-permute-start(bf16[2,192,192]{2,1,0:T(8,128)(2,1)S(1)} %get-tuple-element.37), channel_id=1, source_target_pairs={{0,4},{1,5},{2,6},{3,7},{4,0},{5,1},{6,2},{7,3},{8,12},{9,13},{10,... | collective-permute-start | bytes 442376 | tf_op jit(solution)/shard_map/ppermute | solution.py:18
  17.0 16.7 %collective-permute-start.3 = (bf16[2,2,192,192]{3,2,1,0:T(8,128)(2,1)S(1)}, bf16[2,2,192,192]{3,2,1,0:T(8,128)(2,1)S(1)}, u32[]{:S(2)}, u32[]{:S(2)}) collective-permute-start(bf16[2,2,192,192]{3,2,1,0:T(8,128)(2,1)S(1)} %get-tuple-element.35), channel_id=1, source_target_pairs={{0,2},{1,3},{2,0},{3,1},{4,6},{5,7},{6,4},{7,5},{8,10},{9,11},{10,... | collective-permute-start | bytes 884744 | tf_op jit(solution)/shard_map/ppermute | solution.py:18
  27.5 22.8 %collective-permute-start.7 = (bf16[3,192,768]{2,1,0:T(8,128)(2,1)}, bf16[3,192,768]{2,1,0:T(8,128)(2,1)S(1)}, u32[]{:S(2)}, u32[]{:S(2)}) collective-permute-start(bf16[3,192,768]{2,1,0:T(8,128)(2,1)} %get-tuple-element.32.refs_4_), channel_id=1, source_target_pairs={{0,8},{1,9},{2,10},{3,11},{4,12},{5,13},{6,14},{7,15},{8,0},{9,1},... | collective-permute-start | bytes 2654216 | tf_op jit(solution)/shard_map/ppermute | solution.py:18
  28.8 22.8 %collective-permute-start.8 = (bf16[3,192,768]{2,1,0:T(8,128)(2,1)}, bf16[3,192,768]{2,1,0:T(8,128)(2,1)S(1)}, u32[]{:S(2)}, u32[]{:S(2)}) collective-permute-start(bf16[3,192,768]{2,1,0:T(8,128)(2,1)} %get-tuple-element.30.refs_6_), channel_id=1, source_target_pairs={{0,4},{1,5},{2,6},{3,7},{4,0},{5,1},{6,2},{7,3},{8,12},{9,13},{10,... | collective-permute-start | bytes 2654216 | tf_op jit(solution)/shard_map/ppermute | solution.py:18
  34.6 2.7 %collective-permute-start.4 = (bf16[2,2,2,192,192]{4,3,2,1,0:T(8,128)(2,1)S(1)}, bf16[2,2,2,192,192]{4,3,2,1,0:T(8,128)(2,1)}, u32[]{:S(2)}, u32[]{:S(2)}) collective-permute-start(bf16[2,2,2,192,192]{4,3,2,1,0:T(8,128)(2,1)S(1)} %pad_maximum_fusion.2), channel_id=1, source_target_pairs={{0,1},{1,0},{2,3},{3,2},{4,5},{5,4},{6,7},{7,6},{8,9},{9,8},{10,11... | collective-permute-start | bytes 1769480 | tf_op jit(solution)/shard_map/ppermute | solution.py:18
  34.7 31.6 %collective-permute-start.5 = (bf16[3,192,768]{2,1,0:T(8,128)(2,1)}, bf16[3,192,768]{2,1,0:T(8,128)(2,1)}, u32[]{:S(2)}, u32[]{:S(2)}) collective-permute-start(bf16[3,192,768]{2,1,0:T(8,128)(2,1)} %get-tuple-element.33.refs_4_), channel_id=1, source_target_pairs={{0,8},{1,9},{2,10},{3,11},{4,12},{5,13},{6,14},{7,15},{8,0},{9,1},... | collective-permute-start | bytes 2654216 | tf_op jit(solution)/shard_map/ppermute | solution.py:18
  35.8 31.8 %collective-permute-start.6 = (bf16[3,192,768]{2,1,0:T(8,128)(2,1)}, bf16[3,192,768]{2,1,0:T(8,128)(2,1)}, u32[]{:S(2)}, u32[]{:S(2)}) collective-permute-start(bf16[3,192,768]{2,1,0:T(8,128)(2,1)} %get-tuple-element.31.refs_6_), channel_id=1, source_target_pairs={{0,4},{1,5},{2,6},{3,7},{4,0},{5,1},{6,2},{7,3},{8,12},{9,13},{10,... | collective-permute-start | bytes 2654216 | tf_op jit(solution)/shard_map/ppermute | solution.py:18
  73.1 1.6 %collective-permute-start.9 = (bf16[192,768]{1,0:T(8,128)(2,1)S(1)}, bf16[192,768]{1,0:T(8,128)(2,1)S(1)}, u32[]{:S(2)}, u32[]{:S(2)}) collective-permute-start(bf16[192,768]{1,0:T(8,128)(2,1)S(1)} %get-tuple-element.17), channel_id=1, source_target_pairs={{0,1},{1,0},{2,3},{3,2},{4,5},{5,4},{6,7},{7,6},{8,9},{9,8},{10,11... | collective-permute-start | bytes 884744 | tf_op jit(solution)/shard_map/ppermute | solution.py:18
  77.3 4.6 %collective-permute-start.10 = (bf16[96,384]{1,0:T(8,128)(2,1)}, bf16[96,384]{1,0:T(8,128)(2,1)S(1)}, u32[]{:S(2)}, u32[]{:S(2)}) collective-permute-start(bf16[96,384]{1,0:T(8,128)(2,1)} %get-tuple-element.19), channel_id=1, source_target_pairs={{0,2},{1,3},{2,0},{3,1},{4,6},{5,7},{6,4},{7,5},{8,10},{9,11},{10,... | collective-permute-start | bytes 221192 | tf_op jit(solution)/shard_map/ppermute | solution.py:18
  78.4 4.6 %collective-permute-start.11 = (bf16[96,384]{1,0:T(8,128)(2,1)}, bf16[96,384]{1,0:T(8,128)(2,1)S(1)}, u32[]{:S(2)}, u32[]{:S(2)}) collective-permute-start(bf16[96,384]{1,0:T(8,128)(2,1)} %get-tuple-element.20), channel_id=1, source_target_pairs={{0,8},{1,9},{2,10},{3,11},{4,12},{5,13},{6,14},{7,15},{8,0},{9,1},... | collective-permute-start | bytes 221192 | tf_op jit(solution)/shard_map/ppermute | solution.py:18
  79.4 5.6 %collective-permute-start.12 = (bf16[96,384]{1,0:T(8,128)(2,1)}, bf16[96,384]{1,0:T(8,128)(2,1)S(1)}, u32[]{:S(2)}, u32[]{:S(2)}) collective-permute-start(bf16[96,384]{1,0:T(8,128)(2,1)} %get-tuple-element.21), channel_id=1, source_target_pairs={{0,10},{1,11},{2,8},{3,9},{4,14},{5,15},{6,12},{7,13},{8,2},{9,3},... | collective-permute-start | bytes 221192 | tf_op jit(solution)/shard_map/ppermute | solution.py:18
  87.3 5.5 %collective-permute-start.13 = (bf16[1,96,384]{2,1,0:T(8,128)(2,1)}, bf16[1,96,384]{2,1,0:T(8,128)(2,1)S(1)}, u32[]{:S(2)}, u32[]{:S(2)}) collective-permute-start(bf16[1,96,384]{2,1,0:T(8,128)(2,1)} %bitcast.18), channel_id=1, source_target_pairs={{0,16},{1,17},{2,18},{3,19},{4,20},{5,21},{6,22},{7,23},{8,24},{9,... | collective-permute-start | bytes 221192 | tf_op jit(solution)/shard_map/ppermute | solution.py:18
  93.7 7.4 %collective-permute-start.16 = (bf16[2,96,384]{2,1,0:T(8,128)(2,1)S(1)}, bf16[2,96,384]{2,1,0:T(8,128)(2,1)S(1)}, u32[]{:S(2)}, u32[]{:S(2)}) collective-permute-start(bf16[2,96,384]{2,1,0:T(8,128)(2,1)S(1)} %get-tuple-element.39), channel_id=1, source_target_pairs={{0,6},{1,7},{2,4},{3,5},{4,2},{5,3},{6,0},{7,1},{8,14},{9,15},{10,... | collective-permute-start | bytes 442376 | tf_op jit(solution)/shard_map/ppermute | solution.py:18
  97.0 5.6 %collective-permute-start.14 = (bf16[2,96,384]{2,1,0:T(8,128)(2,1)S(1)}, bf16[2,96,384]{2,1,0:T(8,128)(2,1)S(1)}, u32[]{:S(2)}, u32[]{:S(2)}) collective-permute-start(bf16[2,96,384]{2,1,0:T(8,128)(2,1)S(1)} %get-tuple-element.39), channel_id=1, source_target_pairs={{0,4},{1,5},{2,6},{3,7},{4,0},{5,1},{6,2},{7,3},{8,12},{9,13},{10,... | collective-permute-start | bytes 442376 | tf_op jit(solution)/shard_map/ppermute | solution.py:18
  97.5 5.3 %collective-permute-start.15 = (bf16[2,96,384]{2,1,0:T(8,128)(2,1)S(1)}, bf16[2,96,384]{2,1,0:T(8,128)(2,1)S(1)}, u32[]{:S(2)}, u32[]{:S(2)}) collective-permute-start(bf16[2,96,384]{2,1,0:T(8,128)(2,1)S(1)} %get-tuple-element.39), channel_id=1, source_target_pairs={{0,2},{1,3},{2,0},{3,1},{4,6},{5,7},{6,4},{7,5},{8,10},{9,11},{10,... | collective-permute-start | bytes 442376 | tf_op jit(solution)/shard_map/ppermute | solution.py:18
  102.8 2.9 %collective-permute-start.17 = (bf16[4,2,96,384]{3,2,1,0:T(8,128)(2,1)S(1)}, bf16[4,2,96,384]{3,2,1,0:T(8,128)(2,1)S(1)}, u32[]{:S(2)}, u32[]{:S(2)}) collective-permute-start(bf16[4,2,96,384]{3,2,1,0:T(8,128)(2,1)S(1)} %pad_maximum_fusion.3.pieces_own), channel_id=1, source_target_pairs={{0,1},{1,0},{2,3},{3,2},{4,5},{5,4},{6,7},{7,6},{8,9},{9,8},{10,11... | collective-permute-start | bytes 1769480 | tf_op jit(solution)/shard_map/ppermute | solution.py:18
  116.2 2.0 %collective-permute-start.19 = (bf16[2,384,192]{2,1,0:T(8,128)(2,1)S(1)}, bf16[2,384,192]{2,1,0:T(8,128)(2,1)S(1)}, u32[]{:S(2)}, u32[]{:S(2)}) collective-permute-start(bf16[2,384,192]{2,1,0:T(8,128)(2,1)S(1)} %get-tuple-element.24), channel_id=1, source_target_pairs={{0,1},{1,0},{2,3},{3,2},{4,5},{5,4},{6,7},{7,6},{8,9},{9,8},{10,11... | collective-permute-start | bytes 884744 | tf_op jit(solution)/shard_map/ppermute | solution.py:18
  121.1 11.9 %collective-permute-start.21 = (bf16[336,192]{1,0:T(8,128)(2,1)}, bf16[336,192]{1,0:T(8,128)(2,1)S(1)}, u32[]{:S(2)}, u32[]{:S(2)}) collective-permute-start(bf16[336,192]{1,0:T(8,128)(2,1)} %get-tuple-element.28), channel_id=1, source_target_pairs={{0,8},{1,9},{2,10},{3,11},{4,12},{5,13},{6,14},{7,15},{8,0},{9,1},... | collective-permute-start | bytes 387080 | tf_op jit(solution)/shard_map/ppermute | solution.py:18
  121.6 5.8 %collective-permute-start.18 = (bf16[192,192]{1,0:T(8,128)(2,1)S(1)}, bf16[192,192]{1,0:T(8,128)(2,1)S(1)}, u32[]{:S(2)}, u32[]{:S(2)}) collective-permute-start(bf16[192,192]{1,0:T(8,128)(2,1)S(1)} %get-tuple-element.22), channel_id=1, source_target_pairs={{0,0},{1,1},{2,8},{3,9},{4,4},{5,5},{6,12},{7,13},{8,2},{9,3},{10,... | collective-permute-start | bytes 221192 | tf_op jit(solution)/shard_map/ppermute | solution.py:27
  122.2 10.8 %collective-permute-start.20 = (bf16[192,192]{1,0:T(8,128)(2,1)}, bf16[192,192]{1,0:T(8,128)(2,1)S(1)}, u32[]{:S(2)}, u32[]{:S(2)}) collective-permute-start(bf16[192,192]{1,0:T(8,128)(2,1)} %get-tuple-element.27), channel_id=1, source_target_pairs={{0,2},{1,3},{2,0},{3,1},{4,6},{5,7},{6,4},{7,5},{8,10},{9,11},{10,... | collective-permute-start | bytes 221192 | tf_op jit(solution)/shard_map/ppermute | solution.py:18
  126.6 6.4 %collective-permute-start.22 = (bf16[192,192]{1,0:T(8,128)(2,1)}, bf16[192,192]{1,0:T(8,128)(2,1)S(1)}, u32[]{:S(2)}, u32[]{:S(2)}) collective-permute-start(bf16[192,192]{1,0:T(8,128)(2,1)} %get-tuple-element.29), channel_id=1, source_target_pairs={{0,10},{1,11},{2,8},{3,9},{4,14},{5,15},{6,12},{7,13},{8,2},{9,3},... | collective-permute-start | bytes 221192 | tf_op jit(solution)/shard_map/ppermute | solution.py:18
  (18 other events, 66.3 us)

commit v2 on v0

v2 whole, which is shorter than its diff:
```python
import jax
import jax.numpy as jnp
from jax import lax
from jax.experimental import pallas as pl
from jax.experimental.pallas import tpu as pltpu
from jax.sharding import PartitionSpec as P

GRID_ROWS = 4
GRID_COLS = 4
CORE, XBIT, YBIT, ZBIT = 1, 2, 4, 8
SECTOR_BIT = GRID_ROWS * GRID_COLS
EPSILON = 1e-06
EXTRA_ROWS = 16
MIB = 2**20
PLAN_BITS = 5


def exchange(block, flip, swapped=False):
    route = []
    for i in range(lax.axis_size("sec")):
        x, z = i // XBIT % 2, i // ZBIT % 2
        moved = i - x * XBIT - z * ZBIT + z * XBIT + x * ZBIT if swapped else i
        route.append((i, moved ^ flip))
    return lax.ppermute(block, "sec", route)


def smem():
    return pl.BlockSpec(memory_space=pltpu.SMEM)


def vmem():
    return pl.BlockSpec(memory_space=pltpu.VMEM)


def anywhere():
    return pl.BlockSpec(memory_space=pl.ANY)


def live_block(sizes, row_start, col_start, shape):
    rows = row_start + lax.broadcasted_iota(jnp.int32, shape, 0)
    cols = col_start + lax.broadcasted_iota(jnp.int32, shape, 1)
    return (rows < sizes[0]) & (cols < sizes[1])


def place_copies(sources, target, places, sems):
    tile = sources[0].shape[1]
    found = []
    for k in range(sources[0].shape[0]):
        pair = []
        for slot in range(2):
            row = pl.multiple_of(places[slot] * tile, tile)
            copy = pltpu.make_async_copy(
                sources[slot].at[k], target.at[k, pl.ds(row, tile)], sems.at[k, slot]
            )
            copy.start()
            pair.append(copy)
        found.append(pair)
    return found


def term_of(plan, sectors, terms, k):
    base = PLAN_BITS + 2 * sectors
    return plan[base + k], plan[base + terms + k].astype(jnp.float32)


def mix(plan, sectors, terms, k, left, vector):
    source, weight = term_of(plan, sectors, terms, k)
    product = jnp.dot(left, vector[source], preferred_element_type=jnp.float32)
    return (product * weight).astype(jnp.bfloat16)


def start_kernel(sectors, plan, near, far, left_own, vector, mixed_ref, square_ref, lefts, sems):
    terms, tile, _ = left_own.shape
    width = 2 * tile
    copies = []
    for k in range(terms):
        copy = pltpu.make_async_copy(left_own.at[k], lefts.at[k], sems.at[k])
        copy.start()
        copies.append(copy)
    core, x, y, z = plan[0], plan[1], plan[2], plan[3]
    square = jnp.zeros((8, width), jnp.float32)
    for xr in range(2):
        for yr in range(2):
            for sr in range(sectors):
                sector = plan[4] ^ sr
                row = (2 * (x ^ xr) + (y ^ yr)) * tile
                sizes = plan[PLAN_BITS + 2 * sector], plan[PLAN_BITS + 2 * sector + 1]
                mine, other = near[xr, yr, sr], far[xr, yr, sr]
                low = jnp.where(core == 0, mine, other).astype(jnp.float32)
                high = jnp.where(core == 0, other, mine).astype(jnp.float32)
                both = jnp.concatenate([low, high], axis=1)
                both = jnp.where(live_block(sizes, row, z * width, both.shape), both, 0.0)
                square += jnp.sum((both * both).reshape(tile // 8, 8, width), axis=0)
                at = pl.ds(pl.multiple_of(row, tile), tile)
                vector[sector, at, :] = both.astype(jnp.bfloat16)
    square_ref[...] = jnp.broadcast_to(jnp.sum(square), square_ref.shape)
    for k in range(terms):
        copies[k].wait()
        mixed_ref[:, k * width : (k + 1) * width] = mix(plan, sectors, terms, k, lefts[k], vector)


def first_kernel(
    sectors,
    plan,
    vector,
    mixed_own,
    left_peer,
    right_own,
    right_peer,
    kept_ref,
    sent_ref,
    lefts,
    rights,
    mixed,
    left_sems,
    right_sems,
):
    terms, tile, _ = left_peer.shape
    width = 2 * tile
    left_copies = []
    for k in range(terms):
        copy = pltpu.make_async_copy(left_peer.at[k], lefts.at[k], left_sems.at[k])
        copy.start()
        left_copies.append(copy)
    core, x, y, z = plan[0], plan[1], plan[2], plan[3]
    right_copies = place_copies((right_own, right_peer), rights, (y, 1 - y), right_sems)
    own = pl.ds(pl.multiple_of(z * tile, tile), tile)
    peer = pl.ds(pl.multiple_of((1 - z) * tile, tile), tile)
    mixed[own, :] = mixed_own[...]
    for k in range(terms):
        left_copies[k].wait()
        mixed[peer, k * width : (k + 1) * width] = mix(plan, sectors, terms, k, lefts[k], vector)
    total = collect(mixed, rights, right_copies)
    _, unit_rows, unit_cols = kept_ref.shape
    for core_is in range(2):
        for x_is in range(2):
            for z_is in range(2):

                @pl.when((core == core_is) & (x == x_is) & (z == z_is))
                def _():
                    mine = total[core_is * tile : (core_is + 1) * tile]
                    other = total[(1 - core_is) * tile : (2 - core_is) * tile]
                    for xr in range(2):
                        for zr in range(2):
                            row, col = (x_is ^ xr) * unit_rows, (z_is ^ zr) * unit_cols
                            at = slice(row, row + unit_rows), slice(col, col + unit_cols)
                            kept_ref[2 * zr + xr] = mine[at]
                            sent_ref[2 * zr + xr] = other[at].astype(sent_ref.dtype)


def collect(mixed, rights, copies):
    for pair in copies:
        for copy in pair:
            copy.wait()
    terms, height, width = rights.shape
    flat = rights[...].reshape(terms * height, width)
    return jnp.dot(mixed[...], flat, preferred_element_type=jnp.float32)


def second_kernel(
    sectors,
    plan,
    square_ref,
    start_ref,
    near,
    far,
    left_own,
    left_peer,
    right_own,
    right_peer,
    kept_ref,
    sent_ref,
    start,
    vector,
    lefts,
    rights,
    mixed,
    start_sem,
    left_sems,
    right_sems,
):
    terms, tile, _ = left_own.shape
    width = 2 * tile
    half = tile // 2
    core, x, y, z = plan[0], plan[1], plan[2], plan[3]
    left_copies = place_copies((left_own, left_peer), lefts, (z, 1 - z), left_sems)
    start_copy = pltpu.make_async_copy(start_ref, start, start_sem)
    start_copy.start()
    right_copies = place_copies((right_own, right_peer), rights, (y, 1 - y), right_sems)
    for pieces, z_row in ((near, core), (far, 1 - core)):
        for xr in range(2):
            for yr in range(2):
                for sr in range(sectors):
                    row = (2 * z_row + (y ^ yr)) * tile + (x ^ xr) * half
                    at = pl.ds(pl.multiple_of(row, half), half)
                    vector[plan[4] ^ sr, at, :] = pieces[2 * xr + yr, sr]
    inner = jnp.zeros((8, width), jnp.float32)
    norm = inner
    share = vector.shape[1] // terms
    for k in range(terms):
        for copy in left_copies[k]:
            copy.wait()
        mixed[:, k * width : (k + 1) * width] = mix(plan, sectors, terms, k, lefts[k], vector)
        if k == 0:
            start_copy.wait()
        for sector in range(sectors):
            rows = slice(k * share, (k + 1) * share)
            image = vector[sector, rows, :].astype(jnp.float32)
            before = start[sector, rows, :].astype(jnp.float32)
            inner += jnp.sum((before * image).reshape(share // 8, 8, width), axis=0)
            norm += jnp.sum((image * image).reshape(share // 8, 8, width), axis=0)
    total = collect(mixed, rights, right_copies)
    extra_shape = (EXTRA_ROWS, kept_ref.shape[2])
    lane = lax.broadcasted_iota(jnp.int32, extra_shape, 1)
    zeros = jnp.zeros(extra_shape, jnp.float32)
    own_sums, z_sums = zeros, zeros
    for k, value in enumerate((square_ref[0, 0], jnp.sum(inner), jnp.sum(norm))):
        value = jnp.broadcast_to(value, extra_shape)
        own_sums = jnp.where(lane == k, value, own_sums)
        for level in range(3):
            piece = value.astype(jnp.bfloat16).astype(jnp.float32)
            z_sums = jnp.where(lane == 3 * k + level, piece, z_sums)
            value = value - piece
    for core_is in range(2):
        for x_is in range(2):
            for z_is in range(2):

                @pl.when((core == core_is) & (x == x_is) & (z == z_is))
                def _():
                    for xr in range(2):
                        for zr in range(2):
                            to = 2 * zr + xr
                            rows = slice((z_is ^ zr) * tile, ((z_is ^ zr) + 1) * tile)
                            col = (x_is ^ xr) * width
                            mine = col + core_is * tile
                            other = col + (1 - core_is) * tile
                            kept_ref[to, :tile] = total[rows, mine : mine + tile]
                            sent_ref[to, :tile] = total[rows, other : other + tile].astype(jnp.bfloat16)

    for to in range(4):
        kept_ref[to, tile:] = (own_sums, zeros, z_sums, zeros)[to]
        sent_ref[to, tile:] = zeros.astype(jnp.bfloat16)


def last_kernel(plan, own_ref, from_x, from_z, from_xz, image_ref, first_ref, out_ref):
    _, rows, cols = out_ref.shape
    first_ref[0] = image_ref[...]
    total = own_ref[:rows] + from_x[:rows].astype(jnp.float32)
    total += from_z[:rows].astype(jnp.float32) + from_xz[:rows].astype(jnp.float32)
    own_sums = own_ref[rows : rows + 8]
    z_sums = from_z[rows : rows + EXTRA_ROWS].astype(jnp.float32)[:8]
    lane = lax.broadcasted_iota(jnp.int32, own_sums.shape, 1)

    def pick(values, wanted):
        return jnp.sum(jnp.where(wanted, values, 0.0), axis=1, keepdims=True)[:1]

    sums = []
    for k in range(3):
        z_part = pick(z_sums, (lane >= 3 * k) & (lane < 3 * k + 3))
        sums.append(pick(own_sums, lane == k) + z_part)
    square, inner, norm = sums
    quotient = inner / square
    residual_square = jnp.maximum(norm - quotient * inner, 0.0)
    scale = lax.rsqrt(residual_square / square + EPSILON)
    core, x, y, z, sector = plan[0], plan[1], plan[2], plan[3], plan[4]
    sizes = plan[PLAN_BITS + 2 * sector], plan[PLAN_BITS + 2 * sector + 1]
    keep = live_block(sizes, (2 * z + y) * rows, (2 * x + core) * cols, (rows, cols))
    second = (total - quotient * image_ref[...].astype(jnp.float32)) * scale
    out_ref[0] = jnp.where(keep, second, 0.0).astype(jnp.bfloat16)


def on_device(
    wavefunction, left_environment, right_environment, sector_sizes, pairing, term_mask, coupling
):
    tile = wavefunction.shape[1]
    terms = left_environment.shape[0]
    sectors = lax.axis_size("sec") // SECTOR_BIT
    capacity = tile * GRID_ROWS
    bf16, f32 = jnp.bfloat16, jnp.float32

    def shaped(*shape, dtype=bf16):
        return jax.ShapeDtypeStruct(shape, dtype)

    index = lax.axis_index("sec").astype(jnp.int32)
    bits = [index % 2, index // XBIT % 2, index // YBIT % 2, index // ZBIT % 2, index // SECTOR_BIT]
    sizes = jnp.stack([sector_sizes[0], jnp.take(sector_sizes[1], pairing)], axis=1)
    group = index % GRID_COLS * terms

    def mine(table):
        row = lax.dynamic_slice(table, (bits[4], group), (1, terms))
        return row.reshape(terms)

    plan = jnp.concatenate([jnp.stack(bits), sizes.reshape(-1), mine(coupling), mine(term_mask)])

    tiles = []
    for y_flip in (0, YBIT):
        for sector_flip in range(0, lax.axis_size("sec"), SECTOR_BIT):
            tiles.append(exchange(wavefunction[0], y_flip | sector_flip, swapped=True))
    tiles = jnp.stack(tiles).reshape(2, sectors, tile, tile)
    gate_left, gate_right, gated = lax.optimization_barrier((left_environment, right_environment, tiles))
    tiles = jnp.stack([gated, exchange(gated, XBIT)])
    far_tiles = exchange(tiles, CORE)

    left_peer = exchange(gate_left, ZBIT)
    right_peer = exchange(gate_right, YBIT)

    def work(macs):
        return pl.CostEstimate(flops=2 * macs, bytes_accessed=terms * tile * capacity * 4, transcendentals=0)

    width = 2 * tile
    macs = terms * tile * capacity * width
    vector_shape = (sectors, capacity, width)
    unit = (4, tile // 2, width)

    def params(mib):
        return pltpu.CompilerParams(vmem_limit_bytes=mib * MIB)

    start_vector, mixed_own, square = pl.pallas_call(
        lambda *refs: start_kernel(sectors, *refs),
        out_shape=[shaped(*vector_shape), shaped(tile, terms * width), shaped(8, 128, dtype=f32)],
        in_specs=[smem(), vmem(), vmem(), anywhere()],
        out_specs=[vmem()] * 3,
        scratch_shapes=[pltpu.VMEM((terms, tile, capacity), bf16), pltpu.SemaphoreType.DMA((terms,))],
        compiler_params=params(16),
        cost_estimate=work(macs),
    )(plan, tiles, far_tiles, left_environment)
    kept, sent = pl.pallas_call(
        lambda *refs: first_kernel(sectors, *refs),
        out_shape=[shaped(*unit, dtype=f32), shaped(*unit, dtype=f32)],
        in_specs=[smem(), vmem(), vmem()] + [anywhere()] * 3,
        out_specs=[vmem()] * 2,
        scratch_shapes=[
            pltpu.VMEM((terms, tile, capacity), bf16),
            pltpu.VMEM((terms, width, capacity), bf16),
            pltpu.VMEM((width, terms * width), bf16),
            pltpu.SemaphoreType.DMA((terms,)),
            pltpu.SemaphoreType.DMA((terms, 2)),
        ],
        compiler_params=params(20),
        cost_estimate=work(3 * macs),
    )(plan, start_vector, mixed_own, left_peer, right_environment, right_peer)

    def live(row_start, col_start, shape):
        mine = jnp.take(sizes, bits[4], axis=0)
        return live_block((mine[0], mine[1]), row_start, col_start, shape)

    summed = kept + exchange(sent, CORE)
    image_unit = (
        summed[0]
        + exchange(summed[1].astype(bf16), XBIT).astype(f32)
        + exchange(summed[2].astype(bf16), ZBIT).astype(f32)
        + exchange(summed[3].astype(bf16), XBIT | ZBIT).astype(f32)
    )
    rows, cols = unit[1:]
    keep = live((2 * bits[0] + bits[2]) * tile + bits[1] * rows, bits[3] * cols, (rows, cols))
    units = jnp.where(keep, image_unit, 0.0).astype(bf16)[None]
    flip = SECTOR_BIT
    while flip < lax.axis_size("sec"):
        units = jnp.concatenate([units, exchange(units, flip)])
        flip *= 2
    units = jnp.stack(
        [units, exchange(units, YBIT), exchange(units, XBIT), exchange(units, XBIT | YBIT)]
    )
    far_units = exchange(units, CORE)
    mine = jnp.where(bits[0] == bits[1], units[:, 0], far_units[:, 0])
    mine = jnp.where(bits[1] == 0, jnp.concatenate([mine[0], mine[2]]), jnp.concatenate([mine[2], mine[0]]))
    image_tile = jnp.where(bits[0] == 0, mine[:, :tile], mine[:, tile:])
    first_tile = exchange(image_tile, 0, swapped=True)
    part = (4, tile + EXTRA_ROWS, tile)
    kept, sent = pl.pallas_call(
        lambda *refs: second_kernel(sectors, *refs),
        out_shape=[shaped(*part, dtype=f32), shaped(*part)],
        in_specs=[smem(), vmem(), anywhere(), vmem(), vmem()] + [anywhere()] * 4,
        out_specs=[vmem()] * 2,
        scratch_shapes=[
            pltpu.VMEM(vector_shape, bf16),
            pltpu.VMEM(vector_shape, bf16),
            pltpu.VMEM((terms, width, capacity), bf16),
            pltpu.VMEM((terms, width, capacity), bf16),
            pltpu.VMEM((width, terms * width), bf16),
            pltpu.SemaphoreType.DMA,
            pltpu.SemaphoreType.DMA((terms, 2)),
            pltpu.SemaphoreType.DMA((terms, 2)),
        ],
        compiler_params=params(28),
        cost_estimate=work(4 * macs),
    )(
        plan,
        square,
        start_vector,
        units,
        far_units,
        left_environment,
        left_peer,
        right_environment,
        right_peer,
    )
    summed = kept + exchange(sent, CORE).astype(f32)
    first, second = pl.pallas_call(
        last_kernel,
        out_shape=[shaped(1, tile, tile)] * 2,
        in_specs=[smem()] + [vmem()] * 5,
        out_specs=[vmem()] * 2,
        compiler_params=pltpu.CompilerParams(vmem_limit_bytes=4 * MIB),
    )(
        plan,
        summed[0],
        exchange(summed[1].astype(bf16), XBIT),
        exchange(summed[2].astype(bf16), ZBIT),
        exchange(summed[3].astype(bf16), XBIT | ZBIT),
        first_tile,
    )
    return first, second


def solution(mesh):
    return jax.shard_map(
        on_device,
        mesh=mesh,
        in_specs=(
            P(("groups", "sec"), None, None),
            P(("groups", "sec"), None, None),
            P(("groups", "sec"), None, None),
            P(None, "groups"),
            P("groups"),
            P("groups", None),
            P("groups", None),
        ),
        out_specs=(P(("groups", "sec"), None, None), P(("groups", "sec"), None, None)),
        check_vma=False,
    )
```

time: 363 us -> 119 us (0.33)
  waiting for transfers between devices: 172 us -> 61.7 us
  blocking collectives: 80.3 us -> 0 us
  matrix products: 33.3 us -> 0 us
  local copies, waits for them, and re-layouts: 32 us -> 5.14 us
  starting transfers between devices: 8.18 us -> 29.6 us
  Pallas kernels: 0 us -> 17.9 us
  other arithmetic: 19.9 us -> 3.2 us
  between operations: 16.9 us -> 1 us
    psum x2 -> x0, blocking collectives: 80.3 us -> none  [the longest x1 40.8 us: on_device(): lax.psum((jnp.sum(start_value * first_value), jnp.sum(start_value * start...]
    all_gather x2 -> x0, waiting for transfers between devices: 67.2 us -> none  [fetch(): gathered = lax.all_gather(tile_data[None], 'sec', axis=0, tiled=True)]
    ppermute x6 -> x22, waiting for transfers between devices: 105 us -> 61.7 us  [exchange(): return lax.ppermute(block, 'sec', route)]
    dot_general x4 -> x0, matrix products: 33.3 us -> none  [the longest x2 20.2 us: operate(): jnp.einsum('kria,kijab->krjb', left_split, sources, preferred_element_typ...]
    ppermute x6 -> x22, starting transfers between devices: 8.1 us -> 29.6 us  [exchange(): return lax.ppermute(block, 'sec', route)]
    pallas_call x0 -> x4, Pallas kernels: none -> 17.9 us  [the longest x1 7.66 us: on_device(): pl.pallas_call(lambda *refs: second_kernel(sectors, *refs), out_shape=[sh...]
    reshape x3 -> x2, local copies, waits for them, and re-layouts: 17 us -> 0.16 us  [the longest x1 0.08 us: on_device(): sizes.reshape(-1)]
    gather x2 -> x1, local copies, waits for them, and re-layouts: 14.1 us -> 0.64 us  [on_device(): jnp.take(sector_sizes[1], pairing)]
  transfers between devices with their start and end apart: 8 -> 22, of which waited for: 8 -> 20; matrix products, arithmetic and copies ran while one was open for 9% -> 3% of each run, Pallas kernels for 0% -> 3%
where the time goes in v2:
time: 119 us
  waiting for transfers between devices  61.7 us (52%)
  starting transfers between devices  29.6 us (25%)
  Pallas kernels  17.9 us (15%)
  local copies, waits for them, and re-layouts  5.14 us (4%)
  other arithmetic  3.2 us (3%)
    ppermute x22, waiting for transfers between devices, exchange(): return lax.ppermute(block, 'sec', route)  61.7 us
    ppermute x22, starting transfers between devices, exchange(): return lax.ppermute(block, 'sec', route)  29.6 us
    pallas_call x1, Pallas kernels, on_device(): pl.pallas_call(lambda *refs: second_kernel(sectors, *refs), out_shape=[sh...  7.66 us
    pallas_call x1, Pallas kernels, on_device(): pl.pallas_call(lambda *refs: first_kernel(sectors, *refs), out_shape=[sha...  5.22 us
    pallas_call x1, Pallas kernels, on_device(): pl.pallas_call(lambda *refs: start_kernel(sectors, *refs), out_shape=[sha...  3.74 us
    unnamed x16, local copies, waits for them, and re-layouts  2.77 us
  transfers between devices with their start and end apart: 22, of which 20 were waited for; matrix products, arithmetic and copies ran while one was open for 3% of the time, Pallas kernels for 3%

profile of v2, /device:TPU:0, one launch (start us, length us, event | category | flops | bytes accessed | tf_op | source)
XLA Modules:
  0.0 118.6 jit_solution(8313870105687729184)
XLA Ops:
  0.7 5.1 %collective-permute-start.3 = (bf16[192,192]{1,0:T(8,128)(2,1)}, bf16[192,192]{1,0:T(8,128)(2,1)S(1)}, u32[]{:S(2)}, u32[]{:S(2)}) collective-permute-start(bf16[192,192]{1,0:T(8,128)(2,1)} %bitcast.74), channel_id=1, source_target_pairs={{0,20},{1,21},{2,28},{3,29},{4,16},{5,17},{6,24},{7,25},{8,22},{9,... | collective-permute-start | bytes 221192 | tf_op jit(solution)/shard_map/ppermute | solution.py:24
  6.4 1.5 %collective-permute-start = (bf16[192,192]{1,0:T(8,128)(2,1)}, bf16[192,192]{1,0:T(8,128)(2,1)S(1)}, u32[]{:S(2)}, u32[]{:S(2)}) collective-permute-start(bf16[192,192]{1,0:T(8,128)(2,1)} %bitcast.77), channel_id=1, source_target_pairs={{0,0},{1,1},{2,8},{3,9},{4,4},{5,5},{6,12},{7,13},{8,2},{9,3},{10,... | collective-permute-start | bytes 221192 | tf_op jit(solution)/shard_map/ppermute | solution.py:24
  7.9 2.3 %collective-permute-done.3 = bf16[192,192]{1,0:T(8,128)(2,1)S(1)} collective-permute-done((bf16[192,192]{1,0:T(8,128)(2,1)}, bf16[192,192]{1,0:T(8,128)(2,1)S(1)}, u32[]{:S(2)}, u32[]{:S(2)}) %collective-permute-start.3) | collective-permute-done | bytes 73760 | tf_op jit(solution)/shard_map/ppermute | solution.py:24
  10.8 4.4 %collective-permute-done.1 = bf16[192,192]{1,0:T(8,128)(2,1)S(1)} collective-permute-done((bf16[192,192]{1,0:T(8,128)(2,1)}, bf16[192,192]{1,0:T(8,128)(2,1)S(1)}, u32[]{:S(2)}, u32[]{:S(2)}) %collective-permute-start.1) | collective-permute-done | bytes 73760 | tf_op jit(solution)/shard_map/ppermute | solution.py:24
  15.4 4.1 %collective-permute-start.6 = (bf16[6,192,768]{2,1,0:T(8,128)(2,1)}, bf16[6,192,768]{2,1,0:T(8,128)(2,1)}, u32[]{:S(2)}, u32[]{:S(2)}) collective-permute-start(bf16[6,192,768]{2,1,0:T(8,128)(2,1)} %refs_5_.1), channel_id=1, source_target_pairs={{0,8},{1,9},{2,10},{3,11},{4,12},{5,13},{6,14},{7,15},{8,0},{9,1},... | collective-permute-start | bytes 5308424 | tf_op jit(solution)/shard_map/ppermute | solution.py:24
  19.7 1.8 %collective-permute-start.4 = (bf16[2,2,192,192]{3,2,1,0:T(8,128)(2,1)S(1)}, bf16[2,2,192,192]{3,2,1,0:T(8,128)(2,1)S(1)}, u32[]{:S(2)}, u32[]{:S(2)}) collective-permute-start(bf16[2,2,192,192]{3,2,1,0:T(8,128)(2,1)S(1)} %bitcast.64), channel_id=1, source_target_pairs={{0,2},{1,3},{2,0},{3,1},{4,6},{5,7},{6,4},{7,5},{8,10},{9,11},{10,... | collective-permute-start | bytes 884744 | tf_op jit(solution)/shard_map/ppermute | solution.py:24
  22.3 8.3 %collective-permute-done.4 = bf16[2,2,192,192]{3,2,1,0:T(8,128)(2,1)S(1)} collective-permute-done((bf16[2,2,192,192]{3,2,1,0:T(8,128)(2,1)S(1)}, bf16[2,2,192,192]{3,2,1,0:T(8,128)(2,1)S(1)}, u32[]{:S(2)}, u32[]{:S(2)}) %collective-permute-start.4) | collective-permute-done | bytes 294944 | tf_op jit(solution)/shard_map/ppermute | solution.py:24
  33.1 3.7 %shard_map.86 = (bf16[2,768,384]{2,1,0:T(8,128)(2,1)S(1)}, bf16[192,2304]{1,0:T(8,128)(2,1)S(1)}, f32[8,128]{1,0:T(8,128)S(1)}) custom-call(s32[21]{0:T(128)S(1)} %concatenate.12.refs_0_.plan, bf16[2,2,2,192,192]{4,3,2,1,0:T(8,128)(2,1)S(1)} %pad_maximum_fusion.refs_1_, bf16[2,2,2,192,192]{4,3,2,1,0:T(8,128)(2,1)S(1)} %collective-permute-done.5.refs_2_, ...), custom_call_target="tpu_custom_call" | custom-call | flops 679477248 | bytes 3538944 | tf_op jit(solution)/shard_map/pallas_call | solution.py:318
  36.8 21.5 %collective-permute-done.6.refs_3_.refs_6_ = bf16[6,192,768]{2,1,0:T(8,128)(2,1)} collective-permute-done((bf16[6,192,768]{2,1,0:T(8,128)(2,1)}, bf16[6,192,768]{2,1,0:T(8,128)(2,1)}, u32[]{:S(2)}, u32[]{:S(2)}) %collective-permute-start.6) | collective-permute-done | bytes 1769504 | tf_op jit(solution)/shard_map/ppermute | solution.py:24
  59.8 5.2 %shard_map.87 = (f32[4,96,384]{2,1,0:T(8,128)S(1)}, f32[4,96,384]{2,1,0:T(8,128)S(1)}) custom-call(s32[21]{0:T(128)S(1)} %concatenate.12.refs_0_.plan, bf16[2,768,384]{2,1,0:T(8,128)(2,1)S(1)} %get-tuple-element.14.refs_1_.refs_2_, bf16[192,2304]{1,0:T(8,128)(2,1)S(1)} %get-tuple-element.15.refs_2_, ...), custom_call_target="tpu_custom_call" | custom-call | flops 2038431744 | bytes 3538944 | tf_op jit(solution)/shard_map/pallas_call | solution.py:327
  68.4 3.4 %collective-permute-start.11 = (bf16[96,384]{1,0:T(8,128)(2,1)S(1)}, bf16[96,384]{1,0:T(8,128)(2,1)S(1)}, u32[]{:S(2)}, u32[]{:S(2)}) collective-permute-start(bf16[96,384]{1,0:T(8,128)(2,1)S(1)} %get-tuple-element.43), channel_id=1, source_target_pairs={{0,10},{1,11},{2,8},{3,9},{4,14},{5,15},{6,12},{7,13},{8,2},{9,3},... | collective-permute-start | bytes 221192 | tf_op jit(solution)/shard_map/ppermute | solution.py:24
  73.0 1.8 %collective-permute-done.11 = bf16[96,384]{1,0:T(8,128)(2,1)S(1)} collective-permute-done((bf16[96,384]{1,0:T(8,128)(2,1)S(1)}, bf16[96,384]{1,0:T(8,128)(2,1)S(1)}, u32[]{:S(2)}, u32[]{:S(2)}) %collective-permute-start.11) | collective-permute-done | bytes 73760 | tf_op jit(solution)/shard_map/ppermute | solution.py:24
  76.6 4.0 %collective-permute-start.12 = (bf16[1,96,384]{2,1,0:T(8,128)(2,1)S(1)}, bf16[1,96,384]{2,1,0:T(8,128)(2,1)S(1)}, u32[]{:S(2)}, u32[]{:S(2)}) collective-permute-start(bf16[1,96,384]{2,1,0:T(8,128)(2,1)S(1)} %fusion.5), channel_id=1, source_target_pairs={{0,16},{1,17},{2,18},{3,19},{4,20},{5,21},{6,22},{7,23},{8,24},{9,... | collective-permute-start | bytes 221192 | tf_op jit(solution)/shard_map/ppermute | solution.py:24
  80.5 3.7 %collective-permute-done.12 = bf16[1,96,384]{2,1,0:T(8,128)(2,1)S(1)} collective-permute-done((bf16[1,96,384]{2,1,0:T(8,128)(2,1)S(1)}, bf16[1,96,384]{2,1,0:T(8,128)(2,1)S(1)}, u32[]{:S(2)}, u32[]{:S(2)}) %collective-permute-start.12) | collective-permute-done | bytes 73760 | tf_op jit(solution)/shard_map/ppermute | solution.py:24
  84.8 1.8 %collective-permute-start.14 = (bf16[2,96,384]{2,1,0:T(8,128)(2,1)S(1)}, bf16[2,96,384]{2,1,0:T(8,128)(2,1)S(1)}, u32[]{:S(2)}, u32[]{:S(2)}) collective-permute-start(bf16[2,96,384]{2,1,0:T(8,128)(2,1)S(1)} %get-tuple-element.46), channel_id=1, source_target_pairs={{0,2},{1,3},{2,0},{3,1},{4,6},{5,7},{6,4},{7,5},{8,10},{9,11},{10,... | collective-permute-start | bytes 442376 | tf_op jit(solution)/shard_map/ppermute | solution.py:24
  87.9 4.1 %collective-permute-done.15 = bf16[2,96,384]{2,1,0:T(8,128)(2,1)S(1)} collective-permute-done((bf16[2,96,384]{2,1,0:T(8,128)(2,1)S(1)}, bf16[2,96,384]{2,1,0:T(8,128)(2,1)S(1)}, u32[]{:S(2)}, u32[]{:S(2)}) %collective-permute-start.15) | collective-permute-done | bytes 147488 | tf_op jit(solution)/shard_map/ppermute | solution.py:24
  92.0 1.5 %collective-permute-done.14 = bf16[2,96,384]{2,1,0:T(8,128)(2,1)S(1)} collective-permute-done((bf16[2,96,384]{2,1,0:T(8,128)(2,1)S(1)}, bf16[2,96,384]{2,1,0:T(8,128)(2,1)S(1)}, u32[]{:S(2)}, u32[]{:S(2)}) %collective-permute-start.14) | collective-permute-done | bytes 147488 | tf_op jit(solution)/shard_map/ppermute | solution.py:24
  94.3 2.0 %collective-permute-done.16.refs_4_ = bf16[4,2,96,384]{3,2,1,0:T(8,128)(2,1)S(1)} collective-permute-done((bf16[4,2,96,384]{3,2,1,0:T(8,128)(2,1)S(1)}, bf16[4,2,96,384]{3,2,1,0:T(8,128)(2,1)S(1)}, u32[]{:S(2)}, u32[]{:S(2)}) %collective-permute-start.16) | collective-permute-done | bytes 589856 | tf_op jit(solution)/shard_map/ppermute | solution.py:24
  96.3 1.5 %copy-done.2 = bf16[6,192,768]{2,1,0:T(8,128)(2,1)S(1)} copy-done((bf16[6,192,768]{2,1,0:T(8,128)(2,1)S(1)}, bf16[6,192,768]{2,1,0:T(8,128)(2,1)}, u32[]{:S(2)}) %copy-start.2) | copy-done | bytes 1769496
  99.0 7.7 %shard_map.88 = (f32[4,208,192]{2,1,0:T(8,128)S(1)}, bf16[4,208,192]{2,1,0:T(8,128)(2,1)S(1)}) custom-call(s32[21]{0:T(128)S(1)} %concatenate.12.refs_0_.plan, f32[8,128]{1,0:T(8,128)S(1)} %get-tuple-element.13.refs_1_, bf16[2,768,384]{2,1,0:T(8,128)(2,1)S(1)} %copy-done.4, bf16[4,2,96,384]{3,2,1,0:T(8,128)(2,1)S(1)} %pad_maximum_fusion.1.refs_3_, ...), custom_call_target="tpu_custom_call" | custom-call | flops 2717908992 | bytes 3538944 | tf_op jit(solution)/shard_map/pallas_call | solution.py:370
  109.0 1.5 %collective-permute-start.19 = (bf16[208,192]{1,0:T(8,128)(2,1)S(1)}, bf16[208,192]{1,0:T(8,128)(2,1)S(1)}, u32[]{:S(2)}, u32[]{:S(2)}) collective-permute-start(bf16[208,192]{1,0:T(8,128)(2,1)S(1)} %get-tuple-element.38), channel_id=1, source_target_pairs={{0,8},{1,9},{2,10},{3,11},{4,12},{5,13},{6,14},{7,15},{8,0},{9,1},... | collective-permute-start | bytes 239624 | tf_op jit(solution)/shard_map/ppermute | solution.py:24
  110.5 1.7 %collective-permute-start.20 = (bf16[208,192]{1,0:T(8,128)(2,1)S(1)}, bf16[208,192]{1,0:T(8,128)(2,1)S(1)}, u32[]{:S(2)}, u32[]{:S(2)}) collective-permute-start(bf16[208,192]{1,0:T(8,128)(2,1)S(1)} %get-tuple-element.37), channel_id=1, source_target_pairs={{0,10},{1,11},{2,8},{3,9},{4,14},{5,15},{6,12},{7,13},{8,2},{9,3},... | collective-permute-start | bytes 239624 | tf_op jit(solution)/shard_map/ppermute | solution.py:24
  112.3 1.6 %collective-permute-done.18.from_x = bf16[208,192]{1,0:T(8,128)(2,1)S(1)} collective-permute-done((bf16[208,192]{1,0:T(8,128)(2,1)S(1)}, bf16[208,192]{1,0:T(8,128)(2,1)S(1)}, u32[]{:S(2)}, u32[]{:S(2)}) %collective-permute-start.18) | collective-permute-done | bytes 79904 | tf_op jit(solution)/shard_map/ppermute | solution.py:24
  113.8 2.3 %collective-permute-done.19.from_z = bf16[208,192]{1,0:T(8,128)(2,1)S(1)} collective-permute-done((bf16[208,192]{1,0:T(8,128)(2,1)S(1)}, bf16[208,192]{1,0:T(8,128)(2,1)S(1)}, u32[]{:S(2)}, u32[]{:S(2)}) %collective-permute-start.19) | collective-permute-done | bytes 79904 | tf_op jit(solution)/shard_map/ppermute | solution.py:24
  (68 shorter events, 21.2 us)
Async XLA Ops:
  0.6 32.4 %copy-start = (bf16[6,192,768]{2,1,0:T(8,128)(2,1)S(1)}, bf16[6,192,768]{2,1,0:T(8,128)(2,1)}, u32[]{:S(2)}) copy-start(bf16[6,192,768]{2,1,0:T(8,128)(2,1)} %refs_5_.1) | copy-start | bytes 5308420
  0.7 31.1 %copy-start.5 = (s32[2,24]{1,0:T(2,128)S(1)}, s32[2,24]{1,0:T(2,128)}, u32[]{:S(2)}) copy-start(s32[2,24]{1,0:T(2,128)} %param.12) | copy-start | bytes 580
  0.7 9.5 %collective-permute-start.3 = (bf16[192,192]{1,0:T(8,128)(2,1)}, bf16[192,192]{1,0:T(8,128)(2,1)S(1)}, u32[]{:S(2)}, u32[]{:S(2)}) collective-permute-start(bf16[192,192]{1,0:T(8,128)(2,1)} %bitcast.74), channel_id=1, source_target_pairs={{0,20},{1,21},{2,28},{3,29},{4,16},{5,17},{6,24},{7,25},{8,22},{9,... | collective-permute-start | bytes 221192 | tf_op jit(solution)/shard_map/ppermute | solution.py:24
  5.7 5.1 %collective-permute-start.2 = (bf16[192,192]{1,0:T(8,128)(2,1)}, bf16[192,192]{1,0:T(8,128)(2,1)S(1)}, u32[]{:S(2)}, u32[]{:S(2)}) collective-permute-start(bf16[192,192]{1,0:T(8,128)(2,1)} %bitcast.75), channel_id=1, source_target_pairs={{0,4},{1,5},{2,12},{3,13},{4,0},{5,1},{6,8},{7,9},{8,6},{9,7},{10,... | collective-permute-start | bytes 221192 | tf_op jit(solution)/shard_map/ppermute | solution.py:24
  6.2 9.0 %collective-permute-start.1 = (bf16[192,192]{1,0:T(8,128)(2,1)}, bf16[192,192]{1,0:T(8,128)(2,1)S(1)}, u32[]{:S(2)}, u32[]{:S(2)}) collective-permute-start(bf16[192,192]{1,0:T(8,128)(2,1)} %bitcast.76), channel_id=1, source_target_pairs={{0,16},{1,17},{2,24},{3,25},{4,20},{5,21},{6,28},{7,29},{8,18},{9,... | collective-permute-start | bytes 221192 | tf_op jit(solution)/shard_map/ppermute | solution.py:24
  6.4 8.9 %collective-permute-start = (bf16[192,192]{1,0:T(8,128)(2,1)}, bf16[192,192]{1,0:T(8,128)(2,1)S(1)}, u32[]{:S(2)}, u32[]{:S(2)}) collective-permute-start(bf16[192,192]{1,0:T(8,128)(2,1)} %bitcast.77), channel_id=1, source_target_pairs={{0,0},{1,1},{2,8},{3,9},{4,4},{5,5},{6,12},{7,13},{8,2},{9,3},{10,... | collective-permute-start | bytes 221192 | tf_op jit(solution)/shard_map/ppermute | solution.py:24
  15.4 42.9 %collective-permute-start.6 = (bf16[6,192,768]{2,1,0:T(8,128)(2,1)}, bf16[6,192,768]{2,1,0:T(8,128)(2,1)}, u32[]{:S(2)}, u32[]{:S(2)}) collective-permute-start(bf16[6,192,768]{2,1,0:T(8,128)(2,1)} %refs_5_.1), channel_id=1, source_target_pairs={{0,8},{1,9},{2,10},{3,11},{4,12},{5,13},{6,14},{7,15},{8,0},{9,1},... | collective-permute-start | bytes 5308424 | tf_op jit(solution)/shard_map/ppermute | solution.py:24
  19.5 40.3 %collective-permute-start.7 = (bf16[6,192,768]{2,1,0:T(8,128)(2,1)}, bf16[6,192,768]{2,1,0:T(8,128)(2,1)}, u32[]{:S(2)}, u32[]{:S(2)}) collective-permute-start(bf16[6,192,768]{2,1,0:T(8,128)(2,1)} %refs_7_.1), channel_id=1, source_target_pairs={{0,4},{1,5},{2,6},{3,7},{4,0},{5,1},{6,2},{7,3},{8,12},{9,13},{10,... | collective-permute-start | bytes 5308424 | tf_op jit(solution)/shard_map/ppermute | solution.py:24
  19.7 10.8 %collective-permute-start.4 = (bf16[2,2,192,192]{3,2,1,0:T(8,128)(2,1)S(1)}, bf16[2,2,192,192]{3,2,1,0:T(8,128)(2,1)S(1)}, u32[]{:S(2)}, u32[]{:S(2)}) collective-permute-start(bf16[2,2,192,192]{3,2,1,0:T(8,128)(2,1)S(1)} %bitcast.64), channel_id=1, source_target_pairs={{0,2},{1,3},{2,0},{3,1},{4,6},{5,7},{6,4},{7,5},{8,10},{9,11},{10,... | collective-permute-start | bytes 884744 | tf_op jit(solution)/shard_map/ppermute | solution.py:24
  30.7 2.4 %collective-permute-start.5 = (bf16[2,2,2,192,192]{4,3,2,1,0:T(8,128)(2,1)S(1)}, bf16[2,2,2,192,192]{4,3,2,1,0:T(8,128)(2,1)S(1)}, u32[]{:S(2)}, u32[]{:S(2)}) collective-permute-start(bf16[2,2,2,192,192]{4,3,2,1,0:T(8,128)(2,1)S(1)} %pad_maximum_fusion.refs_1_), channel_id=1, source_target_pairs={{0,1},{1,0},{2,3},{3,2},{4,5},{5,4},{6,7},{7,6},{8,9},{9,8},{10,11... | collective-permute-start | bytes 1769480 | tf_op jit(solution)/shard_map/ppermute | solution.py:24
  65.0 2.2 %collective-permute-start.8 = (f32[4,96,384]{2,1,0:T(8,128)S(1)}, f32[4,96,384]{2,1,0:T(8,128)}, u32[]{:S(2)}, u32[]{:S(2)}) collective-permute-start(f32[4,96,384]{2,1,0:T(8,128)S(1)} %get-tuple-element.19), channel_id=1, source_target_pairs={{0,1},{1,0},{2,3},{3,2},{4,5},{5,4},{6,7},{7,6},{8,9},{9,8},{10,11... | collective-permute-start | bytes 1769480 | tf_op jit(solution)/shard_map/ppermute | solution.py:24
  68.4 6.4 %collective-permute-start.11 = (bf16[96,384]{1,0:T(8,128)(2,1)S(1)}, bf16[96,384]{1,0:T(8,128)(2,1)S(1)}, u32[]{:S(2)}, u32[]{:S(2)}) collective-permute-start(bf16[96,384]{1,0:T(8,128)(2,1)S(1)} %get-tuple-element.43), channel_id=1, source_target_pairs={{0,10},{1,11},{2,8},{3,9},{4,14},{5,15},{6,12},{7,13},{8,2},{9,3},... | collective-permute-start | bytes 221192 | tf_op jit(solution)/shard_map/ppermute | solution.py:24
  71.8 4.4 %collective-permute-start.10 = (bf16[96,384]{1,0:T(8,128)(2,1)S(1)}, bf16[96,384]{1,0:T(8,128)(2,1)S(1)}, u32[]{:S(2)}, u32[]{:S(2)}) collective-permute-start(bf16[96,384]{1,0:T(8,128)(2,1)S(1)} %get-tuple-element.44), channel_id=1, source_target_pairs={{0,8},{1,9},{2,10},{3,11},{4,12},{5,13},{6,14},{7,15},{8,0},{9,1},... | collective-permute-start | bytes 221192 | tf_op jit(solution)/shard_map/ppermute | solution.py:24
  72.1 4.4 %collective-permute-start.9 = (bf16[96,384]{1,0:T(8,128)(2,1)S(1)}, bf16[96,384]{1,0:T(8,128)(2,1)S(1)}, u32[]{:S(2)}, u32[]{:S(2)}) collective-permute-start(bf16[96,384]{1,0:T(8,128)(2,1)S(1)} %get-tuple-element.42), channel_id=1, source_target_pairs={{0,2},{1,3},{2,0},{3,1},{4,6},{5,7},{6,4},{7,5},{8,10},{9,11},{10,... | collective-permute-start | bytes 221192 | tf_op jit(solution)/shard_map/ppermute | solution.py:24
  76.6 7.7 %collective-permute-start.12 = (bf16[1,96,384]{2,1,0:T(8,128)(2,1)S(1)}, bf16[1,96,384]{2,1,0:T(8,128)(2,1)S(1)}, u32[]{:S(2)}, u32[]{:S(2)}) collective-permute-start(bf16[1,96,384]{2,1,0:T(8,128)(2,1)S(1)} %fusion.5), channel_id=1, source_target_pairs={{0,16},{1,17},{2,18},{3,19},{4,20},{5,21},{6,22},{7,23},{8,24},{9,... | collective-permute-start | bytes 221192 | tf_op jit(solution)/shard_map/ppermute | solution.py:24
  84.3 7.7 %collective-permute-start.15 = (bf16[2,96,384]{2,1,0:T(8,128)(2,1)S(1)}, bf16[2,96,384]{2,1,0:T(8,128)(2,1)S(1)}, u32[]{:S(2)}, u32[]{:S(2)}) collective-permute-start(bf16[2,96,384]{2,1,0:T(8,128)(2,1)S(1)} %get-tuple-element.46), channel_id=1, source_target_pairs={{0,6},{1,7},{2,4},{3,5},{4,2},{5,3},{6,0},{7,1},{8,14},{9,15},{10,... | collective-permute-start | bytes 442376 | tf_op jit(solution)/shard_map/ppermute | solution.py:24
  84.8 8.7 %collective-permute-start.14 = (bf16[2,96,384]{2,1,0:T(8,128)(2,1)S(1)}, bf16[2,96,384]{2,1,0:T(8,128)(2,1)S(1)}, u32[]{:S(2)}, u32[]{:S(2)}) collective-permute-start(bf16[2,96,384]{2,1,0:T(8,128)(2,1)S(1)} %get-tuple-element.46), channel_id=1, source_target_pairs={{0,2},{1,3},{2,0},{3,1},{4,6},{5,7},{6,4},{7,5},{8,10},{9,11},{10,... | collective-permute-start | bytes 442376 | tf_op jit(solution)/shard_map/ppermute | solution.py:24
  86.6 7.5 %collective-permute-start.13 = (bf16[2,96,384]{2,1,0:T(8,128)(2,1)S(1)}, bf16[2,96,384]{2,1,0:T(8,128)(2,1)S(1)}, u32[]{:S(2)}, u32[]{:S(2)}) collective-permute-start(bf16[2,96,384]{2,1,0:T(8,128)(2,1)S(1)} %get-tuple-element.46), channel_id=1, source_target_pairs={{0,4},{1,5},{2,6},{3,7},{4,0},{5,1},{6,2},{7,3},{8,12},{9,13},{10,... | collective-permute-start | bytes 442376 | tf_op jit(solution)/shard_map/ppermute | solution.py:24
  94.2 2.1 %collective-permute-start.16 = (bf16[4,2,96,384]{3,2,1,0:T(8,128)(2,1)S(1)}, bf16[4,2,96,384]{3,2,1,0:T(8,128)(2,1)S(1)}, u32[]{:S(2)}, u32[]{:S(2)}) collective-permute-start(bf16[4,2,96,384]{3,2,1,0:T(8,128)(2,1)S(1)} %pad_maximum_fusion.1.refs_3_), channel_id=1, source_target_pairs={{0,1},{1,0},{2,3},{3,2},{4,5},{5,4},{6,7},{7,6},{8,9},{9,8},{10,11... | collective-permute-start | bytes 1769480 | tf_op jit(solution)/shard_map/ppermute | solution.py:24
  106.7 1.8 %collective-permute-start.17 = (bf16[4,208,192]{2,1,0:T(8,128)(2,1)S(1)}, bf16[4,208,192]{2,1,0:T(8,128)(2,1)S(1)}, u32[]{:S(2)}, u32[]{:S(2)}) collective-permute-start(bf16[4,208,192]{2,1,0:T(8,128)(2,1)S(1)} %get-tuple-element.21), channel_id=1, source_target_pairs={{0,1},{1,0},{2,3},{3,2},{4,5},{5,4},{6,7},{7,6},{8,9},{9,8},{10,11... | collective-permute-start | bytes 958472 | tf_op jit(solution)/shard_map/ppermute | solution.py:24
  107.2 5.1 %collective-permute-start.21 = (bf16[192,192]{1,0:T(8,128)(2,1)S(1)}, bf16[192,192]{1,0:T(8,128)(2,1)S(1)}, u32[]{:S(2)}, u32[]{:S(2)}) collective-permute-start(bf16[192,192]{1,0:T(8,128)(2,1)S(1)} %slice_select_fusion.1), channel_id=1, source_target_pairs={{0,0},{1,1},{2,8},{3,9},{4,4},{5,5},{6,12},{7,13},{8,2},{9,3},{10,... | collective-permute-start | bytes 221192 | tf_op jit(solution)/shard_map/ppermute | solution.py:24
  108.7 5.1 %collective-permute-start.18 = (bf16[208,192]{1,0:T(8,128)(2,1)S(1)}, bf16[208,192]{1,0:T(8,128)(2,1)S(1)}, u32[]{:S(2)}, u32[]{:S(2)}) collective-permute-start(bf16[208,192]{1,0:T(8,128)(2,1)S(1)} %get-tuple-element.39), channel_id=1, source_target_pairs={{0,2},{1,3},{2,0},{3,1},{4,6},{5,7},{6,4},{7,5},{8,10},{9,11},{10,... | collective-permute-start | bytes 239624 | tf_op jit(solution)/shard_map/ppermute | solution.py:24
  109.0 7.1 %collective-permute-start.19 = (bf16[208,192]{1,0:T(8,128)(2,1)S(1)}, bf16[208,192]{1,0:T(8,128)(2,1)S(1)}, u32[]{:S(2)}, u32[]{:S(2)}) collective-permute-start(bf16[208,192]{1,0:T(8,128)(2,1)S(1)} %get-tuple-element.38), channel_id=1, source_target_pairs={{0,8},{1,9},{2,10},{3,11},{4,12},{5,13},{6,14},{7,15},{8,0},{9,1},... | collective-permute-start | bytes 239624 | tf_op jit(solution)/shard_map/ppermute | solution.py:24
  110.5 6.8 %collective-permute-start.20 = (bf16[208,192]{1,0:T(8,128)(2,1)S(1)}, bf16[208,192]{1,0:T(8,128)(2,1)S(1)}, u32[]{:S(2)}, u32[]{:S(2)}) collective-permute-start(bf16[208,192]{1,0:T(8,128)(2,1)S(1)} %get-tuple-element.37), channel_id=1, source_target_pairs={{0,10},{1,11},{2,8},{3,9},{4,14},{5,15},{6,12},{7,13},{8,2},{9,3},... | collective-permute-start | bytes 239624 | tf_op jit(solution)/shard_map/ppermute | solution.py:24
  (6 other events, 120.0 us)

commit v3 on v2

v3 whole, which is shorter than its diff:
```python
import jax
import jax.numpy as jnp
from jax import lax
from jax.experimental import pallas as pl
from jax.experimental.pallas import tpu as pltpu
from jax.sharding import PartitionSpec as P

GRID_ROWS = 4
GRID_COLS = 4
CORE, XBIT, YBIT, ZBIT = 1, 2, 4, 8
SECTOR_BIT = GRID_ROWS * GRID_COLS
EPSILON = 1e-06
EXTRA_ROWS = 16
MIB = 2**20
START_COST = 8
PLAN_BITS = 5


def exchange(block, flip, swapped=False):
    route = []
    for i in range(lax.axis_size("sec")):
        x, z = i // XBIT % 2, i // ZBIT % 2
        moved = i - x * XBIT - z * ZBIT + z * XBIT + x * ZBIT if swapped else i
        route.append((i, moved ^ flip))
    return lax.ppermute(block, "sec", route)


def smem():
    return pl.BlockSpec(memory_space=pltpu.SMEM)


def vmem():
    return pl.BlockSpec(memory_space=pltpu.VMEM)


def anywhere():
    return pl.BlockSpec(memory_space=pl.ANY)


def live_block(sizes, row_start, col_start, shape):
    rows = row_start + lax.broadcasted_iota(jnp.int32, shape, 0)
    cols = col_start + lax.broadcasted_iota(jnp.int32, shape, 1)
    return (rows < sizes[0]) & (cols < sizes[1])


def place_copies(sources, target, places, sems):
    tile = sources[0].shape[1]
    found = []
    for k in range(sources[0].shape[0]):
        pair = []
        for slot in range(2):
            row = pl.multiple_of(places[slot] * tile, tile)
            copy = pltpu.make_async_copy(
                sources[slot].at[k], target.at[k, pl.ds(row, tile)], sems.at[k, slot]
            )
            copy.start()
            pair.append(copy)
        found.append(pair)
    return found


def term_of(plan, sectors, terms, k):
    base = PLAN_BITS + 2 * sectors
    return plan[base + k], plan[base + terms + k].astype(jnp.float32)


def mix(plan, sectors, terms, k, left, vector):
    source, weight = term_of(plan, sectors, terms, k)
    product = jnp.dot(left, vector[source], preferred_element_type=jnp.float32)
    return (product * weight).astype(jnp.bfloat16)


def start_kernel(
    sectors, plan, near, far, left_own, right_own, vector, mixed_ref, square_ref, lefts, rights, sems
):
    terms, tile, _ = left_own.shape
    width = 2 * tile
    core, x, y, z = plan[0], plan[1], plan[2], plan[3]
    copies = []
    for k in range(terms):
        copy = pltpu.make_async_copy(left_own.at[k], lefts.at[k], sems.at[k])
        copy.start()
        copies.append(copy)
    copy = pltpu.make_async_copy(right_own, rights, sems.at[terms])
    copy.start()
    copies.append(copy)
    square = jnp.zeros((8, width), jnp.float32)
    for xr in range(2):
        for yr in range(2):
            for sr in range(sectors):
                sector = plan[4] ^ sr
                row = (2 * (x ^ xr) + (y ^ yr)) * tile
                sizes = plan[PLAN_BITS + 2 * sector], plan[PLAN_BITS + 2 * sector + 1]
                mine, other = near[xr, yr, sr], far[xr, yr, sr]
                low = jnp.where(core == 0, mine, other).astype(jnp.float32)
                high = jnp.where(core == 0, other, mine).astype(jnp.float32)
                both = jnp.concatenate([low, high], axis=1)
                both = jnp.where(live_block(sizes, row, z * width, both.shape), both, 0.0)
                square += jnp.sum((both * both).reshape(tile // 8, 8, width), axis=0)
                at = pl.ds(pl.multiple_of(row, tile), tile)
                vector[sector, at, :] = both.astype(jnp.bfloat16)
    square_ref[...] = jnp.broadcast_to(jnp.sum(square), square_ref.shape)
    for k in range(terms):
        copies[k].wait()
        mixed_ref[:, k * width : (k + 1) * width] = mix(plan, sectors, terms, k, lefts[k], vector)
    copies[terms].wait()


def first_kernel(
    sectors,
    plan,
    vector,
    mixed_own,
    left_own,
    left_peer,
    right_own,
    right_peer,
    kept_ref,
    sent_ref,
    lefts,
    rights,
    mixed,
    left_sems,
    right_sems,
    own_sem,
):
    terms, tile, _ = left_peer.shape
    width = 2 * tile
    core, x, y, z = plan[0], plan[1], plan[2], plan[3]
    peer = pl.ds(pl.multiple_of((1 - z) * tile, tile), tile)
    left_copies = []
    for k in range(terms):
        copy = pltpu.make_async_copy(left_peer.at[k], lefts.at[k, peer], left_sems.at[k])
        copy.start()
        left_copies.append(copy)
    right_copies = place_copies((right_own, right_peer), rights, (y, 1 - y), right_sems)
    own = pl.ds(pl.multiple_of(z * tile, tile), tile)
    left_copy = pltpu.make_async_copy(left_own, lefts.at[:, own], own_sem)
    left_copy.start()
    mixed[own, :] = mixed_own[...]
    for k in range(terms):
        left_copies[k].wait()
        mixed[peer, k * width : (k + 1) * width] = mix(plan, sectors, terms, k, lefts[k, peer], vector)
    total = collect(mixed, rights, right_copies)
    left_copy.wait()
    sizes = plan[PLAN_BITS + 2 * plan[4]], plan[PLAN_BITS + 2 * plan[4] + 1]
    parts = []
    for z_row in range(2):
        part = total[z_row * tile : (z_row + 1) * tile]
        keep = live_block(sizes, (2 * z_row + y) * tile, 0, part.shape)
        parts.append(jnp.where(keep, part, 0.0))
    _, unit_rows, unit_cols = kept_ref.shape
    for core_is in range(2):
        for x_is in range(2):
            for z_is in range(2):

                @pl.when((core == core_is) & (x == x_is) & (z == z_is))
                def _():
                    mine, other = parts[core_is], parts[1 - core_is]
                    for xr in range(2):
                        for zr in range(2):
                            row, col = (x_is ^ xr) * unit_rows, (z_is ^ zr) * unit_cols
                            at = slice(row, row + unit_rows), slice(col, col + unit_cols)
                            kept_ref[2 * zr + xr] = mine[at]
                            sent_ref[2 * zr + xr] = other[at].astype(sent_ref.dtype)


def collect(mixed, rights, copies):
    for pair in copies:
        for copy in pair:
            copy.wait()
    terms, height, width = rights.shape
    flat = rights[...].reshape(terms * height, width)
    return jnp.dot(mixed[...], flat, preferred_element_type=jnp.float32)


def second_kernel(
    sectors,
    plan,
    square_ref,
    start,
    near,
    far,
    lefts,
    rights,
    kept_ref,
    sent_ref,
    tiles_ref,
    vector,
    mixed,
):
    terms, width, _ = lefts.shape
    tile = width // 2
    half = tile // 2
    core, x, y, z = plan[0], plan[1], plan[2], plan[3]
    for pieces, z_row in ((near, core), (far, 1 - core)):
        for xr in range(2):
            for yr in range(2):
                for sr in range(sectors):
                    row = (2 * z_row + (y ^ yr)) * tile + (x ^ xr) * half
                    at = pl.ds(pl.multiple_of(row, half), half)
                    vector[plan[4] ^ sr, at, :] = pieces[2 * xr + yr, sr]
    inner = jnp.zeros((8, width), jnp.float32)
    norm = inner
    for k in range(terms):
        mixed[:, k * width : (k + 1) * width] = mix(plan, sectors, terms, k, lefts[k], vector)
        if k < 4:
            for sr in range(sectors):
                row = (2 * core + (y ^ (k % 2))) * tile + (x ^ (k // 2)) * half
                at = pl.ds(pl.multiple_of(row, half), half)
                image = near[k, sr].astype(jnp.float32)
                before = start[plan[4] ^ sr, at, :].astype(jnp.float32)
                inner += jnp.sum((before * image).reshape(half // 8, 8, width), axis=0)
                norm += jnp.sum((image * image).reshape(half // 8, 8, width), axis=0)
    total = collect(mixed, rights, [])
    extra_shape = (EXTRA_ROWS, kept_ref.shape[2])
    lane = lax.broadcasted_iota(jnp.int32, extra_shape, 1)
    zeros = jnp.zeros(extra_shape, jnp.float32)
    own_sums, z_sums = zeros, zeros
    for k, value in enumerate((0.5 * square_ref[0, 0], jnp.sum(inner), jnp.sum(norm))):
        value = jnp.broadcast_to(value, extra_shape)
        own_sums = jnp.where(lane == k, value, own_sums)
        for level in range(3):
            piece = value.astype(jnp.bfloat16).astype(jnp.float32)
            z_sums = jnp.where(lane == 9 * core + 3 * k + level, piece, z_sums)
            value = value - piece

    def packed(block, row, col):
        halves = [block[row + r : row + r + half, col : col + tile] for r in (0, half)]
        return jnp.concatenate(halves, axis=1)

    image_tiles = []
    for z_row in (z, 1 - z):
        row = pl.multiple_of((2 * z_row + y) * tile, tile)
        image_tiles.append(vector[plan[4], pl.ds(row, tile), :].astype(jnp.float32))
    for core_is in range(2):

        @pl.when(core == core_is)
        def _():
            for k in range(2):
                tiles_ref[k] = packed(image_tiles[k], 0, core_is * tile).astype(tiles_ref.dtype)

        for x_is in range(2):
            for z_is in range(2):

                @pl.when((core == core_is) & (x == x_is) & (z == z_is))
                def _():
                    for xr in range(2):
                        for zr in range(2):
                            row = (z_is ^ zr) * tile
                            col = (x_is ^ xr) * width
                            mine = packed(total, row, col + core_is * tile)
                            other = packed(total, row, col + (1 - core_is) * tile)
                            kept_ref[2 * zr + xr, :half] = mine
                            sent_ref[2 * zr + xr, :half] = other

    for to in range(4):
        kept_ref[to, half:] = (own_sums, zeros, z_sums, zeros)[to]
        sent_ref[to, half:] = (own_sums, zeros, z_sums, zeros)[to]


def last_kernel(plan, own_ref, from_x, from_z, from_xz, tiles_ref, first_ref, out_ref):
    _, rows, cols = out_ref.shape
    half = rows // 2
    core, x, y, z, sector = plan[0], plan[1], plan[2], plan[3], plan[4]
    total = own_ref[:half] + from_x[:half].astype(jnp.float32)
    total += from_z[:half].astype(jnp.float32) + from_xz[:half].astype(jnp.float32)
    own_sums = own_ref[half : half + 8]
    z_sums = from_z[half : half + EXTRA_ROWS].astype(jnp.float32)[:8]
    sent_tile = from_z[half + EXTRA_ROWS :].astype(jnp.float32)
    image = jnp.where(x == z, tiles_ref[0].astype(jnp.float32), sent_tile)
    lane = lax.broadcasted_iota(jnp.int32, own_sums.shape, 1)

    def pick(values, wanted):
        return jnp.sum(jnp.where(wanted, values, 0.0), axis=1, keepdims=True)[:1]

    sums = []
    for k in range(3):
        z_part = pick(z_sums, (lane % 9 // 3 == k) & (lane < 18))
        sums.append(pick(own_sums, lane == k) + z_part)
    square, inner, norm = sums
    quotient = inner / square
    residual_square = jnp.maximum(norm - quotient * inner, 0.0)
    scale = lax.rsqrt(residual_square / square + EPSILON)
    sizes = plan[PLAN_BITS + 2 * sector], plan[PLAN_BITS + 2 * sector + 1]
    second = (total - quotient * image) * scale
    for k in range(2):
        at = slice(k * half, (k + 1) * half)
        part = slice(k * cols, (k + 1) * cols)
        first_ref[0, at] = image[:, part].astype(jnp.bfloat16)
        row = (2 * z + y) * rows + k * half
        keep = live_block(sizes, row, (2 * x + core) * cols, (half, cols))
        out_ref[0, at] = jnp.where(keep, second[:, part], 0.0).astype(jnp.bfloat16)


def on_device(
    wavefunction, left_environment, right_environment, sector_sizes, pairing, term_mask, coupling
):
    tile = wavefunction.shape[1]
    terms = left_environment.shape[0]
    sectors = lax.axis_size("sec") // SECTOR_BIT
    capacity = tile * GRID_ROWS
    bf16, f32 = jnp.bfloat16, jnp.float32

    def shaped(*shape, dtype=bf16):
        return jax.ShapeDtypeStruct(shape, dtype)

    index = lax.axis_index("sec").astype(jnp.int32)
    bits = [index % 2, index // XBIT % 2, index // YBIT % 2, index // ZBIT % 2, index // SECTOR_BIT]
    sizes = jnp.stack([sector_sizes[0], jnp.take(sector_sizes[1], pairing)], axis=1)
    group = index % GRID_COLS * terms

    def mine(table):
        row = lax.dynamic_slice(table, (bits[4], group), (1, terms))
        return row.reshape(terms)

    plan = jnp.concatenate([jnp.stack(bits), sizes.reshape(-1), mine(coupling), mine(term_mask)])

    tiles = []
    for y_flip in (0, YBIT):
        for sector_flip in range(0, lax.axis_size("sec"), SECTOR_BIT):
            tiles.append(exchange(wavefunction[0], y_flip | sector_flip, swapped=True))
    tiles = jnp.stack(tiles).reshape(2, sectors, tile, tile)
    tiles = jnp.stack([tiles, exchange(tiles, XBIT)])
    far_tiles = exchange(tiles, CORE)

    left_peer = exchange(left_environment, ZBIT)
    right_peer = exchange(right_environment, YBIT)

    def work(macs):
        return pl.CostEstimate(flops=2 * macs, bytes_accessed=terms * tile * capacity * 4, transcendentals=0)

    width = 2 * tile
    macs = terms * tile * capacity * width
    vector_shape = (sectors, capacity, width)
    unit = (4, tile // 2, width)

    def params(mib):
        return pltpu.CompilerParams(vmem_limit_bytes=mib * MIB)

    environments = shaped(terms, width, capacity)
    start_vector, mixed_own, square, left_own, right_own = pl.pallas_call(
        lambda *refs: start_kernel(sectors, *refs),
        out_shape=[shaped(*vector_shape), shaped(tile, terms * width), shaped(8, 128, dtype=f32)]
        + [shaped(terms, tile, capacity)] * 2,
        in_specs=[smem(), vmem(), vmem(), anywhere(), anywhere()],
        out_specs=[vmem()] * 5,
        scratch_shapes=[pltpu.SemaphoreType.DMA((terms + 1,))],
        compiler_params=params(16),
        cost_estimate=work(START_COST * macs),
    )(plan, tiles, far_tiles, left_environment, right_environment)
    kept, sent, lefts, rights = pl.pallas_call(
        lambda *refs: first_kernel(sectors, *refs),
        out_shape=[shaped(*unit, dtype=f32), shaped(*unit, dtype=f32), environments, environments],
        in_specs=[smem(), vmem(), vmem()] + [anywhere()] * 4,
        out_specs=[vmem()] * 4,
        scratch_shapes=[
            pltpu.VMEM((width, terms * width), bf16),
            pltpu.SemaphoreType.DMA((terms,)),
            pltpu.SemaphoreType.DMA((terms, 2)),
            pltpu.SemaphoreType.DMA,
        ],
        compiler_params=params(20),
        cost_estimate=work(3 * macs),
    )(plan, start_vector, mixed_own, left_own, left_peer, right_own, right_peer)

    summed = kept + exchange(sent, CORE)
    image_unit = (
        summed[0]
        + exchange(summed[1].astype(bf16), XBIT).astype(f32)
        + exchange(summed[2].astype(bf16), ZBIT).astype(f32)
        + exchange(summed[3].astype(bf16), XBIT | ZBIT).astype(f32)
    )
    units = image_unit.astype(bf16)[None]
    flip = SECTOR_BIT
    while flip < lax.axis_size("sec"):
        units = jnp.concatenate([units, exchange(units, flip)])
        flip *= 2
    units = jnp.stack(
        [units, exchange(units, YBIT), exchange(units, XBIT), exchange(units, XBIT | YBIT)]
    )
    far_units = exchange(units, CORE)
    half = tile // 2
    part = (4, half + EXTRA_ROWS, width)
    kept, sent, image_tiles = pl.pallas_call(
        lambda *refs: second_kernel(sectors, *refs),
        out_shape=[shaped(*part, dtype=f32)] * 2 + [shaped(2, half, width)],
        in_specs=[smem()] + [vmem()] * 6,
        out_specs=[vmem()] * 3,
        scratch_shapes=[pltpu.VMEM(vector_shape, bf16), pltpu.VMEM((width, terms * width), bf16)],
        compiler_params=params(24),
        cost_estimate=work(4 * macs),
    )(
        plan,
        square,
        start_vector,
        units,
        far_units,
        lefts,
        rights,
    )
    summed = kept + exchange(sent, CORE)
    to_z = jnp.concatenate([summed[2].astype(bf16), image_tiles[1]])
    first, second = pl.pallas_call(
        last_kernel,
        out_shape=[shaped(1, tile, tile)] * 2,
        in_specs=[smem()] + [vmem()] * 5,
        out_specs=[vmem()] * 2,
        compiler_params=params(4),
    )(
        plan,
        summed[0],
        exchange(summed[1].astype(bf16), XBIT),
        exchange(to_z, ZBIT),
        exchange(summed[3].astype(bf16), XBIT | ZBIT),
        image_tiles,
    )
    return first, second


def solution(mesh):
    return jax.shard_map(
        on_device,
        mesh=mesh,
        in_specs=(
            P(("groups", "sec"), None, None),
            P(("groups", "sec"), None, None),
            P(("groups", "sec"), None, None),
            P(None, "groups"),
            P("groups"),
            P("groups", None),
            P("groups", None),
        ),
        out_specs=(P(("groups", "sec"), None, None), P(("groups", "sec"), None, None)),
        check_vma=False,
    )
```

time: 119 us -> 106 us (0.89)
  waiting for transfers between devices: 61.7 us -> 46.9 us
  starting transfers between devices: 29.6 us -> 33.4 us
    ppermute x22 -> x21, waiting for transfers between devices: 61.7 us -> 46.9 us  [exchange(): return lax.ppermute(block, 'sec', route)]
    ppermute x22 -> x21, starting transfers between devices: 29.6 us -> 33.4 us  [exchange(): return lax.ppermute(block, 'sec', route)]
    pallas_call x1, Pallas kernels: 7.66 us -> 4.74 us  [on_device(): pl.pallas_call(lambda *refs: second_kernel(sectors, *refs), out_shape=[sh...]
    lt x2 -> x0, other arithmetic: 1.24 us -> none  [live_block(): return (rows < sizes[0]) & (cols < sizes[1])]
    pallas_call x1, Pallas kernels: 3.74 us -> 4.96 us  [on_device(): pl.pallas_call(lambda *refs: start_kernel(sectors, *refs), out_shape=[sha...]
    unnamed x16 -> x6, local copies, waits for them, and re-layouts: 2.77 us -> 2.96 us
  transfers between devices with their start and end apart: 22 -> 21, of which waited for: 20 -> 17; matrix products, arithmetic and copies ran while one was open for 3% -> 4% of each run, Pallas kernels for 3% -> 5%
where the time goes in v3:
time: 106 us
  waiting for transfers between devices  46.9 us (44%)
  starting transfers between devices  33.4 us (32%)
  Pallas kernels  16.8 us (16%)
  local copies, waits for them, and re-layouts  5.46 us (5%)
  other arithmetic  2.18 us (2%)
    ppermute x21, waiting for transfers between devices, exchange(): return lax.ppermute(block, 'sec', route)  46.9 us
    ppermute x21, starting transfers between devices, exchange(): return lax.ppermute(block, 'sec', route)  33.4 us
    pallas_call x1, Pallas kernels, on_device(): pl.pallas_call(lambda *refs: first_kernel(sectors, *refs), out_shape=[sha...  5.71 us
    pallas_call x1, Pallas kernels, on_device(): pl.pallas_call(lambda *refs: start_kernel(sectors, *refs), out_shape=[sha...  4.96 us
    pallas_call x1, Pallas kernels, on_device(): pl.pallas_call(lambda *refs: second_kernel(sectors, *refs), out_shape=[sh...  4.74 us
    unnamed x6, local copies, waits for them, and re-layouts  2.96 us
  transfers between devices with their start and end apart: 21, of which 17 were waited for; matrix products, arithmetic and copies ran while one was open for 4% of the time, Pallas kernels for 5%

profile of v3, /device:TPU:0, one launch (start us, length us, event | category | flops | bytes accessed | tf_op | source)
XLA Modules:
  0.0 105.6 jit_solution(3950067254839307248)
XLA Ops:
  0.6 5.1 %collective-permute-start.3 = (bf16[192,192]{1,0:T(8,128)(2,1)}, bf16[192,192]{1,0:T(8,128)(2,1)S(1)}, u32[]{:S(2)}, u32[]{:S(2)}) collective-permute-start(bf16[192,192]{1,0:T(8,128)(2,1)} %bitcast.68), channel_id=1, source_target_pairs={{0,20},{1,21},{2,28},{3,29},{4,16},{5,17},{6,24},{7,25},{8,22},{9,... | collective-permute-start | bytes 221192 | tf_op jit(solution)/shard_map/ppermute | solution.py:25
  6.3 1.5 %collective-permute-start = (bf16[192,192]{1,0:T(8,128)(2,1)}, bf16[192,192]{1,0:T(8,128)(2,1)S(1)}, u32[]{:S(2)}, u32[]{:S(2)}) collective-permute-start(bf16[192,192]{1,0:T(8,128)(2,1)} %bitcast.71), channel_id=1, source_target_pairs={{0,0},{1,1},{2,8},{3,9},{4,4},{5,5},{6,12},{7,13},{8,2},{9,3},{10,... | collective-permute-start | bytes 221192 | tf_op jit(solution)/shard_map/ppermute | solution.py:25
  7.9 5.5 %collective-permute-start.6 = (bf16[6,192,768]{2,1,0:T(8,128)(2,1)}, bf16[6,192,768]{2,1,0:T(8,128)(2,1)S(1)}, u32[]{:S(2)}, u32[]{:S(2)}) collective-permute-start(bf16[6,192,768]{2,1,0:T(8,128)(2,1)} %refs_3_.1), channel_id=1, source_target_pairs={{0,8},{1,9},{2,10},{3,11},{4,12},{5,13},{6,14},{7,15},{8,0},{9,1},... | collective-permute-start | bytes 5308424 | tf_op jit(solution)/shard_map/ppermute | solution.py:25
  15.4 5.7 %collective-permute-start.4 = (bf16[2,2,192,192]{3,2,1,0:T(8,128)(2,1)S(1)}, bf16[2,2,192,192]{3,2,1,0:T(8,128)(2,1)S(1)}, u32[]{:S(2)}, u32[]{:S(2)}) collective-permute-start(bf16[2,2,192,192]{3,2,1,0:T(8,128)(2,1)S(1)} %bitcast.58), channel_id=1, source_target_pairs={{0,2},{1,3},{2,0},{3,1},{4,6},{5,7},{6,4},{7,5},{8,10},{9,11},{10,... | collective-permute-start | bytes 884744 | tf_op jit(solution)/shard_map/ppermute | solution.py:25
  21.8 8.4 %collective-permute-done.4 = bf16[2,2,192,192]{3,2,1,0:T(8,128)(2,1)S(1)} collective-permute-done((bf16[2,2,192,192]{3,2,1,0:T(8,128)(2,1)S(1)}, bf16[2,2,192,192]{3,2,1,0:T(8,128)(2,1)S(1)}, u32[]{:S(2)}, u32[]{:S(2)}) %collective-permute-start.4) | collective-permute-done | bytes 294944 | tf_op jit(solution)/shard_map/ppermute | solution.py:25
  36.9 5.0 %shard_map.86 = (bf16[2,768,384]{2,1,0:T(8,128)(2,1)S(1)}, bf16[192,2304]{1,0:T(8,128)(2,1)S(1)}, f32[8,128]{1,0:T(8,128)S(1)}, bf16[6,192,768]{2,1,0:T(8,128)(2,1)S(1)}, bf16[6,192,768]{2,1,0:T(8,128)(2,1)S(1)}) custom-call(s32[21]{0:T(128)S(1)} %concatenate.9.refs_0_.plan, bf16[2,2,2,192,192]{4,3,2,1,0:T(8,128)(2,1)} %pad_maximum_fusion.refs_1_, ...), custom_call_target="tpu_custom_call" | custom-call | flops 5435817984 | bytes 3538944 | tf_op jit(solution)/shard_map/pallas_call | solution.py:342
  41.9 15.4 %collective-permute-done.6.refs_4_ = bf16[6,192,768]{2,1,0:T(8,128)(2,1)S(1)} collective-permute-done((bf16[6,192,768]{2,1,0:T(8,128)(2,1)}, bf16[6,192,768]{2,1,0:T(8,128)(2,1)S(1)}, u32[]{:S(2)}, u32[]{:S(2)}) %collective-permute-start.6) | collective-permute-done | bytes 1769504 | tf_op jit(solution)/shard_map/ppermute | solution.py:25
  57.3 5.7 %shard_map.87 = (f32[4,96,384]{2,1,0:T(8,128)S(1)}, f32[4,96,384]{2,1,0:T(8,128)S(1)}, bf16[6,384,768]{2,1,0:T(8,128)(2,1)S(1)}, bf16[6,384,768]{2,1,0:T(8,128)(2,1)S(1)}) custom-call(s32[21]{0:T(128)S(1)} %concatenate.9.refs_0_.plan, bf16[2,768,384]{2,1,0:T(8,128)(2,1)S(1)} %get-tuple-element.15.refs_1_.refs_2_, ...), custom_call_target="tpu_custom_call" | custom-call | flops 2038431744 | bytes 3538944 | tf_op jit(solution)/shard_map/pallas_call | solution.py:352
  63.1 2.0 %collective-permute-done.8 = f32[4,96,384]{2,1,0:T(8,128)S(1)} collective-permute-done((f32[4,96,384]{2,1,0:T(8,128)S(1)}, f32[4,96,384]{2,1,0:T(8,128)S(1)}, u32[]{:S(2)}, u32[]{:S(2)}) %collective-permute-start.8) | collective-permute-done | bytes 589856 | tf_op jit(solution)/shard_map/ppermute | solution.py:25
  66.4 2.4 %collective-permute-start.10 = (bf16[96,384]{1,0:T(8,128)(2,1)S(1)}, bf16[96,384]{1,0:T(8,128)(2,1)S(1)}, u32[]{:S(2)}, u32[]{:S(2)}) collective-permute-start(bf16[96,384]{1,0:T(8,128)(2,1)S(1)} %get-tuple-element.35), channel_id=1, source_target_pairs={{0,8},{1,9},{2,10},{3,11},{4,12},{5,13},{6,14},{7,15},{8,0},{9,1},... | collective-permute-start | bytes 221192 | tf_op jit(solution)/shard_map/ppermute | solution.py:25
  68.8 2.3 %collective-permute-done.9 = bf16[96,384]{1,0:T(8,128)(2,1)S(1)} collective-permute-done((bf16[96,384]{1,0:T(8,128)(2,1)S(1)}, bf16[96,384]{1,0:T(8,128)(2,1)S(1)}, u32[]{:S(2)}, u32[]{:S(2)}) %collective-permute-start.9) | collective-permute-done | bytes 73760 | tf_op jit(solution)/shard_map/ppermute | solution.py:25
  72.4 2.4 %collective-permute-start.12 = (bf16[1,96,384]{2,1,0:T(8,128)(2,1)S(1)}, bf16[1,96,384]{2,1,0:T(8,128)(2,1)S(1)}, u32[]{:S(2)}, u32[]{:S(2)}) collective-permute-start(bf16[1,96,384]{2,1,0:T(8,128)(2,1)S(1)} %fusion.4), channel_id=1, source_target_pairs={{0,16},{1,17},{2,18},{3,19},{4,20},{5,21},{6,22},{7,23},{8,24},{9,... | collective-permute-start | bytes 221192 | tf_op jit(solution)/shard_map/ppermute | solution.py:25
  74.8 3.7 %collective-permute-done.12 = bf16[1,96,384]{2,1,0:T(8,128)(2,1)S(1)} collective-permute-done((bf16[1,96,384]{2,1,0:T(8,128)(2,1)S(1)}, bf16[1,96,384]{2,1,0:T(8,128)(2,1)S(1)}, u32[]{:S(2)}, u32[]{:S(2)}) %collective-permute-start.12) | collective-permute-done | bytes 73760 | tf_op jit(solution)/shard_map/ppermute | solution.py:25
  79.7 2.3 %collective-permute-start.15 = (bf16[2,96,384]{2,1,0:T(8,128)(2,1)S(1)}, bf16[2,96,384]{2,1,0:T(8,128)(2,1)S(1)}, u32[]{:S(2)}, u32[]{:S(2)}) collective-permute-start(bf16[2,96,384]{2,1,0:T(8,128)(2,1)S(1)} %get-tuple-element.37), channel_id=1, source_target_pairs={{0,6},{1,7},{2,4},{3,5},{4,2},{5,3},{6,0},{7,1},{8,14},{9,15},{10,... | collective-permute-start | bytes 442376 | tf_op jit(solution)/shard_map/ppermute | solution.py:25
  82.1 1.7 %collective-permute-done.14 = bf16[2,96,384]{2,1,0:T(8,128)(2,1)S(1)} collective-permute-done((bf16[2,96,384]{2,1,0:T(8,128)(2,1)S(1)}, bf16[2,96,384]{2,1,0:T(8,128)(2,1)S(1)}, u32[]{:S(2)}, u32[]{:S(2)}) %collective-permute-start.14) | collective-permute-done | bytes 147488 | tf_op jit(solution)/shard_map/ppermute | solution.py:25
  84.3 1.6 %collective-permute-done.15 = bf16[2,96,384]{2,1,0:T(8,128)(2,1)S(1)} collective-permute-done((bf16[2,96,384]{2,1,0:T(8,128)(2,1)S(1)}, bf16[2,96,384]{2,1,0:T(8,128)(2,1)S(1)}, u32[]{:S(2)}, u32[]{:S(2)}) %collective-permute-start.15) | collective-permute-done | bytes 147488 | tf_op jit(solution)/shard_map/ppermute | solution.py:25
  86.0 2.0 %collective-permute-done.16.refs_4_ = bf16[4,2,96,384]{3,2,1,0:T(8,128)(2,1)S(1)} collective-permute-done((bf16[4,2,96,384]{3,2,1,0:T(8,128)(2,1)S(1)}, bf16[4,2,96,384]{3,2,1,0:T(8,128)(2,1)S(1)}, u32[]{:S(2)}, u32[]{:S(2)}) %collective-permute-start.16) | collective-permute-done | bytes 589856 | tf_op jit(solution)/shard_map/ppermute | solution.py:25
  88.0 4.7 %shard_map.88 = (f32[4,112,384]{2,1,0:T(8,128)S(1)}, f32[4,112,384]{2,1,0:T(8,128)S(1)}, bf16[2,96,384]{2,1,0:T(8,128)(2,1)S(1)}) custom-call(s32[21]{0:T(128)S(1)} %concatenate.9.refs_0_.plan, f32[8,128]{1,0:T(8,128)S(1)} %get-tuple-element.14.refs_1_, bf16[2,768,384]{2,1,0:T(8,128)(2,1)S(1)} %get-tuple-element.15.refs_1_.refs_2_, ...), custom_call_target="tpu_custom_call" | custom-call | flops 2717908992 | bytes 3538944 | tf_op jit(solution)/shard_map/pallas_call | solution.py:385
  93.0 2.0 %collective-permute-done.17 = f32[4,112,384]{2,1,0:T(8,128)S(1)} collective-permute-done((f32[4,112,384]{2,1,0:T(8,128)S(1)}, f32[4,112,384]{2,1,0:T(8,128)S(1)}, u32[]{:S(2)}, u32[]{:S(2)}) %collective-permute-start.17) | collective-permute-done | bytes 688160 | tf_op jit(solution)/shard_map/ppermute | solution.py:25
  95.1 1.8 %collective-permute-start.20 = (bf16[112,384]{1,0:T(8,128)(2,1)S(1)}, bf16[112,384]{1,0:T(8,128)(2,1)S(1)}, u32[]{:S(2)}, u32[]{:S(2)}) collective-permute-start(bf16[112,384]{1,0:T(8,128)(2,1)S(1)} %get-tuple-element.30), channel_id=1, source_target_pairs={{0,10},{1,11},{2,8},{3,9},{4,14},{5,15},{6,12},{7,13},{8,2},{9,3},... | collective-permute-start | bytes 258056 | tf_op jit(solution)/shard_map/ppermute | solution.py:25
  96.9 1.6 %collective-permute-start.18 = (bf16[112,384]{1,0:T(8,128)(2,1)S(1)}, bf16[112,384]{1,0:T(8,128)(2,1)S(1)}, u32[]{:S(2)}, u32[]{:S(2)}) collective-permute-start(bf16[112,384]{1,0:T(8,128)(2,1)S(1)} %get-tuple-element.32), channel_id=1, source_target_pairs={{0,2},{1,3},{2,0},{3,1},{4,6},{5,7},{6,4},{7,5},{8,10},{9,11},{10,... | collective-permute-start | bytes 258056 | tf_op jit(solution)/shard_map/ppermute | solution.py:25
  98.7 2.0 %collective-permute-done.20.from_xz = bf16[112,384]{1,0:T(8,128)(2,1)S(1)} collective-permute-done((bf16[112,384]{1,0:T(8,128)(2,1)S(1)}, bf16[112,384]{1,0:T(8,128)(2,1)S(1)}, u32[]{:S(2)}, u32[]{:S(2)}) %collective-permute-start.20) | collective-permute-done | bytes 86048 | tf_op jit(solution)/shard_map/ppermute | solution.py:25
  100.7 1.7 %collective-permute-done.18.from_x = bf16[112,384]{1,0:T(8,128)(2,1)S(1)} collective-permute-done((bf16[112,384]{1,0:T(8,128)(2,1)S(1)}, bf16[112,384]{1,0:T(8,128)(2,1)S(1)}, u32[]{:S(2)}, u32[]{:S(2)}) %collective-permute-start.18) | collective-permute-done | bytes 86048 | tf_op jit(solution)/shard_map/ppermute | solution.py:25
  102.5 1.7 %collective-permute-done.19.from_z = bf16[208,384]{1,0:T(8,128)(2,1)S(1)} collective-permute-done((bf16[208,384]{1,0:T(8,128)(2,1)S(1)}, bf16[208,384]{1,0:T(8,128)(2,1)S(1)}, u32[]{:S(2)}, u32[]{:S(2)}) %collective-permute-start.19) | collective-permute-done | bytes 159776 | tf_op jit(solution)/shard_map/ppermute | solution.py:25
  (50 shorter events, 16.6 us)
Async XLA Ops:
  0.6 30.7 %copy-start.2 = (s32[2]{0:T(128)S(1)}, s32[2]{0:T(128)}, u32[]{:S(2)}) copy-start(s32[2]{0:T(128)} %param.11) | copy-start | bytes 28
  0.6 12.7 %collective-permute-start.3 = (bf16[192,192]{1,0:T(8,128)(2,1)}, bf16[192,192]{1,0:T(8,128)(2,1)S(1)}, u32[]{:S(2)}, u32[]{:S(2)}) collective-permute-start(bf16[192,192]{1,0:T(8,128)(2,1)} %bitcast.68), channel_id=1, source_target_pairs={{0,20},{1,21},{2,28},{3,29},{4,16},{5,17},{6,24},{7,25},{8,22},{9,... | collective-permute-start | bytes 221192 | tf_op jit(solution)/shard_map/ppermute | solution.py:25
  5.7 9.2 %collective-permute-start.2 = (bf16[192,192]{1,0:T(8,128)(2,1)}, bf16[192,192]{1,0:T(8,128)(2,1)S(1)}, u32[]{:S(2)}, u32[]{:S(2)}) collective-permute-start(bf16[192,192]{1,0:T(8,128)(2,1)} %bitcast.69), channel_id=1, source_target_pairs={{0,4},{1,5},{2,12},{3,13},{4,0},{5,1},{6,8},{7,9},{8,6},{9,7},{10,... | collective-permute-start | bytes 221192 | tf_op jit(solution)/shard_map/ppermute | solution.py:25
  6.2 9.0 %collective-permute-start.1 = (bf16[192,192]{1,0:T(8,128)(2,1)}, bf16[192,192]{1,0:T(8,128)(2,1)S(1)}, u32[]{:S(2)}, u32[]{:S(2)}) collective-permute-start(bf16[192,192]{1,0:T(8,128)(2,1)} %bitcast.70), channel_id=1, source_target_pairs={{0,16},{1,17},{2,24},{3,25},{4,20},{5,21},{6,28},{7,29},{8,18},{9,... | collective-permute-start | bytes 221192 | tf_op jit(solution)/shard_map/ppermute | solution.py:25
  6.3 8.9 %collective-permute-start = (bf16[192,192]{1,0:T(8,128)(2,1)}, bf16[192,192]{1,0:T(8,128)(2,1)S(1)}, u32[]{:S(2)}, u32[]{:S(2)}) collective-permute-start(bf16[192,192]{1,0:T(8,128)(2,1)} %bitcast.71), channel_id=1, source_target_pairs={{0,0},{1,1},{2,8},{3,9},{4,4},{5,5},{6,12},{7,13},{8,2},{9,3},{10,... | collective-permute-start | bytes 221192 | tf_op jit(solution)/shard_map/ppermute | solution.py:25
  7.9 49.4 %collective-permute-start.6 = (bf16[6,192,768]{2,1,0:T(8,128)(2,1)}, bf16[6,192,768]{2,1,0:T(8,128)(2,1)S(1)}, u32[]{:S(2)}, u32[]{:S(2)}) collective-permute-start(bf16[6,192,768]{2,1,0:T(8,128)(2,1)} %refs_3_.1), channel_id=1, source_target_pairs={{0,8},{1,9},{2,10},{3,11},{4,12},{5,13},{6,14},{7,15},{8,0},{9,1},... | collective-permute-start | bytes 5308424 | tf_op jit(solution)/shard_map/ppermute | solution.py:25
  13.4 43.9 %collective-permute-start.7 = (bf16[6,192,768]{2,1,0:T(8,128)(2,1)}, bf16[6,192,768]{2,1,0:T(8,128)(2,1)S(1)}, u32[]{:S(2)}, u32[]{:S(2)}) collective-permute-start(bf16[6,192,768]{2,1,0:T(8,128)(2,1)} %refs_4_.1), channel_id=1, source_target_pairs={{0,4},{1,5},{2,6},{3,7},{4,0},{5,1},{6,2},{7,3},{8,12},{9,13},{10,... | collective-permute-start | bytes 5308424 | tf_op jit(solution)/shard_map/ppermute | solution.py:25
  15.4 14.9 %collective-permute-start.4 = (bf16[2,2,192,192]{3,2,1,0:T(8,128)(2,1)S(1)}, bf16[2,2,192,192]{3,2,1,0:T(8,128)(2,1)S(1)}, u32[]{:S(2)}, u32[]{:S(2)}) collective-permute-start(bf16[2,2,192,192]{3,2,1,0:T(8,128)(2,1)S(1)} %bitcast.58), channel_id=1, source_target_pairs={{0,2},{1,3},{2,0},{3,1},{4,6},{5,7},{6,4},{7,5},{8,10},{9,11},{10,... | collective-permute-start | bytes 884744 | tf_op jit(solution)/shard_map/ppermute | solution.py:25
  31.3 2.6 %collective-permute-start.5 = (bf16[2,2,2,192,192]{4,3,2,1,0:T(8,128)(2,1)}, bf16[2,2,2,192,192]{4,3,2,1,0:T(8,128)(2,1)}, u32[]{:S(2)}, u32[]{:S(2)}) collective-permute-start(bf16[2,2,2,192,192]{4,3,2,1,0:T(8,128)(2,1)} %pad_maximum_fusion.refs_1_), channel_id=1, source_target_pairs={{0,1},{1,0},{2,3},{3,2},{4,5},{5,4},{6,7},{7,6},{8,9},{9,8},{10,11... | collective-permute-start | bytes 1769480 | tf_op jit(solution)/shard_map/ppermute | solution.py:25
  34.0 1.5 %copy-start = (bf16[6,192,768]{2,1,0:T(8,128)(2,1)S(1)}, bf16[6,192,768]{2,1,0:T(8,128)(2,1)}, u32[]{:S(2)}) copy-start(bf16[6,192,768]{2,1,0:T(8,128)(2,1)} %refs_3_.1) | copy-start | bytes 5308420
  35.5 1.5 %copy-start.1 = (bf16[6,192,768]{2,1,0:T(8,128)(2,1)S(1)}, bf16[6,192,768]{2,1,0:T(8,128)(2,1)}, u32[]{:S(2)}) copy-start(bf16[6,192,768]{2,1,0:T(8,128)(2,1)} %refs_4_.1) | copy-start | bytes 5308420
  63.0 2.1 %collective-permute-start.8 = (f32[4,96,384]{2,1,0:T(8,128)S(1)}, f32[4,96,384]{2,1,0:T(8,128)S(1)}, u32[]{:S(2)}, u32[]{:S(2)}) collective-permute-start(f32[4,96,384]{2,1,0:T(8,128)S(1)} %get-tuple-element.20), channel_id=1, source_target_pairs={{0,1},{1,0},{2,3},{3,2},{4,5},{5,4},{6,7},{7,6},{8,9},{9,8},{10,11... | collective-permute-start | bytes 1769480 | tf_op jit(solution)/shard_map/ppermute | solution.py:25
  65.2 5.8 %collective-permute-start.9 = (bf16[96,384]{1,0:T(8,128)(2,1)S(1)}, bf16[96,384]{1,0:T(8,128)(2,1)S(1)}, u32[]{:S(2)}, u32[]{:S(2)}) collective-permute-start(bf16[96,384]{1,0:T(8,128)(2,1)S(1)} %get-tuple-element.33), channel_id=1, source_target_pairs={{0,2},{1,3},{2,0},{3,1},{4,6},{5,7},{6,4},{7,5},{8,10},{9,11},{10,... | collective-permute-start | bytes 221192 | tf_op jit(solution)/shard_map/ppermute | solution.py:25
  65.3 6.1 %collective-permute-start.11 = (bf16[96,384]{1,0:T(8,128)(2,1)S(1)}, bf16[96,384]{1,0:T(8,128)(2,1)S(1)}, u32[]{:S(2)}, u32[]{:S(2)}) collective-permute-start(bf16[96,384]{1,0:T(8,128)(2,1)S(1)} %get-tuple-element.34), channel_id=1, source_target_pairs={{0,10},{1,11},{2,8},{3,9},{4,14},{5,15},{6,12},{7,13},{8,2},{9,3},... | collective-permute-start | bytes 221192 | tf_op jit(solution)/shard_map/ppermute | solution.py:25
  66.4 5.9 %collective-permute-start.10 = (bf16[96,384]{1,0:T(8,128)(2,1)S(1)}, bf16[96,384]{1,0:T(8,128)(2,1)S(1)}, u32[]{:S(2)}, u32[]{:S(2)}) collective-permute-start(bf16[96,384]{1,0:T(8,128)(2,1)S(1)} %get-tuple-element.35), channel_id=1, source_target_pairs={{0,8},{1,9},{2,10},{3,11},{4,12},{5,13},{6,14},{7,15},{8,0},{9,1},... | collective-permute-start | bytes 221192 | tf_op jit(solution)/shard_map/ppermute | solution.py:25
  72.4 6.1 %collective-permute-start.12 = (bf16[1,96,384]{2,1,0:T(8,128)(2,1)S(1)}, bf16[1,96,384]{2,1,0:T(8,128)(2,1)S(1)}, u32[]{:S(2)}, u32[]{:S(2)}) collective-permute-start(bf16[1,96,384]{2,1,0:T(8,128)(2,1)S(1)} %fusion.4), channel_id=1, source_target_pairs={{0,16},{1,17},{2,18},{3,19},{4,20},{5,21},{6,22},{7,23},{8,24},{9,... | collective-permute-start | bytes 221192 | tf_op jit(solution)/shard_map/ppermute | solution.py:25
  78.5 5.2 %collective-permute-start.14 = (bf16[2,96,384]{2,1,0:T(8,128)(2,1)S(1)}, bf16[2,96,384]{2,1,0:T(8,128)(2,1)S(1)}, u32[]{:S(2)}, u32[]{:S(2)}) collective-permute-start(bf16[2,96,384]{2,1,0:T(8,128)(2,1)S(1)} %get-tuple-element.37), channel_id=1, source_target_pairs={{0,2},{1,3},{2,0},{3,1},{4,6},{5,7},{6,4},{7,5},{8,10},{9,11},{10,... | collective-permute-start | bytes 442376 | tf_op jit(solution)/shard_map/ppermute | solution.py:25
  79.1 5.2 %collective-permute-start.13 = (bf16[2,96,384]{2,1,0:T(8,128)(2,1)S(1)}, bf16[2,96,384]{2,1,0:T(8,128)(2,1)S(1)}, u32[]{:S(2)}, u32[]{:S(2)}) collective-permute-start(bf16[2,96,384]{2,1,0:T(8,128)(2,1)S(1)} %get-tuple-element.37), channel_id=1, source_target_pairs={{0,4},{1,5},{2,6},{3,7},{4,0},{5,1},{6,2},{7,3},{8,12},{9,13},{10,... | collective-permute-start | bytes 442376 | tf_op jit(solution)/shard_map/ppermute | solution.py:25
  79.7 6.1 %collective-permute-start.15 = (bf16[2,96,384]{2,1,0:T(8,128)(2,1)S(1)}, bf16[2,96,384]{2,1,0:T(8,128)(2,1)S(1)}, u32[]{:S(2)}, u32[]{:S(2)}) collective-permute-start(bf16[2,96,384]{2,1,0:T(8,128)(2,1)S(1)} %get-tuple-element.37), channel_id=1, source_target_pairs={{0,6},{1,7},{2,4},{3,5},{4,2},{5,3},{6,0},{7,1},{8,14},{9,15},{10,... | collective-permute-start | bytes 442376 | tf_op jit(solution)/shard_map/ppermute | solution.py:25
  85.9 2.1 %collective-permute-start.16 = (bf16[4,2,96,384]{3,2,1,0:T(8,128)(2,1)S(1)}, bf16[4,2,96,384]{3,2,1,0:T(8,128)(2,1)S(1)}, u32[]{:S(2)}, u32[]{:S(2)}) collective-permute-start(bf16[4,2,96,384]{3,2,1,0:T(8,128)(2,1)S(1)} %pad_maximum_fusion.1.refs_3_), channel_id=1, source_target_pairs={{0,1},{1,0},{2,3},{3,2},{4,5},{5,4},{6,7},{7,6},{8,9},{9,8},{10,11... | collective-permute-start | bytes 1769480 | tf_op jit(solution)/shard_map/ppermute | solution.py:25
  92.7 2.2 %collective-permute-start.17 = (f32[4,112,384]{2,1,0:T(8,128)S(1)}, f32[4,112,384]{2,1,0:T(8,128)S(1)}, u32[]{:S(2)}, u32[]{:S(2)}) collective-permute-start(f32[4,112,384]{2,1,0:T(8,128)S(1)} %get-tuple-element.24), channel_id=1, source_target_pairs={{0,1},{1,0},{2,3},{3,2},{4,5},{5,4},{6,7},{7,6},{8,9},{9,8},{10,11... | collective-permute-start | bytes 2064392 | tf_op jit(solution)/shard_map/ppermute | solution.py:25
  95.1 5.6 %collective-permute-start.20 = (bf16[112,384]{1,0:T(8,128)(2,1)S(1)}, bf16[112,384]{1,0:T(8,128)(2,1)S(1)}, u32[]{:S(2)}, u32[]{:S(2)}) collective-permute-start(bf16[112,384]{1,0:T(8,128)(2,1)S(1)} %get-tuple-element.30), channel_id=1, source_target_pairs={{0,10},{1,11},{2,8},{3,9},{4,14},{5,15},{6,12},{7,13},{8,2},{9,3},... | collective-permute-start | bytes 258056 | tf_op jit(solution)/shard_map/ppermute | solution.py:25
  96.9 5.6 %collective-permute-start.18 = (bf16[112,384]{1,0:T(8,128)(2,1)S(1)}, bf16[112,384]{1,0:T(8,128)(2,1)S(1)}, u32[]{:S(2)}, u32[]{:S(2)}) collective-permute-start(bf16[112,384]{1,0:T(8,128)(2,1)S(1)} %get-tuple-element.32), channel_id=1, source_target_pairs={{0,2},{1,3},{2,0},{3,1},{4,6},{5,7},{6,4},{7,5},{8,10},{9,11},{10,... | collective-permute-start | bytes 258056 | tf_op jit(solution)/shard_map/ppermute | solution.py:25
  98.5 5.7 %collective-permute-start.19 = (bf16[208,384]{1,0:T(8,128)(2,1)S(1)}, bf16[208,384]{1,0:T(8,128)(2,1)S(1)}, u32[]{:S(2)}, u32[]{:S(2)}) collective-permute-start(bf16[208,384]{1,0:T(8,128)(2,1)S(1)} %pad_maximum_fusion.3), channel_id=1, source_target_pairs={{0,8},{1,9},{2,10},{3,11},{4,12},{5,13},{6,14},{7,15},{8,0},{9,1},... | collective-permute-start | bytes 479240 | tf_op jit(solution)/shard_map/ppermute | solution.py:25

commit v4 on v3

--- a/solution.py
+++ b/solution.py
@@ -16,13 +16,17 @@
 PLAN_BITS = 5
 
 
-def exchange(block, flip, swapped=False):
+def exchange(block, flip):
+    return lax.ppermute(block, "sec", [(i, i ^ flip) for i in range(lax.axis_size("sec"))])
+
+
+def spread(tile, flip):
     route = []
     for i in range(lax.axis_size("sec")):
         x, z = i // XBIT % 2, i // ZBIT % 2
-        moved = i - x * XBIT - z * ZBIT + z * XBIT + x * ZBIT if swapped else i
-        route.append((i, moved ^ flip))
-    return lax.ppermute(block, "sec", route)
+        new_x = x ^ z if flip >= SECTOR_BIT else z
+        route.append((i, i + (new_x - x) * XBIT + (x - z) * ZBIT ^ flip))
+    return lax.ppermute(tile, "sec", route)
 
 
 def smem():
@@ -89,12 +93,15 @@
         for yr in range(2):
             for sr in range(sectors):
                 sector = plan[4] ^ sr
-                row = (2 * (x ^ xr) + (y ^ yr)) * tile
+                z_row = x ^ xr ^ z if sr else x ^ xr
+                row = (2 * z_row + (y ^ yr)) * tile
                 sizes = plan[PLAN_BITS + 2 * sector], plan[PLAN_BITS + 2 * sector + 1]
                 mine, other = near[xr, yr, sr], far[xr, yr, sr]
                 low = jnp.where(core == 0, mine, other).astype(jnp.float32)
                 high = jnp.where(core == 0, other, mine).astype(jnp.float32)
-                both = jnp.concatenate([low, high], axis=1)
+                top = jnp.concatenate([low[:, :tile], high[:, :tile]], axis=1)
+                bottom = jnp.concatenate([low[:, tile:], high[:, tile:]], axis=1)
+                both = jnp.concatenate([top, bottom], axis=0)
                 both = jnp.where(live_block(sizes, row, z * width, both.shape), both, 0.0)
                 square += jnp.sum((both * both).reshape(tile // 8, 8, width), axis=0)
                 at = pl.ds(pl.multiple_of(row, tile), tile)
@@ -122,27 +129,25 @@
     mixed,
     left_sems,
     right_sems,
-    own_sem,
 ):
     terms, tile, _ = left_peer.shape
     width = 2 * tile
     core, x, y, z = plan[0], plan[1], plan[2], plan[3]
     peer = pl.ds(pl.multiple_of((1 - z) * tile, tile), tile)
-    left_copies = []
-    for k in range(terms):
-        copy = pltpu.make_async_copy(left_peer.at[k], lefts.at[k, peer], left_sems.at[k])
-        copy.start()
-        left_copies.append(copy)
     right_copies = place_copies((right_own, right_peer), rights, (y, 1 - y), right_sems)
     own = pl.ds(pl.multiple_of(z * tile, tile), tile)
-    left_copy = pltpu.make_async_copy(left_own, lefts.at[:, own], own_sem)
-    left_copy.start()
+    left_copies = [
+        pltpu.make_async_copy(left_own, lefts.at[:, own], left_sems.at[0]),
+        pltpu.make_async_copy(left_peer, lefts.at[:, peer], left_sems.at[1]),
+    ]
+    for copy in left_copies:
+        copy.start()
     mixed[own, :] = mixed_own[...]
     for k in range(terms):
-        left_copies[k].wait()
-        mixed[peer, k * width : (k + 1) * width] = mix(plan, sectors, terms, k, lefts[k, peer], vector)
+        mixed[peer, k * width : (k + 1) * width] = mix(plan, sectors, terms, k, left_peer[k], vector)
     total = collect(mixed, rights, right_copies)
-    left_copy.wait()
+    for copy in left_copies:
+        copy.wait()
     sizes = plan[PLAN_BITS + 2 * plan[4]], plan[PLAN_BITS + 2 * plan[4] + 1]
     parts = []
     for z_row in range(2):
@@ -259,7 +264,7 @@
         sent_ref[to, half:] = (own_sums, zeros, z_sums, zeros)[to]
 
 
-def last_kernel(plan, own_ref, from_x, from_z, from_xz, tiles_ref, first_ref, out_ref):
+def last_kernel(plan, own_ref, from_x, from_z, from_xz, tiles_ref, got_ref, first_ref, out_ref):
     _, rows, cols = out_ref.shape
     half = rows // 2
     core, x, y, z, sector = plan[0], plan[1], plan[2], plan[3], plan[4]
@@ -267,8 +272,7 @@
     total += from_z[:half].astype(jnp.float32) + from_xz[:half].astype(jnp.float32)
     own_sums = own_ref[half : half + 8]
     z_sums = from_z[half : half + EXTRA_ROWS].astype(jnp.float32)[:8]
-    sent_tile = from_z[half + EXTRA_ROWS :].astype(jnp.float32)
-    image = jnp.where(x == z, tiles_ref[0].astype(jnp.float32), sent_tile)
+    image = jnp.where(x == z, tiles_ref[0], got_ref[...]).astype(jnp.float32)
     lane = lax.broadcasted_iota(jnp.int32, own_sums.shape, 1)
 
     def pick(values, wanted):
@@ -316,11 +320,12 @@
 
     plan = jnp.concatenate([jnp.stack(bits), sizes.reshape(-1), mine(coupling), mine(term_mask)])
 
+    start_tile = jnp.concatenate([wavefunction[0, : tile // 2], wavefunction[0, tile // 2 :]], axis=1)
     tiles = []
     for y_flip in (0, YBIT):
         for sector_flip in range(0, lax.axis_size("sec"), SECTOR_BIT):
-            tiles.append(exchange(wavefunction[0], y_flip | sector_flip, swapped=True))
-    tiles = jnp.stack(tiles).reshape(2, sectors, tile, tile)
+            tiles.append(spread(start_tile, y_flip | sector_flip))
+    tiles = jnp.stack(tiles).reshape(2, sectors, tile // 2, 2 * tile)
     tiles = jnp.stack([tiles, exchange(tiles, XBIT)])
     far_tiles = exchange(tiles, CORE)
 
@@ -352,13 +357,12 @@
     kept, sent, lefts, rights = pl.pallas_call(
         lambda *refs: first_kernel(sectors, *refs),
         out_shape=[shaped(*unit, dtype=f32), shaped(*unit, dtype=f32), environments, environments],
-        in_specs=[smem(), vmem(), vmem()] + [anywhere()] * 4,
+        in_specs=[smem()] + [vmem()] * 6,
         out_specs=[vmem()] * 4,
         scratch_shapes=[
             pltpu.VMEM((width, terms * width), bf16),
-            pltpu.SemaphoreType.DMA((terms,)),
+            pltpu.SemaphoreType.DMA((2,)),
             pltpu.SemaphoreType.DMA((terms, 2)),
-            pltpu.SemaphoreType.DMA,
         ],
         compiler_params=params(20),
         cost_estimate=work(3 * macs),
@@ -399,21 +403,22 @@
         lefts,
         rights,
     )
+    got_tile = exchange(image_tiles[1], ZBIT)
     summed = kept + exchange(sent, CORE)
-    to_z = jnp.concatenate([summed[2].astype(bf16), image_tiles[1]])
     first, second = pl.pallas_call(
         last_kernel,
         out_shape=[shaped(1, tile, tile)] * 2,
-        in_specs=[smem()] + [vmem()] * 5,
+        in_specs=[smem()] + [vmem()] * 6,
         out_specs=[vmem()] * 2,
         compiler_params=params(4),
     )(
         plan,
         summed[0],
         exchange(summed[1].astype(bf16), XBIT),
-        exchange(to_z, ZBIT),
+        exchange(summed[2].astype(bf16), ZBIT),
         exchange(summed[3].astype(bf16), XBIT | ZBIT),
         image_tiles,
+        got_tile,
     )
     return first, second
 

time: 106 us -> 101 us (0.953)
  waiting for transfers between devices: 46.9 us -> 44.2 us
  Pallas kernels: 16.8 us -> 15.6 us
  starting transfers between devices: 33.4 us -> 32.3 us
    ppermute x21 -> x22, waiting for transfers between devices: 46.9 us -> 44.2 us  [the longest x18 44.1 us: exchange(): lax.ppermute(block, 'sec', [(i, i ^ flip) for i in range(lax.axis_size('s...]
    pallas_call x1, Pallas kernels: 5.71 us -> 4.54 us  [on_device(): pl.pallas_call(lambda *refs: first_kernel(sectors, *refs), out_shape=[sha...]
    ppermute x21 -> x22, starting transfers between devices: 33.4 us -> 32.3 us  [the longest x18 25.9 us: exchange(): lax.ppermute(block, 'sec', [(i, i ^ flip) for i in range(lax.axis_size('s...]
  transfers between devices with their start and end apart: 21 -> 22, of which waited for: 17 -> 15; matrix products, arithmetic and copies ran while one was open for 4% -> 4% of each run, Pallas kernels for 5% -> 5%
where the time goes in v4:
time: 101 us
  waiting for transfers between devices  44.2 us (44%)
  starting transfers between devices  32.3 us (32%)
  Pallas kernels  15.6 us (15%)
  local copies, waits for them, and re-layouts  6.29 us (6%)
  other arithmetic  2.03 us (2%)
    ppermute x18, waiting for transfers between devices, exchange(): lax.ppermute(block, 'sec', [(i, i ^ flip) for i in range(lax.axis_size('s...  44.1 us
    ppermute x18, starting transfers between devices, exchange(): lax.ppermute(block, 'sec', [(i, i ^ flip) for i in range(lax.axis_size('s...  25.9 us
    ppermute x4, starting transfers between devices, spread(): return lax.ppermute(tile, 'sec', route)  6.34 us
    pallas_call x1, Pallas kernels, on_device(): pl.pallas_call(lambda *refs: start_kernel(sectors, *refs), out_shape=[sha...  4.86 us
    pallas_call x1, Pallas kernels, on_device(): pl.pallas_call(lambda *refs: second_kernel(sectors, *refs), out_shape=[sh...  4.74 us
    pallas_call x1, Pallas kernels, on_device(): pl.pallas_call(lambda *refs: first_kernel(sectors, *refs), out_shape=[sha...  4.54 us
    unnamed x6, local copies, waits for them, and re-layouts  2.96 us
  transfers between devices with their start and end apart: 22, of which 15 were waited for; matrix products, arithmetic and copies ran while one was open for 4% of the time, Pallas kernels for 5%

profile of v4, /device:TPU:0, one launch (start us, length us, event | category | flops | bytes accessed | tf_op | source)
XLA Modules:
  0.0 101.2 jit_solution(6086970387237961655)
XLA Ops:
  1.6 5.0 %collective-permute-start.3 = (bf16[96,384]{1,0:T(8,128)(2,1)S(1)}, bf16[96,384]{1,0:T(8,128)(2,1)S(1)}, u32[]{:S(2)}, u32[]{:S(2)}) collective-permute-start(bf16[96,384]{1,0:T(8,128)(2,1)S(1)} %pad_maximum_fusion.4), channel_id=1, source_target_pairs={{0,20},{1,21},{2,30},{3,31},{4,16},{5,17},{6,26},{7,27},{8,22},{9,... | collective-permute-start | bytes 221192 | tf_op jit(solution)/shard_map/ppermute | solution.py:29
  7.9 5.4 %collective-permute-start.6 = (bf16[6,192,768]{2,1,0:T(8,128)(2,1)}, bf16[6,192,768]{2,1,0:T(8,128)(2,1)S(1)}, u32[]{:S(2)}, u32[]{:S(2)}) collective-permute-start(bf16[6,192,768]{2,1,0:T(8,128)(2,1)} %refs_3_.1), channel_id=1, source_target_pairs={{0,8},{1,9},{2,10},{3,11},{4,12},{5,13},{6,14},{7,15},{8,0},{9,1},... | collective-permute-start | bytes 5308424 | tf_op jit(solution)/shard_map/ppermute | solution.py:20
  13.4 1.5 %collective-permute-start.7 = (bf16[6,192,768]{2,1,0:T(8,128)(2,1)}, bf16[6,192,768]{2,1,0:T(8,128)(2,1)S(1)}, u32[]{:S(2)}, u32[]{:S(2)}) collective-permute-start(bf16[6,192,768]{2,1,0:T(8,128)(2,1)} %refs_4_.1), channel_id=1, source_target_pairs={{0,4},{1,5},{2,6},{3,7},{4,0},{5,1},{6,2},{7,3},{8,12},{9,13},{10,... | collective-permute-start | bytes 5308424 | tf_op jit(solution)/shard_map/ppermute | solution.py:20
  15.0 3.9 %collective-permute-start.4 = (bf16[2,2,96,384]{3,2,1,0:T(8,128)(2,1)S(1)}, bf16[2,2,96,384]{3,2,1,0:T(8,128)(2,1)S(1)}, u32[]{:S(2)}, u32[]{:S(2)}) collective-permute-start(bf16[2,2,96,384]{3,2,1,0:T(8,128)(2,1)S(1)} %bitcast.61), channel_id=1, source_target_pairs={{0,2},{1,3},{2,0},{3,1},{4,6},{5,7},{6,4},{7,5},{8,10},{9,11},{10,... | collective-permute-start | bytes 884744 | tf_op jit(solution)/shard_map/ppermute | solution.py:20
  19.6 6.3 %collective-permute-done.4 = bf16[2,2,96,384]{3,2,1,0:T(8,128)(2,1)S(1)} collective-permute-done((bf16[2,2,96,384]{3,2,1,0:T(8,128)(2,1)S(1)}, bf16[2,2,96,384]{3,2,1,0:T(8,128)(2,1)S(1)}, u32[]{:S(2)}, u32[]{:S(2)}) %collective-permute-start.4) | collective-permute-done | bytes 294944 | tf_op jit(solution)/shard_map/ppermute | solution.py:20
  30.8 1.5 %copy-done.1 = bf16[6,192,768]{2,1,0:T(8,128)(2,1)S(1)} copy-done((bf16[6,192,768]{2,1,0:T(8,128)(2,1)S(1)}, bf16[6,192,768]{2,1,0:T(8,128)(2,1)}, u32[]{:S(2)}) %copy-start.1) | copy-done | bytes 1769496
  32.2 4.9 %shard_map.86 = (bf16[2,768,384]{2,1,0:T(8,128)(2,1)S(1)}, bf16[192,2304]{1,0:T(8,128)(2,1)S(1)}, f32[8,128]{1,0:T(8,128)S(1)}, bf16[6,192,768]{2,1,0:T(8,128)(2,1)S(1)}, bf16[6,192,768]{2,1,0:T(8,128)(2,1)S(1)}) custom-call(s32[21]{0:T(128)S(1)} %concatenate.9.refs_0_.plan, bf16[2,2,2,96,384]{4,3,2,1,0:T(8,128)(2,1)} %pad_maximum_fusion.refs_1_, ...), custom_call_target="tpu_custom_call" | custom-call | flops 5435817984 | bytes 3538944 | tf_op jit(solution)/shard_map/pallas_call | solution.py:347
  37.1 18.0 %collective-permute-done.6.refs_4_ = bf16[6,192,768]{2,1,0:T(8,128)(2,1)S(1)} collective-permute-done((bf16[6,192,768]{2,1,0:T(8,128)(2,1)}, bf16[6,192,768]{2,1,0:T(8,128)(2,1)S(1)}, u32[]{:S(2)}, u32[]{:S(2)}) %collective-permute-start.6) | collective-permute-done | bytes 1769504 | tf_op jit(solution)/shard_map/ppermute | solution.py:20
  55.1 4.5 %shard_map.87 = (f32[4,96,384]{2,1,0:T(8,128)S(1)}, f32[4,96,384]{2,1,0:T(8,128)S(1)}, bf16[6,384,768]{2,1,0:T(8,128)(2,1)S(1)}, bf16[6,384,768]{2,1,0:T(8,128)(2,1)S(1)}) custom-call(s32[21]{0:T(128)S(1)} %concatenate.9.refs_0_.plan, bf16[2,768,384]{2,1,0:T(8,128)(2,1)S(1)} %get-tuple-element.15.refs_1_.refs_2_, ...), custom_call_target="tpu_custom_call" | custom-call | flops 2038431744 | bytes 3538944 | tf_op jit(solution)/shard_map/pallas_call | solution.py:357
  59.7 2.0 %collective-permute-done.8 = f32[4,96,384]{2,1,0:T(8,128)S(1)} collective-permute-done((f32[4,96,384]{2,1,0:T(8,128)S(1)}, f32[4,96,384]{2,1,0:T(8,128)S(1)}, u32[]{:S(2)}, u32[]{:S(2)}) %collective-permute-start.8) | collective-permute-done | bytes 589856 | tf_op jit(solution)/shard_map/ppermute | solution.py:20
  63.0 2.4 %collective-permute-start.10 = (bf16[96,384]{1,0:T(8,128)(2,1)S(1)}, bf16[96,384]{1,0:T(8,128)(2,1)S(1)}, u32[]{:S(2)}, u32[]{:S(2)}) collective-permute-start(bf16[96,384]{1,0:T(8,128)(2,1)S(1)} %get-tuple-element.35), channel_id=1, source_target_pairs={{0,8},{1,9},{2,10},{3,11},{4,12},{5,13},{6,14},{7,15},{8,0},{9,1},... | collective-permute-start | bytes 221192 | tf_op jit(solution)/shard_map/ppermute | solution.py:20
  65.4 2.3 %collective-permute-done.9 = bf16[96,384]{1,0:T(8,128)(2,1)S(1)} collective-permute-done((bf16[96,384]{1,0:T(8,128)(2,1)S(1)}, bf16[96,384]{1,0:T(8,128)(2,1)S(1)}, u32[]{:S(2)}, u32[]{:S(2)}) %collective-permute-start.9) | collective-permute-done | bytes 73760 | tf_op jit(solution)/shard_map/ppermute | solution.py:20
  69.0 2.1 %collective-permute-start.12 = (bf16[1,96,384]{2,1,0:T(8,128)(2,1)S(1)}, bf16[1,96,384]{2,1,0:T(8,128)(2,1)S(1)}, u32[]{:S(2)}, u32[]{:S(2)}) collective-permute-start(bf16[1,96,384]{2,1,0:T(8,128)(2,1)S(1)} %fusion.4), channel_id=1, source_target_pairs={{0,16},{1,17},{2,18},{3,19},{4,20},{5,21},{6,22},{7,23},{8,24},{9,... | collective-permute-start | bytes 221192 | tf_op jit(solution)/shard_map/ppermute | solution.py:20
  71.1 4.0 %collective-permute-done.12 = bf16[1,96,384]{2,1,0:T(8,128)(2,1)S(1)} collective-permute-done((bf16[1,96,384]{2,1,0:T(8,128)(2,1)S(1)}, bf16[1,96,384]{2,1,0:T(8,128)(2,1)S(1)}, u32[]{:S(2)}, u32[]{:S(2)}) %collective-permute-start.12) | collective-permute-done | bytes 73760 | tf_op jit(solution)/shard_map/ppermute | solution.py:20
  76.2 2.5 %collective-permute-start.15 = (bf16[2,96,384]{2,1,0:T(8,128)(2,1)S(1)}, bf16[2,96,384]{2,1,0:T(8,128)(2,1)S(1)}, u32[]{:S(2)}, u32[]{:S(2)}) collective-permute-start(bf16[2,96,384]{2,1,0:T(8,128)(2,1)S(1)} %get-tuple-element.37), channel_id=1, source_target_pairs={{0,6},{1,7},{2,4},{3,5},{4,2},{5,3},{6,0},{7,1},{8,14},{9,15},{10,... | collective-permute-start | bytes 442376 | tf_op jit(solution)/shard_map/ppermute | solution.py:20
  78.7 1.7 %collective-permute-done.14 = bf16[2,96,384]{2,1,0:T(8,128)(2,1)S(1)} collective-permute-done((bf16[2,96,384]{2,1,0:T(8,128)(2,1)S(1)}, bf16[2,96,384]{2,1,0:T(8,128)(2,1)S(1)}, u32[]{:S(2)}, u32[]{:S(2)}) %collective-permute-start.14) | collective-permute-done | bytes 147488 | tf_op jit(solution)/shard_map/ppermute | solution.py:20
  80.8 1.6 %collective-permute-done.15 = bf16[2,96,384]{2,1,0:T(8,128)(2,1)S(1)} collective-permute-done((bf16[2,96,384]{2,1,0:T(8,128)(2,1)S(1)}, bf16[2,96,384]{2,1,0:T(8,128)(2,1)S(1)}, u32[]{:S(2)}, u32[]{:S(2)}) %collective-permute-start.15) | collective-permute-done | bytes 147488 | tf_op jit(solution)/shard_map/ppermute | solution.py:20
  82.5 2.0 %collective-permute-done.16.refs_4_ = bf16[4,2,96,384]{3,2,1,0:T(8,128)(2,1)S(1)} collective-permute-done((bf16[4,2,96,384]{3,2,1,0:T(8,128)(2,1)S(1)}, bf16[4,2,96,384]{3,2,1,0:T(8,128)(2,1)S(1)}, u32[]{:S(2)}, u32[]{:S(2)}) %collective-permute-start.16) | collective-permute-done | bytes 589856 | tf_op jit(solution)/shard_map/ppermute | solution.py:20
  84.5 4.7 %shard_map.88 = (f32[4,112,384]{2,1,0:T(8,128)S(1)}, f32[4,112,384]{2,1,0:T(8,128)S(1)}, bf16[2,96,384]{2,1,0:T(8,128)(2,1)S(1)}) custom-call(s32[21]{0:T(128)S(1)} %concatenate.9.refs_0_.plan, f32[8,128]{1,0:T(8,128)S(1)} %get-tuple-element.14.refs_1_, bf16[2,768,384]{2,1,0:T(8,128)(2,1)S(1)} %get-tuple-element.15.refs_1_.refs_2_, ...), custom_call_target="tpu_custom_call" | custom-call | flops 2717908992 | bytes 3538944 | tf_op jit(solution)/shard_map/pallas_call | solution.py:389
  89.5 1.8 %collective-permute-start.21 = (bf16[96,384]{1,0:T(8,128)(2,1)S(1)}, bf16[96,384]{1,0:T(8,128)(2,1)S(1)}, u32[]{:S(2)}, u32[]{:S(2)}) collective-permute-start(bf16[96,384]{1,0:T(8,128)(2,1)S(1)} %slice_bitcast_fusion.8), channel_id=1, source_target_pairs={{0,8},{1,9},{2,10},{3,11},{4,12},{5,13},{6,14},{7,15},{8,0},{9,1},... | collective-permute-start | bytes 221192 | tf_op jit(solution)/shard_map/ppermute | solution.py:20
  91.6 1.8 %collective-permute-start.20 = (bf16[112,384]{1,0:T(8,128)(2,1)S(1)}, bf16[112,384]{1,0:T(8,128)(2,1)S(1)}, u32[]{:S(2)}, u32[]{:S(2)}) collective-permute-start(bf16[112,384]{1,0:T(8,128)(2,1)S(1)} %get-tuple-element.30), channel_id=1, source_target_pairs={{0,10},{1,11},{2,8},{3,9},{4,14},{5,15},{6,12},{7,13},{8,2},{9,3},... | collective-permute-start | bytes 258056 | tf_op jit(solution)/shard_map/ppermute | solution.py:20
  93.4 1.9 %collective-permute-start.19 = (bf16[112,384]{1,0:T(8,128)(2,1)S(1)}, bf16[112,384]{1,0:T(8,128)(2,1)S(1)}, u32[]{:S(2)}, u32[]{:S(2)}) collective-permute-start(bf16[112,384]{1,0:T(8,128)(2,1)S(1)} %get-tuple-element.31), channel_id=1, source_target_pairs={{0,8},{1,9},{2,10},{3,11},{4,12},{5,13},{6,14},{7,15},{8,0},{9,1},... | collective-permute-start | bytes 258056 | tf_op jit(solution)/shard_map/ppermute | solution.py:20
  95.3 2.6 %collective-permute-done.20.from_xz = bf16[112,384]{1,0:T(8,128)(2,1)S(1)} collective-permute-done((bf16[112,384]{1,0:T(8,128)(2,1)S(1)}, bf16[112,384]{1,0:T(8,128)(2,1)S(1)}, u32[]{:S(2)}, u32[]{:S(2)}) %collective-permute-start.20) | collective-permute-done | bytes 86048 | tf_op jit(solution)/shard_map/ppermute | solution.py:20
  97.9 1.7 %collective-permute-done.19.from_z = bf16[112,384]{1,0:T(8,128)(2,1)S(1)} collective-permute-done((bf16[112,384]{1,0:T(8,128)(2,1)S(1)}, bf16[112,384]{1,0:T(8,128)(2,1)S(1)}, u32[]{:S(2)}, u32[]{:S(2)}) %collective-permute-start.19) | collective-permute-done | bytes 86048 | tf_op jit(solution)/shard_map/ppermute | solution.py:20
  (53 shorter events, 14.2 us)
Async XLA Ops:
  0.6 26.2 %copy-start.2 = (s32[2]{0:T(128)S(1)}, s32[2]{0:T(128)}, u32[]{:S(2)}) copy-start(s32[2]{0:T(128)} %param.11) | copy-start | bytes 28
  1.6 11.8 %collective-permute-start.3 = (bf16[96,384]{1,0:T(8,128)(2,1)S(1)}, bf16[96,384]{1,0:T(8,128)(2,1)S(1)}, u32[]{:S(2)}, u32[]{:S(2)}) collective-permute-start(bf16[96,384]{1,0:T(8,128)(2,1)S(1)} %pad_maximum_fusion.4), channel_id=1, source_target_pairs={{0,20},{1,21},{2,30},{3,31},{4,16},{5,17},{6,26},{7,27},{8,22},{9,... | collective-permute-start | bytes 221192 | tf_op jit(solution)/shard_map/ppermute | solution.py:29
  6.6 8.3 %collective-permute-start.2 = (bf16[96,384]{1,0:T(8,128)(2,1)S(1)}, bf16[96,384]{1,0:T(8,128)(2,1)S(1)}, u32[]{:S(2)}, u32[]{:S(2)}) collective-permute-start(bf16[96,384]{1,0:T(8,128)(2,1)S(1)} %pad_maximum_fusion.4), channel_id=1, source_target_pairs={{0,4},{1,5},{2,12},{3,13},{4,0},{5,1},{6,8},{7,9},{8,6},{9,7},{10,... | collective-permute-start | bytes 221192 | tf_op jit(solution)/shard_map/ppermute | solution.py:29
  7.1 7.8 %collective-permute-start.1 = (bf16[96,384]{1,0:T(8,128)(2,1)S(1)}, bf16[96,384]{1,0:T(8,128)(2,1)S(1)}, u32[]{:S(2)}, u32[]{:S(2)}) collective-permute-start(bf16[96,384]{1,0:T(8,128)(2,1)S(1)} %pad_maximum_fusion.4), channel_id=1, source_target_pairs={{0,16},{1,17},{2,26},{3,27},{4,20},{5,21},{6,30},{7,31},{8,18},{9,... | collective-permute-start | bytes 221192 | tf_op jit(solution)/shard_map/ppermute | solution.py:29
  7.3 7.6 %collective-permute-start = (bf16[96,384]{1,0:T(8,128)(2,1)S(1)}, bf16[96,384]{1,0:T(8,128)(2,1)S(1)}, u32[]{:S(2)}, u32[]{:S(2)}) collective-permute-start(bf16[96,384]{1,0:T(8,128)(2,1)S(1)} %pad_maximum_fusion.4), channel_id=1, source_target_pairs={{0,0},{1,1},{2,8},{3,9},{4,4},{5,5},{6,12},{7,13},{8,2},{9,3},{10,... | collective-permute-start | bytes 221192 | tf_op jit(solution)/shard_map/ppermute | solution.py:29
  7.9 47.2 %collective-permute-start.6 = (bf16[6,192,768]{2,1,0:T(8,128)(2,1)}, bf16[6,192,768]{2,1,0:T(8,128)(2,1)S(1)}, u32[]{:S(2)}, u32[]{:S(2)}) collective-permute-start(bf16[6,192,768]{2,1,0:T(8,128)(2,1)} %refs_3_.1), channel_id=1, source_target_pairs={{0,8},{1,9},{2,10},{3,11},{4,12},{5,13},{6,14},{7,15},{8,0},{9,1},... | collective-permute-start | bytes 5308424 | tf_op jit(solution)/shard_map/ppermute | solution.py:20
  13.4 41.7 %collective-permute-start.7 = (bf16[6,192,768]{2,1,0:T(8,128)(2,1)}, bf16[6,192,768]{2,1,0:T(8,128)(2,1)S(1)}, u32[]{:S(2)}, u32[]{:S(2)}) collective-permute-start(bf16[6,192,768]{2,1,0:T(8,128)(2,1)} %refs_4_.1), channel_id=1, source_target_pairs={{0,4},{1,5},{2,6},{3,7},{4,0},{5,1},{6,2},{7,3},{8,12},{9,13},{10,... | collective-permute-start | bytes 5308424 | tf_op jit(solution)/shard_map/ppermute | solution.py:20
  15.0 11.0 %collective-permute-start.4 = (bf16[2,2,96,384]{3,2,1,0:T(8,128)(2,1)S(1)}, bf16[2,2,96,384]{3,2,1,0:T(8,128)(2,1)S(1)}, u32[]{:S(2)}, u32[]{:S(2)}) collective-permute-start(bf16[2,2,96,384]{3,2,1,0:T(8,128)(2,1)S(1)} %bitcast.61), channel_id=1, source_target_pairs={{0,2},{1,3},{2,0},{3,1},{4,6},{5,7},{6,4},{7,5},{8,10},{9,11},{10,... | collective-permute-start | bytes 884744 | tf_op jit(solution)/shard_map/ppermute | solution.py:20
  26.8 2.5 %collective-permute-start.5 = (bf16[2,2,2,96,384]{4,3,2,1,0:T(8,128)(2,1)}, bf16[2,2,2,96,384]{4,3,2,1,0:T(8,128)(2,1)}, u32[]{:S(2)}, u32[]{:S(2)}) collective-permute-start(bf16[2,2,2,96,384]{4,3,2,1,0:T(8,128)(2,1)} %pad_maximum_fusion.refs_1_), channel_id=1, source_target_pairs={{0,1},{1,0},{2,3},{3,2},{4,5},{5,4},{6,7},{7,6},{8,9},{9,8},{10,11... | collective-permute-start | bytes 1769480 | tf_op jit(solution)/shard_map/ppermute | solution.py:20
  29.3 1.5 %copy-start = (bf16[6,192,768]{2,1,0:T(8,128)(2,1)S(1)}, bf16[6,192,768]{2,1,0:T(8,128)(2,1)}, u32[]{:S(2)}) copy-start(bf16[6,192,768]{2,1,0:T(8,128)(2,1)} %refs_3_.1) | copy-start | bytes 5308420
  59.6 2.1 %collective-permute-start.8 = (f32[4,96,384]{2,1,0:T(8,128)S(1)}, f32[4,96,384]{2,1,0:T(8,128)S(1)}, u32[]{:S(2)}, u32[]{:S(2)}) collective-permute-start(f32[4,96,384]{2,1,0:T(8,128)S(1)} %get-tuple-element.20), channel_id=1, source_target_pairs={{0,1},{1,0},{2,3},{3,2},{4,5},{5,4},{6,7},{7,6},{8,9},{9,8},{10,11... | collective-permute-start | bytes 1769480 | tf_op jit(solution)/shard_map/ppermute | solution.py:20
  61.8 5.8 %collective-permute-start.9 = (bf16[96,384]{1,0:T(8,128)(2,1)S(1)}, bf16[96,384]{1,0:T(8,128)(2,1)S(1)}, u32[]{:S(2)}, u32[]{:S(2)}) collective-permute-start(bf16[96,384]{1,0:T(8,128)(2,1)S(1)} %get-tuple-element.33), channel_id=1, source_target_pairs={{0,2},{1,3},{2,0},{3,1},{4,6},{5,7},{6,4},{7,5},{8,10},{9,11},{10,... | collective-permute-start | bytes 221192 | tf_op jit(solution)/shard_map/ppermute | solution.py:20
  61.9 6.1 %collective-permute-start.11 = (bf16[96,384]{1,0:T(8,128)(2,1)S(1)}, bf16[96,384]{1,0:T(8,128)(2,1)S(1)}, u32[]{:S(2)}, u32[]{:S(2)}) collective-permute-start(bf16[96,384]{1,0:T(8,128)(2,1)S(1)} %get-tuple-element.34), channel_id=1, source_target_pairs={{0,10},{1,11},{2,8},{3,9},{4,14},{5,15},{6,12},{7,13},{8,2},{9,3},... | collective-permute-start | bytes 221192 | tf_op jit(solution)/shard_map/ppermute | solution.py:20
  63.0 5.9 %collective-permute-start.10 = (bf16[96,384]{1,0:T(8,128)(2,1)S(1)}, bf16[96,384]{1,0:T(8,128)(2,1)S(1)}, u32[]{:S(2)}, u32[]{:S(2)}) collective-permute-start(bf16[96,384]{1,0:T(8,128)(2,1)S(1)} %get-tuple-element.35), channel_id=1, source_target_pairs={{0,8},{1,9},{2,10},{3,11},{4,12},{5,13},{6,14},{7,15},{8,0},{9,1},... | collective-permute-start | bytes 221192 | tf_op jit(solution)/shard_map/ppermute | solution.py:20
  69.0 6.1 %collective-permute-start.12 = (bf16[1,96,384]{2,1,0:T(8,128)(2,1)S(1)}, bf16[1,96,384]{2,1,0:T(8,128)(2,1)S(1)}, u32[]{:S(2)}, u32[]{:S(2)}) collective-permute-start(bf16[1,96,384]{2,1,0:T(8,128)(2,1)S(1)} %fusion.4), channel_id=1, source_target_pairs={{0,16},{1,17},{2,18},{3,19},{4,20},{5,21},{6,22},{7,23},{8,24},{9,... | collective-permute-start | bytes 221192 | tf_op jit(solution)/shard_map/ppermute | solution.py:20
  75.2 5.2 %collective-permute-start.14 = (bf16[2,96,384]{2,1,0:T(8,128)(2,1)S(1)}, bf16[2,96,384]{2,1,0:T(8,128)(2,1)S(1)}, u32[]{:S(2)}, u32[]{:S(2)}) collective-permute-start(bf16[2,96,384]{2,1,0:T(8,128)(2,1)S(1)} %get-tuple-element.37), channel_id=1, source_target_pairs={{0,2},{1,3},{2,0},{3,1},{4,6},{5,7},{6,4},{7,5},{8,10},{9,11},{10,... | collective-permute-start | bytes 442376 | tf_op jit(solution)/shard_map/ppermute | solution.py:20
  75.5 5.3 %collective-permute-start.13 = (bf16[2,96,384]{2,1,0:T(8,128)(2,1)S(1)}, bf16[2,96,384]{2,1,0:T(8,128)(2,1)S(1)}, u32[]{:S(2)}, u32[]{:S(2)}) collective-permute-start(bf16[2,96,384]{2,1,0:T(8,128)(2,1)S(1)} %get-tuple-element.37), channel_id=1, source_target_pairs={{0,4},{1,5},{2,6},{3,7},{4,0},{5,1},{6,2},{7,3},{8,12},{9,13},{10,... | collective-permute-start | bytes 442376 | tf_op jit(solution)/shard_map/ppermute | solution.py:20
  76.2 6.1 %collective-permute-start.15 = (bf16[2,96,384]{2,1,0:T(8,128)(2,1)S(1)}, bf16[2,96,384]{2,1,0:T(8,128)(2,1)S(1)}, u32[]{:S(2)}, u32[]{:S(2)}) collective-permute-start(bf16[2,96,384]{2,1,0:T(8,128)(2,1)S(1)} %get-tuple-element.37), channel_id=1, source_target_pairs={{0,6},{1,7},{2,4},{3,5},{4,2},{5,3},{6,0},{7,1},{8,14},{9,15},{10,... | collective-permute-start | bytes 442376 | tf_op jit(solution)/shard_map/ppermute | solution.py:20
  82.4 2.1 %collective-permute-start.16 = (bf16[4,2,96,384]{3,2,1,0:T(8,128)(2,1)S(1)}, bf16[4,2,96,384]{3,2,1,0:T(8,128)(2,1)S(1)}, u32[]{:S(2)}, u32[]{:S(2)}) collective-permute-start(bf16[4,2,96,384]{3,2,1,0:T(8,128)(2,1)S(1)} %pad_maximum_fusion.1.refs_3_), channel_id=1, source_target_pairs={{0,1},{1,0},{2,3},{3,2},{4,5},{5,4},{6,7},{7,6},{8,9},{9,8},{10,11... | collective-permute-start | bytes 1769480 | tf_op jit(solution)/shard_map/ppermute | solution.py:20
  89.3 2.2 %collective-permute-start.17 = (f32[4,112,384]{2,1,0:T(8,128)S(1)}, f32[4,112,384]{2,1,0:T(8,128)S(1)}, u32[]{:S(2)}, u32[]{:S(2)}) collective-permute-start(f32[4,112,384]{2,1,0:T(8,128)S(1)} %get-tuple-element.24), channel_id=1, source_target_pairs={{0,1},{1,0},{2,3},{3,2},{4,5},{5,4},{6,7},{7,6},{8,9},{9,8},{10,11... | collective-permute-start | bytes 2064392 | tf_op jit(solution)/shard_map/ppermute | solution.py:20
  89.5 5.8 %collective-permute-start.21 = (bf16[96,384]{1,0:T(8,128)(2,1)S(1)}, bf16[96,384]{1,0:T(8,128)(2,1)S(1)}, u32[]{:S(2)}, u32[]{:S(2)}) collective-permute-start(bf16[96,384]{1,0:T(8,128)(2,1)S(1)} %slice_bitcast_fusion.8), channel_id=1, source_target_pairs={{0,8},{1,9},{2,10},{3,11},{4,12},{5,13},{6,14},{7,15},{8,0},{9,1},... | collective-permute-start | bytes 221192 | tf_op jit(solution)/shard_map/ppermute | solution.py:20
  91.6 6.3 %collective-permute-start.20 = (bf16[112,384]{1,0:T(8,128)(2,1)S(1)}, bf16[112,384]{1,0:T(8,128)(2,1)S(1)}, u32[]{:S(2)}, u32[]{:S(2)}) collective-permute-start(bf16[112,384]{1,0:T(8,128)(2,1)S(1)} %get-tuple-element.30), channel_id=1, source_target_pairs={{0,10},{1,11},{2,8},{3,9},{4,14},{5,15},{6,12},{7,13},{8,2},{9,3},... | collective-permute-start | bytes 258056 | tf_op jit(solution)/shard_map/ppermute | solution.py:20
  93.4 6.3 %collective-permute-start.19 = (bf16[112,384]{1,0:T(8,128)(2,1)S(1)}, bf16[112,384]{1,0:T(8,128)(2,1)S(1)}, u32[]{:S(2)}, u32[]{:S(2)}) collective-permute-start(bf16[112,384]{1,0:T(8,128)(2,1)S(1)} %get-tuple-element.31), channel_id=1, source_target_pairs={{0,8},{1,9},{2,10},{3,11},{4,12},{5,13},{6,14},{7,15},{8,0},{9,1},... | collective-permute-start | bytes 258056 | tf_op jit(solution)/shard_map/ppermute | solution.py:20
  95.3 4.5 %collective-permute-start.18 = (bf16[112,384]{1,0:T(8,128)(2,1)S(1)}, bf16[112,384]{1,0:T(8,128)(2,1)S(1)}, u32[]{:S(2)}, u32[]{:S(2)}) collective-permute-start(bf16[112,384]{1,0:T(8,128)(2,1)S(1)} %get-tuple-element.32), channel_id=1, source_target_pairs={{0,2},{1,3},{2,0},{3,1},{4,6},{5,7},{6,4},{7,5},{8,10},{9,11},{10,... | collective-permute-start | bytes 258056 | tf_op jit(solution)/shard_map/ppermute | solution.py:20
  (1 other events, 1.5 us)

commit v5 on v4

--- a/solution.py
+++ b/solution.py
@@ -12,7 +12,8 @@
 EPSILON = 1e-06
 EXTRA_ROWS = 16
 MIB = 2**20
-START_COST = 8
+START_COST = 3
+PEER_COST = 1
 PLAN_BITS = 5
 
 
@@ -47,22 +48,6 @@
     return (rows < sizes[0]) & (cols < sizes[1])
 
 
-def place_copies(sources, target, places, sems):
-    tile = sources[0].shape[1]
-    found = []
-    for k in range(sources[0].shape[0]):
-        pair = []
-        for slot in range(2):
-            row = pl.multiple_of(places[slot] * tile, tile)
-            copy = pltpu.make_async_copy(
-                sources[slot].at[k], target.at[k, pl.ds(row, tile)], sems.at[k, slot]
-            )
-            copy.start()
-            pair.append(copy)
-        found.append(pair)
-    return found
-
-
 def term_of(plan, sectors, terms, k):
     base = PLAN_BITS + 2 * sectors
     return plan[base + k], plan[base + terms + k].astype(jnp.float32)
@@ -70,8 +55,21 @@
 
 def mix(plan, sectors, terms, k, left, vector):
     source, weight = term_of(plan, sectors, terms, k)
-    product = jnp.dot(left, vector[source], preferred_element_type=jnp.float32)
-    return (product * weight).astype(jnp.bfloat16)
+    return jnp.dot(left, vector[source], preferred_element_type=jnp.float32) * weight
+
+
+def put_pair(mixed, rows, k, pair):
+    tile = pair[0].shape[1] // 2
+    for half in range(2):
+        at = slice(half * tile, (half + 1) * tile)
+        both = jnp.concatenate([product[:, at] for product in pair], axis=1)
+        mixed[half, rows, k * tile : (k + 2) * tile] = both.astype(jnp.bfloat16)
+
+
+def collect(mixed, rights):
+    terms, tile, width = rights.shape
+    flat = rights[...].reshape(terms * tile, width)
+    return jnp.dot(mixed, flat, preferred_element_type=jnp.float32)
 
 
 def start_kernel(
@@ -80,14 +78,12 @@
     terms, tile, _ = left_own.shape
     width = 2 * tile
     core, x, y, z = plan[0], plan[1], plan[2], plan[3]
-    copies = []
-    for k in range(terms):
-        copy = pltpu.make_async_copy(left_own.at[k], lefts.at[k], sems.at[k])
+    copies = [
+        pltpu.make_async_copy(left_own, lefts, sems.at[0]),
+        pltpu.make_async_copy(right_own, rights, sems.at[1]),
+    ]
+    for copy in copies:
         copy.start()
-        copies.append(copy)
-    copy = pltpu.make_async_copy(right_own, rights, sems.at[terms])
-    copy.start()
-    copies.append(copy)
     square = jnp.zeros((8, width), jnp.float32)
     for xr in range(2):
         for yr in range(2):
@@ -107,13 +103,14 @@
                 at = pl.ds(pl.multiple_of(row, tile), tile)
                 vector[sector, at, :] = both.astype(jnp.bfloat16)
     square_ref[...] = jnp.broadcast_to(jnp.sum(square), square_ref.shape)
-    for k in range(terms):
-        copies[k].wait()
-        mixed_ref[:, k * width : (k + 1) * width] = mix(plan, sectors, terms, k, lefts[k], vector)
-    copies[terms].wait()
-
-
-def first_kernel(
+    copies[0].wait()
+    for k in range(0, terms, 2):
+        pair = [mix(plan, sectors, terms, i, lefts[i], vector) for i in (k, k + 1)]
+        put_pair(mixed_ref, slice(None), k, pair)
+    copies[1].wait()
+
+
+def peer_kernel(
     sectors,
     plan,
     vector,
@@ -121,33 +118,49 @@
     left_own,
     left_peer,
     right_own,
-    right_peer,
-    kept_ref,
-    sent_ref,
+    right_early,
+    mixed_ref,
+    total_ref,
     lefts,
-    rights,
     mixed,
-    left_sems,
-    right_sems,
+    sems,
 ):
     terms, tile, _ = left_peer.shape
-    width = 2 * tile
+    early = right_early.shape[0] * tile
+    y, z = plan[2], plan[3]
+    own = pl.ds(pl.multiple_of(z * tile, tile), tile)
+    peer = pl.ds(pl.multiple_of((1 - z) * tile, tile), tile)
+    copies = [
+        pltpu.make_async_copy(left_own, lefts.at[:, own], sems.at[0]),
+        pltpu.make_async_copy(left_peer, lefts.at[:, peer], sems.at[1]),
+    ]
+    for copy in copies:
+        copy.start()
+    mixed[:, own, :] = mixed_own[...]
+    for k in range(0, terms, 2):
+        pair = [mix(plan, sectors, terms, i, left_peer[i], vector) for i in (k, k + 1)]
+        put_pair(mixed, peer, k, pair)
+    rest = mixed[1 - y]
+    total_ref[...] = collect(mixed[y], right_own) + collect(rest[:, :early], right_early)
+    mixed_ref[...] = rest[:, early:]
+    for copy in copies:
+        copy.wait()
+
+
+def first_kernel(plan, mixed, before, right_own, right_early, right_late, kept_ref, sent_ref, rights, sems):
+    early, tile, _ = right_early.shape
+    late = right_late.shape[0]
     core, x, y, z = plan[0], plan[1], plan[2], plan[3]
-    peer = pl.ds(pl.multiple_of((1 - z) * tile, tile), tile)
-    right_copies = place_copies((right_own, right_peer), rights, (y, 1 - y), right_sems)
-    own = pl.ds(pl.multiple_of(z * tile, tile), tile)
-    left_copies = [
-        pltpu.make_async_copy(left_own, lefts.at[:, own], left_sems.at[0]),
-        pltpu.make_async_copy(left_peer, lefts.at[:, peer], left_sems.at[1]),
+    own = pl.ds(pl.multiple_of(y * tile, tile), tile)
+    peer = pl.ds(pl.multiple_of((1 - y) * tile, tile), tile)
+    copies = [
+        pltpu.make_async_copy(right_own, rights.at[:, own], sems.at[0]),
+        pltpu.make_async_copy(right_early, rights.at[pl.ds(0, early), peer], sems.at[1]),
+        pltpu.make_async_copy(right_late, rights.at[pl.ds(early, late), peer], sems.at[2]),
     ]
-    for copy in left_copies:
+    for copy in copies:
         copy.start()
-    mixed[own, :] = mixed_own[...]
-    for k in range(terms):
-        mixed[peer, k * width : (k + 1) * width] = mix(plan, sectors, terms, k, left_peer[k], vector)
-    total = collect(mixed, rights, right_copies)
-    for copy in left_copies:
-        copy.wait()
+    total = before[...] + collect(mixed[...], right_late)
     sizes = plan[PLAN_BITS + 2 * plan[4]], plan[PLAN_BITS + 2 * plan[4] + 1]
     parts = []
     for z_row in range(2):
@@ -167,16 +180,10 @@
                             row, col = (x_is ^ xr) * unit_rows, (z_is ^ zr) * unit_cols
                             at = slice(row, row + unit_rows), slice(col, col + unit_cols)
                             kept_ref[2 * zr + xr] = mine[at]
-                            sent_ref[2 * zr + xr] = other[at].astype(sent_ref.dtype)
-
-
-def collect(mixed, rights, copies):
-    for pair in copies:
-        for copy in pair:
-            copy.wait()
-    terms, height, width = rights.shape
-    flat = rights[...].reshape(terms * height, width)
-    return jnp.dot(mixed[...], flat, preferred_element_type=jnp.float32)
+                            sent_ref[2 * zr + xr] = other[at]
+
+    for copy in copies:
+        copy.wait()
 
 
 def second_kernel(
@@ -208,7 +215,8 @@
     inner = jnp.zeros((8, width), jnp.float32)
     norm = inner
     for k in range(terms):
-        mixed[:, k * width : (k + 1) * width] = mix(plan, sectors, terms, k, lefts[k], vector)
+        product = mix(plan, sectors, terms, k, lefts[k], vector)
+        mixed[:, k * width : (k + 1) * width] = product.astype(jnp.bfloat16)
         if k < 4:
             for sr in range(sectors):
                 row = (2 * core + (y ^ (k % 2))) * tile + (x ^ (k // 2)) * half
@@ -217,7 +225,7 @@
                 before = start[plan[4] ^ sr, at, :].astype(jnp.float32)
                 inner += jnp.sum((before * image).reshape(half // 8, 8, width), axis=0)
                 norm += jnp.sum((image * image).reshape(half // 8, 8, width), axis=0)
-    total = collect(mixed, rights, [])
+    total = collect(mixed[...], rights)
     extra_shape = (EXTRA_ROWS, kept_ref.shape[2])
     lane = lax.broadcasted_iota(jnp.int32, extra_shape, 1)
     zeros = jnp.zeros(extra_shape, jnp.float32)
@@ -321,19 +329,21 @@
     plan = jnp.concatenate([jnp.stack(bits), sizes.reshape(-1), mine(coupling), mine(term_mask)])
 
     start_tile = jnp.concatenate([wavefunction[0, : tile // 2], wavefunction[0, tile // 2 :]], axis=1)
-    tiles = []
-    for y_flip in (0, YBIT):
-        for sector_flip in range(0, lax.axis_size("sec"), SECTOR_BIT):
-            tiles.append(spread(start_tile, y_flip | sector_flip))
-    tiles = jnp.stack(tiles).reshape(2, sectors, tile // 2, 2 * tile)
+    early = terms // 6
+    tiles = [spread(start_tile, flip) for flip in range(0, lax.axis_size("sec"), SECTOR_BIT)]
+    gated, tiles[0] = lax.optimization_barrier((left_environment, tiles[0]))
+    tiles = jnp.stack(tiles)
+    tiles = jnp.stack([tiles, exchange(tiles, YBIT)])
+    right_early = exchange(right_environment[:early], YBIT)
+    tiles, right_early = lax.optimization_barrier((tiles, right_early))
     tiles = jnp.stack([tiles, exchange(tiles, XBIT)])
     far_tiles = exchange(tiles, CORE)
 
-    left_peer = exchange(left_environment, ZBIT)
-    right_peer = exchange(right_environment, YBIT)
+    left_peer = exchange(gated, ZBIT)
+    right_late = exchange(right_environment[early:], YBIT)
 
     def work(macs):
-        return pl.CostEstimate(flops=2 * macs, bytes_accessed=terms * tile * capacity * 4, transcendentals=0)
+        return pl.CostEstimate(flops=int(2 * macs), bytes_accessed=terms * tile * capacity * 4, transcendentals=0)
 
     width = 2 * tile
     macs = terms * tile * capacity * width
@@ -343,30 +353,43 @@
     def params(mib):
         return pltpu.CompilerParams(vmem_limit_bytes=mib * MIB)
 
-    environments = shaped(terms, width, capacity)
     start_vector, mixed_own, square, left_own, right_own = pl.pallas_call(
         lambda *refs: start_kernel(sectors, *refs),
-        out_shape=[shaped(*vector_shape), shaped(tile, terms * width), shaped(8, 128, dtype=f32)]
-        + [shaped(terms, tile, capacity)] * 2,
+        out_shape=[
+            shaped(*vector_shape),
+            shaped(2, tile, terms * tile),
+            shaped(8, 128, dtype=f32),
+            shaped(terms, tile, capacity),
+            shaped(terms, tile, capacity),
+        ],
         in_specs=[smem(), vmem(), vmem(), anywhere(), anywhere()],
         out_specs=[vmem()] * 5,
-        scratch_shapes=[pltpu.SemaphoreType.DMA((terms + 1,))],
+        scratch_shapes=[pltpu.SemaphoreType.DMA((2,))],
         compiler_params=params(16),
         cost_estimate=work(START_COST * macs),
     )(plan, tiles, far_tiles, left_environment, right_environment)
-    kept, sent, lefts, rights = pl.pallas_call(
-        lambda *refs: first_kernel(sectors, *refs),
-        out_shape=[shaped(*unit, dtype=f32), shaped(*unit, dtype=f32), environments, environments],
+    mixed, total, lefts = pl.pallas_call(
+        lambda *refs: peer_kernel(sectors, *refs),
+        out_shape=[
+            shaped(width, (terms - early) * tile),
+            shaped(width, capacity, dtype=f32),
+            shaped(terms, width, capacity),
+        ],
         in_specs=[smem()] + [vmem()] * 6,
-        out_specs=[vmem()] * 4,
-        scratch_shapes=[
-            pltpu.VMEM((width, terms * width), bf16),
-            pltpu.SemaphoreType.DMA((2,)),
-            pltpu.SemaphoreType.DMA((terms, 2)),
-        ],
+        out_specs=[vmem()] * 3,
+        scratch_shapes=[pltpu.VMEM((2, width, terms * tile), bf16), pltpu.SemaphoreType.DMA((2,))],
         compiler_params=params(20),
-        cost_estimate=work(3 * macs),
-    )(plan, start_vector, mixed_own, left_own, left_peer, right_own, right_peer)
+        cost_estimate=work(PEER_COST * macs),
+    )(plan, start_vector, mixed_own, left_own, left_peer, right_own, right_early)
+    kept, sent, rights = pl.pallas_call(
+        first_kernel,
+        out_shape=[shaped(*unit, dtype=f32)] * 2 + [shaped(terms, width, capacity)],
+        in_specs=[smem()] + [vmem()] * 5,
+        out_specs=[vmem()] * 3,
+        scratch_shapes=[pltpu.SemaphoreType.DMA((3,))],
+        compiler_params=params(16),
+        cost_estimate=work(macs),
+    )(plan, mixed, total, right_own, right_early, right_late)
 
     summed = kept + exchange(sent, CORE)
     image_unit = (

time: 101 us -> 99.8 us (0.988)
  starting transfers between devices: 32.3 us -> 27.1 us
  local copies, waits for them, and re-layouts: 6.29 us -> 8.44 us
    slice x0 -> x2, local copies, waits for them, and re-layouts: none -> 3.6 us  [the longest x1 2.62 us: on_device(): right_late = exchange(right_environment[early:], YBIT)]
    ppermute x18 -> x20, starting transfers between devices: 25.9 us -> 22.4 us  [exchange(): lax.ppermute(block, 'sec', [(i, i ^ flip) for i in range(lax.axis_size('s...]
    ppermute x4 -> x2, starting transfers between devices: 6.34 us -> 4.75 us  [spread(): return lax.ppermute(tile, 'sec', route)]
    pallas_call x1 -> x2, Pallas kernels: 4.54 us -> 5.71 us  [the longest x1 3.09 us: on_device(): pl.pallas_call(lambda *refs: peer_kernel(sectors, *refs), out_shape=[shap...]
    ppermute x18 -> x20, waiting for transfers between devices: 44.1 us -> 44.9 us  [exchange(): lax.ppermute(block, 'sec', [(i, i ^ flip) for i in range(lax.axis_size('s...]
    unnamed x6 -> x12, local copies, waits for them, and re-layouts: 2.96 us -> 2.27 us
  transfers between devices with their start and end apart: 22 -> 22, of which waited for: 15 -> 16; matrix products, arithmetic and copies ran while one was open for 4% -> 7% of each run, Pallas kernels for 5% -> 7%
where the time goes in v5:
time: 99.8 us; the launch traced here: 99.4 us
  waiting for transfers between devices  44.9 us (45%)
  starting transfers between devices  27.1 us (27%)
  Pallas kernels  15.9 us (16%)
  local copies, waits for them, and re-layouts  8.44 us (8%)
  other arithmetic  2.11 us (2%)
    ppermute x20, waiting for transfers between devices, exchange(): lax.ppermute(block, 'sec', [(i, i ^ flip) for i in range(lax.axis_size('s...  44.9 us
    ppermute x20, starting transfers between devices, exchange(): lax.ppermute(block, 'sec', [(i, i ^ flip) for i in range(lax.axis_size('s...  22.4 us
    ppermute x2, starting transfers between devices, spread(): return lax.ppermute(tile, 'sec', route)  4.75 us
    pallas_call x1, Pallas kernels, on_device(): pl.pallas_call(lambda *refs: second_kernel(sectors, *refs), out_shape=[sh...  4.74 us
    pallas_call x1, Pallas kernels, on_device(): pl.pallas_call(lambda *refs: start_kernel(sectors, *refs), out_shape=[sha...  4.03 us
    pallas_call x1, Pallas kernels, on_device(): pl.pallas_call(lambda *refs: peer_kernel(sectors, *refs), out_shape=[shap...  3.09 us
    slice x1, local copies, waits for them, and re-layouts, on_device(): right_late = exchange(right_environment[early:], YBIT)  2.62 us
    pallas_call x1, Pallas kernels, on_device(): pl.pallas_call(first_kernel, out_shape=[shaped(*unit, dtype=f32)] * 2 + [...  2.61 us
  transfers between devices with their start and end apart: 22, of which 16 were waited for; matrix products, arithmetic and copies ran while one was open for 7% of the time, Pallas kernels for 7%

profile of v5, /device:TPU:0, one launch (start us, length us, event | category | flops | bytes accessed | tf_op | source)
XLA Modules:
  0.0 99.4 jit_solution(16509125962186165043)
XLA Ops:
  2.2 4.1 %collective-permute-start.1 = (bf16[96,384]{1,0:T(8,128)(2,1)S(1)}, bf16[96,384]{1,0:T(8,128)(2,1)S(1)}, u32[]{:S(2)}, u32[]{:S(2)}) collective-permute-start(bf16[96,384]{1,0:T(8,128)(2,1)S(1)} %pad_maximum_fusion.5), channel_id=1, source_target_pairs={{0,16},{1,17},{2,26},{3,27},{4,20},{5,21},{6,30},{7,31},{8,18},{9,... | collective-permute-start | bytes 221192 | tf_op jit(solution)/shard_map/ppermute | solution.py:30
  7.3 1.6 %collective-permute-start.3 = (bf16[1,192,768]{2,1,0:T(8,128)(2,1)S(1)}, bf16[1,192,768]{2,1,0:T(8,128)(2,1)S(1)}, u32[]{:S(2)}, u32[]{:S(2)}) collective-permute-start(bf16[1,192,768]{2,1,0:T(8,128)(2,1)S(1)} %slice.55), channel_id=1, source_target_pairs={{0,4},{1,5},{2,6},{3,7},{4,0},{5,1},{6,2},{7,3},{8,12},{9,13},{10,... | collective-permute-start | bytes 884744 | tf_op jit(solution)/shard_map/ppermute | solution.py:21
  8.9 4.3 %collective-permute-start.6 = (bf16[6,192,768]{2,1,0:T(8,128)(2,1)}, bf16[6,192,768]{2,1,0:T(8,128)(2,1)S(1)}, u32[]{:S(2)}, u32[]{:S(2)}) collective-permute-start(bf16[6,192,768]{2,1,0:T(8,128)(2,1)} %refs_3_.1), channel_id=1, source_target_pairs={{0,8},{1,9},{2,10},{3,11},{4,12},{5,13},{6,14},{7,15},{8,0},{9,1},... | collective-permute-start | bytes 5308424 | tf_op jit(solution)/shard_map/ppermute | solution.py:21
  14.2 2.6 %slice.56 = bf16[5,192,768]{2,1,0:T(8,128)(2,1)} slice(bf16[6,192,768]{2,1,0:T(8,128)(2,1)} %refs_4_.1), slice={[1:6], [0:192], [0:768]} | slice | bytes 2949120 | tf_op jit(solution)/shard_map/slice | solution.py:343
  17.9 2.2 %collective-permute-done.2 = bf16[2,96,384]{2,1,0:T(8,128)(2,1)S(1)} collective-permute-done((bf16[2,96,384]{2,1,0:T(8,128)(2,1)S(1)}, bf16[2,96,384]{2,1,0:T(8,128)(2,1)S(1)}, u32[]{:S(2)}, u32[]{:S(2)}) %collective-permute-start.2) | collective-permute-done | bytes 147488 | tf_op jit(solution)/shard_map/ppermute | solution.py:21
  20.9 1.8 %collective-permute-start.4 = (bf16[2,2,96,384]{3,2,1,0:T(8,128)(2,1)S(1)}, bf16[2,2,96,384]{3,2,1,0:T(8,128)(2,1)S(1)}, u32[]{:S(2)}, u32[]{:S(2)}) collective-permute-start(bf16[2,2,96,384]{3,2,1,0:T(8,128)(2,1)S(1)} %pad_maximum_fusion.2), channel_id=1, source_target_pairs={{0,2},{1,3},{2,0},{3,1},{4,6},{5,7},{6,4},{7,5},{8,10},{9,11},{10,... | collective-permute-start | bytes 884744 | tf_op jit(solution)/shard_map/ppermute | solution.py:21
  22.7 5.5 %collective-permute-done.4 = bf16[2,2,96,384]{3,2,1,0:T(8,128)(2,1)S(1)} collective-permute-done((bf16[2,2,96,384]{3,2,1,0:T(8,128)(2,1)S(1)}, bf16[2,2,96,384]{3,2,1,0:T(8,128)(2,1)S(1)}, u32[]{:S(2)}, u32[]{:S(2)}) %collective-permute-start.4) | collective-permute-done | bytes 294944 | tf_op jit(solution)/shard_map/ppermute | solution.py:21
  31.6 1.5 %copy-done.3 = bf16[6,192,768]{2,1,0:T(8,128)(2,1)S(1)} copy-done((bf16[6,192,768]{2,1,0:T(8,128)(2,1)S(1)}, bf16[6,192,768]{2,1,0:T(8,128)(2,1)}, u32[]{:S(2)}) %copy-start.3) | copy-done | bytes 1769496
  33.1 4.0 %shard_map.86 = (bf16[2,768,384]{2,1,0:T(8,128)(2,1)S(1)}, bf16[2,192,1152]{2,1,0:T(8,128)(2,1)S(1)}, f32[8,128]{1,0:T(8,128)S(1)}, bf16[6,192,768]{2,1,0:T(8,128)(2,1)S(1)}, bf16[6,192,768]{2,1,0:T(8,128)(2,1)S(1)}) custom-call(s32[21]{0:T(128)S(1)} %concatenate.9.refs_0_.plan, bf16[2,2,2,96,384]{4,3,2,1,0:T(8,128)(2,1)} %pad_maximum_fusion.refs_1_, ...), custom_call_target="tpu_custom_call" | custom-call | flops 2038431744 | bytes 3538944 | tf_op jit(solution)/shard_map/pallas_call | solution.py:356
  37.2 14.5 %collective-permute-done.6.refs_4_ = bf16[6,192,768]{2,1,0:T(8,128)(2,1)S(1)} collective-permute-done((bf16[6,192,768]{2,1,0:T(8,128)(2,1)}, bf16[6,192,768]{2,1,0:T(8,128)(2,1)S(1)}, u32[]{:S(2)}, u32[]{:S(2)}) %collective-permute-start.6) | collective-permute-done | bytes 1769504 | tf_op jit(solution)/shard_map/ppermute | solution.py:21
  51.7 3.1 %shard_map.87 = (bf16[384,960]{1,0:T(8,128)(2,1)S(1)}, f32[384,768]{1,0:T(8,128)S(1)}, bf16[6,384,768]{2,1,0:T(8,128)(2,1)S(1)}) custom-call(s32[21]{0:T(128)S(1)} %concatenate.9.refs_0_.plan, bf16[2,768,384]{2,1,0:T(8,128)(2,1)S(1)} %get-tuple-element.23.refs_1_.refs_2_, bf16[2,192,1152]{2,1,0:T(8,128)(2,1)S(1)} %get-tuple-element.24.refs_2_, ...), custom_call_target="tpu_custom_call" | custom-call | flops 679477248 | bytes 3538944 | tf_op jit(solution)/shard_map/pallas_call | solution.py:371
  54.8 2.6 %shard_map.88 = (f32[4,96,384]{2,1,0:T(8,128)S(1)}, f32[4,96,384]{2,1,0:T(8,128)S(1)}, bf16[6,384,768]{2,1,0:T(8,128)(2,1)S(1)}) custom-call(s32[21]{0:T(128)S(1)} %concatenate.9.refs_0_.plan, bf16[384,960]{1,0:T(8,128)(2,1)S(1)} %get-tuple-element.29.mixed, f32[384,768]{1,0:T(8,128)S(1)} %get-tuple-element.30.before, ...), custom_call_target="tpu_custom_call" | custom-call | flops 679477248 | bytes 3538944 | tf_op jit(solution)/shard_map/pallas_call | solution.py:384
  57.5 2.0 %collective-permute-done.8 = f32[4,96,384]{2,1,0:T(8,128)S(1)} collective-permute-done((f32[4,96,384]{2,1,0:T(8,128)S(1)}, f32[4,96,384]{2,1,0:T(8,128)S(1)}, u32[]{:S(2)}, u32[]{:S(2)}) %collective-permute-start.8) | collective-permute-done | bytes 589856 | tf_op jit(solution)/shard_map/ppermute | solution.py:21
  60.5 1.8 %collective-permute-start.11 = (bf16[96,384]{1,0:T(8,128)(2,1)S(1)}, bf16[96,384]{1,0:T(8,128)(2,1)S(1)}, u32[]{:S(2)}, u32[]{:S(2)}) collective-permute-start(bf16[96,384]{1,0:T(8,128)(2,1)S(1)} %get-tuple-element.46), channel_id=1, source_target_pairs={{0,10},{1,11},{2,8},{3,9},{4,14},{5,15},{6,12},{7,13},{8,2},{9,3},... | collective-permute-start | bytes 221192 | tf_op jit(solution)/shard_map/ppermute | solution.py:21
  63.1 1.7 %collective-permute-done.9 = bf16[96,384]{1,0:T(8,128)(2,1)S(1)} collective-permute-done((bf16[96,384]{1,0:T(8,128)(2,1)S(1)}, bf16[96,384]{1,0:T(8,128)(2,1)S(1)}, u32[]{:S(2)}, u32[]{:S(2)}) %collective-permute-start.9) | collective-permute-done | bytes 73760 | tf_op jit(solution)/shard_map/ppermute | solution.py:21
  64.8 1.5 %collective-permute-done.11 = bf16[96,384]{1,0:T(8,128)(2,1)S(1)} collective-permute-done((bf16[96,384]{1,0:T(8,128)(2,1)S(1)}, bf16[96,384]{1,0:T(8,128)(2,1)S(1)}, u32[]{:S(2)}, u32[]{:S(2)}) %collective-permute-start.11) | collective-permute-done | bytes 73760 | tf_op jit(solution)/shard_map/ppermute | solution.py:21
  68.0 5.0 %collective-permute-done.12 = bf16[1,96,384]{2,1,0:T(8,128)(2,1)S(1)} collective-permute-done((bf16[1,96,384]{2,1,0:T(8,128)(2,1)S(1)}, bf16[1,96,384]{2,1,0:T(8,128)(2,1)S(1)}, u32[]{:S(2)}, u32[]{:S(2)}) %collective-permute-start.12) | collective-permute-done | bytes 73760 | tf_op jit(solution)/shard_map/ppermute | solution.py:21
  73.5 1.7 %collective-permute-start.13 = (bf16[2,96,384]{2,1,0:T(8,128)(2,1)S(1)}, bf16[2,96,384]{2,1,0:T(8,128)(2,1)S(1)}, u32[]{:S(2)}, u32[]{:S(2)}) collective-permute-start(bf16[2,96,384]{2,1,0:T(8,128)(2,1)S(1)} %get-tuple-element.49), channel_id=1, source_target_pairs={{0,4},{1,5},{2,6},{3,7},{4,0},{5,1},{6,2},{7,3},{8,12},{9,13},{10,... | collective-permute-start | bytes 442376 | tf_op jit(solution)/shard_map/ppermute | solution.py:21
  76.6 2.4 %collective-permute-done.14 = bf16[2,96,384]{2,1,0:T(8,128)(2,1)S(1)} collective-permute-done((bf16[2,96,384]{2,1,0:T(8,128)(2,1)S(1)}, bf16[2,96,384]{2,1,0:T(8,128)(2,1)S(1)}, u32[]{:S(2)}, u32[]{:S(2)}) %collective-permute-start.14) | collective-permute-done | bytes 147488 | tf_op jit(solution)/shard_map/ppermute | solution.py:21
  81.5 2.0 %collective-permute-done.16.refs_4_ = bf16[4,2,96,384]{3,2,1,0:T(8,128)(2,1)S(1)} collective-permute-done((bf16[4,2,96,384]{3,2,1,0:T(8,128)(2,1)S(1)}, bf16[4,2,96,384]{3,2,1,0:T(8,128)(2,1)S(1)}, u32[]{:S(2)}, u32[]{:S(2)}) %collective-permute-start.16) | collective-permute-done | bytes 589856 | tf_op jit(solution)/shard_map/ppermute | solution.py:21
  83.5 4.7 %shard_map.89 = (f32[4,112,384]{2,1,0:T(8,128)S(1)}, f32[4,112,384]{2,1,0:T(8,128)S(1)}, bf16[2,96,384]{2,1,0:T(8,128)(2,1)S(1)}) custom-call(s32[21]{0:T(128)S(1)} %concatenate.9.refs_0_.plan, f32[8,128]{1,0:T(8,128)S(1)} %get-tuple-element.22.refs_1_, bf16[2,768,384]{2,1,0:T(8,128)(2,1)S(1)} %get-tuple-element.23.refs_1_.refs_2_, ...), custom_call_target="tpu_custom_call" | custom-call | flops 2717908992 | bytes 3538944 | tf_op jit(solution)/shard_map/pallas_call | solution.py:412
  89.0 1.5 %collective-permute-done.17 = f32[4,112,384]{2,1,0:T(8,128)S(1)} collective-permute-done((f32[4,112,384]{2,1,0:T(8,128)S(1)}, f32[4,112,384]{2,1,0:T(8,128)S(1)}, u32[]{:S(2)}, u32[]{:S(2)}) %collective-permute-start.17) | collective-permute-done | bytes 688160 | tf_op jit(solution)/shard_map/ppermute | solution.py:21
  91.3 1.7 %collective-permute-start.19 = (bf16[112,384]{1,0:T(8,128)(2,1)S(1)}, bf16[112,384]{1,0:T(8,128)(2,1)S(1)}, u32[]{:S(2)}, u32[]{:S(2)}) collective-permute-start(bf16[112,384]{1,0:T(8,128)(2,1)S(1)} %get-tuple-element.43), channel_id=1, source_target_pairs={{0,8},{1,9},{2,10},{3,11},{4,12},{5,13},{6,14},{7,15},{8,0},{9,1},... | collective-permute-start | bytes 258056 | tf_op jit(solution)/shard_map/ppermute | solution.py:21
  94.2 2.8 %collective-permute-done.20.from_xz = bf16[112,384]{1,0:T(8,128)(2,1)S(1)} collective-permute-done((bf16[112,384]{1,0:T(8,128)(2,1)S(1)}, bf16[112,384]{1,0:T(8,128)(2,1)S(1)}, u32[]{:S(2)}, u32[]{:S(2)}) %collective-permute-start.20) | collective-permute-done | bytes 86048 | tf_op jit(solution)/shard_map/ppermute | solution.py:21
  (63 shorter events, 22.0 us)
Async XLA Ops:
  1.6 7.3 %collective-permute-start = (bf16[96,384]{1,0:T(8,128)(2,1)S(1)}, bf16[96,384]{1,0:T(8,128)(2,1)S(1)}, u32[]{:S(2)}, u32[]{:S(2)}) collective-permute-start(bf16[96,384]{1,0:T(8,128)(2,1)S(1)} %pad_maximum_fusion.5), channel_id=1, source_target_pairs={{0,0},{1,1},{2,8},{3,9},{4,4},{5,5},{6,12},{7,13},{8,2},{9,3},{10,... | collective-permute-start | bytes 221192 | tf_op jit(solution)/shard_map/ppermute | solution.py:30
  2.2 10.9 %collective-permute-start.1 = (bf16[96,384]{1,0:T(8,128)(2,1)S(1)}, bf16[96,384]{1,0:T(8,128)(2,1)S(1)}, u32[]{:S(2)}, u32[]{:S(2)}) collective-permute-start(bf16[96,384]{1,0:T(8,128)(2,1)S(1)} %pad_maximum_fusion.5), channel_id=1, source_target_pairs={{0,16},{1,17},{2,26},{3,27},{4,20},{5,21},{6,30},{7,31},{8,18},{9,... | collective-permute-start | bytes 221192 | tf_op jit(solution)/shard_map/ppermute | solution.py:30
  7.3 12.9 %collective-permute-start.3 = (bf16[1,192,768]{2,1,0:T(8,128)(2,1)S(1)}, bf16[1,192,768]{2,1,0:T(8,128)(2,1)S(1)}, u32[]{:S(2)}, u32[]{:S(2)}) collective-permute-start(bf16[1,192,768]{2,1,0:T(8,128)(2,1)S(1)} %slice.55), channel_id=1, source_target_pairs={{0,4},{1,5},{2,6},{3,7},{4,0},{5,1},{6,2},{7,3},{8,12},{9,13},{10,... | collective-permute-start | bytes 884744 | tf_op jit(solution)/shard_map/ppermute | solution.py:21
  8.9 42.8 %collective-permute-start.6 = (bf16[6,192,768]{2,1,0:T(8,128)(2,1)}, bf16[6,192,768]{2,1,0:T(8,128)(2,1)S(1)}, u32[]{:S(2)}, u32[]{:S(2)}) collective-permute-start(bf16[6,192,768]{2,1,0:T(8,128)(2,1)} %refs_3_.1), channel_id=1, source_target_pairs={{0,8},{1,9},{2,10},{3,11},{4,12},{5,13},{6,14},{7,15},{8,0},{9,1},... | collective-permute-start | bytes 5308424 | tf_op jit(solution)/shard_map/ppermute | solution.py:21
  13.2 15.9 %copy-start.5 = (s32[2]{0:T(128)S(1)}, s32[2]{0:T(128)}, u32[]{:S(2)}) copy-start(s32[2]{0:T(128)} %param.11) | copy-start | bytes 28
  13.2 6.9 %collective-permute-start.2 = (bf16[2,96,384]{2,1,0:T(8,128)(2,1)S(1)}, bf16[2,96,384]{2,1,0:T(8,128)(2,1)S(1)}, u32[]{:S(2)}, u32[]{:S(2)}) collective-permute-start(bf16[2,96,384]{2,1,0:T(8,128)(2,1)S(1)} %get-tuple-element.51), channel_id=1, source_target_pairs={{0,4},{1,5},{2,6},{3,7},{4,0},{5,1},{6,2},{7,3},{8,12},{9,13},{10,... | collective-permute-start | bytes 442376 | tf_op jit(solution)/shard_map/ppermute | solution.py:21
  16.8 37.9 %collective-permute-start.7 = (bf16[5,192,768]{2,1,0:T(8,128)(2,1)}, bf16[5,192,768]{2,1,0:T(8,128)(2,1)}, u32[]{:S(2)}, u32[]{:S(2)}) collective-permute-start(bf16[5,192,768]{2,1,0:T(8,128)(2,1)} %slice.56), channel_id=1, source_target_pairs={{0,4},{1,5},{2,6},{3,7},{4,0},{5,1},{6,2},{7,3},{8,12},{9,13},{10,... | collective-permute-start | bytes 4423688 | tf_op jit(solution)/shard_map/ppermute | solution.py:21
  20.9 7.3 %collective-permute-start.4 = (bf16[2,2,96,384]{3,2,1,0:T(8,128)(2,1)S(1)}, bf16[2,2,96,384]{3,2,1,0:T(8,128)(2,1)S(1)}, u32[]{:S(2)}, u32[]{:S(2)}) collective-permute-start(bf16[2,2,96,384]{3,2,1,0:T(8,128)(2,1)S(1)} %pad_maximum_fusion.2), channel_id=1, source_target_pairs={{0,2},{1,3},{2,0},{3,1},{4,6},{5,7},{6,4},{7,5},{8,10},{9,11},{10,... | collective-permute-start | bytes 884744 | tf_op jit(solution)/shard_map/ppermute | solution.py:21
  29.1 2.5 %collective-permute-start.5 = (bf16[2,2,2,96,384]{4,3,2,1,0:T(8,128)(2,1)}, bf16[2,2,2,96,384]{4,3,2,1,0:T(8,128)(2,1)}, u32[]{:S(2)}, u32[]{:S(2)}) collective-permute-start(bf16[2,2,2,96,384]{4,3,2,1,0:T(8,128)(2,1)} %pad_maximum_fusion.refs_1_), channel_id=1, source_target_pairs={{0,1},{1,0},{2,3},{3,2},{4,5},{5,4},{6,7},{7,6},{8,9},{9,8},{10,11... | collective-permute-start | bytes 1769480 | tf_op jit(solution)/shard_map/ppermute | solution.py:21
  31.6 20.1 %copy-start.2 = (bf16[1,192,768]{2,1,0:T(8,128)(2,1)S(1)}, bf16[1,192,768]{2,1,0:T(8,128)(2,1)}, u32[]{:S(2)}) copy-start(bf16[1,192,768]{2,1,0:T(8,128)(2,1)} %copy-done.1) | copy-start | bytes 884740
  57.4 2.1 %collective-permute-start.8 = (f32[4,96,384]{2,1,0:T(8,128)S(1)}, f32[4,96,384]{2,1,0:T(8,128)S(1)}, u32[]{:S(2)}, u32[]{:S(2)}) collective-permute-start(f32[4,96,384]{2,1,0:T(8,128)S(1)} %get-tuple-element.32), channel_id=1, source_target_pairs={{0,1},{1,0},{2,3},{3,2},{4,5},{5,4},{6,7},{7,6},{8,9},{9,8},{10,11... | collective-permute-start | bytes 1769480 | tf_op jit(solution)/shard_map/ppermute | solution.py:21
  59.6 5.2 %collective-permute-start.9 = (bf16[96,384]{1,0:T(8,128)(2,1)S(1)}, bf16[96,384]{1,0:T(8,128)(2,1)S(1)}, u32[]{:S(2)}, u32[]{:S(2)}) collective-permute-start(bf16[96,384]{1,0:T(8,128)(2,1)S(1)} %get-tuple-element.45), channel_id=1, source_target_pairs={{0,2},{1,3},{2,0},{3,1},{4,6},{5,7},{6,4},{7,5},{8,10},{9,11},{10,... | collective-permute-start | bytes 221192 | tf_op jit(solution)/shard_map/ppermute | solution.py:21
  60.5 5.8 %collective-permute-start.11 = (bf16[96,384]{1,0:T(8,128)(2,1)S(1)}, bf16[96,384]{1,0:T(8,128)(2,1)S(1)}, u32[]{:S(2)}, u32[]{:S(2)}) collective-permute-start(bf16[96,384]{1,0:T(8,128)(2,1)S(1)} %get-tuple-element.46), channel_id=1, source_target_pairs={{0,10},{1,11},{2,8},{3,9},{4,14},{5,15},{6,12},{7,13},{8,2},{9,3},... | collective-permute-start | bytes 221192 | tf_op jit(solution)/shard_map/ppermute | solution.py:21
  62.3 4.5 %collective-permute-start.10 = (bf16[96,384]{1,0:T(8,128)(2,1)S(1)}, bf16[96,384]{1,0:T(8,128)(2,1)S(1)}, u32[]{:S(2)}, u32[]{:S(2)}) collective-permute-start(bf16[96,384]{1,0:T(8,128)(2,1)S(1)} %get-tuple-element.47), channel_id=1, source_target_pairs={{0,8},{1,9},{2,10},{3,11},{4,12},{5,13},{6,14},{7,15},{8,0},{9,1},... | collective-permute-start | bytes 221192 | tf_op jit(solution)/shard_map/ppermute | solution.py:21
  66.9 6.1 %collective-permute-start.12 = (bf16[1,96,384]{2,1,0:T(8,128)(2,1)S(1)}, bf16[1,96,384]{2,1,0:T(8,128)(2,1)S(1)}, u32[]{:S(2)}, u32[]{:S(2)}) collective-permute-start(bf16[1,96,384]{2,1,0:T(8,128)(2,1)S(1)} %fusion.4), channel_id=1, source_target_pairs={{0,16},{1,17},{2,18},{3,19},{4,20},{5,21},{6,22},{7,23},{8,24},{9,... | collective-permute-start | bytes 221192 | tf_op jit(solution)/shard_map/ppermute | solution.py:21
  73.1 5.9 %collective-permute-start.14 = (bf16[2,96,384]{2,1,0:T(8,128)(2,1)S(1)}, bf16[2,96,384]{2,1,0:T(8,128)(2,1)S(1)}, u32[]{:S(2)}, u32[]{:S(2)}) collective-permute-start(bf16[2,96,384]{2,1,0:T(8,128)(2,1)S(1)} %get-tuple-element.49), channel_id=1, source_target_pairs={{0,2},{1,3},{2,0},{3,1},{4,6},{5,7},{6,4},{7,5},{8,10},{9,11},{10,... | collective-permute-start | bytes 442376 | tf_op jit(solution)/shard_map/ppermute | solution.py:21
  73.5 6.4 %collective-permute-start.13 = (bf16[2,96,384]{2,1,0:T(8,128)(2,1)S(1)}, bf16[2,96,384]{2,1,0:T(8,128)(2,1)S(1)}, u32[]{:S(2)}, u32[]{:S(2)}) collective-permute-start(bf16[2,96,384]{2,1,0:T(8,128)(2,1)S(1)} %get-tuple-element.49), channel_id=1, source_target_pairs={{0,4},{1,5},{2,6},{3,7},{4,0},{5,1},{6,2},{7,3},{8,12},{9,13},{10,... | collective-permute-start | bytes 442376 | tf_op jit(solution)/shard_map/ppermute | solution.py:21
  75.3 6.0 %collective-permute-start.15 = (bf16[2,96,384]{2,1,0:T(8,128)(2,1)S(1)}, bf16[2,96,384]{2,1,0:T(8,128)(2,1)S(1)}, u32[]{:S(2)}, u32[]{:S(2)}) collective-permute-start(bf16[2,96,384]{2,1,0:T(8,128)(2,1)S(1)} %get-tuple-element.49), channel_id=1, source_target_pairs={{0,6},{1,7},{2,4},{3,5},{4,2},{5,3},{6,0},{7,1},{8,14},{9,15},{10,... | collective-permute-start | bytes 442376 | tf_op jit(solution)/shard_map/ppermute | solution.py:21
  81.4 2.1 %collective-permute-start.16 = (bf16[4,2,96,384]{3,2,1,0:T(8,128)(2,1)S(1)}, bf16[4,2,96,384]{3,2,1,0:T(8,128)(2,1)S(1)}, u32[]{:S(2)}, u32[]{:S(2)}) collective-permute-start(bf16[4,2,96,384]{3,2,1,0:T(8,128)(2,1)S(1)} %pad_maximum_fusion.1.refs_3_), channel_id=1, source_target_pairs={{0,1},{1,0},{2,3},{3,2},{4,5},{5,4},{6,7},{7,6},{8,9},{9,8},{10,11... | collective-permute-start | bytes 1769480 | tf_op jit(solution)/shard_map/ppermute | solution.py:21
  88.2 2.2 %collective-permute-start.17 = (f32[4,112,384]{2,1,0:T(8,128)S(1)}, f32[4,112,384]{2,1,0:T(8,128)S(1)}, u32[]{:S(2)}, u32[]{:S(2)}) collective-permute-start(f32[4,112,384]{2,1,0:T(8,128)S(1)} %get-tuple-element.36), channel_id=1, source_target_pairs={{0,1},{1,0},{2,3},{3,2},{4,5},{5,4},{6,7},{7,6},{8,9},{9,8},{10,11... | collective-permute-start | bytes 2064392 | tf_op jit(solution)/shard_map/ppermute | solution.py:21
  88.4 5.8 %collective-permute-start.21 = (bf16[96,384]{1,0:T(8,128)(2,1)S(1)}, bf16[96,384]{1,0:T(8,128)(2,1)S(1)}, u32[]{:S(2)}, u32[]{:S(2)}) collective-permute-start(bf16[96,384]{1,0:T(8,128)(2,1)S(1)} %slice_bitcast_fusion.8), channel_id=1, source_target_pairs={{0,8},{1,9},{2,10},{3,11},{4,12},{5,13},{6,14},{7,15},{8,0},{9,1},... | collective-permute-start | bytes 221192 | tf_op jit(solution)/shard_map/ppermute | solution.py:21
  90.6 6.3 %collective-permute-start.20 = (bf16[112,384]{1,0:T(8,128)(2,1)S(1)}, bf16[112,384]{1,0:T(8,128)(2,1)S(1)}, u32[]{:S(2)}, u32[]{:S(2)}) collective-permute-start(bf16[112,384]{1,0:T(8,128)(2,1)S(1)} %get-tuple-element.42), channel_id=1, source_target_pairs={{0,10},{1,11},{2,8},{3,9},{4,14},{5,15},{6,12},{7,13},{8,2},{9,3},... | collective-permute-start | bytes 258056 | tf_op jit(solution)/shard_map/ppermute | solution.py:21
  91.3 6.1 %collective-permute-start.19 = (bf16[112,384]{1,0:T(8,128)(2,1)S(1)}, bf16[112,384]{1,0:T(8,128)(2,1)S(1)}, u32[]{:S(2)}, u32[]{:S(2)}) collective-permute-start(bf16[112,384]{1,0:T(8,128)(2,1)S(1)} %get-tuple-element.43), channel_id=1, source_target_pairs={{0,8},{1,9},{2,10},{3,11},{4,12},{5,13},{6,14},{7,15},{8,0},{9,1},... | collective-permute-start | bytes 258056 | tf_op jit(solution)/shard_map/ppermute | solution.py:21
  93.0 5.0 %collective-permute-start.18 = (bf16[112,384]{1,0:T(8,128)(2,1)S(1)}, bf16[112,384]{1,0:T(8,128)(2,1)S(1)}, u32[]{:S(2)}, u32[]{:S(2)}) collective-permute-start(bf16[112,384]{1,0:T(8,128)(2,1)S(1)} %get-tuple-element.44), channel_id=1, source_target_pairs={{0,2},{1,3},{2,0},{3,1},{4,6},{5,7},{6,4},{7,5},{8,10},{9,11},{10,... | collective-permute-start | bytes 258056 | tf_op jit(solution)/shard_map/ppermute | solution.py:21
  (4 other events, 26.5 us)

commit v6 on v5

--- a/solution.py
+++ b/solution.py
@@ -14,6 +14,7 @@
 MIB = 2**20
 START_COST = 3
 PEER_COST = 1
+PEER_MIB = 16
 PLAN_BITS = 5
 
 
@@ -58,12 +59,12 @@
     return jnp.dot(left, vector[source], preferred_element_type=jnp.float32) * weight
 
 
-def put_pair(mixed, rows, k, pair):
+def put_pair(mixed, k, pair):
     tile = pair[0].shape[1] // 2
     for half in range(2):
         at = slice(half * tile, (half + 1) * tile)
         both = jnp.concatenate([product[:, at] for product in pair], axis=1)
-        mixed[half, rows, k * tile : (k + 2) * tile] = both.astype(jnp.bfloat16)
+        mixed[half, :, k * tile : (k + 2) * tile] = both.astype(jnp.bfloat16)
 
 
 def collect(mixed, rights):
@@ -73,9 +74,23 @@
 
 
 def start_kernel(
-    sectors, plan, near, far, left_own, right_own, vector, mixed_ref, square_ref, lefts, rights, sems
+    sectors,
+    plan,
+    near,
+    far,
+    left_own,
+    right_own,
+    right_early,
+    vector,
+    mixed_ref,
+    total_ref,
+    square_ref,
+    lefts,
+    rights,
+    sems,
 ):
     terms, tile, _ = left_own.shape
+    early = right_early.shape[0] * tile
     width = 2 * tile
     core, x, y, z = plan[0], plan[1], plan[2], plan[3]
     copies = [
@@ -106,23 +121,23 @@
     copies[0].wait()
     for k in range(0, terms, 2):
         pair = [mix(plan, sectors, terms, i, lefts[i], vector) for i in (k, k + 1)]
-        put_pair(mixed_ref, slice(None), k, pair)
+        put_pair(mixed_ref, k, pair)
     copies[1].wait()
+    total = collect(mixed_ref[y], rights)
+    total_ref[...] = total + collect(mixed_ref[1 - y][:, :early], right_early)
 
 
 def peer_kernel(
     sectors,
     plan,
     vector,
-    mixed_own,
     left_own,
     left_peer,
     right_own,
     right_early,
-    mixed_ref,
+    mixed,
     total_ref,
     lefts,
-    mixed,
     sems,
 ):
     terms, tile, _ = left_peer.shape
@@ -136,18 +151,29 @@
     ]
     for copy in copies:
         copy.start()
-    mixed[:, own, :] = mixed_own[...]
     for k in range(0, terms, 2):
         pair = [mix(plan, sectors, terms, i, left_peer[i], vector) for i in (k, k + 1)]
-        put_pair(mixed, peer, k, pair)
-    rest = mixed[1 - y]
-    total_ref[...] = collect(mixed[y], right_own) + collect(rest[:, :early], right_early)
-    mixed_ref[...] = rest[:, early:]
+        put_pair(mixed, k, pair)
+    total_ref[...] = collect(mixed[y], right_own) + collect(mixed[1 - y][:, :early], right_early)
     for copy in copies:
         copy.wait()
 
 
-def first_kernel(plan, mixed, before, right_own, right_early, right_late, kept_ref, sent_ref, rights, sems):
+def first_kernel(
+    plan,
+    mixed_own,
+    mixed_peer,
+    before_own,
+    before_peer,
+    right_own,
+    right_early,
+    right_late,
+    kept_ref,
+    sent_ref,
+    rights,
+    parts,
+    sems,
+):
     early, tile, _ = right_early.shape
     late = right_late.shape[0]
     core, x, y, z = plan[0], plan[1], plan[2], plan[3]
@@ -160,28 +186,22 @@
     ]
     for copy in copies:
         copy.start()
-    total = before[...] + collect(mixed[...], right_late)
     sizes = plan[PLAN_BITS + 2 * plan[4]], plan[PLAN_BITS + 2 * plan[4] + 1]
-    parts = []
-    for z_row in range(2):
-        part = total[z_row * tile : (z_row + 1) * tile]
+    for k, (mixed, before, z_row) in enumerate(
+        ((mixed_own, before_own, z), (mixed_peer, before_peer, 1 - z))
+    ):
+        part = before[...] + collect(mixed[1 - y][:, early * tile :], right_late)
         keep = live_block(sizes, (2 * z_row + y) * tile, 0, part.shape)
-        parts.append(jnp.where(keep, part, 0.0))
+        parts[k] = jnp.where(keep, part, 0.0)
     _, unit_rows, unit_cols = kept_ref.shape
-    for core_is in range(2):
-        for x_is in range(2):
-            for z_is in range(2):
-
-                @pl.when((core == core_is) & (x == x_is) & (z == z_is))
-                def _():
-                    mine, other = parts[core_is], parts[1 - core_is]
-                    for xr in range(2):
-                        for zr in range(2):
-                            row, col = (x_is ^ xr) * unit_rows, (z_is ^ zr) * unit_cols
-                            at = slice(row, row + unit_rows), slice(col, col + unit_cols)
-                            kept_ref[2 * zr + xr] = mine[at]
-                            sent_ref[2 * zr + xr] = other[at]
-
+    for xr in range(2):
+        for zr in range(2):
+            at = (
+                pl.ds(pl.multiple_of((x ^ xr) * unit_rows, unit_rows), unit_rows),
+                pl.ds(pl.multiple_of((z ^ zr) * unit_cols, unit_cols), unit_cols),
+            )
+            kept_ref[2 * zr + xr] = parts[(core ^ z, *at)]
+            sent_ref[2 * zr + xr] = parts[(1 - (core ^ z), *at)]
     for copy in copies:
         copy.wait()
 
@@ -200,6 +220,7 @@
     tiles_ref,
     vector,
     mixed,
+    total,
 ):
     terms, width, _ = lefts.shape
     tile = width // 2
@@ -225,7 +246,7 @@
                 before = start[plan[4] ^ sr, at, :].astype(jnp.float32)
                 inner += jnp.sum((before * image).reshape(half // 8, 8, width), axis=0)
                 norm += jnp.sum((image * image).reshape(half // 8, 8, width), axis=0)
-    total = collect(mixed[...], rights)
+    total[...] = collect(mixed[...], rights)
     extra_shape = (EXTRA_ROWS, kept_ref.shape[2])
     lane = lax.broadcasted_iota(jnp.int32, extra_shape, 1)
     zeros = jnp.zeros(extra_shape, jnp.float32)
@@ -238,35 +259,26 @@
             z_sums = jnp.where(lane == 9 * core + 3 * k + level, piece, z_sums)
             value = value - piece
 
-    def packed(block, row, col):
-        halves = [block[row + r : row + r + half, col : col + tile] for r in (0, half)]
-        return jnp.concatenate(halves, axis=1)
-
-    image_tiles = []
-    for z_row in (z, 1 - z):
+    def packed(block):
+        halves = []
+        for col in (0, tile):
+            parts = [block[row : row + half, col : col + tile] for row in (0, half)]
+            halves.append(jnp.concatenate(parts, axis=1))
+        return jnp.where(core == 0, halves[0], halves[1]), jnp.where(core == 0, halves[1], halves[0])
+
+    for k, z_row in enumerate((z, 1 - z)):
         row = pl.multiple_of((2 * z_row + y) * tile, tile)
-        image_tiles.append(vector[plan[4], pl.ds(row, tile), :].astype(jnp.float32))
-    for core_is in range(2):
-
-        @pl.when(core == core_is)
-        def _():
-            for k in range(2):
-                tiles_ref[k] = packed(image_tiles[k], 0, core_is * tile).astype(tiles_ref.dtype)
-
-        for x_is in range(2):
-            for z_is in range(2):
-
-                @pl.when((core == core_is) & (x == x_is) & (z == z_is))
-                def _():
-                    for xr in range(2):
-                        for zr in range(2):
-                            row = (z_is ^ zr) * tile
-                            col = (x_is ^ xr) * width
-                            mine = packed(total, row, col + core_is * tile)
-                            other = packed(total, row, col + (1 - core_is) * tile)
-                            kept_ref[2 * zr + xr, :half] = mine
-                            sent_ref[2 * zr + xr, :half] = other
-
+        image = vector[plan[4], pl.ds(row, tile), :].astype(jnp.float32)
+        tiles_ref[k] = packed(image)[0].astype(tiles_ref.dtype)
+    for xr in range(2):
+        for zr in range(2):
+            at = (
+                pl.ds(pl.multiple_of((z ^ zr) * tile, tile), tile),
+                pl.ds(pl.multiple_of((x ^ xr) * width, width), width),
+            )
+            mine, other = packed(total[at])
+            kept_ref[2 * zr + xr, :half] = mine
+            sent_ref[2 * zr + xr, :half] = other
     for to in range(4):
         kept_ref[to, half:] = (own_sums, zeros, z_sums, zeros)[to]
         sent_ref[to, half:] = (own_sums, zeros, z_sums, zeros)[to]
@@ -353,43 +365,42 @@
     def params(mib):
         return pltpu.CompilerParams(vmem_limit_bytes=mib * MIB)
 
-    start_vector, mixed_own, square, left_own, right_own = pl.pallas_call(
+    total_shape = shaped(tile, capacity, dtype=f32)
+    mixed_shape = shaped(2, tile, terms * tile)
+    start_vector, mixed_own, total_own, square, left_own, right_own = pl.pallas_call(
         lambda *refs: start_kernel(sectors, *refs),
         out_shape=[
             shaped(*vector_shape),
-            shaped(2, tile, terms * tile),
+            mixed_shape,
+            total_shape,
             shaped(8, 128, dtype=f32),
             shaped(terms, tile, capacity),
             shaped(terms, tile, capacity),
         ],
-        in_specs=[smem(), vmem(), vmem(), anywhere(), anywhere()],
-        out_specs=[vmem()] * 5,
+        in_specs=[smem(), vmem(), vmem(), anywhere(), anywhere(), vmem()],
+        out_specs=[vmem()] * 6,
         scratch_shapes=[pltpu.SemaphoreType.DMA((2,))],
         compiler_params=params(16),
         cost_estimate=work(START_COST * macs),
-    )(plan, tiles, far_tiles, left_environment, right_environment)
-    mixed, total, lefts = pl.pallas_call(
+    )(plan, tiles, far_tiles, left_environment, right_environment, right_early)
+    mixed_peer, total_peer, lefts = pl.pallas_call(
         lambda *refs: peer_kernel(sectors, *refs),
-        out_shape=[
-            shaped(width, (terms - early) * tile),
-            shaped(width, capacity, dtype=f32),
-            shaped(terms, width, capacity),
-        ],
-        in_specs=[smem()] + [vmem()] * 6,
+        out_shape=[mixed_shape, total_shape, shaped(terms, width, capacity)],
+        in_specs=[smem()] + [vmem()] * 5,
         out_specs=[vmem()] * 3,
-        scratch_shapes=[pltpu.VMEM((2, width, terms * tile), bf16), pltpu.SemaphoreType.DMA((2,))],
-        compiler_params=params(20),
+        scratch_shapes=[pltpu.SemaphoreType.DMA((2,))],
+        compiler_params=params(PEER_MIB),
         cost_estimate=work(PEER_COST * macs),
-    )(plan, start_vector, mixed_own, left_own, left_peer, right_own, right_early)
+    )(plan, start_vector, left_own, left_peer, right_own, right_early)
     kept, sent, rights = pl.pallas_call(
         first_kernel,
         out_shape=[shaped(*unit, dtype=f32)] * 2 + [shaped(terms, width, capacity)],
-        in_specs=[smem()] + [vmem()] * 5,
+        in_specs=[smem()] + [vmem()] * 7,
         out_specs=[vmem()] * 3,
-        scratch_shapes=[pltpu.SemaphoreType.DMA((3,))],
+        scratch_shapes=[pltpu.VMEM((2, tile, capacity), f32), pltpu.SemaphoreType.DMA((3,))],
         compiler_params=params(16),
         cost_estimate=work(macs),
-    )(plan, mixed, total, right_own, right_early, right_late)
+    )(plan, mixed_own, mixed_peer, total_own, total_peer, right_own, right_early, right_late)
 
     summed = kept + exchange(sent, CORE)
     image_unit = (
@@ -414,7 +425,11 @@
         out_shape=[shaped(*part, dtype=f32)] * 2 + [shaped(2, half, width)],
         in_specs=[smem()] + [vmem()] * 6,
         out_specs=[vmem()] * 3,
-        scratch_shapes=[pltpu.VMEM(vector_shape, bf16), pltpu.VMEM((width, terms * width), bf16)],
+        scratch_shapes=[
+            pltpu.VMEM(vector_shape, bf16),
+            pltpu.VMEM((width, terms * width), bf16),
+            pltpu.VMEM((width, capacity), f32),
+        ],
         compiler_params=params(24),
         cost_estimate=work(4 * macs),
     )(

time: 99.8 us -> 99.3 us (level)
  waiting for transfers between devices: 44.9 us -> 43.3 us
    ppermute x20, waiting for transfers between devices: 44.9 us -> 43.3 us  [exchange(): lax.ppermute(block, 'sec', [(i, i ^ flip) for i in range(lax.axis_size('s...]
  transfers between devices with their start and end apart: 22 -> 22, of which waited for: 16 -> 16; matrix products, arithmetic and copies ran while one was open for 7% -> 7% of each run, Pallas kernels for 7% -> 8%
where the time goes in v6:
time: 99.3 us; the launch traced here: 98.9 us
  waiting for transfers between devices  43.3 us (44%)
  starting transfers between devices  27 us (27%)
  Pallas kernels  16.2 us (16%)
  local copies, waits for them, and re-layouts  9.35 us (9%)
  other arithmetic  2.11 us (2%)
    ppermute x20, waiting for transfers between devices, exchange(): lax.ppermute(block, 'sec', [(i, i ^ flip) for i in range(lax.axis_size('s...  43.3 us
    ppermute x20, starting transfers between devices, exchange(): lax.ppermute(block, 'sec', [(i, i ^ flip) for i in range(lax.axis_size('s...  22.3 us
    pallas_call x1, Pallas kernels, on_device(): pl.pallas_call(lambda *refs: start_kernel(sectors, *refs), out_shape=[sha...  4.82 us
    ppermute x2, starting transfers between devices, spread(): return lax.ppermute(tile, 'sec', route)  4.75 us
    pallas_call x1, Pallas kernels, on_device(): pl.pallas_call(lambda *refs: second_kernel(sectors, *refs), out_shape=[sh...  4.54 us
    unnamed x12, local copies, waits for them, and re-layouts  3.18 us
    pallas_call x1, Pallas kernels, on_device(): pl.pallas_call(lambda *refs: peer_kernel(sectors, *refs), out_shape=[mixe...  2.72 us
    pallas_call x1, Pallas kernels, on_device(): pl.pallas_call(first_kernel, out_shape=[shaped(*unit, dtype=f32)] * 2 + [...  2.67 us
  transfers between devices with their start and end apart: 22, of which 16 were waited for; matrix products, arithmetic and copies ran while one was open for 7% of the time, Pallas kernels for 8%

profile of v6, /device:TPU:0, one launch (start us, length us, event | category | flops | bytes accessed | tf_op | source)
XLA Modules:
  0.0 98.9 jit_solution(11557987717132276041)
XLA Ops:
  2.2 4.1 %collective-permute-start.1 = (bf16[96,384]{1,0:T(8,128)(2,1)S(1)}, bf16[96,384]{1,0:T(8,128)(2,1)S(1)}, u32[]{:S(2)}, u32[]{:S(2)}) collective-permute-start(bf16[96,384]{1,0:T(8,128)(2,1)S(1)} %pad_maximum_fusion.5), channel_id=1, source_target_pairs={{0,16},{1,17},{2,26},{3,27},{4,20},{5,21},{6,30},{7,31},{8,18},{9,... | collective-permute-start | bytes 221192 | tf_op jit(solution)/shard_map/ppermute | solution.py:31
  7.3 1.6 %collective-permute-start.3 = (bf16[1,192,768]{2,1,0:T(8,128)(2,1)S(1)}, bf16[1,192,768]{2,1,0:T(8,128)(2,1)S(1)}, u32[]{:S(2)}, u32[]{:S(2)}) collective-permute-start(bf16[1,192,768]{2,1,0:T(8,128)(2,1)S(1)} %slice.55), channel_id=1, source_target_pairs={{0,4},{1,5},{2,6},{3,7},{4,0},{5,1},{6,2},{7,3},{8,12},{9,13},{10,... | collective-permute-start | bytes 884744 | tf_op jit(solution)/shard_map/ppermute | solution.py:22
  8.9 4.3 %collective-permute-start.6 = (bf16[6,192,768]{2,1,0:T(8,128)(2,1)}, bf16[6,192,768]{2,1,0:T(8,128)(2,1)S(1)}, u32[]{:S(2)}, u32[]{:S(2)}) collective-permute-start(bf16[6,192,768]{2,1,0:T(8,128)(2,1)} %refs_3_.1), channel_id=1, source_target_pairs={{0,8},{1,9},{2,10},{3,11},{4,12},{5,13},{6,14},{7,15},{8,0},{9,1},... | collective-permute-start | bytes 5308424 | tf_op jit(solution)/shard_map/ppermute | solution.py:22
  14.2 2.6 %slice.56 = bf16[5,192,768]{2,1,0:T(8,128)(2,1)} slice(bf16[6,192,768]{2,1,0:T(8,128)(2,1)} %refs_4_.1), slice={[1:6], [0:192], [0:768]} | slice | bytes 2949120 | tf_op jit(solution)/shard_map/slice | solution.py:355
  17.9 2.2 %collective-permute-done.2 = bf16[2,96,384]{2,1,0:T(8,128)(2,1)S(1)} collective-permute-done((bf16[2,96,384]{2,1,0:T(8,128)(2,1)S(1)}, bf16[2,96,384]{2,1,0:T(8,128)(2,1)S(1)}, u32[]{:S(2)}, u32[]{:S(2)}) %collective-permute-start.2) | collective-permute-done | bytes 147488 | tf_op jit(solution)/shard_map/ppermute | solution.py:22
  20.9 1.8 %collective-permute-start.4 = (bf16[2,2,96,384]{3,2,1,0:T(8,128)(2,1)S(1)}, bf16[2,2,96,384]{3,2,1,0:T(8,128)(2,1)S(1)}, u32[]{:S(2)}, u32[]{:S(2)}) collective-permute-start(bf16[2,2,96,384]{3,2,1,0:T(8,128)(2,1)S(1)} %pad_maximum_fusion.2), channel_id=1, source_target_pairs={{0,2},{1,3},{2,0},{3,1},{4,6},{5,7},{6,4},{7,5},{8,10},{9,11},{10,... | collective-permute-start | bytes 884744 | tf_op jit(solution)/shard_map/ppermute | solution.py:22
  22.7 5.5 %collective-permute-done.4 = bf16[2,2,96,384]{3,2,1,0:T(8,128)(2,1)S(1)} collective-permute-done((bf16[2,2,96,384]{3,2,1,0:T(8,128)(2,1)S(1)}, bf16[2,2,96,384]{3,2,1,0:T(8,128)(2,1)S(1)}, u32[]{:S(2)}, u32[]{:S(2)}) %collective-permute-start.4) | collective-permute-done | bytes 294944 | tf_op jit(solution)/shard_map/ppermute | solution.py:22
  32.6 1.5 %copy-done.3 = bf16[6,192,768]{2,1,0:T(8,128)(2,1)S(1)} copy-done((bf16[6,192,768]{2,1,0:T(8,128)(2,1)S(1)}, bf16[6,192,768]{2,1,0:T(8,128)(2,1)}, u32[]{:S(2)}) %copy-start.3) | copy-done | bytes 1769496
  34.1 4.8 %shard_map.86 = (bf16[2,768,384]{2,1,0:T(8,128)(2,1)S(1)}, bf16[2,192,1152]{2,1,0:T(8,128)(2,1)S(1)}, f32[192,768]{1,0:T(8,128)S(1)}, f32[8,128]{1,0:T(8,128)S(1...) custom-call(s32[21]{0:T(128)S(1)} %concatenate.9.refs_0_.plan, ...), custom_call_target="tpu_custom_call" | custom-call | flops 2038431744 | bytes 3538944 | tf_op jit(solution)/shard_map/pallas_call | solution.py:370
  38.9 12.8 %collective-permute-done.6.refs_3_ = bf16[6,192,768]{2,1,0:T(8,128)(2,1)S(1)} collective-permute-done((bf16[6,192,768]{2,1,0:T(8,128)(2,1)}, bf16[6,192,768]{2,1,0:T(8,128)(2,1)S(1)}, u32[]{:S(2)}, u32[]{:S(2)}) %collective-permute-start.6) | collective-permute-done | bytes 1769504 | tf_op jit(solution)/shard_map/ppermute | solution.py:22
  51.7 2.7 %shard_map.87 = (bf16[2,192,1152]{2,1,0:T(8,128)(2,1)S(1)}, f32[192,768]{1,0:T(8,128)S(1)}, bf16[6,384,768]{2,1,0:T(8,128)(2,1)S(1)}) custom-call(s32[21]{0:T(128)S(1)} %concatenate.9.refs_0_.plan, bf16[2,768,384]{2,1,0:T(8,128)(2,1)S(1)} %get-tuple-element.25.refs_1_.refs_2_, bf16[6,192,768]{2,1,0:T(8,128)(2,1)S(1)} %get-tuple-element.27.refs_2_, ...), custom_call_target="tpu_custom_call" | custom-call | flops 679477248 | bytes 3538944 | tf_op jit(solution)/shard_map/pallas_call | solution.py:386
  54.4 2.7 %shard_map.88 = (f32[4,96,384]{2,1,0:T(8,128)S(1)}, f32[4,96,384]{2,1,0:T(8,128)S(1)}, bf16[6,384,768]{2,1,0:T(8,128)(2,1)S(1)}) custom-call(s32[21]{0:T(128)S(1)} %concatenate.9.refs_0_.plan, bf16[2,192,1152]{2,1,0:T(8,128)(2,1)S(1)} %get-tuple-element.26.mixed_own, bf16[2,192,1152]{2,1,0:T(8,128)(2,1)S(1)} %get-tuple-element.30.mixed_peer, ...), custom_call_target="tpu_custom_call" | custom-call | flops 679477248 | bytes 3538944 | tf_op jit(solution)/shard_map/pallas_call | solution.py:395
  57.2 2.0 %collective-permute-done.8 = f32[4,96,384]{2,1,0:T(8,128)S(1)} collective-permute-done((f32[4,96,384]{2,1,0:T(8,128)S(1)}, f32[4,96,384]{2,1,0:T(8,128)S(1)}, u32[]{:S(2)}, u32[]{:S(2)}) %collective-permute-start.8) | collective-permute-done | bytes 589856 | tf_op jit(solution)/shard_map/ppermute | solution.py:22
  60.2 1.8 %collective-permute-start.11 = (bf16[96,384]{1,0:T(8,128)(2,1)S(1)}, bf16[96,384]{1,0:T(8,128)(2,1)S(1)}, u32[]{:S(2)}, u32[]{:S(2)}) collective-permute-start(bf16[96,384]{1,0:T(8,128)(2,1)S(1)} %get-tuple-element.48), channel_id=1, source_target_pairs={{0,10},{1,11},{2,8},{3,9},{4,14},{5,15},{6,12},{7,13},{8,2},{9,3},... | collective-permute-start | bytes 221192 | tf_op jit(solution)/shard_map/ppermute | solution.py:22
  62.8 1.7 %collective-permute-done.9 = bf16[96,384]{1,0:T(8,128)(2,1)S(1)} collective-permute-done((bf16[96,384]{1,0:T(8,128)(2,1)S(1)}, bf16[96,384]{1,0:T(8,128)(2,1)S(1)}, u32[]{:S(2)}, u32[]{:S(2)}) %collective-permute-start.9) | collective-permute-done | bytes 73760 | tf_op jit(solution)/shard_map/ppermute | solution.py:22
  64.5 1.5 %collective-permute-done.11 = bf16[96,384]{1,0:T(8,128)(2,1)S(1)} collective-permute-done((bf16[96,384]{1,0:T(8,128)(2,1)S(1)}, bf16[96,384]{1,0:T(8,128)(2,1)S(1)}, u32[]{:S(2)}, u32[]{:S(2)}) %collective-permute-start.11) | collective-permute-done | bytes 73760 | tf_op jit(solution)/shard_map/ppermute | solution.py:22
  67.7 5.0 %collective-permute-done.12 = bf16[1,96,384]{2,1,0:T(8,128)(2,1)S(1)} collective-permute-done((bf16[1,96,384]{2,1,0:T(8,128)(2,1)S(1)}, bf16[1,96,384]{2,1,0:T(8,128)(2,1)S(1)}, u32[]{:S(2)}, u32[]{:S(2)}) %collective-permute-start.12) | collective-permute-done | bytes 73760 | tf_op jit(solution)/shard_map/ppermute | solution.py:22
  73.2 1.7 %collective-permute-start.13 = (bf16[2,96,384]{2,1,0:T(8,128)(2,1)S(1)}, bf16[2,96,384]{2,1,0:T(8,128)(2,1)S(1)}, u32[]{:S(2)}, u32[]{:S(2)}) collective-permute-start(bf16[2,96,384]{2,1,0:T(8,128)(2,1)S(1)} %get-tuple-element.51), channel_id=1, source_target_pairs={{0,4},{1,5},{2,6},{3,7},{4,0},{5,1},{6,2},{7,3},{8,12},{9,13},{10,... | collective-permute-start | bytes 442376 | tf_op jit(solution)/shard_map/ppermute | solution.py:22
  76.3 2.4 %collective-permute-done.14 = bf16[2,96,384]{2,1,0:T(8,128)(2,1)S(1)} collective-permute-done((bf16[2,96,384]{2,1,0:T(8,128)(2,1)S(1)}, bf16[2,96,384]{2,1,0:T(8,128)(2,1)S(1)}, u32[]{:S(2)}, u32[]{:S(2)}) %collective-permute-start.14) | collective-permute-done | bytes 147488 | tf_op jit(solution)/shard_map/ppermute | solution.py:22
  81.1 2.0 %collective-permute-done.16.refs_4_ = bf16[4,2,96,384]{3,2,1,0:T(8,128)(2,1)S(1)} collective-permute-done((bf16[4,2,96,384]{3,2,1,0:T(8,128)(2,1)S(1)}, bf16[4,2,96,384]{3,2,1,0:T(8,128)(2,1)S(1)}, u32[]{:S(2)}, u32[]{:S(2)}) %collective-permute-start.16) | collective-permute-done | bytes 589856 | tf_op jit(solution)/shard_map/ppermute | solution.py:22
  83.1 4.5 %shard_map.89 = (f32[4,112,384]{2,1,0:T(8,128)S(1)}, f32[4,112,384]{2,1,0:T(8,128)S(1)}, bf16[2,96,384]{2,1,0:T(8,128)(2,1)S(1)}) custom-call(s32[21]{0:T(128)S(1)} %concatenate.9.refs_0_.plan, f32[8,128]{1,0:T(8,128)S(1)} %get-tuple-element.24.refs_1_, bf16[2,768,384]{2,1,0:T(8,128)(2,1)S(1)} %get-tuple-element.25.refs_1_.refs_2_, ...), custom_call_target="tpu_custom_call" | custom-call | flops 2717908992 | bytes 3538944 | tf_op jit(solution)/shard_map/pallas_call | solution.py:423
  88.3 1.6 %collective-permute-done.17 = f32[4,112,384]{2,1,0:T(8,128)S(1)} collective-permute-done((f32[4,112,384]{2,1,0:T(8,128)S(1)}, f32[4,112,384]{2,1,0:T(8,128)S(1)}, u32[]{:S(2)}, u32[]{:S(2)}) %collective-permute-start.17) | collective-permute-done | bytes 688160 | tf_op jit(solution)/shard_map/ppermute | solution.py:22
  90.8 1.7 %collective-permute-start.19 = (bf16[112,384]{1,0:T(8,128)(2,1)S(1)}, bf16[112,384]{1,0:T(8,128)(2,1)S(1)}, u32[]{:S(2)}, u32[]{:S(2)}) collective-permute-start(bf16[112,384]{1,0:T(8,128)(2,1)S(1)} %get-tuple-element.45), channel_id=1, source_target_pairs={{0,8},{1,9},{2,10},{3,11},{4,12},{5,13},{6,14},{7,15},{8,0},{9,1},... | collective-permute-start | bytes 258056 | tf_op jit(solution)/shard_map/ppermute | solution.py:22
  93.6 2.8 %collective-permute-done.20.from_xz = bf16[112,384]{1,0:T(8,128)(2,1)S(1)} collective-permute-done((bf16[112,384]{1,0:T(8,128)(2,1)S(1)}, bf16[112,384]{1,0:T(8,128)(2,1)S(1)}, u32[]{:S(2)}, u32[]{:S(2)}) %collective-permute-start.20) | collective-permute-done | bytes 86048 | tf_op jit(solution)/shard_map/ppermute | solution.py:22
  (63 shorter events, 22.8 us)
Async XLA Ops:
  1.6 7.3 %collective-permute-start = (bf16[96,384]{1,0:T(8,128)(2,1)S(1)}, bf16[96,384]{1,0:T(8,128)(2,1)S(1)}, u32[]{:S(2)}, u32[]{:S(2)}) collective-permute-start(bf16[96,384]{1,0:T(8,128)(2,1)S(1)} %pad_maximum_fusion.5), channel_id=1, source_target_pairs={{0,0},{1,1},{2,8},{3,9},{4,4},{5,5},{6,12},{7,13},{8,2},{9,3},{10,... | collective-permute-start | bytes 221192 | tf_op jit(solution)/shard_map/ppermute | solution.py:31
  2.2 10.9 %collective-permute-start.1 = (bf16[96,384]{1,0:T(8,128)(2,1)S(1)}, bf16[96,384]{1,0:T(8,128)(2,1)S(1)}, u32[]{:S(2)}, u32[]{:S(2)}) collective-permute-start(bf16[96,384]{1,0:T(8,128)(2,1)S(1)} %pad_maximum_fusion.5), channel_id=1, source_target_pairs={{0,16},{1,17},{2,26},{3,27},{4,20},{5,21},{6,30},{7,31},{8,18},{9,... | collective-permute-start | bytes 221192 | tf_op jit(solution)/shard_map/ppermute | solution.py:31
  7.3 12.9 %collective-permute-start.3 = (bf16[1,192,768]{2,1,0:T(8,128)(2,1)S(1)}, bf16[1,192,768]{2,1,0:T(8,128)(2,1)S(1)}, u32[]{:S(2)}, u32[]{:S(2)}) collective-permute-start(bf16[1,192,768]{2,1,0:T(8,128)(2,1)S(1)} %slice.55), channel_id=1, source_target_pairs={{0,4},{1,5},{2,6},{3,7},{4,0},{5,1},{6,2},{7,3},{8,12},{9,13},{10,... | collective-permute-start | bytes 884744 | tf_op jit(solution)/shard_map/ppermute | solution.py:22
  8.9 42.8 %collective-permute-start.6 = (bf16[6,192,768]{2,1,0:T(8,128)(2,1)}, bf16[6,192,768]{2,1,0:T(8,128)(2,1)S(1)}, u32[]{:S(2)}, u32[]{:S(2)}) collective-permute-start(bf16[6,192,768]{2,1,0:T(8,128)(2,1)} %refs_3_.1), channel_id=1, source_target_pairs={{0,8},{1,9},{2,10},{3,11},{4,12},{5,13},{6,14},{7,15},{8,0},{9,1},... | collective-permute-start | bytes 5308424 | tf_op jit(solution)/shard_map/ppermute | solution.py:22
  13.2 15.9 %copy-start.5 = (s32[2]{0:T(128)S(1)}, s32[2]{0:T(128)}, u32[]{:S(2)}) copy-start(s32[2]{0:T(128)} %param.11) | copy-start | bytes 28
  13.2 6.9 %collective-permute-start.2 = (bf16[2,96,384]{2,1,0:T(8,128)(2,1)S(1)}, bf16[2,96,384]{2,1,0:T(8,128)(2,1)S(1)}, u32[]{:S(2)}, u32[]{:S(2)}) collective-permute-start(bf16[2,96,384]{2,1,0:T(8,128)(2,1)S(1)} %get-tuple-element.53), channel_id=1, source_target_pairs={{0,4},{1,5},{2,6},{3,7},{4,0},{5,1},{6,2},{7,3},{8,12},{9,13},{10,... | collective-permute-start | bytes 442376 | tf_op jit(solution)/shard_map/ppermute | solution.py:22
  16.8 14.8 %copy-start = (bf16[6,192,768]{2,1,0:T(8,128)(2,1)S(1)}, bf16[6,192,768]{2,1,0:T(8,128)(2,1)}, u32[]{:S(2)}) copy-start(bf16[6,192,768]{2,1,0:T(8,128)(2,1)} %refs_4_.1) | copy-start | bytes 5308420
  16.8 37.6 %collective-permute-start.7 = (bf16[5,192,768]{2,1,0:T(8,128)(2,1)}, bf16[5,192,768]{2,1,0:T(8,128)(2,1)}, u32[]{:S(2)}, u32[]{:S(2)}) collective-permute-start(bf16[5,192,768]{2,1,0:T(8,128)(2,1)} %slice.56), channel_id=1, source_target_pairs={{0,4},{1,5},{2,6},{3,7},{4,0},{5,1},{6,2},{7,3},{8,12},{9,13},{10,... | collective-permute-start | bytes 4423688 | tf_op jit(solution)/shard_map/ppermute | solution.py:22
  20.9 7.3 %collective-permute-start.4 = (bf16[2,2,96,384]{3,2,1,0:T(8,128)(2,1)S(1)}, bf16[2,2,96,384]{3,2,1,0:T(8,128)(2,1)S(1)}, u32[]{:S(2)}, u32[]{:S(2)}) collective-permute-start(bf16[2,2,96,384]{3,2,1,0:T(8,128)(2,1)S(1)} %pad_maximum_fusion.2), channel_id=1, source_target_pairs={{0,2},{1,3},{2,0},{3,1},{4,6},{5,7},{6,4},{7,5},{8,10},{9,11},{10,... | collective-permute-start | bytes 884744 | tf_op jit(solution)/shard_map/ppermute | solution.py:22
  29.1 2.5 %collective-permute-start.5 = (bf16[2,2,2,96,384]{4,3,2,1,0:T(8,128)(2,1)}, bf16[2,2,2,96,384]{4,3,2,1,0:T(8,128)(2,1)}, u32[]{:S(2)}, u32[]{:S(2)}) collective-permute-start(bf16[2,2,2,96,384]{4,3,2,1,0:T(8,128)(2,1)} %pad_maximum_fusion.refs_1_), channel_id=1, source_target_pairs={{0,1},{1,0},{2,3},{3,2},{4,5},{5,4},{6,7},{7,6},{8,9},{9,8},{10,11... | collective-permute-start | bytes 1769480 | tf_op jit(solution)/shard_map/ppermute | solution.py:22
  57.1 2.1 %collective-permute-start.8 = (f32[4,96,384]{2,1,0:T(8,128)S(1)}, f32[4,96,384]{2,1,0:T(8,128)S(1)}, u32[]{:S(2)}, u32[]{:S(2)}) collective-permute-start(f32[4,96,384]{2,1,0:T(8,128)S(1)} %get-tuple-element.34), channel_id=1, source_target_pairs={{0,1},{1,0},{2,3},{3,2},{4,5},{5,4},{6,7},{7,6},{8,9},{9,8},{10,11... | collective-permute-start | bytes 1769480 | tf_op jit(solution)/shard_map/ppermute | solution.py:22
  59.3 5.2 %collective-permute-start.9 = (bf16[96,384]{1,0:T(8,128)(2,1)S(1)}, bf16[96,384]{1,0:T(8,128)(2,1)S(1)}, u32[]{:S(2)}, u32[]{:S(2)}) collective-permute-start(bf16[96,384]{1,0:T(8,128)(2,1)S(1)} %get-tuple-element.47), channel_id=1, source_target_pairs={{0,2},{1,3},{2,0},{3,1},{4,6},{5,7},{6,4},{7,5},{8,10},{9,11},{10,... | collective-permute-start | bytes 221192 | tf_op jit(solution)/shard_map/ppermute | solution.py:22
  60.2 5.8 %collective-permute-start.11 = (bf16[96,384]{1,0:T(8,128)(2,1)S(1)}, bf16[96,384]{1,0:T(8,128)(2,1)S(1)}, u32[]{:S(2)}, u32[]{:S(2)}) collective-permute-start(bf16[96,384]{1,0:T(8,128)(2,1)S(1)} %get-tuple-element.48), channel_id=1, source_target_pairs={{0,10},{1,11},{2,8},{3,9},{4,14},{5,15},{6,12},{7,13},{8,2},{9,3},... | collective-permute-start | bytes 221192 | tf_op jit(solution)/shard_map/ppermute | solution.py:22
  62.0 4.5 %collective-permute-start.10 = (bf16[96,384]{1,0:T(8,128)(2,1)S(1)}, bf16[96,384]{1,0:T(8,128)(2,1)S(1)}, u32[]{:S(2)}, u32[]{:S(2)}) collective-permute-start(bf16[96,384]{1,0:T(8,128)(2,1)S(1)} %get-tuple-element.49), channel_id=1, source_target_pairs={{0,8},{1,9},{2,10},{3,11},{4,12},{5,13},{6,14},{7,15},{8,0},{9,1},... | collective-permute-start | bytes 221192 | tf_op jit(solution)/shard_map/ppermute | solution.py:22
  66.6 6.1 %collective-permute-start.12 = (bf16[1,96,384]{2,1,0:T(8,128)(2,1)S(1)}, bf16[1,96,384]{2,1,0:T(8,128)(2,1)S(1)}, u32[]{:S(2)}, u32[]{:S(2)}) collective-permute-start(bf16[1,96,384]{2,1,0:T(8,128)(2,1)S(1)} %fusion.4), channel_id=1, source_target_pairs={{0,16},{1,17},{2,18},{3,19},{4,20},{5,21},{6,22},{7,23},{8,24},{9,... | collective-permute-start | bytes 221192 | tf_op jit(solution)/shard_map/ppermute | solution.py:22
  72.7 5.9 %collective-permute-start.14 = (bf16[2,96,384]{2,1,0:T(8,128)(2,1)S(1)}, bf16[2,96,384]{2,1,0:T(8,128)(2,1)S(1)}, u32[]{:S(2)}, u32[]{:S(2)}) collective-permute-start(bf16[2,96,384]{2,1,0:T(8,128)(2,1)S(1)} %get-tuple-element.51), channel_id=1, source_target_pairs={{0,2},{1,3},{2,0},{3,1},{4,6},{5,7},{6,4},{7,5},{8,10},{9,11},{10,... | collective-permute-start | bytes 442376 | tf_op jit(solution)/shard_map/ppermute | solution.py:22
  73.2 6.4 %collective-permute-start.13 = (bf16[2,96,384]{2,1,0:T(8,128)(2,1)S(1)}, bf16[2,96,384]{2,1,0:T(8,128)(2,1)S(1)}, u32[]{:S(2)}, u32[]{:S(2)}) collective-permute-start(bf16[2,96,384]{2,1,0:T(8,128)(2,1)S(1)} %get-tuple-element.51), channel_id=1, source_target_pairs={{0,4},{1,5},{2,6},{3,7},{4,0},{5,1},{6,2},{7,3},{8,12},{9,13},{10,... | collective-permute-start | bytes 442376 | tf_op jit(solution)/shard_map/ppermute | solution.py:22
  74.9 6.0 %collective-permute-start.15 = (bf16[2,96,384]{2,1,0:T(8,128)(2,1)S(1)}, bf16[2,96,384]{2,1,0:T(8,128)(2,1)S(1)}, u32[]{:S(2)}, u32[]{:S(2)}) collective-permute-start(bf16[2,96,384]{2,1,0:T(8,128)(2,1)S(1)} %get-tuple-element.51), channel_id=1, source_target_pairs={{0,6},{1,7},{2,4},{3,5},{4,2},{5,3},{6,0},{7,1},{8,14},{9,15},{10,... | collective-permute-start | bytes 442376 | tf_op jit(solution)/shard_map/ppermute | solution.py:22
  81.1 2.1 %collective-permute-start.16 = (bf16[4,2,96,384]{3,2,1,0:T(8,128)(2,1)S(1)}, bf16[4,2,96,384]{3,2,1,0:T(8,128)(2,1)S(1)}, u32[]{:S(2)}, u32[]{:S(2)}) collective-permute-start(bf16[4,2,96,384]{3,2,1,0:T(8,128)(2,1)S(1)} %pad_maximum_fusion.1.refs_3_), channel_id=1, source_target_pairs={{0,1},{1,0},{2,3},{3,2},{4,5},{5,4},{6,7},{7,6},{8,9},{9,8},{10,11... | collective-permute-start | bytes 1769480 | tf_op jit(solution)/shard_map/ppermute | solution.py:22
  87.7 2.2 %collective-permute-start.17 = (f32[4,112,384]{2,1,0:T(8,128)S(1)}, f32[4,112,384]{2,1,0:T(8,128)S(1)}, u32[]{:S(2)}, u32[]{:S(2)}) collective-permute-start(f32[4,112,384]{2,1,0:T(8,128)S(1)} %get-tuple-element.38), channel_id=1, source_target_pairs={{0,1},{1,0},{2,3},{3,2},{4,5},{5,4},{6,7},{7,6},{8,9},{9,8},{10,11... | collective-permute-start | bytes 2064392 | tf_op jit(solution)/shard_map/ppermute | solution.py:22
  87.9 5.8 %collective-permute-start.21 = (bf16[96,384]{1,0:T(8,128)(2,1)S(1)}, bf16[96,384]{1,0:T(8,128)(2,1)S(1)}, u32[]{:S(2)}, u32[]{:S(2)}) collective-permute-start(bf16[96,384]{1,0:T(8,128)(2,1)S(1)} %slice_bitcast_fusion.8), channel_id=1, source_target_pairs={{0,8},{1,9},{2,10},{3,11},{4,12},{5,13},{6,14},{7,15},{8,0},{9,1},... | collective-permute-start | bytes 221192 | tf_op jit(solution)/shard_map/ppermute | solution.py:22
  90.1 6.3 %collective-permute-start.20 = (bf16[112,384]{1,0:T(8,128)(2,1)S(1)}, bf16[112,384]{1,0:T(8,128)(2,1)S(1)}, u32[]{:S(2)}, u32[]{:S(2)}) collective-permute-start(bf16[112,384]{1,0:T(8,128)(2,1)S(1)} %get-tuple-element.44), channel_id=1, source_target_pairs={{0,10},{1,11},{2,8},{3,9},{4,14},{5,15},{6,12},{7,13},{8,2},{9,3},... | collective-permute-start | bytes 258056 | tf_op jit(solution)/shard_map/ppermute | solution.py:22
  90.8 6.1 %collective-permute-start.19 = (bf16[112,384]{1,0:T(8,128)(2,1)S(1)}, bf16[112,384]{1,0:T(8,128)(2,1)S(1)}, u32[]{:S(2)}, u32[]{:S(2)}) collective-permute-start(bf16[112,384]{1,0:T(8,128)(2,1)S(1)} %get-tuple-element.45), channel_id=1, source_target_pairs={{0,8},{1,9},{2,10},{3,11},{4,12},{5,13},{6,14},{7,15},{8,0},{9,1},... | collective-permute-start | bytes 258056 | tf_op jit(solution)/shard_map/ppermute | solution.py:22
  92.5 5.0 %collective-permute-start.18 = (bf16[112,384]{1,0:T(8,128)(2,1)S(1)}, bf16[112,384]{1,0:T(8,128)(2,1)S(1)}, u32[]{:S(2)}, u32[]{:S(2)}) collective-permute-start(bf16[112,384]{1,0:T(8,128)(2,1)S(1)} %get-tuple-element.46), channel_id=1, source_target_pairs={{0,2},{1,3},{2,0},{3,1},{4,6},{5,7},{6,4},{7,5},{8,10},{9,11},{10,... | collective-permute-start | bytes 258056 | tf_op jit(solution)/shard_map/ppermute | solution.py:22
  (4 other events, 12.7 us)

commit v7 on v6

--- a/solution.py
+++ b/solution.py
@@ -159,7 +159,38 @@
         copy.wait()
 
 
-def first_kernel(
+def finish_rows(plan, mine, rows, right_late, unit_ref, scratch):
+    late, tile, _ = right_late.shape
+    x, y, z = plan[1], plan[2], plan[3]
+    (mixed_own, before_own), (mixed_peer, before_peer) = rows
+    is_own = mine == z
+    first = mixed_own.shape[2] - late * tile
+    mixed = jnp.where(is_own, mixed_own[1 - y], mixed_peer[1 - y])[:, first:]
+    total = jnp.where(is_own, before_own[...], before_peer[...]) + collect(mixed, right_late)
+    sizes = plan[PLAN_BITS + 2 * plan[4]], plan[PLAN_BITS + 2 * plan[4] + 1]
+    keep = live_block(sizes, (2 * mine + y) * tile, 0, total.shape)
+    scratch[...] = jnp.where(keep, total, 0.0)
+    _, unit_rows, unit_cols = unit_ref.shape
+    for xr in range(2):
+        for zr in range(2):
+            at = (
+                pl.ds(pl.multiple_of((x ^ xr) * unit_rows, unit_rows), unit_rows),
+                pl.ds(pl.multiple_of((z ^ zr) * unit_cols, unit_cols), unit_cols),
+            )
+            unit_ref[2 * zr + xr] = scratch[at]
+
+
+def sent_kernel(
+    plan, mixed_own, mixed_peer, before_own, before_peer, right_late, sent_ref, late_ref, scratch, sem
+):
+    copy = pltpu.make_async_copy(right_late, late_ref, sem)
+    copy.start()
+    rows = ((mixed_own, before_own), (mixed_peer, before_peer))
+    finish_rows(plan, 1 - plan[0], rows, right_late, sent_ref, scratch)
+    copy.wait()
+
+
+def kept_kernel(
     plan,
     mixed_own,
     mixed_peer,
@@ -169,14 +200,13 @@
     right_early,
     right_late,
     kept_ref,
-    sent_ref,
     rights,
-    parts,
+    scratch,
     sems,
 ):
     early, tile, _ = right_early.shape
     late = right_late.shape[0]
-    core, x, y, z = plan[0], plan[1], plan[2], plan[3]
+    y = plan[2]
     own = pl.ds(pl.multiple_of(y * tile, tile), tile)
     peer = pl.ds(pl.multiple_of((1 - y) * tile, tile), tile)
     copies = [
@@ -186,31 +216,52 @@
     ]
     for copy in copies:
         copy.start()
-    sizes = plan[PLAN_BITS + 2 * plan[4]], plan[PLAN_BITS + 2 * plan[4] + 1]
-    for k, (mixed, before, z_row) in enumerate(
-        ((mixed_own, before_own, z), (mixed_peer, before_peer, 1 - z))
-    ):
-        part = before[...] + collect(mixed[1 - y][:, early * tile :], right_late)
-        keep = live_block(sizes, (2 * z_row + y) * tile, 0, part.shape)
-        parts[k] = jnp.where(keep, part, 0.0)
-    _, unit_rows, unit_cols = kept_ref.shape
-    for xr in range(2):
-        for zr in range(2):
-            at = (
-                pl.ds(pl.multiple_of((x ^ xr) * unit_rows, unit_rows), unit_rows),
-                pl.ds(pl.multiple_of((z ^ zr) * unit_cols, unit_cols), unit_cols),
-            )
-            kept_ref[2 * zr + xr] = parts[(core ^ z, *at)]
-            sent_ref[2 * zr + xr] = parts[(1 - (core ^ z), *at)]
+    rows = ((mixed_own, before_own), (mixed_peer, before_peer))
+    finish_rows(plan, plan[0], rows, right_late, kept_ref, scratch)
     for copy in copies:
         copy.wait()
+
+
+def gather_pieces(plan, pieces, vector):
+    x, y = plan[1], plan[2]
+    _, sectors, half, _ = pieces.shape
+    for xr in range(2):
+        for yr in range(2):
+            for sr in range(sectors):
+                row = (y ^ yr) * 2 * half + (x ^ xr) * half
+                at = pl.ds(pl.multiple_of(row, half), half)
+                vector[plan[4] ^ sr, at, :] = pieces[2 * xr + yr, sr]
+
+
+def near_kernel(sectors, plan, start, near, lefts, partial_ref, sums_ref, vector):
+    terms, width, _ = lefts.shape
+    half = width // 4
+    core, x, y = plan[0], plan[1], plan[2]
+    gather_pieces(plan, near, vector)
+    cols = pl.ds(pl.multiple_of(core * width, width), width)
+    inner = jnp.zeros((8, width), jnp.float32)
+    norm = inner
+    for k in range(terms):
+        source, _ = term_of(plan, sectors, terms, k)
+        partial_ref[k] = jnp.dot(lefts[k, :, cols], vector[source], preferred_element_type=jnp.float32)
+        if k < 4:
+            for sr in range(sectors):
+                row = core * width + (y ^ (k % 2)) * 2 * half + (x ^ (k // 2)) * half
+                at = pl.ds(pl.multiple_of(row, half), half)
+                image = near[k, sr].astype(jnp.float32)
+                before = start[plan[4] ^ sr, at, :].astype(jnp.float32)
+                inner += jnp.sum((before * image).reshape(half // 8, 8, width), axis=0)
+                norm += jnp.sum((image * image).reshape(half // 8, 8, width), axis=0)
+    for k, value in enumerate((inner, norm)):
+        sums_ref[k] = jnp.broadcast_to(jnp.sum(value), sums_ref.shape[1:])
 
 
 def second_kernel(
     sectors,
     plan,
     square_ref,
-    start,
+    sums_ref,
+    partial,
     near,
     far,
     lefts,
@@ -226,32 +277,19 @@
     tile = width // 2
     half = tile // 2
     core, x, y, z = plan[0], plan[1], plan[2], plan[3]
-    for pieces, z_row in ((near, core), (far, 1 - core)):
-        for xr in range(2):
-            for yr in range(2):
-                for sr in range(sectors):
-                    row = (2 * z_row + (y ^ yr)) * tile + (x ^ xr) * half
-                    at = pl.ds(pl.multiple_of(row, half), half)
-                    vector[plan[4] ^ sr, at, :] = pieces[2 * xr + yr, sr]
-    inner = jnp.zeros((8, width), jnp.float32)
-    norm = inner
+    gather_pieces(plan, far, vector)
+    cols = pl.ds(pl.multiple_of((1 - core) * width, width), width)
     for k in range(terms):
-        product = mix(plan, sectors, terms, k, lefts[k], vector)
+        source, weight = term_of(plan, sectors, terms, k)
+        product = jnp.dot(lefts[k, :, cols], vector[source], preferred_element_type=jnp.float32)
+        product = (partial[k] + product) * weight
         mixed[:, k * width : (k + 1) * width] = product.astype(jnp.bfloat16)
-        if k < 4:
-            for sr in range(sectors):
-                row = (2 * core + (y ^ (k % 2))) * tile + (x ^ (k // 2)) * half
-                at = pl.ds(pl.multiple_of(row, half), half)
-                image = near[k, sr].astype(jnp.float32)
-                before = start[plan[4] ^ sr, at, :].astype(jnp.float32)
-                inner += jnp.sum((before * image).reshape(half // 8, 8, width), axis=0)
-                norm += jnp.sum((image * image).reshape(half // 8, 8, width), axis=0)
     total[...] = collect(mixed[...], rights)
     extra_shape = (EXTRA_ROWS, kept_ref.shape[2])
     lane = lax.broadcasted_iota(jnp.int32, extra_shape, 1)
     zeros = jnp.zeros(extra_shape, jnp.float32)
     own_sums, z_sums = zeros, zeros
-    for k, value in enumerate((0.5 * square_ref[0, 0], jnp.sum(inner), jnp.sum(norm))):
+    for k, value in enumerate((0.5 * square_ref[0, 0], sums_ref[0, 0, 0], sums_ref[1, 0, 0])):
         value = jnp.broadcast_to(value, extra_shape)
         own_sums = jnp.where(lane == k, value, own_sums)
         for level in range(3):
@@ -259,24 +297,27 @@
             z_sums = jnp.where(lane == 9 * core + 3 * k + level, piece, z_sums)
             value = value - piece
 
-    def packed(block):
-        halves = []
-        for col in (0, tile):
-            parts = [block[row : row + half, col : col + tile] for row in (0, half)]
-            halves.append(jnp.concatenate(parts, axis=1))
+    def packed(top, bottom):
+        halves = [
+            jnp.concatenate([top[:, col : col + tile], bottom[:, col : col + tile]], axis=1)
+            for col in (0, tile)
+        ]
         return jnp.where(core == 0, halves[0], halves[1]), jnp.where(core == 0, halves[1], halves[0])
 
     for k, z_row in enumerate((z, 1 - z)):
-        row = pl.multiple_of((2 * z_row + y) * tile, tile)
-        image = vector[plan[4], pl.ds(row, tile), :].astype(jnp.float32)
-        tiles_ref[k] = packed(image)[0].astype(tiles_ref.dtype)
+        image = []
+        for lower in range(2):
+            piece = 2 * (x ^ lower)
+            image.append(jnp.where(z_row == core, near[piece, 0], far[piece, 0]).astype(jnp.float32))
+        tiles_ref[k] = packed(*image)[0].astype(tiles_ref.dtype)
     for xr in range(2):
         for zr in range(2):
             at = (
                 pl.ds(pl.multiple_of((z ^ zr) * tile, tile), tile),
                 pl.ds(pl.multiple_of((x ^ xr) * width, width), width),
             )
-            mine, other = packed(total[at])
+            block = total[at]
+            mine, other = packed(block[:half], block[half:])
             kept_ref[2 * zr + xr, :half] = mine
             sent_ref[2 * zr + xr, :half] = other
     for to in range(4):
@@ -392,12 +433,22 @@
         compiler_params=params(PEER_MIB),
         cost_estimate=work(PEER_COST * macs),
     )(plan, start_vector, left_own, left_peer, right_own, right_early)
-    kept, sent, rights = pl.pallas_call(
-        first_kernel,
-        out_shape=[shaped(*unit, dtype=f32)] * 2 + [shaped(terms, width, capacity)],
+    late_shape = shaped(terms - early, tile, capacity)
+    sent, right_late = pl.pallas_call(
+        sent_kernel,
+        out_shape=[shaped(*unit, dtype=f32), late_shape],
+        in_specs=[smem()] + [vmem()] * 5,
+        out_specs=[vmem()] * 2,
+        scratch_shapes=[pltpu.VMEM((tile, capacity), f32), pltpu.SemaphoreType.DMA],
+        compiler_params=params(16),
+        cost_estimate=work(macs),
+    )(plan, mixed_own, mixed_peer, total_own, total_peer, right_late)
+    kept, rights = pl.pallas_call(
+        kept_kernel,
+        out_shape=[shaped(*unit, dtype=f32), shaped(terms, width, capacity)],
         in_specs=[smem()] + [vmem()] * 7,
-        out_specs=[vmem()] * 3,
-        scratch_shapes=[pltpu.VMEM((2, tile, capacity), f32), pltpu.SemaphoreType.DMA((3,))],
+        out_specs=[vmem()] * 2,
+        scratch_shapes=[pltpu.VMEM((tile, capacity), f32), pltpu.SemaphoreType.DMA((3,))],
         compiler_params=params(16),
         cost_estimate=work(macs),
     )(plan, mixed_own, mixed_peer, total_own, total_peer, right_own, right_early, right_late)
@@ -420,27 +471,29 @@
     far_units = exchange(units, CORE)
     half = tile // 2
     part = (4, half + EXTRA_ROWS, width)
+    near_shape = (sectors, width, width)
+    partial, sums = pl.pallas_call(
+        lambda *refs: near_kernel(sectors, *refs),
+        out_shape=[shaped(terms, width, width, dtype=f32), shaped(2, 8, 128, dtype=f32)],
+        in_specs=[smem()] + [vmem()] * 3,
+        out_specs=[vmem()] * 2,
+        scratch_shapes=[pltpu.VMEM(near_shape, bf16)],
+        compiler_params=params(20),
+        cost_estimate=work(macs),
+    )(plan, start_vector, units, lefts)
     kept, sent, image_tiles = pl.pallas_call(
         lambda *refs: second_kernel(sectors, *refs),
         out_shape=[shaped(*part, dtype=f32)] * 2 + [shaped(2, half, width)],
-        in_specs=[smem()] + [vmem()] * 6,
+        in_specs=[smem()] + [vmem()] * 7,
         out_specs=[vmem()] * 3,
         scratch_shapes=[
-            pltpu.VMEM(vector_shape, bf16),
+            pltpu.VMEM(near_shape, bf16),
             pltpu.VMEM((width, terms * width), bf16),
             pltpu.VMEM((width, capacity), f32),
         ],
         compiler_params=params(24),
-        cost_estimate=work(4 * macs),
-    )(
-        plan,
-        square,
-        start_vector,
-        units,
-        far_units,
-        lefts,
-        rights,
-    )
+        cost_estimate=work(3 * macs),
+    )(plan, square, sums, partial, units, far_units, lefts, rights)
     got_tile = exchange(image_tiles[1], ZBIT)
     summed = kept + exchange(sent, CORE)
     first, second = pl.pallas_call(

time: 99.3 us -> 98.6 us (level)
  waiting for transfers between devices: 43.3 us -> 39.9 us
  Pallas kernels: 16.2 us -> 18.6 us
    ppermute x20, waiting for transfers between devices: 43.3 us -> 39.9 us  [exchange(): lax.ppermute(block, 'sec', [(i, i ^ flip) for i in range(lax.axis_size('s...]
    pallas_call x1 -> x3, Pallas kernels: 2.67 us -> 5.76 us  [the longest x1 2.35 us: on_device(): pl.pallas_call(sent_kernel, out_shape=[shaped(*unit, dtype=f32), late_sha...]
    unnamed x12 -> x14, local copies, waits for them, and re-layouts: 3.18 us -> 3.17 us
  transfers between devices with their start and end apart: 22 -> 22, of which waited for: 16 -> 16; matrix products, arithmetic and copies ran while one was open for 7% -> 7% of each run, Pallas kernels for 8% -> 11%
where the time goes in v7:
time: 98.6 us; the launch traced here: 98.2 us
  waiting for transfers between devices  39.9 us (40%)
  starting transfers between devices  27.3 us (28%)
  Pallas kernels  18.6 us (19%)
  local copies, waits for them, and re-layouts  9.35 us (9%)
  other arithmetic  2.1 us (2%)
    ppermute x20, waiting for transfers between devices, exchange(): lax.ppermute(block, 'sec', [(i, i ^ flip) for i in range(lax.axis_size('s...  39.9 us
    ppermute x20, starting transfers between devices, exchange(): lax.ppermute(block, 'sec', [(i, i ^ flip) for i in range(lax.axis_size('s...  22.5 us
    pallas_call x1, Pallas kernels, on_device(): pl.pallas_call(lambda *refs: start_kernel(sectors, *refs), out_shape=[sha...  4.82 us
    ppermute x2, starting transfers between devices, spread(): return lax.ppermute(tile, 'sec', route)  4.75 us
    pallas_call x1, Pallas kernels, on_device(): pl.pallas_call(lambda *refs: second_kernel(sectors, *refs), out_shape=[sh...  3.9 us
    unnamed x14, local copies, waits for them, and re-layouts  3.17 us
    pallas_call x1, Pallas kernels, on_device(): pl.pallas_call(lambda *refs: peer_kernel(sectors, *refs), out_shape=[mixe...  2.72 us
    slice x1, local copies, waits for them, and re-layouts, on_device(): right_late = exchange(right_environment[early:], YBIT)  2.62 us
  transfers between devices with their start and end apart: 22, of which 16 were waited for; matrix products, arithmetic and copies ran while one was open for 7% of the time, Pallas kernels for 11%

profile of v7, /device:TPU:0, one launch (start us, length us, event | category | flops | bytes accessed | tf_op | source)
XLA Modules:
  0.0 98.2 jit_solution(6322331610386041145)
XLA Ops:
  2.2 4.1 %collective-permute-start.1 = (bf16[96,384]{1,0:T(8,128)(2,1)S(1)}, bf16[96,384]{1,0:T(8,128)(2,1)S(1)}, u32[]{:S(2)}, u32[]{:S(2)}) collective-permute-start(bf16[96,384]{1,0:T(8,128)(2,1)S(1)} %pad_maximum_fusion.5), channel_id=1, source_target_pairs={{0,16},{1,17},{2,26},{3,27},{4,20},{5,21},{6,30},{7,31},{8,18},{9,... | collective-permute-start | bytes 221192 | tf_op jit(solution)/shard_map/ppermute | solution.py:31
  7.3 1.6 %collective-permute-start.3 = (bf16[1,192,768]{2,1,0:T(8,128)(2,1)S(1)}, bf16[1,192,768]{2,1,0:T(8,128)(2,1)S(1)}, u32[]{:S(2)}, u32[]{:S(2)}) collective-permute-start(bf16[1,192,768]{2,1,0:T(8,128)(2,1)S(1)} %slice.55), channel_id=1, source_target_pairs={{0,4},{1,5},{2,6},{3,7},{4,0},{5,1},{6,2},{7,3},{8,12},{9,13},{10,... | collective-permute-start | bytes 884744 | tf_op jit(solution)/shard_map/ppermute | solution.py:22
  8.9 4.3 %collective-permute-start.6 = (bf16[6,192,768]{2,1,0:T(8,128)(2,1)}, bf16[6,192,768]{2,1,0:T(8,128)(2,1)S(1)}, u32[]{:S(2)}, u32[]{:S(2)}) collective-permute-start(bf16[6,192,768]{2,1,0:T(8,128)(2,1)} %refs_3_.1), channel_id=1, source_target_pairs={{0,8},{1,9},{2,10},{3,11},{4,12},{5,13},{6,14},{7,15},{8,0},{9,1},... | collective-permute-start | bytes 5308424 | tf_op jit(solution)/shard_map/ppermute | solution.py:22
  14.2 2.6 %slice.56 = bf16[5,192,768]{2,1,0:T(8,128)(2,1)} slice(bf16[6,192,768]{2,1,0:T(8,128)(2,1)} %refs_4_.1), slice={[1:6], [0:192], [0:768]} | slice | bytes 2949120 | tf_op jit(solution)/shard_map/slice | solution.py:396
  17.9 2.2 %collective-permute-done.2 = bf16[2,96,384]{2,1,0:T(8,128)(2,1)S(1)} collective-permute-done((bf16[2,96,384]{2,1,0:T(8,128)(2,1)S(1)}, bf16[2,96,384]{2,1,0:T(8,128)(2,1)S(1)}, u32[]{:S(2)}, u32[]{:S(2)}) %collective-permute-start.2) | collective-permute-done | bytes 147488 | tf_op jit(solution)/shard_map/ppermute | solution.py:22
  20.9 1.8 %collective-permute-start.4 = (bf16[2,2,96,384]{3,2,1,0:T(8,128)(2,1)S(1)}, bf16[2,2,96,384]{3,2,1,0:T(8,128)(2,1)S(1)}, u32[]{:S(2)}, u32[]{:S(2)}) collective-permute-start(bf16[2,2,96,384]{3,2,1,0:T(8,128)(2,1)S(1)} %pad_maximum_fusion.2), channel_id=1, source_target_pairs={{0,2},{1,3},{2,0},{3,1},{4,6},{5,7},{6,4},{7,5},{8,10},{9,11},{10,... | collective-permute-start | bytes 884744 | tf_op jit(solution)/shard_map/ppermute | solution.py:22
  22.7 5.5 %collective-permute-done.4 = bf16[2,2,96,384]{3,2,1,0:T(8,128)(2,1)S(1)} collective-permute-done((bf16[2,2,96,384]{3,2,1,0:T(8,128)(2,1)S(1)}, bf16[2,2,96,384]{3,2,1,0:T(8,128)(2,1)S(1)}, u32[]{:S(2)}, u32[]{:S(2)}) %collective-permute-start.4) | collective-permute-done | bytes 294944 | tf_op jit(solution)/shard_map/ppermute | solution.py:22
  32.6 1.5 %copy-done.4 = bf16[6,192,768]{2,1,0:T(8,128)(2,1)S(1)} copy-done((bf16[6,192,768]{2,1,0:T(8,128)(2,1)S(1)}, bf16[6,192,768]{2,1,0:T(8,128)(2,1)}, u32[]{:S(2)}) %copy-start.4) | copy-done | bytes 1769496
  34.0 4.8 %shard_map.86 = (bf16[2,768,384]{2,1,0:T(8,128)(2,1)S(1)}, bf16[2,192,1152]{2,1,0:T(8,128)(2,1)S(1)}, f32[192,768]{1,0:T(8,128)S(1)}, f32[8,128]{1,0:T(8,128)S(1...) custom-call(s32[21]{0:T(128)S(1)} %concatenate.9.refs_0_.plan, ...), custom_call_target="tpu_custom_call" | custom-call | flops 2038431744 | bytes 3538944 | tf_op jit(solution)/shard_map/pallas_call | solution.py:411
  38.9 12.8 %collective-permute-done.6.refs_3_ = bf16[6,192,768]{2,1,0:T(8,128)(2,1)S(1)} collective-permute-done((bf16[6,192,768]{2,1,0:T(8,128)(2,1)}, bf16[6,192,768]{2,1,0:T(8,128)(2,1)S(1)}, u32[]{:S(2)}, u32[]{:S(2)}) %collective-permute-start.6) | collective-permute-done | bytes 1769504 | tf_op jit(solution)/shard_map/ppermute | solution.py:22
  51.7 2.7 %shard_map.87 = (bf16[2,192,1152]{2,1,0:T(8,128)(2,1)S(1)}, f32[192,768]{1,0:T(8,128)S(1)}, bf16[6,384,768]{2,1,0:T(8,128)(2,1)S(1)}) custom-call(s32[21]{0:T(128)S(1)} %concatenate.9.refs_0_.plan, bf16[2,768,384]{2,1,0:T(8,128)(2,1)S(1)} %get-tuple-element.28.refs_1_, bf16[6,192,768]{2,1,0:T(8,128)(2,1)S(1)} %get-tuple-element.30.refs_2_, ...), custom_call_target="tpu_custom_call" | custom-call | flops 679477248 | bytes 3538944 | tf_op jit(solution)/shard_map/pallas_call | solution.py:427
  54.4 2.3 %shard_map.88 = (f32[4,96,384]{2,1,0:T(8,128)S(1)}, bf16[5,192,768]{2,1,0:T(8,128)(2,1)S(1)}) custom-call(s32[21]{0:T(128)S(1)} %concatenate.9.refs_0_.plan, bf16[2,192,1152]{2,1,0:T(8,128)(2,1)S(1)} %get-tuple-element.29.mixed_own, bf16[2,192,1152]{2,1,0:T(8,128)(2,1)S(1)} %get-tuple-element.33.mixed_peer, f32[192,768]{1,0:T(8,128)S(1)} %get-tuple-element.34.before_own, ...), custom_call_target="tpu_custom_call" | custom-call | flops 679477248 | bytes 3538944 | tf_op jit(solution)/shard_map/pallas_call | solution.py:437
  56.9 1.5 %shard_map.89 = (f32[4,96,384]{2,1,0:T(8,128)S(1)}, bf16[6,384,768]{2,1,0:T(8,128)(2,1)S(1)}) custom-call(s32[21]{0:T(128)S(1)} %concatenate.9.refs_0_.plan, bf16[2,192,1152]{2,1,0:T(8,128)(2,1)S(1)} %get-tuple-element.29.mixed_own, bf16[2,192,1152]{2,1,0:T(8,128)(2,1)S(1)} %get-tuple-element.33.mixed_peer, f32[192,768]{1,0:T(8,128)S(1)} %get-tuple-element.34.before_own, ...), custom_call_target="tpu_custom_call" | custom-call | flops 679477248 | bytes 3538944 | tf_op jit(solution)/shard_map/pallas_call | solution.py:446
  59.9 1.8 %collective-permute-start.11 = (bf16[96,384]{1,0:T(8,128)(2,1)S(1)}, bf16[96,384]{1,0:T(8,128)(2,1)S(1)}, u32[]{:S(2)}, u32[]{:S(2)}) collective-permute-start(bf16[96,384]{1,0:T(8,128)(2,1)S(1)} %get-tuple-element.54), channel_id=1, source_target_pairs={{0,10},{1,11},{2,8},{3,9},{4,14},{5,15},{6,12},{7,13},{8,2},{9,3},... | collective-permute-start | bytes 221192 | tf_op jit(solution)/shard_map/ppermute | solution.py:22
  62.5 1.7 %collective-permute-done.9 = bf16[96,384]{1,0:T(8,128)(2,1)S(1)} collective-permute-done((bf16[96,384]{1,0:T(8,128)(2,1)S(1)}, bf16[96,384]{1,0:T(8,128)(2,1)S(1)}, u32[]{:S(2)}, u32[]{:S(2)}) %collective-permute-start.9) | collective-permute-done | bytes 73760 | tf_op jit(solution)/shard_map/ppermute | solution.py:22
  64.2 1.5 %collective-permute-done.11 = bf16[96,384]{1,0:T(8,128)(2,1)S(1)} collective-permute-done((bf16[96,384]{1,0:T(8,128)(2,1)S(1)}, bf16[96,384]{1,0:T(8,128)(2,1)S(1)}, u32[]{:S(2)}, u32[]{:S(2)}) %collective-permute-start.11) | collective-permute-done | bytes 73760 | tf_op jit(solution)/shard_map/ppermute | solution.py:22
  67.4 5.0 %collective-permute-done.12 = bf16[1,96,384]{2,1,0:T(8,128)(2,1)S(1)} collective-permute-done((bf16[1,96,384]{2,1,0:T(8,128)(2,1)S(1)}, bf16[1,96,384]{2,1,0:T(8,128)(2,1)S(1)}, u32[]{:S(2)}, u32[]{:S(2)}) %collective-permute-start.12) | collective-permute-done | bytes 73760 | tf_op jit(solution)/shard_map/ppermute | solution.py:22
  72.9 1.7 %collective-permute-start.13 = (bf16[2,96,384]{2,1,0:T(8,128)(2,1)S(1)}, bf16[2,96,384]{2,1,0:T(8,128)(2,1)S(1)}, u32[]{:S(2)}, u32[]{:S(2)}) collective-permute-start(bf16[2,96,384]{2,1,0:T(8,128)(2,1)S(1)} %get-tuple-element.57), channel_id=1, source_target_pairs={{0,4},{1,5},{2,6},{3,7},{4,0},{5,1},{6,2},{7,3},{8,12},{9,13},{10,... | collective-permute-start | bytes 442376 | tf_op jit(solution)/shard_map/ppermute | solution.py:22
  76.0 2.4 %collective-permute-done.14 = bf16[2,96,384]{2,1,0:T(8,128)(2,1)S(1)} collective-permute-done((bf16[2,96,384]{2,1,0:T(8,128)(2,1)S(1)}, bf16[2,96,384]{2,1,0:T(8,128)(2,1)S(1)}, u32[]{:S(2)}, u32[]{:S(2)}) %collective-permute-start.14) | collective-permute-done | bytes 147488 | tf_op jit(solution)/shard_map/ppermute | solution.py:22
  80.8 1.9 %shard_map.90 = (f32[6,384,384]{2,1,0:T(8,128)S(1)}, f32[2,8,128]{2,1,0:T(8,128)S(1)}) custom-call(s32[21]{0:T(128)S(1)} %concatenate.9.refs_0_.plan, bf16[2,768,384]{2,1,0:T(8,128)(2,1)S(1)} %get-tuple-element.28.refs_1_, bf16[4,2,96,384]{3,2,1,0:T(8,128)(2,1)S(1)} %pad_maximum_fusion.1.refs_2_.refs_4_, ...), custom_call_target="tpu_custom_call" | custom-call | flops 679477248 | bytes 3538944 | tf_op jit(solution)/shard_map/pallas_call | solution.py:475
  82.8 3.9 %shard_map.91 = (f32[4,112,384]{2,1,0:T(8,128)S(1)}, f32[4,112,384]{2,1,0:T(8,128)S(1)}, bf16[2,96,384]{2,1,0:T(8,128)(2,1)S(1)}) custom-call(s32[21]{0:T(128)S(1)} %concatenate.9.refs_0_.plan, f32[8,128]{1,0:T(8,128)S(1)} %get-tuple-element.27.refs_1_, f32[2,8,128]{2,1,0:T(8,128)S(1)} %get-tuple-element.40.refs_2_, ...), custom_call_target="tpu_custom_call" | custom-call | flops 2038431744 | bytes 3538944 | tf_op jit(solution)/shard_map/pallas_call | solution.py:484
  89.9 1.7 %collective-permute-start.19 = (bf16[112,384]{1,0:T(8,128)(2,1)S(1)}, bf16[112,384]{1,0:T(8,128)(2,1)S(1)}, u32[]{:S(2)}, u32[]{:S(2)}) collective-permute-start(bf16[112,384]{1,0:T(8,128)(2,1)S(1)} %get-tuple-element.51), channel_id=1, source_target_pairs={{0,8},{1,9},{2,10},{3,11},{4,12},{5,13},{6,14},{7,15},{8,0},{9,1},... | collective-permute-start | bytes 258056 | tf_op jit(solution)/shard_map/ppermute | solution.py:22
  92.7 2.7 %collective-permute-done.20.from_xz = bf16[112,384]{1,0:T(8,128)(2,1)S(1)} collective-permute-done((bf16[112,384]{1,0:T(8,128)(2,1)S(1)}, bf16[112,384]{1,0:T(8,128)(2,1)S(1)}, u32[]{:S(2)}, u32[]{:S(2)}) %collective-permute-start.20) | collective-permute-done | bytes 86048 | tf_op jit(solution)/shard_map/ppermute | solution.py:22
  96.7 1.4 %shard_map.92 = (bf16[1,192,192]{2,1,0:T(8,128)(2,1)}, bf16[1,192,192]{2,1,0:T(8,128)(2,1)}) custom-call(s32[21]{0:T(128)S(1)} %concatenate.9.refs_0_.plan, f32[112,384]{1,0:T(8,128)S(1)} %slice_bitcast_fusion.own_ref, bf16[112,384]{1,0:T(8,128)(2,1)S(1)} %collective-permute-done.18.from_x, bf16[112,384]{1,0:T(8,128)(2,1)S(1)} %collective-permute-done.19.from_z, ...), custom_call_target="tpu_custom_call" | custom-call | tf_op jit(solution)/shard_map/pallas_call | solution.py:499
  (67 shorter events, 23.8 us)
Async XLA Ops:
  1.6 7.3 %collective-permute-start = (bf16[96,384]{1,0:T(8,128)(2,1)S(1)}, bf16[96,384]{1,0:T(8,128)(2,1)S(1)}, u32[]{:S(2)}, u32[]{:S(2)}) collective-permute-start(bf16[96,384]{1,0:T(8,128)(2,1)S(1)} %pad_maximum_fusion.5), channel_id=1, source_target_pairs={{0,0},{1,1},{2,8},{3,9},{4,4},{5,5},{6,12},{7,13},{8,2},{9,3},{10,... | collective-permute-start | bytes 221192 | tf_op jit(solution)/shard_map/ppermute | solution.py:31
  2.2 10.9 %collective-permute-start.1 = (bf16[96,384]{1,0:T(8,128)(2,1)S(1)}, bf16[96,384]{1,0:T(8,128)(2,1)S(1)}, u32[]{:S(2)}, u32[]{:S(2)}) collective-permute-start(bf16[96,384]{1,0:T(8,128)(2,1)S(1)} %pad_maximum_fusion.5), channel_id=1, source_target_pairs={{0,16},{1,17},{2,26},{3,27},{4,20},{5,21},{6,30},{7,31},{8,18},{9,... | collective-permute-start | bytes 221192 | tf_op jit(solution)/shard_map/ppermute | solution.py:31
  7.3 12.9 %collective-permute-start.3 = (bf16[1,192,768]{2,1,0:T(8,128)(2,1)S(1)}, bf16[1,192,768]{2,1,0:T(8,128)(2,1)S(1)}, u32[]{:S(2)}, u32[]{:S(2)}) collective-permute-start(bf16[1,192,768]{2,1,0:T(8,128)(2,1)S(1)} %slice.55), channel_id=1, source_target_pairs={{0,4},{1,5},{2,6},{3,7},{4,0},{5,1},{6,2},{7,3},{8,12},{9,13},{10,... | collective-permute-start | bytes 884744 | tf_op jit(solution)/shard_map/ppermute | solution.py:22
  8.9 42.8 %collective-permute-start.6 = (bf16[6,192,768]{2,1,0:T(8,128)(2,1)}, bf16[6,192,768]{2,1,0:T(8,128)(2,1)S(1)}, u32[]{:S(2)}, u32[]{:S(2)}) collective-permute-start(bf16[6,192,768]{2,1,0:T(8,128)(2,1)} %refs_3_.1), channel_id=1, source_target_pairs={{0,8},{1,9},{2,10},{3,11},{4,12},{5,13},{6,14},{7,15},{8,0},{9,1},... | collective-permute-start | bytes 5308424 | tf_op jit(solution)/shard_map/ppermute | solution.py:22
  13.2 15.9 %copy-start.6 = (s32[2]{0:T(128)S(1)}, s32[2]{0:T(128)}, u32[]{:S(2)}) copy-start(s32[2]{0:T(128)} %param.11) | copy-start | bytes 28
  13.2 6.9 %collective-permute-start.2 = (bf16[2,96,384]{2,1,0:T(8,128)(2,1)S(1)}, bf16[2,96,384]{2,1,0:T(8,128)(2,1)S(1)}, u32[]{:S(2)}, u32[]{:S(2)}) collective-permute-start(bf16[2,96,384]{2,1,0:T(8,128)(2,1)S(1)} %get-tuple-element.59), channel_id=1, source_target_pairs={{0,4},{1,5},{2,6},{3,7},{4,0},{5,1},{6,2},{7,3},{8,12},{9,13},{10,... | collective-permute-start | bytes 442376 | tf_op jit(solution)/shard_map/ppermute | solution.py:22
  16.8 14.7 %copy-start = (bf16[6,192,768]{2,1,0:T(8,128)(2,1)S(1)}, bf16[6,192,768]{2,1,0:T(8,128)(2,1)}, u32[]{:S(2)}) copy-start(bf16[6,192,768]{2,1,0:T(8,128)(2,1)} %refs_4_.1) | copy-start | bytes 5308420
  16.8 37.6 %collective-permute-start.7 = (bf16[5,192,768]{2,1,0:T(8,128)(2,1)}, bf16[5,192,768]{2,1,0:T(8,128)(2,1)}, u32[]{:S(2)}, u32[]{:S(2)}) collective-permute-start(bf16[5,192,768]{2,1,0:T(8,128)(2,1)} %slice.56), channel_id=1, source_target_pairs={{0,4},{1,5},{2,6},{3,7},{4,0},{5,1},{6,2},{7,3},{8,12},{9,13},{10,... | collective-permute-start | bytes 4423688 | tf_op jit(solution)/shard_map/ppermute | solution.py:22
  20.9 7.3 %collective-permute-start.4 = (bf16[2,2,96,384]{3,2,1,0:T(8,128)(2,1)S(1)}, bf16[2,2,96,384]{3,2,1,0:T(8,128)(2,1)S(1)}, u32[]{:S(2)}, u32[]{:S(2)}) collective-permute-start(bf16[2,2,96,384]{3,2,1,0:T(8,128)(2,1)S(1)} %pad_maximum_fusion.2), channel_id=1, source_target_pairs={{0,2},{1,3},{2,0},{3,1},{4,6},{5,7},{6,4},{7,5},{8,10},{9,11},{10,... | collective-permute-start | bytes 884744 | tf_op jit(solution)/shard_map/ppermute | solution.py:22
  29.1 2.5 %collective-permute-start.5 = (bf16[2,2,2,96,384]{4,3,2,1,0:T(8,128)(2,1)}, bf16[2,2,2,96,384]{4,3,2,1,0:T(8,128)(2,1)}, u32[]{:S(2)}, u32[]{:S(2)}) collective-permute-start(bf16[2,2,2,96,384]{4,3,2,1,0:T(8,128)(2,1)} %pad_maximum_fusion.refs_1_), channel_id=1, source_target_pairs={{0,1},{1,0},{2,3},{3,2},{4,5},{5,4},{6,7},{7,6},{8,9},{9,8},{10,11... | collective-permute-start | bytes 1769480 | tf_op jit(solution)/shard_map/ppermute | solution.py:22
  56.8 2.1 %collective-permute-start.8 = (f32[4,96,384]{2,1,0:T(8,128)S(1)}, f32[4,96,384]{2,1,0:T(8,128)S(1)}, u32[]{:S(2)}, u32[]{:S(2)}) collective-permute-start(f32[4,96,384]{2,1,0:T(8,128)S(1)} %get-tuple-element.38), channel_id=1, source_target_pairs={{0,1},{1,0},{2,3},{3,2},{4,5},{5,4},{6,7},{7,6},{8,9},{9,8},{10,11... | collective-permute-start | bytes 1769480 | tf_op jit(solution)/shard_map/ppermute | solution.py:22
  59.0 5.2 %collective-permute-start.9 = (bf16[96,384]{1,0:T(8,128)(2,1)S(1)}, bf16[96,384]{1,0:T(8,128)(2,1)S(1)}, u32[]{:S(2)}, u32[]{:S(2)}) collective-permute-start(bf16[96,384]{1,0:T(8,128)(2,1)S(1)} %get-tuple-element.53), channel_id=1, source_target_pairs={{0,2},{1,3},{2,0},{3,1},{4,6},{5,7},{6,4},{7,5},{8,10},{9,11},{10,... | collective-permute-start | bytes 221192 | tf_op jit(solution)/shard_map/ppermute | solution.py:22
  59.9 5.8 %collective-permute-start.11 = (bf16[96,384]{1,0:T(8,128)(2,1)S(1)}, bf16[96,384]{1,0:T(8,128)(2,1)S(1)}, u32[]{:S(2)}, u32[]{:S(2)}) collective-permute-start(bf16[96,384]{1,0:T(8,128)(2,1)S(1)} %get-tuple-element.54), channel_id=1, source_target_pairs={{0,10},{1,11},{2,8},{3,9},{4,14},{5,15},{6,12},{7,13},{8,2},{9,3},... | collective-permute-start | bytes 221192 | tf_op jit(solution)/shard_map/ppermute | solution.py:22
  61.7 4.5 %collective-permute-start.10 = (bf16[96,384]{1,0:T(8,128)(2,1)S(1)}, bf16[96,384]{1,0:T(8,128)(2,1)S(1)}, u32[]{:S(2)}, u32[]{:S(2)}) collective-permute-start(bf16[96,384]{1,0:T(8,128)(2,1)S(1)} %get-tuple-element.55), channel_id=1, source_target_pairs={{0,8},{1,9},{2,10},{3,11},{4,12},{5,13},{6,14},{7,15},{8,0},{9,1},... | collective-permute-start | bytes 221192 | tf_op jit(solution)/shard_map/ppermute | solution.py:22
  66.3 6.1 %collective-permute-start.12 = (bf16[1,96,384]{2,1,0:T(8,128)(2,1)S(1)}, bf16[1,96,384]{2,1,0:T(8,128)(2,1)S(1)}, u32[]{:S(2)}, u32[]{:S(2)}) collective-permute-start(bf16[1,96,384]{2,1,0:T(8,128)(2,1)S(1)} %fusion.4), channel_id=1, source_target_pairs={{0,16},{1,17},{2,18},{3,19},{4,20},{5,21},{6,22},{7,23},{8,24},{9,... | collective-permute-start | bytes 221192 | tf_op jit(solution)/shard_map/ppermute | solution.py:22
  72.4 5.9 %collective-permute-start.14 = (bf16[2,96,384]{2,1,0:T(8,128)(2,1)S(1)}, bf16[2,96,384]{2,1,0:T(8,128)(2,1)S(1)}, u32[]{:S(2)}, u32[]{:S(2)}) collective-permute-start(bf16[2,96,384]{2,1,0:T(8,128)(2,1)S(1)} %get-tuple-element.57), channel_id=1, source_target_pairs={{0,2},{1,3},{2,0},{3,1},{4,6},{5,7},{6,4},{7,5},{8,10},{9,11},{10,... | collective-permute-start | bytes 442376 | tf_op jit(solution)/shard_map/ppermute | solution.py:22
  72.9 6.4 %collective-permute-start.13 = (bf16[2,96,384]{2,1,0:T(8,128)(2,1)S(1)}, bf16[2,96,384]{2,1,0:T(8,128)(2,1)S(1)}, u32[]{:S(2)}, u32[]{:S(2)}) collective-permute-start(bf16[2,96,384]{2,1,0:T(8,128)(2,1)S(1)} %get-tuple-element.57), channel_id=1, source_target_pairs={{0,4},{1,5},{2,6},{3,7},{4,0},{5,1},{6,2},{7,3},{8,12},{9,13},{10,... | collective-permute-start | bytes 442376 | tf_op jit(solution)/shard_map/ppermute | solution.py:22
  74.6 6.0 %collective-permute-start.15 = (bf16[2,96,384]{2,1,0:T(8,128)(2,1)S(1)}, bf16[2,96,384]{2,1,0:T(8,128)(2,1)S(1)}, u32[]{:S(2)}, u32[]{:S(2)}) collective-permute-start(bf16[2,96,384]{2,1,0:T(8,128)(2,1)S(1)} %get-tuple-element.57), channel_id=1, source_target_pairs={{0,6},{1,7},{2,4},{3,5},{4,2},{5,3},{6,0},{7,1},{8,14},{9,15},{10,... | collective-permute-start | bytes 442376 | tf_op jit(solution)/shard_map/ppermute | solution.py:22
  80.8 2.1 %collective-permute-start.16 = (bf16[4,2,96,384]{3,2,1,0:T(8,128)(2,1)S(1)}, bf16[4,2,96,384]{3,2,1,0:T(8,128)(2,1)S(1)}, u32[]{:S(2)}, u32[]{:S(2)}) collective-permute-start(bf16[4,2,96,384]{3,2,1,0:T(8,128)(2,1)S(1)} %pad_maximum_fusion.1.refs_2_.refs_4_), channel_id=1, source_target_pairs={{0,1},{1,0},{2,3},{3,2},{4,5},{5,4},{6,7},{7,6},{8,9},{9,8},{10,11... | collective-permute-start | bytes 1769480 | tf_op jit(solution)/shard_map/ppermute | solution.py:22
  86.8 2.2 %collective-permute-start.17 = (f32[4,112,384]{2,1,0:T(8,128)S(1)}, f32[4,112,384]{2,1,0:T(8,128)S(1)}, u32[]{:S(2)}, u32[]{:S(2)}) collective-permute-start(f32[4,112,384]{2,1,0:T(8,128)S(1)} %get-tuple-element.44), channel_id=1, source_target_pairs={{0,1},{1,0},{2,3},{3,2},{4,5},{5,4},{6,7},{7,6},{8,9},{9,8},{10,11... | collective-permute-start | bytes 2064392 | tf_op jit(solution)/shard_map/ppermute | solution.py:22
  87.2 5.5 %collective-permute-start.21 = (bf16[96,384]{1,0:T(8,128)(2,1)S(1)}, bf16[96,384]{1,0:T(8,128)(2,1)S(1)}, u32[]{:S(2)}, u32[]{:S(2)}) collective-permute-start(bf16[96,384]{1,0:T(8,128)(2,1)S(1)} %slice_bitcast_fusion.8), channel_id=1, source_target_pairs={{0,8},{1,9},{2,10},{3,11},{4,12},{5,13},{6,14},{7,15},{8,0},{9,1},... | collective-permute-start | bytes 221192 | tf_op jit(solution)/shard_map/ppermute | solution.py:22
  89.1 6.3 %collective-permute-start.20 = (bf16[112,384]{1,0:T(8,128)(2,1)S(1)}, bf16[112,384]{1,0:T(8,128)(2,1)S(1)}, u32[]{:S(2)}, u32[]{:S(2)}) collective-permute-start(bf16[112,384]{1,0:T(8,128)(2,1)S(1)} %get-tuple-element.50), channel_id=1, source_target_pairs={{0,10},{1,11},{2,8},{3,9},{4,14},{5,15},{6,12},{7,13},{8,2},{9,3},... | collective-permute-start | bytes 258056 | tf_op jit(solution)/shard_map/ppermute | solution.py:22
  89.9 6.3 %collective-permute-start.19 = (bf16[112,384]{1,0:T(8,128)(2,1)S(1)}, bf16[112,384]{1,0:T(8,128)(2,1)S(1)}, u32[]{:S(2)}, u32[]{:S(2)}) collective-permute-start(bf16[112,384]{1,0:T(8,128)(2,1)S(1)} %get-tuple-element.51), channel_id=1, source_target_pairs={{0,8},{1,9},{2,10},{3,11},{4,12},{5,13},{6,14},{7,15},{8,0},{9,1},... | collective-permute-start | bytes 258056 | tf_op jit(solution)/shard_map/ppermute | solution.py:22
  91.6 5.2 %collective-permute-start.18 = (bf16[112,384]{1,0:T(8,128)(2,1)S(1)}, bf16[112,384]{1,0:T(8,128)(2,1)S(1)}, u32[]{:S(2)}, u32[]{:S(2)}) collective-permute-start(bf16[112,384]{1,0:T(8,128)(2,1)S(1)} %get-tuple-element.52), channel_id=1, source_target_pairs={{0,2},{1,3},{2,0},{3,1},{4,6},{5,7},{6,4},{7,5},{8,10},{9,11},{10,... | collective-permute-start | bytes 258056 | tf_op jit(solution)/shard_map/ppermute | solution.py:22
  (5 other events, 15.1 us)

commit v8 on v7

--- a/solution.py
+++ b/solution.py
@@ -460,14 +460,19 @@
         + exchange(summed[2].astype(bf16), ZBIT).astype(f32)
         + exchange(summed[3].astype(bf16), XBIT | ZBIT).astype(f32)
     )
-    units = image_unit.astype(bf16)[None]
+    own_unit = image_unit.astype(bf16)[None]
+    gathered = own_unit
     flip = SECTOR_BIT
     while flip < lax.axis_size("sec"):
-        units = jnp.concatenate([units, exchange(units, flip)])
+        gathered = jnp.concatenate([gathered, exchange(gathered, flip)])
         flip *= 2
-    units = jnp.stack(
-        [units, exchange(units, YBIT), exchange(units, XBIT), exchange(units, XBIT | YBIT)]
-    )
+    units = [gathered]
+    for way in (YBIT, XBIT, XBIT | YBIT):
+        parts = [exchange(own_unit, way)]
+        if sectors > 1:
+            parts.append(exchange(gathered[1:], way))
+        units.append(jnp.concatenate(parts))
+    units = jnp.stack(units)
     far_units = exchange(units, CORE)
     half = tile // 2
     part = (4, half + EXTRA_ROWS, width)

time: 98.6 us -> 97.2 us (0.986)
  waiting for transfers between devices: 39.9 us -> 34.9 us
  starting transfers between devices: 27.3 us -> 30.8 us
    ppermute x20 -> x23, waiting for transfers between devices: 39.9 us -> 34.9 us  [exchange(): lax.ppermute(block, 'sec', [(i, i ^ flip) for i in range(lax.axis_size('s...]
    ppermute x20 -> x23, starting transfers between devices: 22.5 us -> 26 us  [exchange(): lax.ppermute(block, 'sec', [(i, i ^ flip) for i in range(lax.axis_size('s...]
  transfers between devices with their start and end apart: 22 -> 25, of which waited for: 16 -> 16; matrix products, arithmetic and copies ran while one was open for 7% -> 7% of each run, Pallas kernels for 11% -> 11%
where the time goes in v8:
time: 97.2 us; the launch traced here: 96.8 us
  waiting for transfers between devices  34.9 us (36%)
  starting transfers between devices  30.8 us (32%)
  Pallas kernels  18.6 us (19%)
  local copies, waits for them, and re-layouts  9.36 us (10%)
  other arithmetic  2.15 us (2%)
  between operations  1 us (1%)
    ppermute x23, waiting for transfers between devices, exchange(): lax.ppermute(block, 'sec', [(i, i ^ flip) for i in range(lax.axis_size('s...  34.9 us
    ppermute x23, starting transfers between devices, exchange(): lax.ppermute(block, 'sec', [(i, i ^ flip) for i in range(lax.axis_size('s...  26 us
    pallas_call x1, Pallas kernels, on_device(): pl.pallas_call(lambda *refs: start_kernel(sectors, *refs), out_shape=[sha...  4.81 us
    ppermute x2, starting transfers between devices, spread(): return lax.ppermute(tile, 'sec', route)  4.75 us
    pallas_call x1, Pallas kernels, on_device(): pl.pallas_call(lambda *refs: second_kernel(sectors, *refs), out_shape=[sh...  3.91 us
    unnamed x14, local copies, waits for them, and re-layouts  3.17 us
    pallas_call x1, Pallas kernels, on_device(): pl.pallas_call(lambda *refs: peer_kernel(sectors, *refs), out_shape=[mixe...  2.72 us
    slice x1, local copies, waits for them, and re-layouts, on_device(): right_late = exchange(right_environment[early:], YBIT)  2.63 us
  transfers between devices with their start and end apart: 25, of which 16 were waited for; matrix products, arithmetic and copies ran while one was open for 7% of the time, Pallas kernels for 11%

profile of v8, /device:TPU:0, one launch (start us, length us, event | category | flops | bytes accessed | tf_op | source)
XLA Modules:
  0.0 96.8 jit_solution(11108562110586924301)
XLA Ops:
  2.2 4.1 %collective-permute-start.1 = (bf16[96,384]{1,0:T(8,128)(2,1)S(1)}, bf16[96,384]{1,0:T(8,128)(2,1)S(1)}, u32[]{:S(2)}, u32[]{:S(2)}) collective-permute-start(bf16[96,384]{1,0:T(8,128)(2,1)S(1)} %pad_maximum_fusion.4), channel_id=1, source_target_pairs={{0,16},{1,17},{2,26},{3,27},{4,20},{5,21},{6,30},{7,31},{8,18},{9,... | collective-permute-start | bytes 221192 | tf_op jit(solution)/shard_map/ppermute | solution.py:31
  7.3 1.6 %collective-permute-start.3 = (bf16[1,192,768]{2,1,0:T(8,128)(2,1)S(1)}, bf16[1,192,768]{2,1,0:T(8,128)(2,1)S(1)}, u32[]{:S(2)}, u32[]{:S(2)}) collective-permute-start(bf16[1,192,768]{2,1,0:T(8,128)(2,1)S(1)} %slice.55), channel_id=1, source_target_pairs={{0,4},{1,5},{2,6},{3,7},{4,0},{5,1},{6,2},{7,3},{8,12},{9,13},{10,... | collective-permute-start | bytes 884744 | tf_op jit(solution)/shard_map/ppermute | solution.py:22
  8.9 4.3 %collective-permute-start.6 = (bf16[6,192,768]{2,1,0:T(8,128)(2,1)}, bf16[6,192,768]{2,1,0:T(8,128)(2,1)S(1)}, u32[]{:S(2)}, u32[]{:S(2)}) collective-permute-start(bf16[6,192,768]{2,1,0:T(8,128)(2,1)} %refs_3_.1), channel_id=1, source_target_pairs={{0,8},{1,9},{2,10},{3,11},{4,12},{5,13},{6,14},{7,15},{8,0},{9,1},... | collective-permute-start | bytes 5308424 | tf_op jit(solution)/shard_map/ppermute | solution.py:22
  14.2 2.6 %slice.56 = bf16[5,192,768]{2,1,0:T(8,128)(2,1)} slice(bf16[6,192,768]{2,1,0:T(8,128)(2,1)} %refs_4_.1), slice={[1:6], [0:192], [0:768]} | slice | bytes 2949120 | tf_op jit(solution)/shard_map/slice | solution.py:396
  17.9 2.2 %collective-permute-done.2 = bf16[2,96,384]{2,1,0:T(8,128)(2,1)S(1)} collective-permute-done((bf16[2,96,384]{2,1,0:T(8,128)(2,1)S(1)}, bf16[2,96,384]{2,1,0:T(8,128)(2,1)S(1)}, u32[]{:S(2)}, u32[]{:S(2)}) %collective-permute-start.2) | collective-permute-done | bytes 147488 | tf_op jit(solution)/shard_map/ppermute | solution.py:22
  20.9 1.7 %collective-permute-start.4 = (bf16[2,2,96,384]{3,2,1,0:T(8,128)(2,1)S(1)}, bf16[2,2,96,384]{3,2,1,0:T(8,128)(2,1)S(1)}, u32[]{:S(2)}, u32[]{:S(2)}) collective-permute-start(bf16[2,2,96,384]{3,2,1,0:T(8,128)(2,1)S(1)} %pad_maximum_fusion.2), channel_id=1, source_target_pairs={{0,2},{1,3},{2,0},{3,1},{4,6},{5,7},{6,4},{7,5},{8,10},{9,11},{10,... | collective-permute-start | bytes 884744 | tf_op jit(solution)/shard_map/ppermute | solution.py:22
  22.7 5.6 %collective-permute-done.4 = bf16[2,2,96,384]{3,2,1,0:T(8,128)(2,1)S(1)} collective-permute-done((bf16[2,2,96,384]{3,2,1,0:T(8,128)(2,1)S(1)}, bf16[2,2,96,384]{3,2,1,0:T(8,128)(2,1)S(1)}, u32[]{:S(2)}, u32[]{:S(2)}) %collective-permute-start.4) | collective-permute-done | bytes 294944 | tf_op jit(solution)/shard_map/ppermute | solution.py:22
  32.6 1.5 %copy-done.4 = bf16[6,192,768]{2,1,0:T(8,128)(2,1)S(1)} copy-done((bf16[6,192,768]{2,1,0:T(8,128)(2,1)S(1)}, bf16[6,192,768]{2,1,0:T(8,128)(2,1)}, u32[]{:S(2)}) %copy-start.4) | copy-done | bytes 1769496
  34.0 4.8 %shard_map.86 = (bf16[2,768,384]{2,1,0:T(8,128)(2,1)S(1)}, bf16[2,192,1152]{2,1,0:T(8,128)(2,1)S(1)}, f32[192,768]{1,0:T(8,128)S(1)}, f32[8,128]{1,0:T(8,128)S(1...) custom-call(s32[21]{0:T(128)S(1)} %concatenate.18.refs_0_.plan, ...), custom_call_target="tpu_custom_call" | custom-call | flops 2038431744 | bytes 3538944 | tf_op jit(solution)/shard_map/pallas_call | solution.py:411
  38.8 12.8 %collective-permute-done.6.refs_3_ = bf16[6,192,768]{2,1,0:T(8,128)(2,1)S(1)} collective-permute-done((bf16[6,192,768]{2,1,0:T(8,128)(2,1)}, bf16[6,192,768]{2,1,0:T(8,128)(2,1)S(1)}, u32[]{:S(2)}, u32[]{:S(2)}) %collective-permute-start.6) | collective-permute-done | bytes 1769504 | tf_op jit(solution)/shard_map/ppermute | solution.py:22
  51.7 2.7 %shard_map.87 = (bf16[2,192,1152]{2,1,0:T(8,128)(2,1)S(1)}, f32[192,768]{1,0:T(8,128)S(1)}, bf16[6,384,768]{2,1,0:T(8,128)(2,1)S(1)}) custom-call(s32[21]{0:T(128)S(1)} %concatenate.18.refs_0_.plan, bf16[2,768,384]{2,1,0:T(8,128)(2,1)S(1)} %get-tuple-element.28.refs_1_, bf16[6,192,768]{2,1,0:T(8,128)(2,1)S(1)} %get-tuple-element.30.refs_2_, ...), custom_call_target="tpu_custom_call" | custom-call | flops 679477248 | bytes 3538944 | tf_op jit(solution)/shard_map/pallas_call | solution.py:427
  54.4 2.3 %shard_map.88 = (f32[4,96,384]{2,1,0:T(8,128)S(1)}, bf16[5,192,768]{2,1,0:T(8,128)(2,1)S(1)}) custom-call(s32[21]{0:T(128)S(1)} %concatenate.18.refs_0_.plan, bf16[2,192,1152]{2,1,0:T(8,128)(2,1)S(1)} %get-tuple-element.29.mixed_own, bf16[2,192,1152]{2,1,0:T(8,128)(2,1)S(1)} %get-tuple-element.33.mixed_peer, f32[192,768]{1,0:T(8,128)S(1)} %get-tuple-element.34.before_own, ...), custom_call_target="tpu_custom_call" | custom-call | flops 679477248 | bytes 3538944 | tf_op jit(solution)/shard_map/pallas_call | solution.py:437
  56.9 1.5 %shard_map.89 = (f32[4,96,384]{2,1,0:T(8,128)S(1)}, bf16[6,384,768]{2,1,0:T(8,128)(2,1)S(1)}) custom-call(s32[21]{0:T(128)S(1)} %concatenate.18.refs_0_.plan, bf16[2,192,1152]{2,1,0:T(8,128)(2,1)S(1)} %get-tuple-element.29.mixed_own, bf16[2,192,1152]{2,1,0:T(8,128)(2,1)S(1)} %get-tuple-element.33.mixed_peer, f32[192,768]{1,0:T(8,128)S(1)} %get-tuple-element.34.before_own, ...), custom_call_target="tpu_custom_call" | custom-call | flops 679477248 | bytes 3538944 | tf_op jit(solution)/shard_map/pallas_call | solution.py:446
  59.9 1.8 %collective-permute-start.11 = (bf16[96,384]{1,0:T(8,128)(2,1)S(1)}, bf16[96,384]{1,0:T(8,128)(2,1)S(1)}, u32[]{:S(2)}, u32[]{:S(2)}) collective-permute-start(bf16[96,384]{1,0:T(8,128)(2,1)S(1)} %get-tuple-element.54), channel_id=1, source_target_pairs={{0,10},{1,11},{2,8},{3,9},{4,14},{5,15},{6,12},{7,13},{8,2},{9,3},... | collective-permute-start | bytes 221192 | tf_op jit(solution)/shard_map/ppermute | solution.py:22
  62.5 1.7 %collective-permute-done.9 = bf16[96,384]{1,0:T(8,128)(2,1)S(1)} collective-permute-done((bf16[96,384]{1,0:T(8,128)(2,1)S(1)}, bf16[96,384]{1,0:T(8,128)(2,1)S(1)}, u32[]{:S(2)}, u32[]{:S(2)}) %collective-permute-start.9) | collective-permute-done | bytes 73760 | tf_op jit(solution)/shard_map/ppermute | solution.py:22
  64.2 1.5 %collective-permute-done.11 = bf16[96,384]{1,0:T(8,128)(2,1)S(1)} collective-permute-done((bf16[96,384]{1,0:T(8,128)(2,1)S(1)}, bf16[96,384]{1,0:T(8,128)(2,1)S(1)}, u32[]{:S(2)}, u32[]{:S(2)}) %collective-permute-start.11) | collective-permute-done | bytes 73760 | tf_op jit(solution)/shard_map/ppermute | solution.py:22
  67.4 2.4 %collective-permute-start.17 = (bf16[1,96,384]{2,1,0:T(8,128)(2,1)S(1)}, bf16[1,96,384]{2,1,0:T(8,128)(2,1)S(1)}, u32[]{:S(2)}, u32[]{:S(2)}) collective-permute-start(bf16[1,96,384]{2,1,0:T(8,128)(2,1)S(1)} %fusion.4), channel_id=1, source_target_pairs={{0,6},{1,7},{2,4},{3,5},{4,2},{5,3},{6,0},{7,1},{8,14},{9,15},{10,... | collective-permute-start | bytes 221192 | tf_op jit(solution)/shard_map/ppermute | solution.py:22
  70.9 1.5 %collective-permute-done.12 = bf16[1,96,384]{2,1,0:T(8,128)(2,1)S(1)} collective-permute-done((bf16[1,96,384]{2,1,0:T(8,128)(2,1)S(1)}, bf16[1,96,384]{2,1,0:T(8,128)(2,1)S(1)}, u32[]{:S(2)}, u32[]{:S(2)}) %collective-permute-start.12) | collective-permute-done | bytes 73760 | tf_op jit(solution)/shard_map/ppermute | solution.py:22
  72.4 1.6 %collective-permute-start.18 = (bf16[1,96,384]{2,1,0:T(8,128)(2,1)S(1)}, bf16[1,96,384]{2,1,0:T(8,128)(2,1)S(1)}, u32[]{:S(2)}, u32[]{:S(2)}) collective-permute-start(bf16[1,96,384]{2,1,0:T(8,128)(2,1)S(1)} %collective-permute-done.12), channel_id=1, source_target_pairs={{0,6},{1,7},{2,4},{3,5},{4,2},{5,3},{6,0},{7,1},{8,14},{9,15},{10,... | collective-permute-start | bytes 221192 | tf_op jit(solution)/shard_map/ppermute | solution.py:22
  76.0 1.7 %collective-permute-done.18 = bf16[1,96,384]{2,1,0:T(8,128)(2,1)S(1)} collective-permute-done((bf16[1,96,384]{2,1,0:T(8,128)(2,1)S(1)}, bf16[1,96,384]{2,1,0:T(8,128)(2,1)S(1)}, u32[]{:S(2)}, u32[]{:S(2)}) %collective-permute-start.18) | collective-permute-done | bytes 73760 | tf_op jit(solution)/shard_map/ppermute | solution.py:22
  79.5 1.9 %shard_map.90 = (f32[6,384,384]{2,1,0:T(8,128)S(1)}, f32[2,8,128]{2,1,0:T(8,128)S(1)}) custom-call(s32[21]{0:T(128)S(1)} %concatenate.18.refs_0_.plan, bf16[2,768,384]{2,1,0:T(8,128)(2,1)S(1)} %get-tuple-element.28.refs_1_, bf16[4,2,96,384]{3,2,1,0:T(8,128)(2,1)S(1)} %pad_maximum_fusion.1.refs_2_.refs_4_, ...), custom_call_target="tpu_custom_call" | custom-call | flops 679477248 | bytes 3538944 | tf_op jit(solution)/shard_map/pallas_call | solution.py:480
  81.5 3.9 %shard_map.91 = (f32[4,112,384]{2,1,0:T(8,128)S(1)}, f32[4,112,384]{2,1,0:T(8,128)S(1)}, bf16[2,96,384]{2,1,0:T(8,128)(2,1)S(1)}) custom-call(s32[21]{0:T(128)S(1)} %concatenate.18.refs_0_.plan, f32[8,128]{1,0:T(8,128)S(1)} %get-tuple-element.27.refs_1_, f32[2,8,128]{2,1,0:T(8,128)S(1)} %get-tuple-element.40.refs_2_, ...), custom_call_target="tpu_custom_call" | custom-call | flops 2038431744 | bytes 3538944 | tf_op jit(solution)/shard_map/pallas_call | solution.py:489
  91.4 2.7 %collective-permute-done.23.from_xz = bf16[112,384]{1,0:T(8,128)(2,1)S(1)} collective-permute-done((bf16[112,384]{1,0:T(8,128)(2,1)S(1)}, bf16[112,384]{1,0:T(8,128)(2,1)S(1)}, u32[]{:S(2)}, u32[]{:S(2)}) %collective-permute-start.23) | collective-permute-done | bytes 86048 | tf_op jit(solution)/shard_map/ppermute | solution.py:22
  95.4 1.4 %shard_map.92 = (bf16[1,192,192]{2,1,0:T(8,128)(2,1)}, bf16[1,192,192]{2,1,0:T(8,128)(2,1)}) custom-call(s32[21]{0:T(128)S(1)} %concatenate.18.refs_0_.plan, f32[112,384]{1,0:T(8,128)S(1)} %slice_bitcast_fusion.own_ref, bf16[112,384]{1,0:T(8,128)(2,1)S(1)} %collective-permute-done.21.from_x, bf16[112,384]{1,0:T(8,128)(2,1)S(1)} %collective-permute-done.22.from_z, ...), custom_call_target="tpu_custom_call" | custom-call | tf_op jit(solution)/shard_map/pallas_call | solution.py:504
  (76 shorter events, 26.0 us)
Async XLA Ops:
  1.6 7.3 %collective-permute-start = (bf16[96,384]{1,0:T(8,128)(2,1)S(1)}, bf16[96,384]{1,0:T(8,128)(2,1)S(1)}, u32[]{:S(2)}, u32[]{:S(2)}) collective-permute-start(bf16[96,384]{1,0:T(8,128)(2,1)S(1)} %pad_maximum_fusion.4), channel_id=1, source_target_pairs={{0,0},{1,1},{2,8},{3,9},{4,4},{5,5},{6,12},{7,13},{8,2},{9,3},{10,... | collective-permute-start | bytes 221192 | tf_op jit(solution)/shard_map/ppermute | solution.py:31
  2.2 10.9 %collective-permute-start.1 = (bf16[96,384]{1,0:T(8,128)(2,1)S(1)}, bf16[96,384]{1,0:T(8,128)(2,1)S(1)}, u32[]{:S(2)}, u32[]{:S(2)}) collective-permute-start(bf16[96,384]{1,0:T(8,128)(2,1)S(1)} %pad_maximum_fusion.4), channel_id=1, source_target_pairs={{0,16},{1,17},{2,26},{3,27},{4,20},{5,21},{6,30},{7,31},{8,18},{9,... | collective-permute-start | bytes 221192 | tf_op jit(solution)/shard_map/ppermute | solution.py:31
  7.3 12.9 %collective-permute-start.3 = (bf16[1,192,768]{2,1,0:T(8,128)(2,1)S(1)}, bf16[1,192,768]{2,1,0:T(8,128)(2,1)S(1)}, u32[]{:S(2)}, u32[]{:S(2)}) collective-permute-start(bf16[1,192,768]{2,1,0:T(8,128)(2,1)S(1)} %slice.55), channel_id=1, source_target_pairs={{0,4},{1,5},{2,6},{3,7},{4,0},{5,1},{6,2},{7,3},{8,12},{9,13},{10,... | collective-permute-start | bytes 884744 | tf_op jit(solution)/shard_map/ppermute | solution.py:22
  8.9 42.8 %collective-permute-start.6 = (bf16[6,192,768]{2,1,0:T(8,128)(2,1)}, bf16[6,192,768]{2,1,0:T(8,128)(2,1)S(1)}, u32[]{:S(2)}, u32[]{:S(2)}) collective-permute-start(bf16[6,192,768]{2,1,0:T(8,128)(2,1)} %refs_3_.1), channel_id=1, source_target_pairs={{0,8},{1,9},{2,10},{3,11},{4,12},{5,13},{6,14},{7,15},{8,0},{9,1},... | collective-permute-start | bytes 5308424 | tf_op jit(solution)/shard_map/ppermute | solution.py:22
  13.2 6.9 %collective-permute-start.2 = (bf16[2,96,384]{2,1,0:T(8,128)(2,1)S(1)}, bf16[2,96,384]{2,1,0:T(8,128)(2,1)S(1)}, u32[]{:S(2)}, u32[]{:S(2)}) collective-permute-start(bf16[2,96,384]{2,1,0:T(8,128)(2,1)S(1)} %get-tuple-element.57), channel_id=1, source_target_pairs={{0,4},{1,5},{2,6},{3,7},{4,0},{5,1},{6,2},{7,3},{8,12},{9,13},{10,... | collective-permute-start | bytes 442376 | tf_op jit(solution)/shard_map/ppermute | solution.py:22
  16.9 37.6 %collective-permute-start.7 = (bf16[5,192,768]{2,1,0:T(8,128)(2,1)}, bf16[5,192,768]{2,1,0:T(8,128)(2,1)}, u32[]{:S(2)}, u32[]{:S(2)}) collective-permute-start(bf16[5,192,768]{2,1,0:T(8,128)(2,1)} %slice.56), channel_id=1, source_target_pairs={{0,4},{1,5},{2,6},{3,7},{4,0},{5,1},{6,2},{7,3},{8,12},{9,13},{10,... | collective-permute-start | bytes 4423688 | tf_op jit(solution)/shard_map/ppermute | solution.py:22
  20.9 7.3 %collective-permute-start.4 = (bf16[2,2,96,384]{3,2,1,0:T(8,128)(2,1)S(1)}, bf16[2,2,96,384]{3,2,1,0:T(8,128)(2,1)S(1)}, u32[]{:S(2)}, u32[]{:S(2)}) collective-permute-start(bf16[2,2,96,384]{3,2,1,0:T(8,128)(2,1)S(1)} %pad_maximum_fusion.2), channel_id=1, source_target_pairs={{0,2},{1,3},{2,0},{3,1},{4,6},{5,7},{6,4},{7,5},{8,10},{9,11},{10,... | collective-permute-start | bytes 884744 | tf_op jit(solution)/shard_map/ppermute | solution.py:22
  29.1 2.5 %collective-permute-start.5 = (bf16[2,2,2,96,384]{4,3,2,1,0:T(8,128)(2,1)}, bf16[2,2,2,96,384]{4,3,2,1,0:T(8,128)(2,1)}, u32[]{:S(2)}, u32[]{:S(2)}) collective-permute-start(bf16[2,2,2,96,384]{4,3,2,1,0:T(8,128)(2,1)} %pad_maximum_fusion.refs_1_), channel_id=1, source_target_pairs={{0,1},{1,0},{2,3},{3,2},{4,5},{5,4},{6,7},{7,6},{8,9},{9,8},{10,11... | collective-permute-start | bytes 1769480 | tf_op jit(solution)/shard_map/ppermute | solution.py:22
  56.8 2.1 %collective-permute-start.8 = (f32[4,96,384]{2,1,0:T(8,128)S(1)}, f32[4,96,384]{2,1,0:T(8,128)S(1)}, u32[]{:S(2)}, u32[]{:S(2)}) collective-permute-start(f32[4,96,384]{2,1,0:T(8,128)S(1)} %get-tuple-element.38), channel_id=1, source_target_pairs={{0,1},{1,0},{2,3},{3,2},{4,5},{5,4},{6,7},{7,6},{8,9},{9,8},{10,11... | collective-permute-start | bytes 1769480 | tf_op jit(solution)/shard_map/ppermute | solution.py:22
  59.0 5.2 %collective-permute-start.9 = (bf16[96,384]{1,0:T(8,128)(2,1)S(1)}, bf16[96,384]{1,0:T(8,128)(2,1)S(1)}, u32[]{:S(2)}, u32[]{:S(2)}) collective-permute-start(bf16[96,384]{1,0:T(8,128)(2,1)S(1)} %get-tuple-element.53), channel_id=1, source_target_pairs={{0,2},{1,3},{2,0},{3,1},{4,6},{5,7},{6,4},{7,5},{8,10},{9,11},{10,... | collective-permute-start | bytes 221192 | tf_op jit(solution)/shard_map/ppermute | solution.py:22
  59.9 5.8 %collective-permute-start.11 = (bf16[96,384]{1,0:T(8,128)(2,1)S(1)}, bf16[96,384]{1,0:T(8,128)(2,1)S(1)}, u32[]{:S(2)}, u32[]{:S(2)}) collective-permute-start(bf16[96,384]{1,0:T(8,128)(2,1)S(1)} %get-tuple-element.54), channel_id=1, source_target_pairs={{0,10},{1,11},{2,8},{3,9},{4,14},{5,15},{6,12},{7,13},{8,2},{9,3},... | collective-permute-start | bytes 221192 | tf_op jit(solution)/shard_map/ppermute | solution.py:22
  61.7 4.5 %collective-permute-start.10 = (bf16[96,384]{1,0:T(8,128)(2,1)S(1)}, bf16[96,384]{1,0:T(8,128)(2,1)S(1)}, u32[]{:S(2)}, u32[]{:S(2)}) collective-permute-start(bf16[96,384]{1,0:T(8,128)(2,1)S(1)} %get-tuple-element.55), channel_id=1, source_target_pairs={{0,8},{1,9},{2,10},{3,11},{4,12},{5,13},{6,14},{7,15},{8,0},{9,1},... | collective-permute-start | bytes 221192 | tf_op jit(solution)/shard_map/ppermute | solution.py:22
  66.3 6.1 %collective-permute-start.12 = (bf16[1,96,384]{2,1,0:T(8,128)(2,1)S(1)}, bf16[1,96,384]{2,1,0:T(8,128)(2,1)S(1)}, u32[]{:S(2)}, u32[]{:S(2)}) collective-permute-start(bf16[1,96,384]{2,1,0:T(8,128)(2,1)S(1)} %fusion.4), channel_id=1, source_target_pairs={{0,16},{1,17},{2,18},{3,19},{4,20},{5,21},{6,22},{7,23},{8,24},{9,... | collective-permute-start | bytes 221192 | tf_op jit(solution)/shard_map/ppermute | solution.py:22
  67.4 7.5 %collective-permute-start.17 = (bf16[1,96,384]{2,1,0:T(8,128)(2,1)S(1)}, bf16[1,96,384]{2,1,0:T(8,128)(2,1)S(1)}, u32[]{:S(2)}, u32[]{:S(2)}) collective-permute-start(bf16[1,96,384]{2,1,0:T(8,128)(2,1)S(1)} %fusion.4), channel_id=1, source_target_pairs={{0,6},{1,7},{2,4},{3,5},{4,2},{5,3},{6,0},{7,1},{8,14},{9,15},{10,... | collective-permute-start | bytes 221192 | tf_op jit(solution)/shard_map/ppermute | solution.py:22
  69.8 7.8 %collective-permute-start.15 = (bf16[1,96,384]{2,1,0:T(8,128)(2,1)S(1)}, bf16[1,96,384]{2,1,0:T(8,128)(2,1)S(1)}, u32[]{:S(2)}, u32[]{:S(2)}) collective-permute-start(bf16[1,96,384]{2,1,0:T(8,128)(2,1)S(1)} %fusion.4), channel_id=1, source_target_pairs={{0,2},{1,3},{2,0},{3,1},{4,6},{5,7},{6,4},{7,5},{8,10},{9,11},{10,... | collective-permute-start | bytes 221192 | tf_op jit(solution)/shard_map/ppermute | solution.py:22
  70.4 8.0 %collective-permute-start.13 = (bf16[1,96,384]{2,1,0:T(8,128)(2,1)S(1)}, bf16[1,96,384]{2,1,0:T(8,128)(2,1)S(1)}, u32[]{:S(2)}, u32[]{:S(2)}) collective-permute-start(bf16[1,96,384]{2,1,0:T(8,128)(2,1)S(1)} %fusion.4), channel_id=1, source_target_pairs={{0,4},{1,5},{2,6},{3,7},{4,0},{5,1},{6,2},{7,3},{8,12},{9,13},{10,... | collective-permute-start | bytes 221192 | tf_op jit(solution)/shard_map/ppermute | solution.py:22
  72.4 5.3 %collective-permute-start.18 = (bf16[1,96,384]{2,1,0:T(8,128)(2,1)S(1)}, bf16[1,96,384]{2,1,0:T(8,128)(2,1)S(1)}, u32[]{:S(2)}, u32[]{:S(2)}) collective-permute-start(bf16[1,96,384]{2,1,0:T(8,128)(2,1)S(1)} %collective-permute-done.12), channel_id=1, source_target_pairs={{0,6},{1,7},{2,4},{3,5},{4,2},{5,3},{6,0},{7,1},{8,14},{9,15},{10,... | collective-permute-start | bytes 221192 | tf_op jit(solution)/shard_map/ppermute | solution.py:22
  74.0 4.4 %collective-permute-start.16 = (bf16[1,96,384]{2,1,0:T(8,128)(2,1)S(1)}, bf16[1,96,384]{2,1,0:T(8,128)(2,1)S(1)}, u32[]{:S(2)}, u32[]{:S(2)}) collective-permute-start(bf16[1,96,384]{2,1,0:T(8,128)(2,1)S(1)} %collective-permute-done.12), channel_id=1, source_target_pairs={{0,2},{1,3},{2,0},{3,1},{4,6},{5,7},{6,4},{7,5},{8,10},{9,11},{10,... | collective-permute-start | bytes 221192 | tf_op jit(solution)/shard_map/ppermute | solution.py:22
  74.9 4.4 %collective-permute-start.14 = (bf16[1,96,384]{2,1,0:T(8,128)(2,1)S(1)}, bf16[1,96,384]{2,1,0:T(8,128)(2,1)S(1)}, u32[]{:S(2)}, u32[]{:S(2)}) collective-permute-start(bf16[1,96,384]{2,1,0:T(8,128)(2,1)S(1)} %collective-permute-done.12), channel_id=1, source_target_pairs={{0,4},{1,5},{2,6},{3,7},{4,0},{5,1},{6,2},{7,3},{8,12},{9,13},{10,... | collective-permute-start | bytes 221192 | tf_op jit(solution)/shard_map/ppermute | solution.py:22
  85.4 2.2 %collective-permute-start.20 = (f32[4,112,384]{2,1,0:T(8,128)S(1)}, f32[4,112,384]{2,1,0:T(8,128)S(1)}, u32[]{:S(2)}, u32[]{:S(2)}) collective-permute-start(f32[4,112,384]{2,1,0:T(8,128)S(1)} %get-tuple-element.44), channel_id=1, source_target_pairs={{0,1},{1,0},{2,3},{3,2},{4,5},{5,4},{6,7},{7,6},{8,9},{9,8},{10,11... | collective-permute-start | bytes 2064392 | tf_op jit(solution)/shard_map/ppermute | solution.py:22
  85.8 5.5 %collective-permute-start.24 = (bf16[96,384]{1,0:T(8,128)(2,1)S(1)}, bf16[96,384]{1,0:T(8,128)(2,1)S(1)}, u32[]{:S(2)}, u32[]{:S(2)}) collective-permute-start(bf16[96,384]{1,0:T(8,128)(2,1)S(1)} %slice_bitcast_fusion.8), channel_id=1, source_target_pairs={{0,8},{1,9},{2,10},{3,11},{4,12},{5,13},{6,14},{7,15},{8,0},{9,1},... | collective-permute-start | bytes 221192 | tf_op jit(solution)/shard_map/ppermute | solution.py:22
  87.8 6.3 %collective-permute-start.23 = (bf16[112,384]{1,0:T(8,128)(2,1)S(1)}, bf16[112,384]{1,0:T(8,128)(2,1)S(1)}, u32[]{:S(2)}, u32[]{:S(2)}) collective-permute-start(bf16[112,384]{1,0:T(8,128)(2,1)S(1)} %get-tuple-element.50), channel_id=1, source_target_pairs={{0,10},{1,11},{2,8},{3,9},{4,14},{5,15},{6,12},{7,13},{8,2},{9,3},... | collective-permute-start | bytes 258056 | tf_op jit(solution)/shard_map/ppermute | solution.py:22
  89.1 6.0 %collective-permute-start.22 = (bf16[112,384]{1,0:T(8,128)(2,1)S(1)}, bf16[112,384]{1,0:T(8,128)(2,1)S(1)}, u32[]{:S(2)}, u32[]{:S(2)}) collective-permute-start(bf16[112,384]{1,0:T(8,128)(2,1)S(1)} %get-tuple-element.51), channel_id=1, source_target_pairs={{0,8},{1,9},{2,10},{3,11},{4,12},{5,13},{6,14},{7,15},{8,0},{9,1},... | collective-permute-start | bytes 258056 | tf_op jit(solution)/shard_map/ppermute | solution.py:22
  90.5 4.9 %collective-permute-start.21 = (bf16[112,384]{1,0:T(8,128)(2,1)S(1)}, bf16[112,384]{1,0:T(8,128)(2,1)S(1)}, u32[]{:S(2)}, u32[]{:S(2)}) collective-permute-start(bf16[112,384]{1,0:T(8,128)(2,1)S(1)} %get-tuple-element.52), channel_id=1, source_target_pairs={{0,2},{1,3},{2,0},{3,1},{4,6},{5,7},{6,4},{7,5},{8,10},{9,11},{10,... | collective-permute-start | bytes 258056 | tf_op jit(solution)/shard_map/ppermute | solution.py:22
  (8 other events, 47.8 us)

commit v9 on v8

--- a/solution.py
+++ b/solution.py
@@ -510,9 +510,9 @@
     )(
         plan,
         summed[0],
-        exchange(summed[1].astype(bf16), XBIT),
+        exchange(summed[1, :half].astype(bf16), XBIT),
         exchange(summed[2].astype(bf16), ZBIT),
-        exchange(summed[3].astype(bf16), XBIT | ZBIT),
+        exchange(summed[3, :half].astype(bf16), XBIT | ZBIT),
         image_tiles,
         got_tile,
     )

time: 97.2 us -> 96.6 us (level)
  transfers between devices with their start and end apart: 25 -> 25, of which waited for: 16 -> 15; matrix products, arithmetic and copies ran while one was open for 7% -> 7% of each run, Pallas kernels for 11% -> 11%
where the time goes in v9:
time: 96.6 us; the launch traced here: 96.3 us
  waiting for transfers between devices  34.4 us (36%)
  starting transfers between devices  30.8 us (32%)
  Pallas kernels  18.6 us (19%)
  local copies, waits for them, and re-layouts  9.36 us (10%)
  other arithmetic  2.09 us (2%)
  between operations  1.01 us (1%)
    ppermute x23, waiting for transfers between devices, exchange(): lax.ppermute(block, 'sec', [(i, i ^ flip) for i in range(lax.axis_size('s...  34.4 us
    ppermute x23, starting transfers between devices, exchange(): lax.ppermute(block, 'sec', [(i, i ^ flip) for i in range(lax.axis_size('s...  26 us
    pallas_call x1, Pallas kernels, on_device(): pl.pallas_call(lambda *refs: start_kernel(sectors, *refs), out_shape=[sha...  4.81 us
    ppermute x2, starting transfers between devices, spread(): return lax.ppermute(tile, 'sec', route)  4.75 us
    pallas_call x1, Pallas kernels, on_device(): pl.pallas_call(lambda *refs: second_kernel(sectors, *refs), out_shape=[sh...  3.91 us
    unnamed x14, local copies, waits for them, and re-layouts  3.17 us
    pallas_call x1, Pallas kernels, on_device(): pl.pallas_call(lambda *refs: peer_kernel(sectors, *refs), out_shape=[mixe...  2.72 us
    slice x1, local copies, waits for them, and re-layouts, on_device(): right_late = exchange(right_environment[early:], YBIT)  2.63 us
  transfers between devices with their start and end apart: 25, of which 15 were waited for; matrix products, arithmetic and copies ran while one was open for 7% of the time, Pallas kernels for 11%

profile of v9, /device:TPU:0, one launch (start us, length us, event | category | flops | bytes accessed | tf_op | source)
XLA Modules:
  0.0 96.3 jit_solution(15497235446808155736)
XLA Ops:
  2.2 4.1 %collective-permute-start.1 = (bf16[96,384]{1,0:T(8,128)(2,1)S(1)}, bf16[96,384]{1,0:T(8,128)(2,1)S(1)}, u32[]{:S(2)}, u32[]{:S(2)}) collective-permute-start(bf16[96,384]{1,0:T(8,128)(2,1)S(1)} %pad_maximum_fusion.4), channel_id=1, source_target_pairs={{0,16},{1,17},{2,26},{3,27},{4,20},{5,21},{6,30},{7,31},{8,18},{9,... | collective-permute-start | bytes 221192 | tf_op jit(solution)/shard_map/ppermute | solution.py:31
  7.3 1.6 %collective-permute-start.3 = (bf16[1,192,768]{2,1,0:T(8,128)(2,1)S(1)}, bf16[1,192,768]{2,1,0:T(8,128)(2,1)S(1)}, u32[]{:S(2)}, u32[]{:S(2)}) collective-permute-start(bf16[1,192,768]{2,1,0:T(8,128)(2,1)S(1)} %slice.55), channel_id=1, source_target_pairs={{0,4},{1,5},{2,6},{3,7},{4,0},{5,1},{6,2},{7,3},{8,12},{9,13},{10,... | collective-permute-start | bytes 884744 | tf_op jit(solution)/shard_map/ppermute | solution.py:22
  8.9 4.3 %collective-permute-start.6 = (bf16[6,192,768]{2,1,0:T(8,128)(2,1)}, bf16[6,192,768]{2,1,0:T(8,128)(2,1)S(1)}, u32[]{:S(2)}, u32[]{:S(2)}) collective-permute-start(bf16[6,192,768]{2,1,0:T(8,128)(2,1)} %refs_3_.1), channel_id=1, source_target_pairs={{0,8},{1,9},{2,10},{3,11},{4,12},{5,13},{6,14},{7,15},{8,0},{9,1},... | collective-permute-start | bytes 5308424 | tf_op jit(solution)/shard_map/ppermute | solution.py:22
  14.2 2.6 %slice.56 = bf16[5,192,768]{2,1,0:T(8,128)(2,1)} slice(bf16[6,192,768]{2,1,0:T(8,128)(2,1)} %refs_4_.1), slice={[1:6], [0:192], [0:768]} | slice | bytes 2949120 | tf_op jit(solution)/shard_map/slice | solution.py:396
  17.9 2.2 %collective-permute-done.2 = bf16[2,96,384]{2,1,0:T(8,128)(2,1)S(1)} collective-permute-done((bf16[2,96,384]{2,1,0:T(8,128)(2,1)S(1)}, bf16[2,96,384]{2,1,0:T(8,128)(2,1)S(1)}, u32[]{:S(2)}, u32[]{:S(2)}) %collective-permute-start.2) | collective-permute-done | bytes 147488 | tf_op jit(solution)/shard_map/ppermute | solution.py:22
  20.9 1.7 %collective-permute-start.4 = (bf16[2,2,96,384]{3,2,1,0:T(8,128)(2,1)S(1)}, bf16[2,2,96,384]{3,2,1,0:T(8,128)(2,1)S(1)}, u32[]{:S(2)}, u32[]{:S(2)}) collective-permute-start(bf16[2,2,96,384]{3,2,1,0:T(8,128)(2,1)S(1)} %pad_maximum_fusion.2), channel_id=1, source_target_pairs={{0,2},{1,3},{2,0},{3,1},{4,6},{5,7},{6,4},{7,5},{8,10},{9,11},{10,... | collective-permute-start | bytes 884744 | tf_op jit(solution)/shard_map/ppermute | solution.py:22
  22.7 5.6 %collective-permute-done.4 = bf16[2,2,96,384]{3,2,1,0:T(8,128)(2,1)S(1)} collective-permute-done((bf16[2,2,96,384]{3,2,1,0:T(8,128)(2,1)S(1)}, bf16[2,2,96,384]{3,2,1,0:T(8,128)(2,1)S(1)}, u32[]{:S(2)}, u32[]{:S(2)}) %collective-permute-start.4) | collective-permute-done | bytes 294944 | tf_op jit(solution)/shard_map/ppermute | solution.py:22
  32.6 1.5 %copy-done.4 = bf16[6,192,768]{2,1,0:T(8,128)(2,1)S(1)} copy-done((bf16[6,192,768]{2,1,0:T(8,128)(2,1)S(1)}, bf16[6,192,768]{2,1,0:T(8,128)(2,1)}, u32[]{:S(2)}) %copy-start.4) | copy-done | bytes 1769496
  34.0 4.8 %shard_map.86 = (bf16[2,768,384]{2,1,0:T(8,128)(2,1)S(1)}, bf16[2,192,1152]{2,1,0:T(8,128)(2,1)S(1)}, f32[192,768]{1,0:T(8,128)S(1)}, f32[8,128]{1,0:T(8,128)S(1...) custom-call(s32[21]{0:T(128)S(1)} %concatenate.18.refs_0_.plan, ...), custom_call_target="tpu_custom_call" | custom-call | flops 2038431744 | bytes 3538944 | tf_op jit(solution)/shard_map/pallas_call | solution.py:411
  38.8 12.8 %collective-permute-done.6.refs_3_ = bf16[6,192,768]{2,1,0:T(8,128)(2,1)S(1)} collective-permute-done((bf16[6,192,768]{2,1,0:T(8,128)(2,1)}, bf16[6,192,768]{2,1,0:T(8,128)(2,1)S(1)}, u32[]{:S(2)}, u32[]{:S(2)}) %collective-permute-start.6) | collective-permute-done | bytes 1769504 | tf_op jit(solution)/shard_map/ppermute | solution.py:22
  51.7 2.7 %shard_map.87 = (bf16[2,192,1152]{2,1,0:T(8,128)(2,1)S(1)}, f32[192,768]{1,0:T(8,128)S(1)}, bf16[6,384,768]{2,1,0:T(8,128)(2,1)S(1)}) custom-call(s32[21]{0:T(128)S(1)} %concatenate.18.refs_0_.plan, bf16[2,768,384]{2,1,0:T(8,128)(2,1)S(1)} %get-tuple-element.28.refs_1_, bf16[6,192,768]{2,1,0:T(8,128)(2,1)S(1)} %get-tuple-element.30.refs_2_, ...), custom_call_target="tpu_custom_call" | custom-call | flops 679477248 | bytes 3538944 | tf_op jit(solution)/shard_map/pallas_call | solution.py:427
  54.4 2.3 %shard_map.88 = (f32[4,96,384]{2,1,0:T(8,128)S(1)}, bf16[5,192,768]{2,1,0:T(8,128)(2,1)S(1)}) custom-call(s32[21]{0:T(128)S(1)} %concatenate.18.refs_0_.plan, bf16[2,192,1152]{2,1,0:T(8,128)(2,1)S(1)} %get-tuple-element.29.mixed_own, bf16[2,192,1152]{2,1,0:T(8,128)(2,1)S(1)} %get-tuple-element.33.mixed_peer, f32[192,768]{1,0:T(8,128)S(1)} %get-tuple-element.34.before_own, ...), custom_call_target="tpu_custom_call" | custom-call | flops 679477248 | bytes 3538944 | tf_op jit(solution)/shard_map/pallas_call | solution.py:437
  56.9 1.5 %shard_map.89 = (f32[4,96,384]{2,1,0:T(8,128)S(1)}, bf16[6,384,768]{2,1,0:T(8,128)(2,1)S(1)}) custom-call(s32[21]{0:T(128)S(1)} %concatenate.18.refs_0_.plan, bf16[2,192,1152]{2,1,0:T(8,128)(2,1)S(1)} %get-tuple-element.29.mixed_own, bf16[2,192,1152]{2,1,0:T(8,128)(2,1)S(1)} %get-tuple-element.33.mixed_peer, f32[192,768]{1,0:T(8,128)S(1)} %get-tuple-element.34.before_own, ...), custom_call_target="tpu_custom_call" | custom-call | flops 679477248 | bytes 3538944 | tf_op jit(solution)/shard_map/pallas_call | solution.py:446
  59.9 1.8 %collective-permute-start.11 = (bf16[96,384]{1,0:T(8,128)(2,1)S(1)}, bf16[96,384]{1,0:T(8,128)(2,1)S(1)}, u32[]{:S(2)}, u32[]{:S(2)}) collective-permute-start(bf16[96,384]{1,0:T(8,128)(2,1)S(1)} %get-tuple-element.53), channel_id=1, source_target_pairs={{0,10},{1,11},{2,8},{3,9},{4,14},{5,15},{6,12},{7,13},{8,2},{9,3},... | collective-permute-start | bytes 221192 | tf_op jit(solution)/shard_map/ppermute | solution.py:22
  62.5 1.7 %collective-permute-done.9 = bf16[96,384]{1,0:T(8,128)(2,1)S(1)} collective-permute-done((bf16[96,384]{1,0:T(8,128)(2,1)S(1)}, bf16[96,384]{1,0:T(8,128)(2,1)S(1)}, u32[]{:S(2)}, u32[]{:S(2)}) %collective-permute-start.9) | collective-permute-done | bytes 73760 | tf_op jit(solution)/shard_map/ppermute | solution.py:22
  64.2 1.5 %collective-permute-done.11 = bf16[96,384]{1,0:T(8,128)(2,1)S(1)} collective-permute-done((bf16[96,384]{1,0:T(8,128)(2,1)S(1)}, bf16[96,384]{1,0:T(8,128)(2,1)S(1)}, u32[]{:S(2)}, u32[]{:S(2)}) %collective-permute-start.11) | collective-permute-done | bytes 73760 | tf_op jit(solution)/shard_map/ppermute | solution.py:22
  67.4 2.4 %collective-permute-start.17 = (bf16[1,96,384]{2,1,0:T(8,128)(2,1)S(1)}, bf16[1,96,384]{2,1,0:T(8,128)(2,1)S(1)}, u32[]{:S(2)}, u32[]{:S(2)}) collective-permute-start(bf16[1,96,384]{2,1,0:T(8,128)(2,1)S(1)} %fusion.4), channel_id=1, source_target_pairs={{0,6},{1,7},{2,4},{3,5},{4,2},{5,3},{6,0},{7,1},{8,14},{9,15},{10,... | collective-permute-start | bytes 221192 | tf_op jit(solution)/shard_map/ppermute | solution.py:22
  70.9 1.5 %collective-permute-done.12 = bf16[1,96,384]{2,1,0:T(8,128)(2,1)S(1)} collective-permute-done((bf16[1,96,384]{2,1,0:T(8,128)(2,1)S(1)}, bf16[1,96,384]{2,1,0:T(8,128)(2,1)S(1)}, u32[]{:S(2)}, u32[]{:S(2)}) %collective-permute-start.12) | collective-permute-done | bytes 73760 | tf_op jit(solution)/shard_map/ppermute | solution.py:22
  72.4 1.6 %collective-permute-start.18 = (bf16[1,96,384]{2,1,0:T(8,128)(2,1)S(1)}, bf16[1,96,384]{2,1,0:T(8,128)(2,1)S(1)}, u32[]{:S(2)}, u32[]{:S(2)}) collective-permute-start(bf16[1,96,384]{2,1,0:T(8,128)(2,1)S(1)} %collective-permute-done.12), channel_id=1, source_target_pairs={{0,6},{1,7},{2,4},{3,5},{4,2},{5,3},{6,0},{7,1},{8,14},{9,15},{10,... | collective-permute-start | bytes 221192 | tf_op jit(solution)/shard_map/ppermute | solution.py:22
  76.0 1.7 %collective-permute-done.18 = bf16[1,96,384]{2,1,0:T(8,128)(2,1)S(1)} collective-permute-done((bf16[1,96,384]{2,1,0:T(8,128)(2,1)S(1)}, bf16[1,96,384]{2,1,0:T(8,128)(2,1)S(1)}, u32[]{:S(2)}, u32[]{:S(2)}) %collective-permute-start.18) | collective-permute-done | bytes 73760 | tf_op jit(solution)/shard_map/ppermute | solution.py:22
  79.5 1.9 %shard_map.90 = (f32[6,384,384]{2,1,0:T(8,128)S(1)}, f32[2,8,128]{2,1,0:T(8,128)S(1)}) custom-call(s32[21]{0:T(128)S(1)} %concatenate.18.refs_0_.plan, bf16[2,768,384]{2,1,0:T(8,128)(2,1)S(1)} %get-tuple-element.28.refs_1_, bf16[4,2,96,384]{3,2,1,0:T(8,128)(2,1)S(1)} %pad_maximum_fusion.1.refs_2_.refs_4_, ...), custom_call_target="tpu_custom_call" | custom-call | flops 679477248 | bytes 3538944 | tf_op jit(solution)/shard_map/pallas_call | solution.py:480
  81.5 3.9 %shard_map.91 = (f32[4,112,384]{2,1,0:T(8,128)S(1)}, f32[4,112,384]{2,1,0:T(8,128)S(1)}, bf16[2,96,384]{2,1,0:T(8,128)(2,1)S(1)}) custom-call(s32[21]{0:T(128)S(1)} %concatenate.18.refs_0_.plan, f32[8,128]{1,0:T(8,128)S(1)} %get-tuple-element.27.refs_1_, f32[2,8,128]{2,1,0:T(8,128)S(1)} %get-tuple-element.40.refs_2_, ...), custom_call_target="tpu_custom_call" | custom-call | flops 2038431744 | bytes 3538944 | tf_op jit(solution)/shard_map/pallas_call | solution.py:489
  89.7 1.6 %collective-permute-start.22 = (bf16[112,384]{1,0:T(8,128)(2,1)S(1)}, bf16[112,384]{1,0:T(8,128)(2,1)S(1)}, u32[]{:S(2)}, u32[]{:S(2)}) collective-permute-start(bf16[112,384]{1,0:T(8,128)(2,1)S(1)} %slice_bitcast_fusion.2), channel_id=1, source_target_pairs={{0,8},{1,9},{2,10},{3,11},{4,12},{5,13},{6,14},{7,15},{8,0},{9,1},... | collective-permute-start | bytes 258056 | tf_op jit(solution)/shard_map/ppermute | solution.py:22
  91.3 2.3 %collective-permute-done.23.from_xz = bf16[96,384]{1,0:T(8,128)(2,1)S(1)} collective-permute-done((bf16[96,384]{1,0:T(8,128)(2,1)S(1)}, bf16[96,384]{1,0:T(8,128)(2,1)S(1)}, u32[]{:S(2)}, u32[]{:S(2)}) %collective-permute-start.23) | collective-permute-done | bytes 73760 | tf_op jit(solution)/shard_map/ppermute | solution.py:22
  (77 shorter events, 25.6 us)
Async XLA Ops:
  1.6 7.3 %collective-permute-start = (bf16[96,384]{1,0:T(8,128)(2,1)S(1)}, bf16[96,384]{1,0:T(8,128)(2,1)S(1)}, u32[]{:S(2)}, u32[]{:S(2)}) collective-permute-start(bf16[96,384]{1,0:T(8,128)(2,1)S(1)} %pad_maximum_fusion.4), channel_id=1, source_target_pairs={{0,0},{1,1},{2,8},{3,9},{4,4},{5,5},{6,12},{7,13},{8,2},{9,3},{10,... | collective-permute-start | bytes 221192 | tf_op jit(solution)/shard_map/ppermute | solution.py:31
  2.2 10.9 %collective-permute-start.1 = (bf16[96,384]{1,0:T(8,128)(2,1)S(1)}, bf16[96,384]{1,0:T(8,128)(2,1)S(1)}, u32[]{:S(2)}, u32[]{:S(2)}) collective-permute-start(bf16[96,384]{1,0:T(8,128)(2,1)S(1)} %pad_maximum_fusion.4), channel_id=1, source_target_pairs={{0,16},{1,17},{2,26},{3,27},{4,20},{5,21},{6,30},{7,31},{8,18},{9,... | collective-permute-start | bytes 221192 | tf_op jit(solution)/shard_map/ppermute | solution.py:31
  7.3 12.9 %collective-permute-start.3 = (bf16[1,192,768]{2,1,0:T(8,128)(2,1)S(1)}, bf16[1,192,768]{2,1,0:T(8,128)(2,1)S(1)}, u32[]{:S(2)}, u32[]{:S(2)}) collective-permute-start(bf16[1,192,768]{2,1,0:T(8,128)(2,1)S(1)} %slice.55), channel_id=1, source_target_pairs={{0,4},{1,5},{2,6},{3,7},{4,0},{5,1},{6,2},{7,3},{8,12},{9,13},{10,... | collective-permute-start | bytes 884744 | tf_op jit(solution)/shard_map/ppermute | solution.py:22
  8.9 42.8 %collective-permute-start.6 = (bf16[6,192,768]{2,1,0:T(8,128)(2,1)}, bf16[6,192,768]{2,1,0:T(8,128)(2,1)S(1)}, u32[]{:S(2)}, u32[]{:S(2)}) collective-permute-start(bf16[6,192,768]{2,1,0:T(8,128)(2,1)} %refs_3_.1), channel_id=1, source_target_pairs={{0,8},{1,9},{2,10},{3,11},{4,12},{5,13},{6,14},{7,15},{8,0},{9,1},... | collective-permute-start | bytes 5308424 | tf_op jit(solution)/shard_map/ppermute | solution.py:22
  13.2 6.9 %collective-permute-start.2 = (bf16[2,96,384]{2,1,0:T(8,128)(2,1)S(1)}, bf16[2,96,384]{2,1,0:T(8,128)(2,1)S(1)}, u32[]{:S(2)}, u32[]{:S(2)}) collective-permute-start(bf16[2,96,384]{2,1,0:T(8,128)(2,1)S(1)} %get-tuple-element.56), channel_id=1, source_target_pairs={{0,4},{1,5},{2,6},{3,7},{4,0},{5,1},{6,2},{7,3},{8,12},{9,13},{10,... | collective-permute-start | bytes 442376 | tf_op jit(solution)/shard_map/ppermute | solution.py:22
  16.9 37.6 %collective-permute-start.7 = (bf16[5,192,768]{2,1,0:T(8,128)(2,1)}, bf16[5,192,768]{2,1,0:T(8,128)(2,1)}, u32[]{:S(2)}, u32[]{:S(2)}) collective-permute-start(bf16[5,192,768]{2,1,0:T(8,128)(2,1)} %slice.56), channel_id=1, source_target_pairs={{0,4},{1,5},{2,6},{3,7},{4,0},{5,1},{6,2},{7,3},{8,12},{9,13},{10,... | collective-permute-start | bytes 4423688 | tf_op jit(solution)/shard_map/ppermute | solution.py:22
  20.9 7.3 %collective-permute-start.4 = (bf16[2,2,96,384]{3,2,1,0:T(8,128)(2,1)S(1)}, bf16[2,2,96,384]{3,2,1,0:T(8,128)(2,1)S(1)}, u32[]{:S(2)}, u32[]{:S(2)}) collective-permute-start(bf16[2,2,96,384]{3,2,1,0:T(8,128)(2,1)S(1)} %pad_maximum_fusion.2), channel_id=1, source_target_pairs={{0,2},{1,3},{2,0},{3,1},{4,6},{5,7},{6,4},{7,5},{8,10},{9,11},{10,... | collective-permute-start | bytes 884744 | tf_op jit(solution)/shard_map/ppermute | solution.py:22
  29.1 2.5 %collective-permute-start.5 = (bf16[2,2,2,96,384]{4,3,2,1,0:T(8,128)(2,1)}, bf16[2,2,2,96,384]{4,3,2,1,0:T(8,128)(2,1)}, u32[]{:S(2)}, u32[]{:S(2)}) collective-permute-start(bf16[2,2,2,96,384]{4,3,2,1,0:T(8,128)(2,1)} %pad_maximum_fusion.refs_1_), channel_id=1, source_target_pairs={{0,1},{1,0},{2,3},{3,2},{4,5},{5,4},{6,7},{7,6},{8,9},{9,8},{10,11... | collective-permute-start | bytes 1769480 | tf_op jit(solution)/shard_map/ppermute | solution.py:22
  56.8 2.1 %collective-permute-start.8 = (f32[4,96,384]{2,1,0:T(8,128)S(1)}, f32[4,96,384]{2,1,0:T(8,128)S(1)}, u32[]{:S(2)}, u32[]{:S(2)}) collective-permute-start(f32[4,96,384]{2,1,0:T(8,128)S(1)} %get-tuple-element.38), channel_id=1, source_target_pairs={{0,1},{1,0},{2,3},{3,2},{4,5},{5,4},{6,7},{7,6},{8,9},{9,8},{10,11... | collective-permute-start | bytes 1769480 | tf_op jit(solution)/shard_map/ppermute | solution.py:22
  59.0 5.2 %collective-permute-start.9 = (bf16[96,384]{1,0:T(8,128)(2,1)S(1)}, bf16[96,384]{1,0:T(8,128)(2,1)S(1)}, u32[]{:S(2)}, u32[]{:S(2)}) collective-permute-start(bf16[96,384]{1,0:T(8,128)(2,1)S(1)} %get-tuple-element.52), channel_id=1, source_target_pairs={{0,2},{1,3},{2,0},{3,1},{4,6},{5,7},{6,4},{7,5},{8,10},{9,11},{10,... | collective-permute-start | bytes 221192 | tf_op jit(solution)/shard_map/ppermute | solution.py:22
  59.9 5.8 %collective-permute-start.11 = (bf16[96,384]{1,0:T(8,128)(2,1)S(1)}, bf16[96,384]{1,0:T(8,128)(2,1)S(1)}, u32[]{:S(2)}, u32[]{:S(2)}) collective-permute-start(bf16[96,384]{1,0:T(8,128)(2,1)S(1)} %get-tuple-element.53), channel_id=1, source_target_pairs={{0,10},{1,11},{2,8},{3,9},{4,14},{5,15},{6,12},{7,13},{8,2},{9,3},... | collective-permute-start | bytes 221192 | tf_op jit(solution)/shard_map/ppermute | solution.py:22
  61.7 4.5 %collective-permute-start.10 = (bf16[96,384]{1,0:T(8,128)(2,1)S(1)}, bf16[96,384]{1,0:T(8,128)(2,1)S(1)}, u32[]{:S(2)}, u32[]{:S(2)}) collective-permute-start(bf16[96,384]{1,0:T(8,128)(2,1)S(1)} %get-tuple-element.54), channel_id=1, source_target_pairs={{0,8},{1,9},{2,10},{3,11},{4,12},{5,13},{6,14},{7,15},{8,0},{9,1},... | collective-permute-start | bytes 221192 | tf_op jit(solution)/shard_map/ppermute | solution.py:22
  66.3 6.1 %collective-permute-start.12 = (bf16[1,96,384]{2,1,0:T(8,128)(2,1)S(1)}, bf16[1,96,384]{2,1,0:T(8,128)(2,1)S(1)}, u32[]{:S(2)}, u32[]{:S(2)}) collective-permute-start(bf16[1,96,384]{2,1,0:T(8,128)(2,1)S(1)} %fusion.4), channel_id=1, source_target_pairs={{0,16},{1,17},{2,18},{3,19},{4,20},{5,21},{6,22},{7,23},{8,24},{9,... | collective-permute-start | bytes 221192 | tf_op jit(solution)/shard_map/ppermute | solution.py:22
  67.4 7.5 %collective-permute-start.17 = (bf16[1,96,384]{2,1,0:T(8,128)(2,1)S(1)}, bf16[1,96,384]{2,1,0:T(8,128)(2,1)S(1)}, u32[]{:S(2)}, u32[]{:S(2)}) collective-permute-start(bf16[1,96,384]{2,1,0:T(8,128)(2,1)S(1)} %fusion.4), channel_id=1, source_target_pairs={{0,6},{1,7},{2,4},{3,5},{4,2},{5,3},{6,0},{7,1},{8,14},{9,15},{10,... | collective-permute-start | bytes 221192 | tf_op jit(solution)/shard_map/ppermute | solution.py:22
  69.8 7.8 %collective-permute-start.15 = (bf16[1,96,384]{2,1,0:T(8,128)(2,1)S(1)}, bf16[1,96,384]{2,1,0:T(8,128)(2,1)S(1)}, u32[]{:S(2)}, u32[]{:S(2)}) collective-permute-start(bf16[1,96,384]{2,1,0:T(8,128)(2,1)S(1)} %fusion.4), channel_id=1, source_target_pairs={{0,2},{1,3},{2,0},{3,1},{4,6},{5,7},{6,4},{7,5},{8,10},{9,11},{10,... | collective-permute-start | bytes 221192 | tf_op jit(solution)/shard_map/ppermute | solution.py:22
  70.4 8.0 %collective-permute-start.13 = (bf16[1,96,384]{2,1,0:T(8,128)(2,1)S(1)}, bf16[1,96,384]{2,1,0:T(8,128)(2,1)S(1)}, u32[]{:S(2)}, u32[]{:S(2)}) collective-permute-start(bf16[1,96,384]{2,1,0:T(8,128)(2,1)S(1)} %fusion.4), channel_id=1, source_target_pairs={{0,4},{1,5},{2,6},{3,7},{4,0},{5,1},{6,2},{7,3},{8,12},{9,13},{10,... | collective-permute-start | bytes 221192 | tf_op jit(solution)/shard_map/ppermute | solution.py:22
  72.4 5.3 %collective-permute-start.18 = (bf16[1,96,384]{2,1,0:T(8,128)(2,1)S(1)}, bf16[1,96,384]{2,1,0:T(8,128)(2,1)S(1)}, u32[]{:S(2)}, u32[]{:S(2)}) collective-permute-start(bf16[1,96,384]{2,1,0:T(8,128)(2,1)S(1)} %collective-permute-done.12), channel_id=1, source_target_pairs={{0,6},{1,7},{2,4},{3,5},{4,2},{5,3},{6,0},{7,1},{8,14},{9,15},{10,... | collective-permute-start | bytes 221192 | tf_op jit(solution)/shard_map/ppermute | solution.py:22
  74.0 4.4 %collective-permute-start.16 = (bf16[1,96,384]{2,1,0:T(8,128)(2,1)S(1)}, bf16[1,96,384]{2,1,0:T(8,128)(2,1)S(1)}, u32[]{:S(2)}, u32[]{:S(2)}) collective-permute-start(bf16[1,96,384]{2,1,0:T(8,128)(2,1)S(1)} %collective-permute-done.12), channel_id=1, source_target_pairs={{0,2},{1,3},{2,0},{3,1},{4,6},{5,7},{6,4},{7,5},{8,10},{9,11},{10,... | collective-permute-start | bytes 221192 | tf_op jit(solution)/shard_map/ppermute | solution.py:22
  74.9 4.4 %collective-permute-start.14 = (bf16[1,96,384]{2,1,0:T(8,128)(2,1)S(1)}, bf16[1,96,384]{2,1,0:T(8,128)(2,1)S(1)}, u32[]{:S(2)}, u32[]{:S(2)}) collective-permute-start(bf16[1,96,384]{2,1,0:T(8,128)(2,1)S(1)} %collective-permute-done.12), channel_id=1, source_target_pairs={{0,4},{1,5},{2,6},{3,7},{4,0},{5,1},{6,2},{7,3},{8,12},{9,13},{10,... | collective-permute-start | bytes 221192 | tf_op jit(solution)/shard_map/ppermute | solution.py:22
  85.4 2.2 %collective-permute-start.20 = (f32[4,112,384]{2,1,0:T(8,128)S(1)}, f32[4,112,384]{2,1,0:T(8,128)S(1)}, u32[]{:S(2)}, u32[]{:S(2)}) collective-permute-start(f32[4,112,384]{2,1,0:T(8,128)S(1)} %get-tuple-element.44), channel_id=1, source_target_pairs={{0,1},{1,0},{2,3},{3,2},{4,5},{5,4},{6,7},{7,6},{8,9},{9,8},{10,11... | collective-permute-start | bytes 2064392 | tf_op jit(solution)/shard_map/ppermute | solution.py:22
  85.8 5.5 %collective-permute-start.24 = (bf16[96,384]{1,0:T(8,128)(2,1)S(1)}, bf16[96,384]{1,0:T(8,128)(2,1)S(1)}, u32[]{:S(2)}, u32[]{:S(2)}) collective-permute-start(bf16[96,384]{1,0:T(8,128)(2,1)S(1)} %slice_bitcast_fusion.8), channel_id=1, source_target_pairs={{0,8},{1,9},{2,10},{3,11},{4,12},{5,13},{6,14},{7,15},{8,0},{9,1},... | collective-permute-start | bytes 221192 | tf_op jit(solution)/shard_map/ppermute | solution.py:22
  87.7 5.9 %collective-permute-start.23 = (bf16[96,384]{1,0:T(8,128)(2,1)S(1)}, bf16[96,384]{1,0:T(8,128)(2,1)S(1)}, u32[]{:S(2)}, u32[]{:S(2)}) collective-permute-start(bf16[96,384]{1,0:T(8,128)(2,1)S(1)} %get-tuple-element.50), channel_id=1, source_target_pairs={{0,10},{1,11},{2,8},{3,9},{4,14},{5,15},{6,12},{7,13},{8,2},{9,3},... | collective-permute-start | bytes 221192 | tf_op jit(solution)/shard_map/ppermute | solution.py:22
  89.0 5.8 %collective-permute-start.21 = (bf16[96,384]{1,0:T(8,128)(2,1)S(1)}, bf16[96,384]{1,0:T(8,128)(2,1)S(1)}, u32[]{:S(2)}, u32[]{:S(2)}) collective-permute-start(bf16[96,384]{1,0:T(8,128)(2,1)S(1)} %get-tuple-element.51), channel_id=1, source_target_pairs={{0,2},{1,3},{2,0},{3,1},{4,6},{5,7},{6,4},{7,5},{8,10},{9,11},{10,... | collective-permute-start | bytes 221192 | tf_op jit(solution)/shard_map/ppermute | solution.py:22
  89.7 5.1 %collective-permute-start.22 = (bf16[112,384]{1,0:T(8,128)(2,1)S(1)}, bf16[112,384]{1,0:T(8,128)(2,1)S(1)}, u32[]{:S(2)}, u32[]{:S(2)}) collective-permute-start(bf16[112,384]{1,0:T(8,128)(2,1)S(1)} %slice_bitcast_fusion.2), channel_id=1, source_target_pairs={{0,8},{1,9},{2,10},{3,11},{4,12},{5,13},{6,14},{7,15},{8,0},{9,1},... | collective-permute-start | bytes 258056 | tf_op jit(solution)/shard_map/ppermute | solution.py:22
  (8 other events, 47.8 us)
